TPU v7x, 128 devices: a whole 4x4x4 slice. The times are simulated.
128 devices in a mesh: gx: 8 (over x_lo, y), gy: 16 (over z, x_hi, core).
Axes of the slice: x: 4 (x_hi: 2, x_lo: 2; x = x_hi * 2 + x_lo), y: 4, z: 4, core: 2. Of those that a mesh axis runs over, the one named last changes fastest.
Arguments:
- log_dens: float32 [8, 256, 32768], P(None, 'gx', 'gy'), may hold values from -5 to 5
- theta: float32 [8], replicated, may hold values from -4 to 4
- cotangent: float32 [256, 32768], P('gx', 'gy'), may hold values from -6 to 6
Outputs:
- barycenter: float32 [256, 32768], P('gx', 'gy')
- grad_dens: float32 [8, 256, 32768], P(None, 'gx', 'gy')
- grad_theta: float32 [8], replicated
All inputs are finite; a program needn't handle non-finite values.
Results may differ from a plain program's by a relative error of at most 0.0003.
Values sent between devices are 32-bit elements; how exact they have to be, the bound alone decides.
No kernel may reach another device: no remote copies, remote signals or barrier semaphores. Data moves between devices by JAX's collectives and lax.ppermute only.
A program may use at most 192 MiB of HBM per device.

v0:
```python
import math

import jax
import jax.numpy as jnp
from jax import lax
from jax.sharding import PartitionSpec as P

ITERS = 2
NZ = 64


def with_halo(shard, sides, width):
    for axis, dim in sides:
        count, length = (lax.axis_size(axis), shard.shape[dim])
        up = [(i, (i + 1) % count) for i in range(count - 1)]
        down = [(j, i) for i, j in up]
        last = lax.slice_in_dim(shard, length - width, length, axis=dim)
        leading = lax.slice_in_dim(shard, 0, width, axis=dim)
        before = lax.ppermute(last, axis, up)
        after = lax.ppermute(leading, axis, down)
        shard = jnp.concatenate([before, shard, after], axis=dim)
    return shard


def tap_list():
    raw_taps = [math.exp(-(offset * offset) / 8.0) for offset in range(-4, 5)]
    tap_total = 0.0
    for value in raw_taps:
        tap_total = tap_total + value
    return [value / tap_total for value in raw_taps]


def band_matrix(depth):
    row_index = jnp.arange(depth, dtype=jnp.int32)[:, None]
    col_index = jnp.arange(depth, dtype=jnp.int32)[None, :]
    offsets = row_index - col_index
    result = jnp.zeros((depth, depth), jnp.float32)
    for position, weight in enumerate(tap_list()):
        result = result + weight * (offsets == position - 4).astype(jnp.float32)
    return result


def smooth_field(values, matrix):
    taps = tap_list()
    count_k, width_x, merged = values.shape
    width_y = merged // NZ
    padded = with_halo(values, (("gx", 1),), 4)
    along_x = taps[0] * padded[:, 0:width_x]
    for position in range(1, 9):
        along_x = along_x + taps[position] * padded[:, position : position + width_x]
    padded_y = with_halo(along_x, (("gy", 2),), 4 * NZ)
    flat_y = taps[0] * padded_y[:, :, 0:merged]
    for position in range(1, 9):
        flat_y = flat_y + taps[position] * padded_y[:, :, position * NZ : position * NZ + merged]
    along_y = flat_y.reshape(count_k, width_x, width_y, NZ)
    result = jnp.einsum("abcz,zw->abcw", along_y, matrix, precision=lax.Precision.HIGHEST)
    return result.reshape(count_k, width_x, merged)


def shards(log_dens, theta, cotangent):
    matrix = band_matrix(NZ)
    count_k, width_x, merged = log_dens.shape
    local_mass = jnp.sum(jnp.exp(log_dens), axis=(1, 2))
    total_mass = lax.psum(local_mass, ("gx", "gy"))
    cell_count = width_x * lax.axis_size("gx") * merged * lax.axis_size("gy")
    log_p = log_dens - jnp.log(total_mass)[:, None, None] + jnp.log(jnp.float32(cell_count))
    weights = jax.nn.softmax(theta)
    potential = jnp.zeros_like(log_p)
    saved = []
    for iteration in range(ITERS):
        smooth = jnp.log(smooth_field(jnp.exp(potential), matrix))
        log_u = log_p - smooth
        spread = jnp.log(smooth_field(jnp.exp(log_u), matrix))
        log_q = jnp.sum(weights[:, None, None] * spread, axis=0)
        saved.append((potential, smooth, log_u, spread))
        potential = log_q[None] - spread
    barycenter = jnp.exp(log_q)
    back_q = cotangent * barycenter
    back_v = jnp.zeros_like(log_p)
    grad_p = jnp.zeros_like(log_p)
    weight_grad = jnp.zeros((count_k,), jnp.float32)
    for iteration in reversed(range(ITERS)):
        potential, smooth, log_u, spread = saved[iteration]
        combined = jnp.sum(back_v, axis=0)
        if iteration == ITERS - 1:
            combined = combined + back_q
        back_r = weights[:, None, None] * combined[None] - back_v
        weight_term = jnp.sum(combined[None] * spread, axis=(1, 2))
        weight_grad = weight_grad + lax.psum(weight_term, ("gx", "gy"))
        back_u = jnp.exp(log_u) * smooth_field(back_r * jnp.exp(-spread), matrix)
        grad_p = grad_p + back_u
        if iteration > 0:
            back_v = -(jnp.exp(potential) * smooth_field(back_u * jnp.exp(-smooth), matrix))
    local_sums = jnp.sum(grad_p, axis=(1, 2))
    grad_sums = lax.psum(local_sums, ("gx", "gy"))
    grad_dens = grad_p - jnp.exp(log_dens) / total_mass[:, None, None] * grad_sums[:, None, None]
    grad_theta = weights * (weight_grad - jnp.sum(weights * weight_grad))
    return (barycenter, grad_dens, grad_theta)


def solution(mesh):
    placed = (P(None, "gx", "gy"), P(), P("gx", "gy"))
    return jax.shard_map(
        shards,
        mesh=mesh,
        in_specs=placed,
        out_specs=(P("gx", "gy"), P(None, "gx", "gy"), P()),
        check_vma=False,
    )
```

profile of v0, /device:TPU:1, one launch (start us, length us, event | category | flops | bytes accessed | tf_op | source)
XLA Modules:
  0.0 525.5 jit_solution(15191216381491818426)
XLA Ops:
  2.1 4.7 collective-permute-start
  6.8 3.7 collective-permute-done.1
  13.4 6.6 %collective-permute-start.2 = (f32[8,32,256]{2,1,0:T(8,128)S(1)}, f32[8,32,256]{2,1,0:T(8,128)S(1)}, u32[]{:S(2)}, u32[]{:S(2)}) collective-permute-start(f32[8,32,256]{2,1,0:T(8,128)S(1)} %get-tuple-element.33), channel_id=1, source_target_pairs={{0,1},{1,2},{2,3},{3,4},{4,5},{5,6},{6,7},{7,8},{8,9},{9,10},{10,1... | collective-permute-start | bytes 786440 | tf_op jit(solution)/shard_map/ppermute | solution.py:19
  22.4 71.3 %psum.28 = f32[8]{0:T(128)S(1)} all-reduce(f32[8]{0:T(128)S(1)} %exponential_reduce_fusion), channel_id=1, replica_groups=mesh['gx'=8,'gy'=16] {'gx','gy'}, use_global_device_ids=true, to_apply=%region_3.0 | all-reduce | flops 8 | bytes 64 | tf_op jit(solution)/shard_map/psum | solution.py:64
  93.7 10.5 %fusion.123 = f32[8,32,2048]{2,1,0:T(8,128)S(1)} fusion(f32[8,32,2048]{2,1,0:T(8,128)} %copy-done.3, f32[8,32,256]{2,1,0:T(8,128)S(1)} %collective-permute-done.3, f32[8,32,256]{2,1,0:T(8,128)S(1)} %collective-permute-done.2), kind=kLoop, calls=%fused_computation.296 | loop fusion | flops 13107200 | bytes 4718592 | tf_op jit(solution)/shard_map/add | solution.py:54
  104.3 3.0 reshape.71
  107.3 6.7 %convolution_log_fusion.2 = f32[8,32,32,64]{3,2,1,0:T(8,128)} fusion(f32[8,32,32,64]{3,2,1,0:T(8,128)} %reshape.71), kind=kOutput, calls=%fused_computation.172 | convolution fusion | flops 402763776 | bytes 4194304 | tf_op jit(solution)/shard_map/abcz,zw->abcw/dot_general | solution.py:56
  114.0 5.0 log.32
  128.0 4.1 collective-permute-done.5
  132.1 2.9 fusion.243
  135.1 4.7 collective-permute-start.6
  144.5 4.5 collective-permute-done.7
  149.0 4.3 fusion.103
  153.3 4.9 reshape.72
  158.2 6.9 %multiply_reduce_fusion.4 = (f32[32,32,64]{2,1,0:T(8,128)S(1)}, f32[8,32,32,64]{3,2,1,0:T(8,128)}) fusion(f32[8]{0:T(128)S(1)} %broadcast_divide_fusion, f32[8,32,32,64]{3,2,1,0:T(8,128)} %reshape.72), kind=kOutput, calls=%fused_computation.49 | convolution fusion | flops 403746816 | bytes 4456480 | tf_op jit(solution)/shard_map/abcz,zw->abcw/dot_general | solution.py:56
  165.3 5.0 log.34
  172.3 3.0 collective-permute-start.8
  178.6 4.2 collective-permute-done.9
  182.8 2.9 fusion.223
  185.7 3.6 collective-permute-start.10
  192.6 7.4 %collective-permute-done.11 = f32[8,32,256]{2,1,0:T(8,128)S(1)} collective-permute-done((f32[8,32,256]{2,1,0:T(8,128)S(1)}, f32[8,32,256]{2,1,0:T(8,128)S(1)}, u32[]{:S(2)}, u32[]{:S(2)}) %collective-permute-start.11) | collective-permute-done | bytes 262176 | tf_op jit(solution)/shard_map/ppermute | solution.py:20
  200.1 4.3 fusion.83
  204.4 4.9 reshape.73
  209.3 6.6 %convolution_log_fusion = f32[8,32,32,64]{3,2,1,0:T(8,128)} fusion(f32[8,32,32,64]{3,2,1,0:T(8,128)} %reshape.73), kind=kOutput, calls=%fused_computation.170 | convolution fusion | flops 402763776 | bytes 4194304 | tf_op jit(solution)/shard_map/abcz,zw->abcw/dot_general | solution.py:56
  215.9 5.0 log.36
  223.7 5.1 collective-permute-start.12
  232.1 4.4 collective-permute-done.13
  236.5 2.9 fusion.203
  239.4 2.9 collective-permute-start.14
  245.6 8.4 %collective-permute-done.15 = f32[8,32,256]{2,1,0:T(8,128)S(1)} collective-permute-done((f32[8,32,256]{2,1,0:T(8,128)S(1)}, f32[8,32,256]{2,1,0:T(8,128)S(1)}, u32[]{:S(2)}, u32[]{:S(2)}) %collective-permute-start.15) | collective-permute-done | bytes 262176 | tf_op jit(solution)/shard_map/ppermute | solution.py:20
  254.1 4.3 fusion.63
  258.4 4.9 reshape.74
  263.3 6.9 %multiply_reduce_fusion.3 = (f32[32,32,64]{2,1,0:T(8,128)S(1)}, f32[8,32,32,64]{3,2,1,0:T(8,128)}) fusion(f32[8]{0:T(128)S(1)} %broadcast_divide_fusion, f32[8,32,32,64]{3,2,1,0:T(8,128)} %reshape.74), kind=kOutput, calls=%fused_computation.48 | convolution fusion | flops 403746816 | bytes 4456480 | tf_op jit(solution)/shard_map/abcz,zw->abcw/dot_general | solution.py:56
  273.3 6.0 %multiply_reduce_fusion.1 = (f32[8]{0:T(128)S(1)}, f32[8,32,32,64]{3,2,1,0:T(8,128)}) fusion(f32[8,32,32,64]{3,2,1,0:T(8,128)} %get-tuple-element.38, f32[32,32,64]{2,1,0:T(8,128)} %mul.764), kind=kLoop, calls=%fused_computation.45 | loop fusion | flops 1572856 | bytes 4456480 | tf_op jit(solution)/shard_map/reduce_sum | solution.py:88
  279.3 5.0 exp.49
  286.2 3.9 collective-permute-start.16
  293.4 4.0 collective-permute-done.17
  300.3 3.1 collective-permute-start.18
  306.6 7.8 %collective-permute-done.19 = f32[8,32,256]{2,1,0:T(8,128)S(1)} collective-permute-done((f32[8,32,256]{2,1,0:T(8,128)S(1)}, f32[8,32,256]{2,1,0:T(8,128)S(1)}, u32[]{:S(2)}, u32[]{:S(2)}) %collective-permute-start.19) | collective-permute-done | bytes 262176 | tf_op jit(solution)/shard_map/ppermute | solution.py:20
  314.4 4.3 fusion.43
  318.7 4.9 reshape.75
  323.6 6.6 %fusion.306 = f32[8,32,32,64]{3,2,1,0:T(8,128)} fusion(f32[8,32,32,64]{3,2,1,0:T(8,128)} %reshape.75), kind=kOutput, calls=%fused_computation.515 | convolution fusion | flops 402763776 | bytes 4194304 | tf_op jit(solution)/shard_map/abcz,zw->abcw/dot_general | solution.py:56
  330.2 5.0 reshape.76
  335.2 4.9 exponential_multiply_fusion.1
  340.2 3.2 collective-permute-start.20
  346.8 4.4 collective-permute-done.21
  354.1 2.9 collective-permute-start.22
  360.3 10.1 %collective-permute-done.23 = f32[8,32,256]{2,1,0:T(8,128)S(1)} collective-permute-done((f32[8,32,256]{2,1,0:T(8,128)S(1)}, f32[8,32,256]{2,1,0:T(8,128)S(1)}, u32[]{:S(2)}, u32[]{:S(2)}) %collective-permute-start.23) | collective-permute-done | bytes 262176 | tf_op jit(solution)/shard_map/ppermute | solution.py:20
  370.4 4.3 fusion.23
  374.7 4.9 reshape.77
  379.6 7.7 %multiply_reduce_fusion.2 = (f32[32,32,64]{2,1,0:T(8,128)S(1)}, f32[8,32,32,64]{3,2,1,0:T(8,128)}) fusion(f32[8,32,32,64]{3,2,1,0:T(8,128)} %get-tuple-element.36, f32[32,32,64]{2,1,0:T(8,128)S(1)} %get-tuple-element.35, f32[8,32,32,64]{3,2,1,0:T(8,128)} %reshape.77), kind=kOutput, calls=%fused_computation.46 | convolution fusion | flops 404271104 | bytes 6815744 | tf_op jit(solution)/shard_map/abcz,zw->abcw/dot_general | solution.py:56
  387.6 5.0 reshape.78
  392.5 2.9 exponential_multiply_fusion
  395.6 4.1 collective-permute-start.24
  403.0 4.1 collective-permute-done.25
  407.1 2.9 fusion.143
  410.0 3.2 collective-permute-start.26
  416.5 8.1 %collective-permute-done.27 = f32[8,32,256]{2,1,0:T(8,128)S(1)} collective-permute-done((f32[8,32,256]{2,1,0:T(8,128)S(1)}, f32[8,32,256]{2,1,0:T(8,128)S(1)}, u32[]{:S(2)}, u32[]{:S(2)}) %collective-permute-start.27) | collective-permute-done | bytes 262176 | tf_op jit(solution)/shard_map/ppermute | solution.py:20
  424.6 4.3 fusion.3
  428.9 4.9 reshape.79
  433.8 6.7 %fusion.302 = f32[8,32,32,64]{3,2,1,0:T(8,128)} fusion(f32[8,32,32,64]{3,2,1,0:T(8,128)} %reshape.79), kind=kOutput, calls=%fused_computation.511 | convolution fusion | flops 402763776 | bytes 4194304 | tf_op jit(solution)/shard_map/abcz,zw->abcw/dot_general | solution.py:56
  440.5 5.0 reshape.80
  448.1 67.5 %all-reduce.2 = (f32[8]{0:T(128)S(1)}, f32[8]{0:T(128)S(1)}) all-reduce(f32[8]{0:T(128)S(1)} %fusion.428, f32[8]{0:T(128)S(1)} %add.605), channel_id=1, replica_groups=mesh['gx'=8,'gy'=16] {'gx','gy'}, use_global_device_ids=true, to_apply=%region_8.0 | all-reduce | flops 16 | bytes 128 | tf_op jit(solution)/shard_map/psum | solution.py:95
  519.8 5.3 multiply_subtract_fusion
  (78 shorter events, 76.5 us)
Async XLA Ops:
  0.6 21.4 %copy-start.1 = (f32[8,32,2048]{2,1,0:T(8,128)S(1)}, f32[8,32,2048]{2,1,0:T(8,128)}, u32[]{:S(2)}) copy-start(f32[8,32,2048]{2,1,0:T(8,128)} %param.3) | copy-start | bytes 6291460
  0.7 9.8 %collective-permute-start.1 = (f32[8,4,2048]{2,1,0:T(4,128)S(1)}, f32[8,4,2048]{2,1,0:T(4,128)S(1)}, u32[]{:S(2)}, u32[]{:S(2)}) collective-permute-start(f32[8,4,2048]{2,1,0:T(4,128)S(1)} %broadcast.60), channel_id=1, source_target_pairs={{16,0},{32,16},{48,32},{64,48},{80,64},{96,80},{112,96},{17,1},{33... | collective-permute-start | bytes 786440 | tf_op jit(solution)/shard_map/ppermute | solution.py:20
  2.1 9.2 %collective-permute-start = (f32[8,4,2048]{2,1,0:T(4,128)S(1)}, f32[8,4,2048]{2,1,0:T(4,128)S(1)}, u32[]{:S(2)}, u32[]{:S(2)}) collective-permute-start(f32[8,4,2048]{2,1,0:T(4,128)S(1)} %broadcast.60), channel_id=1, source_target_pairs={{0,16},{16,32},{32,48},{48,64},{64,80},{80,96},{96,112},{1,17},{17... | collective-permute-start | bytes 786440 | tf_op jit(solution)/shard_map/ppermute | solution.py:19
  12.0 1.3 copy-start.3
  13.4 80.3 %collective-permute-start.2 = (f32[8,32,256]{2,1,0:T(8,128)S(1)}, f32[8,32,256]{2,1,0:T(8,128)S(1)}, u32[]{:S(2)}, u32[]{:S(2)}) collective-permute-start(f32[8,32,256]{2,1,0:T(8,128)S(1)} %get-tuple-element.33), channel_id=1, source_target_pairs={{0,1},{1,2},{2,3},{3,4},{4,5},{5,6},{6,7},{7,8},{8,9},{9,10},{10,1... | collective-permute-start | bytes 786440 | tf_op jit(solution)/shard_map/ppermute | solution.py:19
  20.1 73.7 %collective-permute-start.3 = (f32[8,32,256]{2,1,0:T(8,128)S(1)}, f32[8,32,256]{2,1,0:T(8,128)S(1)}, u32[]{:S(2)}, u32[]{:S(2)}) collective-permute-start(f32[8,32,256]{2,1,0:T(8,128)S(1)} %get-tuple-element.34), channel_id=1, source_target_pairs={{1,0},{2,1},{3,2},{4,3},{5,4},{6,5},{7,6},{8,7},{9,8},{10,9},{11,1... | collective-permute-start | bytes 786440 | tf_op jit(solution)/shard_map/ppermute | solution.py:20
  119.0 5.6 %copy-start.4 = (f32[8]{0:T(128)S(1)}, f32[8]{0:T(128)}, u32[]{:S(2)}) copy-start(f32[8]{0:T(128)} %param.4) | copy-start | bytes 100
  121.9 6.1 %collective-permute-start.4 = (f32[8,4,2048]{2,1,0:T(4,128)S(1)}, f32[8,4,2048]{2,1,0:T(4,128)S(1)}, u32[]{:S(2)}, u32[]{:S(2)}) collective-permute-start(f32[8,4,2048]{2,1,0:T(4,128)S(1)} %get-tuple-element.31), channel_id=1, source_target_pairs={{0,16},{16,32},{32,48},{48,64},{64,80},{80,96},{96,112},{1,17},{17... | collective-permute-start | bytes 786440 | tf_op jit(solution)/shard_map/ppermute | solution.py:19
  123.2 8.9 %collective-permute-start.5 = (f32[8,4,2048]{2,1,0:T(4,128)S(1)}, f32[8,4,2048]{2,1,0:T(4,128)S(1)}, u32[]{:S(2)}, u32[]{:S(2)}) collective-permute-start(f32[8,4,2048]{2,1,0:T(4,128)S(1)} %get-tuple-element.32), channel_id=1, source_target_pairs={{16,0},{32,16},{48,32},{64,48},{80,64},{96,80},{112,96},{17,1},{33... | collective-permute-start | bytes 786440 | tf_op jit(solution)/shard_map/ppermute | solution.py:20
  135.1 9.5 %collective-permute-start.6 = (f32[8,32,256]{2,1,0:T(8,128)S(1)}, f32[8,32,256]{2,1,0:T(8,128)S(1)}, u32[]{:S(2)}, u32[]{:S(2)}) collective-permute-start(f32[8,32,256]{2,1,0:T(8,128)S(1)} %get-tuple-element.29), channel_id=1, source_target_pairs={{0,1},{1,2},{2,3},{3,4},{4,5},{5,6},{6,7},{7,8},{8,9},{9,10},{10,1... | collective-permute-start | bytes 786440 | tf_op jit(solution)/shard_map/ppermute | solution.py:19
  139.8 9.2 %collective-permute-start.7 = (f32[8,32,256]{2,1,0:T(8,128)S(1)}, f32[8,32,256]{2,1,0:T(8,128)S(1)}, u32[]{:S(2)}, u32[]{:S(2)}) collective-permute-start(f32[8,32,256]{2,1,0:T(8,128)S(1)} %get-tuple-element.30), channel_id=1, source_target_pairs={{1,0},{2,1},{3,2},{4,3},{5,4},{6,5},{7,6},{8,7},{9,8},{10,9},{11,1... | collective-permute-start | bytes 786440 | tf_op jit(solution)/shard_map/ppermute | solution.py:20
  172.3 6.3 %collective-permute-start.8 = (f32[8,4,2048]{2,1,0:T(4,128)S(1)}, f32[8,4,2048]{2,1,0:T(4,128)S(1)}, u32[]{:S(2)}, u32[]{:S(2)}) collective-permute-start(f32[8,4,2048]{2,1,0:T(4,128)S(1)} %get-tuple-element.27), channel_id=1, source_target_pairs={{0,16},{16,32},{32,48},{48,64},{64,80},{80,96},{96,112},{1,17},{17... | collective-permute-start | bytes 786440 | tf_op jit(solution)/shard_map/ppermute | solution.py:19
  175.3 7.5 %collective-permute-start.9 = (f32[8,4,2048]{2,1,0:T(4,128)S(1)}, f32[8,4,2048]{2,1,0:T(4,128)S(1)}, u32[]{:S(2)}, u32[]{:S(2)}) collective-permute-start(f32[8,4,2048]{2,1,0:T(4,128)S(1)} %get-tuple-element.28), channel_id=1, source_target_pairs={{16,0},{32,16},{48,32},{64,48},{80,64},{96,80},{112,96},{17,1},{33... | collective-permute-start | bytes 786440 | tf_op jit(solution)/shard_map/ppermute | solution.py:20
  185.7 6.9 %collective-permute-start.10 = (f32[8,32,256]{2,1,0:T(8,128)S(1)}, f32[8,32,256]{2,1,0:T(8,128)S(1)}, u32[]{:S(2)}, u32[]{:S(2)}) collective-permute-start(f32[8,32,256]{2,1,0:T(8,128)S(1)} %get-tuple-element.25), channel_id=1, source_target_pairs={{0,1},{1,2},{2,3},{3,4},{4,5},{5,6},{6,7},{7,8},{8,9},{9,10},{10,1... | collective-permute-start | bytes 786440 | tf_op jit(solution)/shard_map/ppermute | solution.py:19
  189.3 10.7 %collective-permute-start.11 = (f32[8,32,256]{2,1,0:T(8,128)S(1)}, f32[8,32,256]{2,1,0:T(8,128)S(1)}, u32[]{:S(2)}, u32[]{:S(2)}) collective-permute-start(f32[8,32,256]{2,1,0:T(8,128)S(1)} %get-tuple-element.26), channel_id=1, source_target_pairs={{1,0},{2,1},{3,2},{4,3},{5,4},{6,5},{7,6},{8,7},{9,8},{10,9},{11,1... | collective-permute-start | bytes 786440 | tf_op jit(solution)/shard_map/ppermute | solution.py:20
  223.6 15.8 %copy-start.2 = (f32[8,32,2048]{2,1,0:T(8,128)}, f32[8,32,2048]{2,1,0:T(8,128)S(1)}, u32[]{:S(2)}) copy-start(f32[8,32,2048]{2,1,0:T(8,128)S(1)} %subtract_exponential_fusion) | copy-start | bytes 6291460
  223.7 8.4 %collective-permute-start.12 = (f32[8,4,2048]{2,1,0:T(4,128)S(1)}, f32[8,4,2048]{2,1,0:T(4,128)S(1)}, u32[]{:S(2)}, u32[]{:S(2)}) collective-permute-start(f32[8,4,2048]{2,1,0:T(4,128)S(1)} %get-tuple-element.23), channel_id=1, source_target_pairs={{0,16},{16,32},{32,48},{48,64},{64,80},{80,96},{96,112},{1,17},{17... | collective-permute-start | bytes 786440 | tf_op jit(solution)/shard_map/ppermute | solution.py:19
  228.8 7.7 %collective-permute-start.13 = (f32[8,4,2048]{2,1,0:T(4,128)S(1)}, f32[8,4,2048]{2,1,0:T(4,128)S(1)}, u32[]{:S(2)}, u32[]{:S(2)}) collective-permute-start(f32[8,4,2048]{2,1,0:T(4,128)S(1)} %get-tuple-element.24), channel_id=1, source_target_pairs={{16,0},{32,16},{48,32},{64,48},{80,64},{96,80},{112,96},{17,1},{33... | collective-permute-start | bytes 786440 | tf_op jit(solution)/shard_map/ppermute | solution.py:20
  239.4 6.2 %collective-permute-start.14 = (f32[8,32,256]{2,1,0:T(8,128)S(1)}, f32[8,32,256]{2,1,0:T(8,128)S(1)}, u32[]{:S(2)}, u32[]{:S(2)}) collective-permute-start(f32[8,32,256]{2,1,0:T(8,128)S(1)} %get-tuple-element.21), channel_id=1, source_target_pairs={{0,1},{1,2},{2,3},{3,4},{4,5},{5,6},{6,7},{7,8},{8,9},{9,10},{10,1... | collective-permute-start | bytes 786440 | tf_op jit(solution)/shard_map/ppermute | solution.py:19
  242.4 11.7 %collective-permute-start.15 = (f32[8,32,256]{2,1,0:T(8,128)S(1)}, f32[8,32,256]{2,1,0:T(8,128)S(1)}, u32[]{:S(2)}, u32[]{:S(2)}) collective-permute-start(f32[8,32,256]{2,1,0:T(8,128)S(1)} %get-tuple-element.22), channel_id=1, source_target_pairs={{1,0},{2,1},{3,2},{4,3},{5,4},{6,5},{7,6},{8,7},{9,8},{10,9},{11,1... | collective-permute-start | bytes 786440 | tf_op jit(solution)/shard_map/ppermute | solution.py:20
  286.2 7.1 %collective-permute-start.16 = (f32[8,4,2048]{2,1,0:T(4,128)S(1)}, f32[8,4,2048]{2,1,0:T(4,128)S(1)}, u32[]{:S(2)}, u32[]{:S(2)}) collective-permute-start(f32[8,4,2048]{2,1,0:T(4,128)S(1)} %get-tuple-element.19), channel_id=1, source_target_pairs={{0,16},{16,32},{32,48},{48,64},{64,80},{80,96},{96,112},{1,17},{17... | collective-permute-start | bytes 786440 | tf_op jit(solution)/shard_map/ppermute | solution.py:19
  290.1 7.2 %collective-permute-start.17 = (f32[8,4,2048]{2,1,0:T(4,128)S(1)}, f32[8,4,2048]{2,1,0:T(4,128)S(1)}, u32[]{:S(2)}, u32[]{:S(2)}) collective-permute-start(f32[8,4,2048]{2,1,0:T(4,128)S(1)} %get-tuple-element.20), channel_id=1, source_target_pairs={{16,0},{32,16},{48,32},{64,48},{80,64},{96,80},{112,96},{17,1},{33... | collective-permute-start | bytes 786440 | tf_op jit(solution)/shard_map/ppermute | solution.py:20
  300.3 6.4 %collective-permute-start.18 = (f32[8,32,256]{2,1,0:T(8,128)S(1)}, f32[8,32,256]{2,1,0:T(8,128)S(1)}, u32[]{:S(2)}, u32[]{:S(2)}) collective-permute-start(f32[8,32,256]{2,1,0:T(8,128)S(1)} %get-tuple-element.17), channel_id=1, source_target_pairs={{0,1},{1,2},{2,3},{3,4},{4,5},{5,6},{6,7},{7,8},{8,9},{9,10},{10,1... | collective-permute-start | bytes 786440 | tf_op jit(solution)/shard_map/ppermute | solution.py:19
  303.3 11.1 %collective-permute-start.19 = (f32[8,32,256]{2,1,0:T(8,128)S(1)}, f32[8,32,256]{2,1,0:T(8,128)S(1)}, u32[]{:S(2)}, u32[]{:S(2)}) collective-permute-start(f32[8,32,256]{2,1,0:T(8,128)S(1)} %get-tuple-element.18), channel_id=1, source_target_pairs={{1,0},{2,1},{3,2},{4,3},{5,4},{6,5},{7,6},{8,7},{9,8},{10,9},{11,1... | collective-permute-start | bytes 786440 | tf_op jit(solution)/shard_map/ppermute | solution.py:20
  340.2 6.5 %collective-permute-start.20 = (f32[8,4,2048]{2,1,0:T(4,128)S(1)}, f32[8,4,2048]{2,1,0:T(4,128)S(1)}, u32[]{:S(2)}, u32[]{:S(2)}) collective-permute-start(f32[8,4,2048]{2,1,0:T(4,128)S(1)} %get-tuple-element.15), channel_id=1, source_target_pairs={{0,16},{16,32},{32,48},{48,64},{64,80},{80,96},{96,112},{1,17},{17... | collective-permute-start | bytes 786440 | tf_op jit(solution)/shard_map/ppermute | solution.py:19
  343.5 7.7 %collective-permute-start.21 = (f32[8,4,2048]{2,1,0:T(4,128)S(1)}, f32[8,4,2048]{2,1,0:T(4,128)S(1)}, u32[]{:S(2)}, u32[]{:S(2)}) collective-permute-start(f32[8,4,2048]{2,1,0:T(4,128)S(1)} %get-tuple-element.16), channel_id=1, source_target_pairs={{16,0},{32,16},{48,32},{64,48},{80,64},{96,80},{112,96},{17,1},{33... | collective-permute-start | bytes 786440 | tf_op jit(solution)/shard_map/ppermute | solution.py:20
  354.1 6.2 %collective-permute-start.22 = (f32[8,32,256]{2,1,0:T(8,128)S(1)}, f32[8,32,256]{2,1,0:T(8,128)S(1)}, u32[]{:S(2)}, u32[]{:S(2)}) collective-permute-start(f32[8,32,256]{2,1,0:T(8,128)S(1)} %get-tuple-element.13), channel_id=1, source_target_pairs={{0,1},{1,2},{2,3},{3,4},{4,5},{5,6},{6,7},{7,8},{8,9},{9,10},{10,1... | collective-permute-start | bytes 786440 | tf_op jit(solution)/shard_map/ppermute | solution.py:19
  357.0 13.3 %collective-permute-start.23 = (f32[8,32,256]{2,1,0:T(8,128)S(1)}, f32[8,32,256]{2,1,0:T(8,128)S(1)}, u32[]{:S(2)}, u32[]{:S(2)}) collective-permute-start(f32[8,32,256]{2,1,0:T(8,128)S(1)} %get-tuple-element.14), channel_id=1, source_target_pairs={{1,0},{2,1},{3,2},{4,3},{5,4},{6,5},{7,6},{8,7},{9,8},{10,9},{11,1... | collective-permute-start | bytes 786440 | tf_op jit(solution)/shard_map/ppermute | solution.py:20
  395.6 7.4 %collective-permute-start.24 = (f32[8,4,2048]{2,1,0:T(4,128)S(1)}, f32[8,4,2048]{2,1,0:T(4,128)S(1)}, u32[]{:S(2)}, u32[]{:S(2)}) collective-permute-start(f32[8,4,2048]{2,1,0:T(4,128)S(1)} %get-tuple-element.11), channel_id=1, source_target_pairs={{0,16},{16,32},{32,48},{48,64},{64,80},{80,96},{96,112},{1,17},{17... | collective-permute-start | bytes 786440 | tf_op jit(solution)/shard_map/ppermute | solution.py:19
  399.7 15.7 %copy-start = (f32[8,32,32,64]{3,2,1,0:T(8,128)S(1)}, f32[8,32,32,64]{3,2,1,0:T(8,128)}, u32[]{:S(2)}) copy-start(f32[8,32,32,64]{3,2,1,0:T(8,128)} %get-tuple-element.36) | copy-start | bytes 6291460
  399.7 7.4 %collective-permute-start.25 = (f32[8,4,2048]{2,1,0:T(4,128)S(1)}, f32[8,4,2048]{2,1,0:T(4,128)S(1)}, u32[]{:S(2)}, u32[]{:S(2)}) collective-permute-start(f32[8,4,2048]{2,1,0:T(4,128)S(1)} %get-tuple-element.12), channel_id=1, source_target_pairs={{16,0},{32,16},{48,32},{64,48},{80,64},{96,80},{112,96},{17,1},{33... | collective-permute-start | bytes 786440 | tf_op jit(solution)/shard_map/ppermute | solution.py:20
  410.0 6.5 %collective-permute-start.26 = (f32[8,32,256]{2,1,0:T(8,128)S(1)}, f32[8,32,256]{2,1,0:T(8,128)S(1)}, u32[]{:S(2)}, u32[]{:S(2)}) collective-permute-start(f32[8,32,256]{2,1,0:T(8,128)S(1)} %get-tuple-element.9), channel_id=1, source_target_pairs={{0,1},{1,2},{2,3},{3,4},{4,5},{5,6},{6,7},{7,8},{8,9},{9,10},{10,1... | collective-permute-start | bytes 786440 | tf_op jit(solution)/shard_map/ppermute | solution.py:19
  413.2 11.4 %collective-permute-start.27 = (f32[8,32,256]{2,1,0:T(8,128)S(1)}, f32[8,32,256]{2,1,0:T(8,128)S(1)}, u32[]{:S(2)}, u32[]{:S(2)}) collective-permute-start(f32[8,32,256]{2,1,0:T(8,128)S(1)} %get-tuple-element.10), channel_id=1, source_target_pairs={{1,0},{2,1},{3,2},{4,3},{5,4},{6,5},{7,6},{8,7},{9,8},{10,9},{11,1... | collective-permute-start | bytes 786440 | tf_op jit(solution)/shard_map/ppermute | solution.py:20
where the time goes:
time: 535 us; the launch traced here: 526 us
  blocking collectives  139 us (26%)
  other arithmetic  95 us (18%)
  waiting for transfers between devices  93.2 us (17%)
  starting transfers between devices  76.8 us (14%)
  local copies, waits for them, and re-layouts  71.9 us (13%)
  matrix products  48.2 us (9%)
    ppermute x14, waiting for transfers between devices, with_halo(): after = lax.ppermute(leading, axis, down)  75.2 us
    psum x1, blocking collectives, shards(): total_mass = lax.psum(local_mass, ('gx', 'gy'))  71.3 us
    psum x1, blocking collectives, shards(): grad_sums = lax.psum(local_sums, ('gx', 'gy'))  67.5 us
    ppermute x14, starting transfers between devices, with_halo(): before = lax.ppermute(last, axis, up)  52.3 us
    dot_general x7, matrix products, smooth_field(): jnp.einsum('abcz,zw->abcw', along_y, matrix, precision=lax.Precision.HIGH...  48.2 us
    add x7, other arithmetic, smooth_field(): flat_y + taps[position] * padded_y[:, :, position * NZ:position * NZ + me...  36.4 us
    reshape x7, local copies, waits for them, and re-layouts, smooth_field(): along_y = flat_y.reshape(count_k, width_x, width_y, NZ)  32.5 us
    ppermute x14, starting transfers between devices, with_halo(): after = lax.ppermute(leading, axis, down)  24.4 us
  transfers between devices with their start and end apart: 28, of which 25 were waited for; matrix products, arithmetic and copies ran while one was open for 1% of the time, Pallas kernels for 0%

commit v1 on v0

v1 whole, which is shorter than its diff:
```python
import math

import jax
import jax.numpy as jnp
import numpy as np
from jax import lax
from jax.experimental import pallas as pl
from jax.experimental.pallas import tpu as pltpu
from jax.sharding import PartitionSpec as P

NZ = 64
K = 8
L = 128
HALO = 8
HT = HALO * NZ // L
VMEM = 56 * 1024 * 1024
F32 = jnp.float32
BF16 = jnp.bfloat16


def tap_list():
    raw_taps = [math.exp(-(offset * offset) / 8.0) for offset in range(-4, 5)]
    tap_total = 0.0
    for value in raw_taps:
        tap_total = tap_total + value
    return [value / tap_total for value in raw_taps]


G4, G3, G2, G1, G0 = tap_list()[:5]


def depth_weights():
    taps = tap_list()
    band = np.zeros((L, L), np.float32)
    for i in range(L):
        for j in range(L):
            if i // NZ == j // NZ and abs(i - j) <= 4:
                band[i, j] = taps[i - j + 4]
    high = band.astype(BF16)
    low = (band - high.astype(np.float32)).astype(BF16)
    half = np.concatenate([high, low], axis=1)
    return np.concatenate([half, half], axis=0)


def nine(at):
    return (G0 * at(4) + G1 * (at(3) + at(5))) + (G2 * (at(2) + at(6)) + G3 * (at(1) + at(7))) + G4 * (at(0) + at(8))


def conv_x(src, dst):
    rows, tiles = dst.shape[0], dst.shape[1]

    def column(t, carry):
        for first in range(0, rows, 8):
            block = src[first : first + 16, t]
            dst[first : first + 8, t] = nine(lambda j: block[j : j + 8])
        return carry

    lax.fori_loop(0, tiles, column, 0)


def conv_yz(src, first, rows, w_ref):
    value = src[pl.ds(first, rows)]
    tiles = value.shape[1]
    n = tiles - 4
    flat = (rows * (tiles - 1) * K, L)
    lane = lax.broadcasted_iota(jnp.int32, flat, 1)
    mixed = jnp.where(lane < NZ, value[:, 1:].reshape(flat), value[:, :-1].reshape(flat))
    odd = pltpu.roll(mixed, NZ, axis=1).reshape(rows, tiles - 1, K, L)
    along = (G0 * value[:, 2 : n + 2] + G1 * (odd[:, 1 : n + 1] + odd[:, 2 : n + 2])) + (
        G2 * (value[:, 1 : n + 1] + value[:, 3 : n + 3]) + G3 * (odd[:, 0:n] + odd[:, 3 : n + 3])
    ) + G4 * (value[:, 0:n] + value[:, 4 : n + 4])
    along = along.reshape(rows * n * K, L)
    high = along.astype(BF16)
    low = (along - high.astype(F32)).astype(BF16)
    both = jnp.dot(jnp.concatenate([high, low], axis=1), w_ref[...], preferred_element_type=F32)
    return (both[:, :L] + both[:, L:]).reshape(rows, n, K, L)


def parities():
    return lax.rem(lax.axis_index("gx"), 2), lax.rem(lax.axis_index("gy"), 2)


def assemble(big, own, xa, xb, ya, yb, ca, cb):
    rows, tiles = own.shape[0], own.shape[1]
    px, py = parities()
    row_a, row_b = (1 - px) * (rows + HALO), px * (rows + HALO)
    col_a, col_b = (1 - py) * (tiles + HT), py * (tiles + HT)
    big[pl.ds(HALO, rows), pl.ds(HT, tiles)] = own[...]
    big[pl.ds(row_a, HALO), pl.ds(HT, tiles)] = xa[0:HALO]
    big[pl.ds(row_b, HALO), pl.ds(HT, tiles)] = xb[0:HALO]
    slabs = xa.shape[0]
    for col, y, c in ((col_a, ya, ca), (col_b, yb, cb)):
        big[pl.ds(HALO, rows), pl.ds(col, HT)] = y[0:rows]
        big[pl.ds(row_a, HALO), pl.ds(col, HT)] = c[0:HALO]
        big[pl.ds(row_b, HALO), pl.ds(col, HT)] = c[slabs : slabs + HALO]


def give_edges(own, xa, xb, ya, yb):
    rows, tiles = own.shape[0], own.shape[1]
    px, py = parities()
    xa[0:HALO] = own[pl.ds((1 - px) * (rows - HALO), HALO)]
    xb[0:HALO] = own[pl.ds(px * (rows - HALO), HALO)]
    ya[0:rows] = own[:, pl.ds((1 - py) * (tiles - HT), HT)]
    yb[0:rows] = own[:, pl.ds(py * (tiles - HT), HT)]


def clear_outside(*fields):
    rows, tiles = fields[0].shape[0], fields[0].shape[1]
    gx, gy = lax.axis_index("gx"), lax.axis_index("gy")

    def zero(rs, ts):
        def write():
            for f in fields:
                f[rs, ts] = jnp.zeros_like(f[rs, ts])

        return write

    pl.when(gx == 0)(zero(slice(0, 4), slice(0, tiles)))
    pl.when(gx == lax.axis_size("gx") - 1)(zero(slice(rows - 4, rows), slice(0, tiles)))
    pl.when(gy == 0)(zero(slice(0, rows), slice(0, 2)))
    pl.when(gy == lax.axis_size("gy") - 1)(zero(slice(0, rows), slice(tiles - 2, tiles)))


def start_kernel(log_ref, rx_ref, ryz_ref, dens, e, mass, xa, xb, ya, yb, turn):
    rows, tiles = dens.shape[0], dens.shape[1]
    for t in range(tiles):
        turn[t] = log_ref[:, t * L : (t + 1) * L]

    def row(i, acc):
        for t in range(tiles):
            d = jnp.exp(turn[t, pl.ds(i, K, stride=rows), :])
            dens[i, t] = d
            e[i, t] = d * (ryz_ref[:, t * L : (t + 1) * L] * rx_ref[pl.ds(i, 1), :])
            acc = acc + d
        return acc

    mass[...] = lax.fori_loop(0, rows, row, jnp.zeros((K, L), F32))
    give_edges(e, xa, xb, ya, yb)


def first_kernel(w_ref, wb, dens, cot, own, rxa, rxb, rya, ryb, rca, rcb, inv_a, v, u, inv_s, xa, xb, ya, yb, big, tmp, tmp2):
    rows, tiles = own.shape[0], own.shape[1]
    assemble(big, own, rxa, rxb, rya, ryb, rca, rcb)
    conv_x(big, tmp)

    def ring(c, carry):
        spread = jnp.log(conv_yz(tmp, c * 4, 4, w_ref))
        log_q = jnp.sum(wb[...] * spread, axis=2, keepdims=True)
        v[pl.ds(c * 4, 4)] = jnp.exp(log_q - spread)
        inv_a[pl.ds(c * 4, 4)] = jnp.exp(-spread)
        return carry

    lax.fori_loop(0, (rows + 8) // 4, ring, 0)
    clear_outside(v, inv_a)
    conv_x(v, tmp2)

    def inner(c, carry):
        inv = 1.0 / conv_yz(tmp2, c * 4, 4, w_ref)
        inv_s[pl.ds(c * 4, 4)] = inv
        u[pl.ds(c * 4, 4)] = dens[pl.ds(c * 4, 4)] * inv
        return carry

    lax.fori_loop(0, rows // 4, inner, 0)
    give_edges(u, xa, xb, ya, yb)
    px, py = parities()
    for t in range(tiles):
        xa[HALO, t] = cot[pl.ds(pl.multiple_of((1 - px) * (rows - 8), 8), 8), t * L : (t + 1) * L]
        xb[HALO, t] = cot[pl.ds(pl.multiple_of(px * (rows - 8), 8), 8), t * L : (t + 1) * L]
    for out, side in ((ya, 1 - py), (yb, py)):
        for t in range(HT):
            lanes = pl.ds(pl.multiple_of((side * (tiles - HT) + t) * L, L), L)
            for b in range(rows // 8):
                out[rows + b, t] = cot[b * 8 : b * 8 + 8, lanes]


def second_kernel(w_ref, wb, cot, inv_s, own, rxa, rxb, rya, ryb, rca, rcb, bu, z, q, sums, xa, xb, ya, yb, big, tmp, r, tmp2, cots):
    rows, tiles = own.shape[0], own.shape[1]
    assemble(big, own, rxa, rxb, rya, ryb, rca, rcb)
    px, py = parities()
    row_a, row_b = (1 - px) * (rows + HALO), px * (rows + HALO)
    col_a, col_b = (1 - py) * (tiles + HT), py * (tiles + HT)
    row_a, row_b = pl.multiple_of(row_a, 8), pl.multiple_of(row_b, 8)
    for t in range(tiles):
        cots[HT + t, HALO : HALO + rows] = cot[:, t * L : (t + 1) * L]
        cots[HT + t, pl.ds(row_a, 8)] = rxa[HALO, t]
        cots[HT + t, pl.ds(row_b, 8)] = rxb[HALO, t]
    for col, y, c in ((col_a, rya, rca), (col_b, ryb, rcb)):
        for t in range(HT):
            for b in range(rows // 8):
                cots[col + t, HALO + b * 8 : HALO + b * 8 + 8] = y[rows + b, t]
            cots[col + t, pl.ds(row_a, 8)] = c[HALO, t]
            cots[col + t, pl.ds(row_b, 8)] = c[2 * HALO + 1, t]
    conv_x(big, tmp)

    def ring(c, mine):
        spread = jnp.log(conv_yz(tmp, c * 4, 4, w_ref))
        log_q = jnp.sum(wb[...] * spread, axis=2, keepdims=True)
        ratio = wb[...] * jnp.exp(log_q - spread)
        acc_k = jnp.zeros((K, L), F32)
        acc_s = jnp.zeros((1, L), F32)
        for i in range(4):
            for t in range(tiles + 4):
                cell = cots[t + 2, pl.ds(c * 4 + i + 4, 1), :]
                r[c * 4 + i, t] = ratio[i, t] * cell
                if mine and 2 <= t < tiles + 2:
                    row_q = jnp.exp(log_q[i, t])
                    q[t - 2, pl.ds(c * 4 + i - 4, 1), :] = row_q[0:1]
                    combined = cell * row_q[0:1]
                    acc_s = acc_s + combined
                    acc_k = acc_k + combined * spread[i, t]
        if mine:
            sums[0] += acc_k
            sums[1, 0:1] += acc_s

    sums[...] = jnp.zeros_like(sums)
    ring(0, False)
    ring((rows + 4) // 4, False)

    def middle(c, carry):
        ring(c, True)
        return carry

    lax.fori_loop(1, (rows + 4) // 4, middle, 0)
    clear_outside(r)
    conv_x(r, tmp2)

    def inner(c, carry):
        s = pl.ds(c * 4, 4)
        back = own[s] * conv_yz(tmp2, c * 4, 4, w_ref)
        bu[s] = back
        z[s] = back * inv_s[s]
        return carry

    lax.fori_loop(0, rows // 4, inner, 0)
    give_edges(z, xa, xb, ya, yb)


def third_kernel(w_ref, wb, inv_a, v, e, bu, own, rxa, rxb, rya, ryb, rca, rcb, gp, sums, big, tmp, r, tmp2):
    rows, tiles = own.shape[0], own.shape[1]
    assemble(big, own, rxa, rxb, rya, ryb, rca, rcb)
    conv_x(big, tmp)

    def ring(c, mine):
        s = pl.ds(c * 4, 4)
        back_v = -(v[s] * conv_yz(tmp, c * 4, 4, w_ref))
        combined = jnp.sum(back_v, axis=2, keepdims=True)
        inv = inv_a[s]
        r[s] = (wb[...] * combined - back_v) * inv
        if mine:
            part = combined[:, 2 : tiles + 2]
            sums[0] += jnp.sum(part * -jnp.log(inv[:, 2 : tiles + 2]), axis=(0, 1))
            sums[1, 0:1] += jnp.sum(part, axis=(0, 1))

    sums[...] = jnp.zeros_like(sums)
    ring(0, False)
    ring((rows + 4) // 4, False)

    def middle(c, carry):
        ring(c, True)
        return carry

    lax.fori_loop(1, (rows + 4) // 4, middle, 0)
    conv_x(r, tmp2)

    def inner(c, carry):
        s = pl.ds(c * 4, 4)
        gp[s] = bu[s] + e[s] * conv_yz(tmp2, c * 4, 4, w_ref)
        return carry

    lax.fori_loop(0, rows // 4, inner, 0)


def last_kernel(scale, coef, gp, dens, q, out, bary, turn):
    rows, tiles = gp.shape[0], gp.shape[1]

    def row(i, carry):
        for t in range(tiles):
            turn[t, pl.ds(i, K, stride=rows), :] = gp[i, t] * scale[...] - dens[i, t] * coef[...]
        return carry

    lax.fori_loop(0, rows, row, 0)
    for t in range(tiles):
        out[:, t * L : (t + 1) * L] = turn[t]
        bary[:, t * L : (t + 1) * L] = q[t] * scale[0:1, :]


def call(kernel, outs, scratch, *args):
    vmem = pl.BlockSpec(memory_space=pltpu.VMEM)
    return pl.pallas_call(
        kernel,
        out_shape=[jax.ShapeDtypeStruct(s, F32) for s in outs],
        in_specs=[vmem] * len(args),
        out_specs=[vmem] * len(outs),
        scratch_shapes=[pltpu.VMEM(s, F32) for s in scratch],
        compiler_params=pltpu.CompilerParams(vmem_limit_bytes=VMEM),
    )(*args)


def swap(value, axis, parity):
    count = lax.axis_size(axis)
    pairs = []
    for i in range(count):
        j = i + 1 if i % 2 == parity else i - 1
        if 0 <= j < count:
            pairs.append((i, j))
    return lax.ppermute(value, axis, pairs)


def exchange(xa, xb, ya, yb, tiles):
    rxa, rxb = swap(xa, "gx", 0), swap(xb, "gx", 1)
    rya, ryb = swap(ya, "gy", 0), swap(yb, "gy", 1)
    py = lax.rem(lax.axis_index("gy"), 2)

    def corner(side):
        first = side * (tiles - HT)
        return jnp.concatenate([lax.dynamic_slice_in_dim(r, first, HT, axis=1) for r in (rxa, rxb)], axis=0)

    rca, rcb = swap(corner(1 - py), "gy", 0), swap(corner(py), "gy", 1)
    return rxa, rxb, rya, ryb, rca, rcb


def inside_sum(axis, length):
    count = lax.axis_size(axis) * length
    at = lax.axis_index(axis) * length + jnp.arange(length)
    total = jnp.zeros((length,), F32)
    for offset, tap in zip(range(-4, 5), tap_list()):
        total = total + tap * ((at + offset >= 0) & (at + offset < count)).astype(F32)
    return total


def depth_sum():
    at = jnp.arange(NZ)
    total = jnp.zeros((NZ,), F32)
    for offset, tap in zip(range(-4, 5), tap_list()):
        total = total + tap * ((at + offset >= 0) & (at + offset < NZ)).astype(F32)
    return total


def shards(log_dens, theta, cotangent):
    _, rows, merged = log_dens.shape
    tiles = merged // L
    devices = lax.axis_size("gx") * lax.axis_size("gy")
    cells = devices * rows * merged
    weights = jax.nn.softmax(theta)
    wb = jnp.broadcast_to(weights[:, None], (K, L))
    w = jnp.asarray(depth_weights())
    rx = jnp.broadcast_to((1.0 / inside_sum("gx", rows))[:, None], (rows, L))
    ryz = (1.0 / (inside_sum("gy", merged // NZ)[:, None] * depth_sum()[None, :])).reshape(1, merged)

    field, ringed, full = (rows, tiles, K, L), (rows + 8, tiles + 4, K, L), (rows + 16, tiles + 8, K, L)
    tmp, tmp2 = (rows + 8, tiles + 8, K, L), (rows, tiles + 4, K, L)
    acc = (2, K, L)

    def edges(x_extra, y_extra):
        return [(HALO + x_extra, tiles, K, L)] * 2 + [(rows + y_extra, HT, K, L)] * 2

    dens, e, mass, *sent = call(start_kernel, [field, field, (K, L)] + edges(0, 0), [(tiles, K * rows, L)], log_dens.reshape(K * rows, merged), rx, ryz)
    got = exchange(*sent, tiles)
    inv_a, v, u, inv_s, *sent = call(
        first_kernel, [ringed, ringed, field, field] + edges(1, rows // 8), [full, tmp, tmp2], w, wb, dens, cotangent, e, *got
    )
    got = exchange(*sent, tiles)
    bu, z, q, sums1, *sent = call(
        second_kernel,
        [field, field, (tiles, rows, L), acc] + edges(0, 0),
        [full, tmp, ringed, tmp2, (tiles + 8, rows + 16, L)],
        w, wb, cotangent, inv_s, u, *got,
    )
    got = exchange(*sent, tiles)
    gp, sums0 = call(third_kernel, [field, acc], [full, tmp, ringed, tmp2], w, wb, inv_a, v, e, bu, z, *got)

    local = jnp.concatenate([mass[None], sums1, sums0], axis=0).sum(axis=2).reshape(1, 5 * K)
    local = jnp.broadcast_to(jnp.pad(local, ((0, 0), (0, L - 5 * K))), (devices, L))
    total = lax.all_to_all(local, ("gx", "gy"), 0, 0, tiled=True).sum(axis=0)
    total_mass, wg1, s1, wg0, s0 = total[:K], total[K : 2 * K], total[2 * K], total[3 * K : 4 * K], total[4 * K]

    shift_k = jnp.log(F32(cells)) - jnp.log(total_mass)
    shift = jnp.sum(weights * shift_k)
    scale = jnp.exp(shift)
    weight_grad = scale * (wg1 + (2.0 * shift_k - shift) * s1 + wg0 + shift_k * s0)
    grad_theta = weights * (weight_grad - jnp.sum(weights * weight_grad))
    late = weights * (scale * s1)
    grad_sums = late + (late - weights * jnp.sum(late))
    coef = jnp.broadcast_to((grad_sums / total_mass)[:, None], (K, L))
    grad, bary = call(last_kernel, [(K * rows, merged), (rows, merged)], [(tiles, K * rows, L)], jnp.broadcast_to(scale, (K, L)), coef, gp, dens, q)
    return bary, grad.reshape(K, rows, merged), grad_theta


def solution(mesh):
    placed = (P(None, "gx", "gy"), P(), P("gx", "gy"))
    return jax.shard_map(
        shards,
        mesh=mesh,
        in_specs=placed,
        out_specs=(P("gx", "gy"), P(None, "gx", "gy"), P()),
        check_vma=False,
    )
```

time: 535 us -> 209 us (0.39); the launches traced: 526 us -> 208 us
  blocking collectives: 139 us -> 35.7 us
  other arithmetic: 95 us -> 13.6 us
  waiting for transfers between devices: 93.2 us -> 25.5 us
  local copies, waits for them, and re-layouts: 71.9 us -> 5.59 us
  Pallas kernels: 0 us -> 65.2 us
  matrix products: 48.2 us -> 0 us
  starting transfers between devices: 76.8 us -> 60.4 us
    psum x2 -> x0, blocking collectives: 139 us -> none  [the longest x1 71.3 us: shards(): total_mass = lax.psum(local_mass, ('gx', 'gy'))]
    ppermute x28 -> x18, waiting for transfers between devices: 93.2 us -> 25.5 us  [swap(): return lax.ppermute(value, axis, pairs)]
    pallas_call x0 -> x5, Pallas kernels: none -> 65.2 us  [call(): pl.pallas_call(kernel, out_shape=[jax.ShapeDtypeStruct(s, F32) for s in o...]
    add x15 -> x2, other arithmetic: 54.4 us -> 0.04 us  [the longest x1 0.02 us: inside_sum(): total + tap * ((at + offset >= 0) & (at + offset < count)).astype(F32)]
    dot_general x7 -> x0, matrix products: 48.2 us -> none  [smooth_field(): jnp.einsum('abcz,zw->abcw', along_y, matrix, precision=lax.Precision.HIGH...]
    reshape x10 -> x1, local copies, waits for them, and re-layouts: 47.4 us -> 0.08 us  [shards(): jnp.concatenate([mass[None], sums1, sums0], axis=0).sum(axis=2)]
    all_to_all x0 -> x1, blocking collectives: none -> 35.7 us  [shards(): total = lax.all_to_all(local, ('gx', 'gy'), 0, 0, tiled=True).sum(axis=0)]
    ppermute x28 -> x18, starting transfers between devices: 76.8 us -> 60.4 us  [swap(): return lax.ppermute(value, axis, pairs)]
  transfers between devices with their start and end apart: 28 -> 18, of which waited for: 25 -> 7; matrix products, arithmetic and copies ran while one was open for 1% -> 2% of each run, Pallas kernels for 0% -> 0%
where the time goes in v1:
time: 209 us; the launch traced here: 208 us
  Pallas kernels  65.2 us (31%)
  starting transfers between devices  60.4 us (29%)
  blocking collectives  35.7 us (17%)
  waiting for transfers between devices  25.5 us (12%)
  other arithmetic  13.6 us (7%)
  local copies, waits for them, and re-layouts  5.59 us (3%)
  between operations  2.44 us (1%)
    pallas_call x5, Pallas kernels, call(): pl.pallas_call(kernel, out_shape=[jax.ShapeDtypeStruct(s, F32) for s in o...  65.2 us
    ppermute x18, starting transfers between devices, swap(): return lax.ppermute(value, axis, pairs)  60.4 us
    all_to_all x1, blocking collectives, shards(): total = lax.all_to_all(local, ('gx', 'gy'), 0, 0, tiled=True).sum(axis=0)  35.7 us
    ppermute x18, waiting for transfers between devices, swap(): return lax.ppermute(value, axis, pairs)  25.5 us
  transfers between devices with their start and end apart: 18, of which 7 were waited for; matrix products, arithmetic and copies ran while one was open for 2% of the time, Pallas kernels for 0%

profile of v1, /device:TPU:1, one launch (start us, length us, event | category | flops | bytes accessed | tf_op | source)
XLA Modules:
  0.0 208.5 jit_solution(13855689073993177207)
XLA Ops:
  0.7 0.1 multiply_divide_fusion
  0.8 0.7 div.43.ryz_ref
  1.5 0.7 broadcast_in_dim.12.rx_ref
  2.1 7.2 %shard_map.67 = (f32[32,16,8,128]{3,2,1,0:T(8,128)}, f32[32,16,8,128]{3,2,1,0:T(8,128)}, f32[8,128]{1,0:T(8,128)}, f32[8,16,8,128]{3,2,1,0:T(8,128)}, f32[8,16,8...) custom-call(f32[256,2048]{1,0:T(8,128)} %bitcast.8, f32[32,128]{1,0:T(8,128)} %broadcast_in_dim.12.rx_ref, ...), custom_call_target="tpu_custom_call" | custom-call | tf_op jit(solution)/shard_map/pallas_call | solution.py:289
  9.3 2.1 %collective-permute-start = (f32[8,16,8,128]{3,2,1,0:T(8,128)}, f32[8,16,8,128]{3,2,1,0:T(8,128)S(1)}, u32[]{:S(2)}, u32[]{:S(2)}) collective-permute-start(f32[8,16,8,128]{3,2,1,0:T(8,128)} %get-tuple-element.33), channel_id=1, source_target_pairs={{0,16},{16,0},{32,48},{48,32},{64,80},{80,64},{96,112},{112,96},{1... | collective-permute-start | bytes 1572872 | tf_op jit(solution)/shard_map/ppermute | solution.py:306
  11.4 0.7 collective-permute-start.1
  12.1 1.0 collective-permute-start.2
  13.1 4.5 %collective-permute-start.3 = (f32[32,4,8,128]{3,2,1,0:T(8,128)}, f32[32,4,8,128]{3,2,1,0:T(8,128)S(1)}, u32[]{:S(2)}, u32[]{:S(2)}) collective-permute-start(f32[32,4,8,128]{3,2,1,0:T(8,128)} %get-tuple-element.36), channel_id=1, source_target_pairs={{1,2},{2,1},{3,4},{4,3},{5,6},{6,5},{7,8},{8,7},{9,10},{10,9},{11,... | collective-permute-start | bytes 1572872 | tf_op jit(solution)/shard_map/ppermute | solution.py:306
  17.7 0.0 copy-done.18
  17.7 0.7 reduce_max.9
  18.4 4.5 %collective-permute-done.rxa = f32[8,16,8,128]{3,2,1,0:T(8,128)S(1)} collective-permute-done((f32[8,16,8,128]{3,2,1,0:T(8,128)}, f32[8,16,8,128]{3,2,1,0:T(8,128)S(1)}, u32[]{:S(2)}, u32[]{:S(2)}) %collective-permute-start) | collective-permute-done | bytes 524320 | tf_op jit(solution)/shard_map/ppermute | solution.py:306
  22.9 0.0 collective-permute-done.1.rxb
  22.9 0.0 copy-start.3
  23.0 1.7 collective-permute-start.4
  24.7 4.7 %collective-permute-start.5 = (f32[16,4,8,128]{3,2,1,0:T(8,128)S(1)}, f32[16,4,8,128]{3,2,1,0:T(8,128)S(1)}, u32[]{:S(2)}, u32[]{:S(2)}) collective-permute-start(f32[16,4,8,128]{3,2,1,0:T(8,128)S(1)} %pad_maximum_fusion.3), channel_id=1, source_target_pairs={{1,2},{2,1},{3,4},{4,3},{5,6},{6,5},{7,8},{8,7},{9,10},{10,9},{11,... | collective-permute-start | bytes 786440 | tf_op jit(solution)/shard_map/ppermute | solution.py:306
  29.4 1.4 fusion.27
  30.8 1.4 broadcast_divide_fusion
  32.2 0.0 collective-permute-done.2.rya
  32.2 0.0 collective-permute-done.3.ryb
  32.2 0.0 collective-permute-done.4.rca
  32.2 0.0 copy-start.16
  32.2 3.6 %collective-permute-done.5.rcb = f32[16,4,8,128]{3,2,1,0:T(8,128)S(1)} collective-permute-done((f32[16,4,8,128]{3,2,1,0:T(8,128)S(1)}, f32[16,4,8,128]{3,2,1,0:T(8,128)S(1)}, u32[]{:S(2)}, u32[]{:S(2)}) %collective-permute-start.5) | collective-permute-done | bytes 262176 | tf_op jit(solution)/shard_map/ppermute | solution.py:306
  35.9 0.7 broadcast_in_dim.14.wb
  36.6 0.0 copy-done.3
  36.6 0.0 copy-done.17
  36.6 18.3 %shard_map.68 = (f32[40,20,8,128]{3,2,1,0:T(8,128)}, f32[40,20,8,128]{3,2,1,0:T(8,128)}, f32[32,16,8,128]{3,2,1,0:T(8,128)}, f32[32,16,8,128]{3,2,1,0:T(8,128)},...) custom-call(bf16[256,256]{1,0:T(8,128)(2,1)} %constant.110.clone.w_r, ...), custom_call_target="tpu_custom_call" | custom-call | tf_op jit(solution)/shard_map/pallas_call | solution.py:289
  54.9 4.3 %collective-permute-start.6 = (f32[9,16,8,128]{3,2,1,0:T(8,128)}, f32[9,16,8,128]{3,2,1,0:T(8,128)S(1)}, u32[]{:S(2)}, u32[]{:S(2)}) collective-permute-start(f32[9,16,8,128]{3,2,1,0:T(8,128)} %get-tuple-element.39), channel_id=1, source_target_pairs={{0,16},{16,0},{32,48},{48,32},{64,80},{80,64},{96,112},{112,96},{1... | collective-permute-start | bytes 1769480 | tf_op jit(solution)/shard_map/ppermute | solution.py:306
  59.2 0.7 collective-permute-start.7
  59.9 0.1 collective-permute-start.8
  60.0 6.3 %collective-permute-start.9 = (f32[36,4,8,128]{3,2,1,0:T(8,128)}, f32[36,4,8,128]{3,2,1,0:T(8,128)S(1)}, u32[]{:S(2)}, u32[]{:S(2)}) collective-permute-start(f32[36,4,8,128]{3,2,1,0:T(8,128)} %get-tuple-element.42), channel_id=1, source_target_pairs={{1,2},{2,1},{3,4},{4,3},{5,6},{6,5},{7,8},{8,7},{9,10},{10,9},{11,... | collective-permute-start | bytes 1769480 | tf_op jit(solution)/shard_map/ppermute | solution.py:306
  66.3 0.3 collective-permute-done.6.rxa
  66.7 0.0 collective-permute-done.7.rxb
  66.8 0.1 collective-permute-start.10
  66.9 9.7 %collective-permute-start.11 = (f32[18,4,8,128]{3,2,1,0:T(8,128)S(1)}, f32[18,4,8,128]{3,2,1,0:T(8,128)S(1)}, u32[]{:S(2)}, u32[]{:S(2)}) collective-permute-start(f32[18,4,8,128]{3,2,1,0:T(8,128)S(1)} %pad_maximum_fusion.1), channel_id=1, source_target_pairs={{1,2},{2,1},{3,4},{4,3},{5,6},{6,5},{7,8},{8,7},{9,10},{10,9},{11,... | collective-permute-start | bytes 884744 | tf_op jit(solution)/shard_map/ppermute | solution.py:306
  76.6 0.0 collective-permute-done.8.rya
  76.6 3.2 %collective-permute-done.9.ryb = f32[36,4,8,128]{3,2,1,0:T(8,128)S(1)} collective-permute-done((f32[36,4,8,128]{3,2,1,0:T(8,128)}, f32[36,4,8,128]{3,2,1,0:T(8,128)S(1)}, u32[]{:S(2)}, u32[]{:S(2)}) %collective-permute-start.9) | collective-permute-done | bytes 589856 | tf_op jit(solution)/shard_map/ppermute | solution.py:306
  79.8 0.0 collective-permute-done.10.rca
  79.9 6.0 %collective-permute-done.11.rcb = f32[18,4,8,128]{3,2,1,0:T(8,128)S(1)} collective-permute-done((f32[18,4,8,128]{3,2,1,0:T(8,128)S(1)}, f32[18,4,8,128]{3,2,1,0:T(8,128)S(1)}, u32[]{:S(2)}, u32[]{:S(2)}) %collective-permute-start.11) | collective-permute-done | bytes 294944 | tf_op jit(solution)/shard_map/ppermute | solution.py:306
  85.8 0.7 copy-done.13
  86.5 16.7 %shard_map.69 = (f32[32,16,8,128]{3,2,1,0:T(8,128)}, f32[32,16,8,128]{3,2,1,0:T(8,128)}, f32[16,32,128]{2,1,0:T(8,128)}, f32[2,8,128]{2,1,0:T(8,128)}, f32[8,16,...) custom-call(bf16[256,256]{1,0:T(8,128)(2,1)} %constant.110.clone.w_ref, ...), custom_call_target="tpu_custom_call" | custom-call | tf_op jit(solution)/shard_map/pallas_call | solution.py:289
  103.2 8.4 %collective-permute-start.12 = (f32[8,16,8,128]{3,2,1,0:T(8,128)}, f32[8,16,8,128]{3,2,1,0:T(8,128)S(1)}, u32[]{:S(2)}, u32[]{:S(2)}) collective-permute-start(f32[8,16,8,128]{3,2,1,0:T(8,128)} %get-tuple-element.48), channel_id=1, source_target_pairs={{0,16},{16,0},{32,48},{48,32},{64,80},{80,64},{96,112},{112,96},{1... | collective-permute-start | bytes 1572872 | tf_op jit(solution)/shard_map/ppermute | solution.py:306
  111.6 0.7 collective-permute-start.13
  112.3 0.1 collective-permute-start.14
  112.4 6.7 %collective-permute-start.15 = (f32[32,4,8,128]{3,2,1,0:T(8,128)}, f32[32,4,8,128]{3,2,1,0:T(8,128)S(1)}, u32[]{:S(2)}, u32[]{:S(2)}) collective-permute-start(f32[32,4,8,128]{3,2,1,0:T(8,128)} %get-tuple-element.51), channel_id=1, source_target_pairs={{1,2},{2,1},{3,4},{4,3},{5,6},{6,5},{7,8},{8,7},{9,10},{10,9},{11,... | collective-permute-start | bytes 1572872 | tf_op jit(solution)/shard_map/ppermute | solution.py:306
  119.1 0.0 collective-permute-done.12.rxa
  119.2 0.0 collective-permute-done.13.rxb
  119.3 0.1 collective-permute-start.16
  119.4 8.5 %collective-permute-start.17 = (f32[16,4,8,128]{3,2,1,0:T(8,128)S(1)}, f32[16,4,8,128]{3,2,1,0:T(8,128)S(1)}, u32[]{:S(2)}, u32[]{:S(2)}) collective-permute-start(f32[16,4,8,128]{3,2,1,0:T(8,128)S(1)} %pad_maximum_fusion.5), channel_id=1, source_target_pairs={{1,2},{2,1},{3,4},{4,3},{5,6},{6,5},{7,8},{8,7},{9,10},{10,9},{11,... | collective-permute-start | bytes 786440 | tf_op jit(solution)/shard_map/ppermute | solution.py:306
  127.9 0.0 collective-permute-done.14.rya
  127.9 2.5 %collective-permute-done.15.ryb = f32[32,4,8,128]{3,2,1,0:T(8,128)S(1)} collective-permute-done((f32[32,4,8,128]{3,2,1,0:T(8,128)}, f32[32,4,8,128]{3,2,1,0:T(8,128)S(1)}, u32[]{:S(2)}, u32[]{:S(2)}) %collective-permute-start.15) | collective-permute-done | bytes 524320 | tf_op jit(solution)/shard_map/ppermute | solution.py:306
  130.4 0.0 collective-permute-done.16.rca
  130.4 5.4 %collective-permute-done.17.rcb = f32[16,4,8,128]{3,2,1,0:T(8,128)S(1)} collective-permute-done((f32[16,4,8,128]{3,2,1,0:T(8,128)S(1)}, f32[16,4,8,128]{3,2,1,0:T(8,128)S(1)}, u32[]{:S(2)}, u32[]{:S(2)}) %collective-permute-start.17) | collective-permute-done | bytes 262176 | tf_op jit(solution)/shard_map/ppermute | solution.py:306
  135.8 0.7 copy-done.15
  136.4 16.9 %shard_map.70 = (f32[32,16,8,128]{3,2,1,0:T(8,128)}, f32[2,8,128]{2,1,0:T(8,128)}) custom-call(bf16[256,256]{1,0:T(8,128)(2,1)} %constant.110.clone.w_ref, f32[8,128]{1,0:T(8,128)} %broadcast_in_dim.14.wb, f32[40,20,8,128]{3,2,1,0:T(8,128)} %get-tuple-element.44.inv_a, f32[40,20,8,128]{3,2,1,0:T(8,128)} %get-tuple-element.45.v, ...), custom_call_target="tpu_custom_call" | custom-call | tf_op jit(solution)/shard_map/pallas_call | solution.py:289
  153.4 0.8 maximum_reduce_fusion
  154.1 0.1 reshape.228
  154.3 35.7 %all_to_all.6 = f32[128,1,128]{2,1,0:T(1,128)S(1)} all-to-all(f32[128,1,128]{2,1,0:T(1,128)S(1)} %broadcast_in_dim.15), channel_id=1, replica_groups=mesh['gx'=8,'gy'=16] {'gx','gy'}, dimensions={0} | all-to-all | bytes 131072 | tf_op jit(solution)/shard_map/all_to_all | solution.py:374
  190.0 2.0 multiply_reduce_fusion.1
  192.0 0.6 fusion.28
  193.9 4.1 %multiply_reduce_fusion = (f32[]{:T(128)}, f32[]{:T(128)}, f32[8]{0:T(128)S(1)}) fusion(f32[]{:T(128)S(6)} %mul.202, f32[]{:T(128)} %bitcast.6, f32[128]{0:T(128)S(1)} %reduce_sum.56, f32[]{:T(128)} %bitcast.4, f32[]{:T(128)} %multiply_reduce_fusion.1, f32[]{:T(128)S(6)} %exp.7, f32[]{:T(128)} %fusion.27, f32[8]{0:T(128)S(1)} %copy-done.18, f32[]{:T(128)} %reduce_max.9), kind=kLoop, calls=%fused_computation.83 | loop fusion | flops 118 | bytes 196 | tf_op jit(solution)/shard_map/reduce_sum | solution.py:381
  198.0 3.1 %subtract_multiply_fusion = (f32[8]{0:T(128)}, f32[8]{0:T(128)S(1)}) fusion(f32[8]{0:T(128)S(1)} %get-tuple-element.59, f32[]{:T(128)} %get-tuple-element.57, f32[128]{0:T(128)S(1)} %reduce_sum.56, f32[]{:T(128)} %get-tuple-element.58, f32[]{:T(128)S(6)} %mul.202, f32[]{:T(128)} %fusion.27, f32[8]{0:T(128)S(1)} %copy-done.18, f32[]{:T(128)} %reduce_max.9), kind=kLoop, calls=%fused_computation.82 | loop fusion | flops 72 | bytes 180 | tf_op jit(solution)/shard_map/mul | solution.py:381
  201.1 0.6 broadcast_in_dim.16.scale
  201.7 0.7 broadcast_in_dim.17.coef
  202.4 6.1 %shard_map.71 = (f32[256,2048]{1,0:T(8,128)}, f32[32,2048]{1,0:T(8,128)}) custom-call(f32[8,128]{1,0:T(8,128)} %broadcast_in_dim.16.scale, f32[8,128]{1,0:T(8,128)} %broadcast_in_dim.17.coef, f32[32,16,8,128]{3,2,1,0:T(8,128)} %get-tuple-element.53.gp, f32[32,16,8,128]{3,2,1,0:T(8,128)} %get-tuple-element.31.dens, f32[16,32,128]{2,1,0:T(8,128)} %get-tuple-element.54.q), custom_call_target="tpu_custom_call" | custom-call | tf_op jit(solution)/shard_map/pallas_call | solution.py:289
  (52 shorter events, 0.4 us)
Async XLA Ops:
  0.6 17.1 %copy-start.18 = (f32[8]{0:T(128)S(1)}, f32[8]{0:T(128)}, u32[]{:S(2)}) copy-start(f32[8]{0:T(128)} %param.5) | copy-start | bytes 100
  9.3 13.6 %collective-permute-start = (f32[8,16,8,128]{3,2,1,0:T(8,128)}, f32[8,16,8,128]{3,2,1,0:T(8,128)S(1)}, u32[]{:S(2)}, u32[]{:S(2)}) collective-permute-start(f32[8,16,8,128]{3,2,1,0:T(8,128)} %get-tuple-element.33), channel_id=1, source_target_pairs={{0,16},{16,0},{32,48},{48,32},{64,80},{80,64},{96,112},{112,96},{1... | collective-permute-start | bytes 1572872 | tf_op jit(solution)/shard_map/ppermute | solution.py:306
  11.4 11.5 %collective-permute-start.1 = (f32[8,16,8,128]{3,2,1,0:T(8,128)}, f32[8,16,8,128]{3,2,1,0:T(8,128)S(1)}, u32[]{:S(2)}, u32[]{:S(2)}) collective-permute-start(f32[8,16,8,128]{3,2,1,0:T(8,128)} %get-tuple-element.34), channel_id=1, source_target_pairs={{16,32},{32,16},{48,64},{64,48},{80,96},{96,80},{17,33},{33,17},{4... | collective-permute-start | bytes 1572872 | tf_op jit(solution)/shard_map/ppermute | solution.py:306
  12.1 20.1 %collective-permute-start.2 = (f32[32,4,8,128]{3,2,1,0:T(8,128)}, f32[32,4,8,128]{3,2,1,0:T(8,128)S(1)}, u32[]{:S(2)}, u32[]{:S(2)}) collective-permute-start(f32[32,4,8,128]{3,2,1,0:T(8,128)} %get-tuple-element.35), channel_id=1, source_target_pairs={{0,1},{1,0},{2,3},{3,2},{4,5},{5,4},{6,7},{7,6},{8,9},{9,8},{10,11... | collective-permute-start | bytes 1572872 | tf_op jit(solution)/shard_map/ppermute | solution.py:306
  13.1 19.1 %collective-permute-start.3 = (f32[32,4,8,128]{3,2,1,0:T(8,128)}, f32[32,4,8,128]{3,2,1,0:T(8,128)S(1)}, u32[]{:S(2)}, u32[]{:S(2)}) collective-permute-start(f32[32,4,8,128]{3,2,1,0:T(8,128)} %get-tuple-element.36), channel_id=1, source_target_pairs={{1,2},{2,1},{3,4},{4,3},{5,6},{6,5},{7,8},{8,7},{9,10},{10,9},{11,... | collective-permute-start | bytes 1572872 | tf_op jit(solution)/shard_map/ppermute | solution.py:306
  22.9 13.7 %copy-start.2 = (f32[8,16,8,128]{3,2,1,0:T(8,128)}, f32[8,16,8,128]{3,2,1,0:T(8,128)S(1)}, u32[]{:S(2)}) copy-start(f32[8,16,8,128]{3,2,1,0:T(8,128)S(1)} %collective-permute-done.rxa) | copy-start | bytes 1572868
  22.9 13.7 %copy-start.3 = (f32[8,16,8,128]{3,2,1,0:T(8,128)}, f32[8,16,8,128]{3,2,1,0:T(8,128)S(1)}, u32[]{:S(2)}) copy-start(f32[8,16,8,128]{3,2,1,0:T(8,128)S(1)} %collective-permute-done.1.rxb) | copy-start | bytes 1572868
  23.0 9.3 %collective-permute-start.4 = (f32[16,4,8,128]{3,2,1,0:T(8,128)S(1)}, f32[16,4,8,128]{3,2,1,0:T(8,128)S(1)}, u32[]{:S(2)}, u32[]{:S(2)}) collective-permute-start(f32[16,4,8,128]{3,2,1,0:T(8,128)S(1)} %pad_maximum_fusion.2), channel_id=1, source_target_pairs={{0,1},{1,0},{2,3},{3,2},{4,5},{5,4},{6,7},{7,6},{8,9},{9,8},{10,11... | collective-permute-start | bytes 786440 | tf_op jit(solution)/shard_map/ppermute | solution.py:306
  24.7 11.2 %collective-permute-start.5 = (f32[16,4,8,128]{3,2,1,0:T(8,128)S(1)}, f32[16,4,8,128]{3,2,1,0:T(8,128)S(1)}, u32[]{:S(2)}, u32[]{:S(2)}) collective-permute-start(f32[16,4,8,128]{3,2,1,0:T(8,128)S(1)} %pad_maximum_fusion.3), channel_id=1, source_target_pairs={{1,2},{2,1},{3,4},{4,3},{5,6},{6,5},{7,8},{8,7},{9,10},{10,9},{11,... | collective-permute-start | bytes 786440 | tf_op jit(solution)/shard_map/ppermute | solution.py:306
  32.2 4.4 %copy-start.8 = (f32[32,4,8,128]{3,2,1,0:T(8,128)}, f32[32,4,8,128]{3,2,1,0:T(8,128)S(1)}, u32[]{:S(2)}) copy-start(f32[32,4,8,128]{3,2,1,0:T(8,128)S(1)} %collective-permute-done.2.rya) | copy-start | bytes 1572868
  32.2 4.4 %copy-start.9 = (f32[32,4,8,128]{3,2,1,0:T(8,128)}, f32[32,4,8,128]{3,2,1,0:T(8,128)S(1)}, u32[]{:S(2)}) copy-start(f32[32,4,8,128]{3,2,1,0:T(8,128)S(1)} %collective-permute-done.3.ryb) | copy-start | bytes 1572868
  32.2 4.3 %copy-start.16 = (f32[16,4,8,128]{3,2,1,0:T(8,128)}, f32[16,4,8,128]{3,2,1,0:T(8,128)S(1)}, u32[]{:S(2)}) copy-start(f32[16,4,8,128]{3,2,1,0:T(8,128)S(1)} %collective-permute-done.4.rca) | copy-start | bytes 786436
  35.9 0.7 copy-start.17
  54.9 11.8 %collective-permute-start.6 = (f32[9,16,8,128]{3,2,1,0:T(8,128)}, f32[9,16,8,128]{3,2,1,0:T(8,128)S(1)}, u32[]{:S(2)}, u32[]{:S(2)}) collective-permute-start(f32[9,16,8,128]{3,2,1,0:T(8,128)} %get-tuple-element.39), channel_id=1, source_target_pairs={{0,16},{16,0},{32,48},{48,32},{64,80},{80,64},{96,112},{112,96},{1... | collective-permute-start | bytes 1769480 | tf_op jit(solution)/shard_map/ppermute | solution.py:306
  59.2 7.5 %collective-permute-start.7 = (f32[9,16,8,128]{3,2,1,0:T(8,128)}, f32[9,16,8,128]{3,2,1,0:T(8,128)S(1)}, u32[]{:S(2)}, u32[]{:S(2)}) collective-permute-start(f32[9,16,8,128]{3,2,1,0:T(8,128)} %get-tuple-element.40), channel_id=1, source_target_pairs={{16,32},{32,16},{48,64},{64,48},{80,96},{96,80},{17,33},{33,17},{4... | collective-permute-start | bytes 1769480 | tf_op jit(solution)/shard_map/ppermute | solution.py:306
  59.9 16.7 %collective-permute-start.8 = (f32[36,4,8,128]{3,2,1,0:T(8,128)}, f32[36,4,8,128]{3,2,1,0:T(8,128)S(1)}, u32[]{:S(2)}, u32[]{:S(2)}) collective-permute-start(f32[36,4,8,128]{3,2,1,0:T(8,128)} %get-tuple-element.41), channel_id=1, source_target_pairs={{0,1},{1,0},{2,3},{3,2},{4,5},{5,4},{6,7},{7,6},{8,9},{9,8},{10,11... | collective-permute-start | bytes 1769480 | tf_op jit(solution)/shard_map/ppermute | solution.py:306
  60.0 19.9 %collective-permute-start.9 = (f32[36,4,8,128]{3,2,1,0:T(8,128)}, f32[36,4,8,128]{3,2,1,0:T(8,128)S(1)}, u32[]{:S(2)}, u32[]{:S(2)}) collective-permute-start(f32[36,4,8,128]{3,2,1,0:T(8,128)} %get-tuple-element.42), channel_id=1, source_target_pairs={{1,2},{2,1},{3,4},{4,3},{5,6},{6,5},{7,8},{8,7},{9,10},{10,9},{11,... | collective-permute-start | bytes 1769480 | tf_op jit(solution)/shard_map/ppermute | solution.py:306
  66.7 19.2 %copy-start = (f32[9,16,8,128]{3,2,1,0:T(8,128)}, f32[9,16,8,128]{3,2,1,0:T(8,128)S(1)}, u32[]{:S(2)}) copy-start(f32[9,16,8,128]{3,2,1,0:T(8,128)S(1)} %collective-permute-done.6.rxa) | copy-start | bytes 1769476
  66.7 19.1 %copy-start.1 = (f32[9,16,8,128]{3,2,1,0:T(8,128)}, f32[9,16,8,128]{3,2,1,0:T(8,128)S(1)}, u32[]{:S(2)}) copy-start(f32[9,16,8,128]{3,2,1,0:T(8,128)S(1)} %collective-permute-done.7.rxb) | copy-start | bytes 1769476
  66.8 13.1 %collective-permute-start.10 = (f32[18,4,8,128]{3,2,1,0:T(8,128)S(1)}, f32[18,4,8,128]{3,2,1,0:T(8,128)S(1)}, u32[]{:S(2)}, u32[]{:S(2)}) collective-permute-start(f32[18,4,8,128]{3,2,1,0:T(8,128)S(1)} %pad_maximum_fusion), channel_id=1, source_target_pairs={{0,1},{1,0},{2,3},{3,2},{4,5},{5,4},{6,7},{7,6},{8,9},{9,8},{10,11... | collective-permute-start | bytes 884744 | tf_op jit(solution)/shard_map/ppermute | solution.py:306
  66.9 18.9 %collective-permute-start.11 = (f32[18,4,8,128]{3,2,1,0:T(8,128)S(1)}, f32[18,4,8,128]{3,2,1,0:T(8,128)S(1)}, u32[]{:S(2)}, u32[]{:S(2)}) collective-permute-start(f32[18,4,8,128]{3,2,1,0:T(8,128)S(1)} %pad_maximum_fusion.1), channel_id=1, source_target_pairs={{1,2},{2,1},{3,4},{4,3},{5,6},{6,5},{7,8},{8,7},{9,10},{10,9},{11,... | collective-permute-start | bytes 884744 | tf_op jit(solution)/shard_map/ppermute | solution.py:306
  76.6 9.2 %copy-start.6 = (f32[36,4,8,128]{3,2,1,0:T(8,128)}, f32[36,4,8,128]{3,2,1,0:T(8,128)S(1)}, u32[]{:S(2)}) copy-start(f32[36,4,8,128]{3,2,1,0:T(8,128)S(1)} %collective-permute-done.8.rya) | copy-start | bytes 1769476
  79.8 6.0 %copy-start.7 = (f32[36,4,8,128]{3,2,1,0:T(8,128)}, f32[36,4,8,128]{3,2,1,0:T(8,128)S(1)}, u32[]{:S(2)}) copy-start(f32[36,4,8,128]{3,2,1,0:T(8,128)S(1)} %collective-permute-done.9.ryb) | copy-start | bytes 1769476
  79.8 6.0 %copy-start.12 = (f32[18,4,8,128]{3,2,1,0:T(8,128)}, f32[18,4,8,128]{3,2,1,0:T(8,128)S(1)}, u32[]{:S(2)}) copy-start(f32[18,4,8,128]{3,2,1,0:T(8,128)S(1)} %collective-permute-done.10.rca) | copy-start | bytes 884740
  85.8 0.7 copy-start.13
  103.2 15.9 %collective-permute-start.12 = (f32[8,16,8,128]{3,2,1,0:T(8,128)}, f32[8,16,8,128]{3,2,1,0:T(8,128)S(1)}, u32[]{:S(2)}, u32[]{:S(2)}) collective-permute-start(f32[8,16,8,128]{3,2,1,0:T(8,128)} %get-tuple-element.48), channel_id=1, source_target_pairs={{0,16},{16,0},{32,48},{48,32},{64,80},{80,64},{96,112},{112,96},{1... | collective-permute-start | bytes 1572872 | tf_op jit(solution)/shard_map/ppermute | solution.py:306
  111.6 7.6 %collective-permute-start.13 = (f32[8,16,8,128]{3,2,1,0:T(8,128)}, f32[8,16,8,128]{3,2,1,0:T(8,128)S(1)}, u32[]{:S(2)}, u32[]{:S(2)}) collective-permute-start(f32[8,16,8,128]{3,2,1,0:T(8,128)} %get-tuple-element.49), channel_id=1, source_target_pairs={{16,32},{32,16},{48,64},{64,48},{80,96},{96,80},{17,33},{33,17},{4... | collective-permute-start | bytes 1572872 | tf_op jit(solution)/shard_map/ppermute | solution.py:306
  112.3 15.5 %collective-permute-start.14 = (f32[32,4,8,128]{3,2,1,0:T(8,128)}, f32[32,4,8,128]{3,2,1,0:T(8,128)S(1)}, u32[]{:S(2)}, u32[]{:S(2)}) collective-permute-start(f32[32,4,8,128]{3,2,1,0:T(8,128)} %get-tuple-element.50), channel_id=1, source_target_pairs={{0,1},{1,0},{2,3},{3,2},{4,5},{5,4},{6,7},{7,6},{8,9},{9,8},{10,11... | collective-permute-start | bytes 1572872 | tf_op jit(solution)/shard_map/ppermute | solution.py:306
  112.4 17.9 %collective-permute-start.15 = (f32[32,4,8,128]{3,2,1,0:T(8,128)}, f32[32,4,8,128]{3,2,1,0:T(8,128)S(1)}, u32[]{:S(2)}, u32[]{:S(2)}) collective-permute-start(f32[32,4,8,128]{3,2,1,0:T(8,128)} %get-tuple-element.51), channel_id=1, source_target_pairs={{1,2},{2,1},{3,4},{4,3},{5,6},{6,5},{7,8},{8,7},{9,10},{10,9},{11,... | collective-permute-start | bytes 1572872 | tf_op jit(solution)/shard_map/ppermute | solution.py:306
  119.1 16.6 %copy-start.4 = (f32[8,16,8,128]{3,2,1,0:T(8,128)}, f32[8,16,8,128]{3,2,1,0:T(8,128)S(1)}, u32[]{:S(2)}) copy-start(f32[8,16,8,128]{3,2,1,0:T(8,128)S(1)} %collective-permute-done.12.rxa) | copy-start | bytes 1572868
  119.2 16.5 %copy-start.5 = (f32[8,16,8,128]{3,2,1,0:T(8,128)}, f32[8,16,8,128]{3,2,1,0:T(8,128)S(1)}, u32[]{:S(2)}) copy-start(f32[8,16,8,128]{3,2,1,0:T(8,128)S(1)} %collective-permute-done.13.rxb) | copy-start | bytes 1572868
  119.3 11.1 %collective-permute-start.16 = (f32[16,4,8,128]{3,2,1,0:T(8,128)S(1)}, f32[16,4,8,128]{3,2,1,0:T(8,128)S(1)}, u32[]{:S(2)}, u32[]{:S(2)}) collective-permute-start(f32[16,4,8,128]{3,2,1,0:T(8,128)S(1)} %pad_maximum_fusion.4), channel_id=1, source_target_pairs={{0,1},{1,0},{2,3},{3,2},{4,5},{5,4},{6,7},{7,6},{8,9},{9,8},{10,11... | collective-permute-start | bytes 786440 | tf_op jit(solution)/shard_map/ppermute | solution.py:306
  119.4 16.3 %collective-permute-start.17 = (f32[16,4,8,128]{3,2,1,0:T(8,128)S(1)}, f32[16,4,8,128]{3,2,1,0:T(8,128)S(1)}, u32[]{:S(2)}, u32[]{:S(2)}) collective-permute-start(f32[16,4,8,128]{3,2,1,0:T(8,128)S(1)} %pad_maximum_fusion.5), channel_id=1, source_target_pairs={{1,2},{2,1},{3,4},{4,3},{5,6},{6,5},{7,8},{8,7},{9,10},{10,9},{11,... | collective-permute-start | bytes 786440 | tf_op jit(solution)/shard_map/ppermute | solution.py:306
  127.9 7.9 %copy-start.10 = (f32[32,4,8,128]{3,2,1,0:T(8,128)}, f32[32,4,8,128]{3,2,1,0:T(8,128)S(1)}, u32[]{:S(2)}) copy-start(f32[32,4,8,128]{3,2,1,0:T(8,128)S(1)} %collective-permute-done.14.rya) | copy-start | bytes 1572868
  130.4 5.4 %copy-start.11 = (f32[32,4,8,128]{3,2,1,0:T(8,128)}, f32[32,4,8,128]{3,2,1,0:T(8,128)S(1)}, u32[]{:S(2)}) copy-start(f32[32,4,8,128]{3,2,1,0:T(8,128)S(1)} %collective-permute-done.15.ryb) | copy-start | bytes 1572868
  130.4 5.4 %copy-start.14 = (f32[16,4,8,128]{3,2,1,0:T(8,128)}, f32[16,4,8,128]{3,2,1,0:T(8,128)S(1)}, u32[]{:S(2)}) copy-start(f32[16,4,8,128]{3,2,1,0:T(8,128)S(1)} %collective-permute-done.16.rca) | copy-start | bytes 786436
  135.7 0.7 copy-start.15
  136.4 16.9 %copy-start.19 = (f32[2,8,128]{2,1,0:T(8,128)S(1)}, f32[2,8,128]{2,1,0:T(8,128)}, u32[]{:S(2)}) copy-start(f32[2,8,128]{2,1,0:T(8,128)} %get-tuple-element.43) | copy-start | bytes 24580
  136.4 16.9 %copy-start.20 = (f32[8,128]{1,0:T(8,128)S(1)}, f32[8,128]{1,0:T(8,128)}, u32[]{:S(2)}) copy-start(f32[8,128]{1,0:T(8,128)} %get-tuple-element.30) | copy-start | bytes 12292

commit v2 on v1

v2 whole, which is shorter than its diff:
```python
import functools
import math

import jax
import jax.numpy as jnp
import numpy as np
from jax import lax
from jax.experimental import pallas as pl
from jax.experimental.pallas import tpu as pltpu
from jax.sharding import PartitionSpec as P

NZ = 64
K = 8
L = 128
HALO = 8
HT = HALO * NZ // L
VMEM = 24 * 1024 * 1024
F32 = jnp.float32
BF16 = jnp.bfloat16


def tap_list():
    raw_taps = [math.exp(-(offset * offset) / 8.0) for offset in range(-4, 5)]
    tap_total = 0.0
    for value in raw_taps:
        tap_total = tap_total + value
    return [value / tap_total for value in raw_taps]


G4, G3, G2, G1, G0 = tap_list()[:5]


def depth_weights():
    taps = tap_list()
    band = np.zeros((L, L), np.float32)
    for i in range(L):
        for j in range(L):
            if i // NZ == j // NZ and abs(i - j) <= 4:
                band[i, j] = taps[i - j + 4]
    high = band.astype(BF16)
    low = (band - high.astype(np.float32)).astype(BF16)
    half = np.concatenate([high, low], axis=1)
    return np.concatenate([half, half], axis=0)


def nine(at):
    return (G0 * at(4) + G1 * (at(3) + at(5))) + (G2 * (at(2) + at(6)) + G3 * (at(1) + at(7))) + G4 * (at(0) + at(8))


def conv_x(src, dst):
    rows, tiles = dst.shape[0], dst.shape[1]

    def column(t, carry):
        for first in range(0, rows, 8):
            block = src[first : first + 16, t]
            dst[first : first + 8, t] = nine(lambda j: block[j : j + 8])
        return carry

    lax.fori_loop(0, tiles, column, 0)


def conv_yz(src, first, rows, w_ref):
    value = src[pl.ds(first, rows)]
    tiles = value.shape[1]
    n = tiles - 4
    flat = (rows * (tiles - 1) * K, L)
    lane = lax.broadcasted_iota(jnp.int32, flat, 1)
    mixed = jnp.where(lane < NZ, value[:, 1:].reshape(flat), value[:, :-1].reshape(flat))
    odd = pltpu.roll(mixed, NZ, axis=1).reshape(rows, tiles - 1, K, L)
    along = (G0 * value[:, 2 : n + 2] + G1 * (odd[:, 1 : n + 1] + odd[:, 2 : n + 2])) + (
        G2 * (value[:, 1 : n + 1] + value[:, 3 : n + 3]) + G3 * (odd[:, 0:n] + odd[:, 3 : n + 3])
    ) + G4 * (value[:, 0:n] + value[:, 4 : n + 4])
    along = along.reshape(rows * n * K, L)
    high = along.astype(BF16)
    low = (along - high.astype(F32)).astype(BF16)
    both = jnp.dot(jnp.concatenate([high, low], axis=1), w_ref[...], preferred_element_type=F32)
    return (both[:, :L] + both[:, L:]).reshape(rows, n, K, L)


def parities():
    return lax.rem(lax.axis_index("gx"), 2), lax.rem(lax.axis_index("gy"), 2)


def sides(rows, tiles):
    px, py = parities()
    return ((1 - px) * (rows + HALO), px * (rows + HALO)), ((1 - py) * (tiles + HT), py * (tiles + HT))


def assemble(big, own, got):
    rows, tiles = own.shape[0], own.shape[1]
    xa, xb, ya, yb, ca, cb = got
    (row_a, row_b), (col_a, col_b) = sides(rows, tiles)
    middle, slabs = pl.ds(HALO, rows), xa.shape[0]
    big[middle, pl.ds(HT, tiles)] = own[...]
    big[pl.ds(row_a, HALO), pl.ds(HT, tiles)] = xa[0:HALO]
    big[pl.ds(row_b, HALO), pl.ds(HT, tiles)] = xb[0:HALO]
    for col, y, c in ((col_a, ya, ca), (col_b, yb, cb)):
        big[middle, pl.ds(col, HT)] = y[0:rows]
        big[pl.ds(row_a, HALO), pl.ds(col, HT)] = c[0:HALO]
        big[pl.ds(row_b, HALO), pl.ds(col, HT)] = c[slabs : slabs + HALO]


def give_edges(own, outs):
    xa, xb, ya, yb = outs
    rows, tiles = own.shape[0], own.shape[1]
    px, py = parities()
    xa[0:HALO] = own[pl.ds((1 - px) * (rows - HALO), HALO)]
    xb[0:HALO] = own[pl.ds(px * (rows - HALO), HALO)]
    ya[0:rows] = own[:, pl.ds((1 - py) * (tiles - HT), HT)]
    yb[0:rows] = own[:, pl.ds(py * (tiles - HT), HT)]


def clear_outside(*fields):
    rows, tiles = fields[0].shape[0], fields[0].shape[1]
    gx, gy = lax.axis_index("gx"), lax.axis_index("gy")

    def zero(rs, ts):
        def write():
            for f in fields:
                f[rs, ts] = jnp.zeros_like(f[rs, ts])

        return write

    pl.when(gx == 0)(zero(slice(0, 4), slice(0, tiles)))
    pl.when(gx == lax.axis_size("gx") - 1)(zero(slice(rows - 4, rows), slice(0, tiles)))
    pl.when(gy == 0)(zero(slice(0, rows), slice(0, 2)))
    pl.when(gy == lax.axis_size("gy") - 1)(zero(slice(0, rows), slice(tiles - 2, tiles)))


def inside(at, count):
    total = jnp.zeros(at.shape, F32)
    for offset, tap in zip(range(-4, 5), tap_list()):
        total = total + jnp.where((at + offset >= 0) & (at + offset < count), F32(tap), F32(0.0))
    return total


def in_lanes(*columns):
    lane = lax.broadcasted_iota(jnp.int32, (K, L), 1)
    out = jnp.zeros((K, L), F32)
    for i, c in enumerate(columns):
        out = jnp.where(lane == i, c, out)
    return out


def over_lanes(value):
    return jnp.sum(value, axis=1, keepdims=True)


def centre(field):
    return jnp.log(over_lanes(field[field.shape[0] // 2, field.shape[1] // 2]) * (1.0 / L))


def start_kernel(log_ref, dens, e, mass, *rest):
    edges, (turn, around, sem) = rest[:4], rest[4:]
    rows, tiles = dens.shape[0], dens.shape[1]
    loads = [pltpu.make_async_copy(log_ref.at[:, pl.ds(t * L, L)], turn.at[t], sem.at[t]) for t in range(tiles)]
    for c in loads:
        c.start()
    lane = lax.broadcasted_iota(jnp.int32, (K, L), 1)
    depth = inside(lane % NZ, NZ)
    first = lax.axis_index("gy") * (tiles * L // NZ)
    for t in range(tiles):
        along = inside(first + t * (L // NZ) + lane // NZ, lax.axis_size("gy") * (tiles * L // NZ))
        around[t] = 1.0 / (along * depth)
    for c in loads:
        c.wait()

    def row(x, acc):
        across = 1.0 / inside(jnp.full((K, L), lax.axis_index("gx") * rows + x), lax.axis_size("gx") * rows)
        for t in range(tiles):
            d = jnp.exp(turn[t, pl.ds(x, K, stride=rows), :])
            dens[x, t] = d
            e[x, t] = d * (around[t] * across)
            acc = acc + d
        return acc

    mass[...] = lax.fori_loop(0, rows, row, jnp.zeros((K, L), F32))
    give_edges(e, edges)


def first_kernel(w_ref, wb, cot, dens, own, *rest):
    got, (inv_a, v, u, inv_s), edges, (big, tmp) = rest[:6], rest[6:10], rest[10:14], rest[14:]
    rows, tiles = own.shape[0], own.shape[1]
    assemble(big, own, got)
    conv_x(big, tmp)

    def ring(c, carry):
        s = pl.ds(c * 4, 4)
        spread = jnp.log(conv_yz(tmp, c * 4, 4, w_ref))
        log_q = jnp.sum(wb[...] * spread, axis=2, keepdims=True)
        v[s] = jnp.exp(log_q - spread)
        inv_a[s] = jnp.exp(-spread)
        return carry

    lax.fori_loop(0, (rows + 8) // 4, ring, 0)
    clear_outside(v, inv_a)
    tmp2 = tmp.at[pl.ds(0, rows), pl.ds(0, tiles + 4)]
    conv_x(v, tmp2)

    def inner(c, carry):
        s = pl.ds(c * 4, 4)
        inv = 1.0 / conv_yz(tmp2, c * 4, 4, w_ref)
        inv_s[s] = inv
        u[s] = dens[s] * inv
        return carry

    lax.fori_loop(0, rows // 4, inner, 0)
    give_edges(u, edges)
    xa, xb, ya, yb = edges
    px, py = parities()
    row_a = pl.ds(pl.multiple_of((1 - px) * (rows - 8), 8), 8)
    row_b = pl.ds(pl.multiple_of(px * (rows - 8), 8), 8)
    for t in range(tiles):
        xa[HALO, t] = cot[row_a, t * L : (t + 1) * L]
        xb[HALO, t] = cot[row_b, t * L : (t + 1) * L]
    for out, side in ((ya, 1 - py), (yb, py)):
        for t in range(HT):
            lanes = pl.ds(pl.multiple_of((side * (tiles - HT) + t) * L, L), L)
            for b in range(rows // 8):
                out[rows + b, t] = cot[b * 8 : b * 8 + 8, lanes]


def second_kernel(w_ref, wb, mass, cot, inv_s, own, *rest):
    got, (bu, z, q, told), edges, (big, tmp, r, cots, sums) = rest[:6], rest[6:10], rest[10:14], rest[14:]
    rows, tiles = own.shape[0], own.shape[1]
    assemble(big, own, got)
    (row_a, row_b), (col_a, col_b) = sides(rows, tiles)
    rxa, rxb, rya, ryb, rca, rcb = got
    slab = rxa.shape[0]
    ra, rb = pl.ds(pl.multiple_of(row_a, 8), 8), pl.ds(pl.multiple_of(row_b, 8), 8)
    for t in range(tiles):
        cots[HT + t, HALO : HALO + rows] = cot[:, t * L : (t + 1) * L]
        cots[HT + t, ra] = rxa[HALO, t]
        cots[HT + t, rb] = rxb[HALO, t]
    for col, y, c in ((col_a, rya, rca), (col_b, ryb, rcb)):
        for t in range(HT):
            for b in range(rows // 8):
                cots[col + t, HALO + b * 8 : HALO + b * 8 + 8] = y[rows + b, t]
            cots[col + t, ra] = c[HALO, t]
            cots[col + t, rb] = c[slab + HALO, t]
    conv_x(big, tmp)
    mean = centre(own)

    def ring(c, mine):
        spread = jnp.log(conv_yz(tmp, c * 4, 4, w_ref))
        log_q = jnp.sum(wb[...] * spread, axis=2, keepdims=True)
        ratio = wb[...] * jnp.exp(log_q - spread)
        acc_k = jnp.zeros((K, L), F32)
        acc_s = jnp.zeros((1, L), F32)
        for i in range(4):
            for t in range(tiles + 4):
                cell = cots[t + 2, pl.ds(c * 4 + i + 4, 1), :]
                r[c * 4 + i, t] = ratio[i, t] * cell
                if mine and 2 <= t < tiles + 2:
                    row_q = jnp.exp(log_q[i, t])
                    q[t - 2, pl.ds(c * 4 + i - 4, 1), :] = row_q[0:1]
                    combined = cell * row_q[0:1]
                    acc_s = acc_s + combined
                    acc_k = acc_k + combined * (spread[i, t] - mean)
        if mine:
            sums[0] += acc_k
            sums[1, 0:1] += acc_s

    sums[...] = jnp.zeros_like(sums)
    ring(0, False)
    ring((rows + 4) // 4, False)

    def middle(c, carry):
        ring(c, True)
        return carry

    lax.fori_loop(1, (rows + 4) // 4, middle, 0)
    clear_outside(r)
    told[...] = in_lanes(over_lanes(mass[...]), over_lanes(sums[0]), over_lanes(sums[1, 0:1]), mean)
    tmp2 = tmp.at[pl.ds(0, rows), pl.ds(0, tiles + 4)]
    conv_x(r, tmp2)

    def inner(c, carry):
        s = pl.ds(c * 4, 4)
        back = own[s] * conv_yz(tmp2, c * 4, 4, w_ref)
        bu[s] = back
        z[s] = back * inv_s[s]
        return carry

    lax.fori_loop(0, rows // 4, inner, 0)
    give_edges(z, edges)


def third_kernel(w_ref, wb, before, inv_a, v, e, own, *rest):
    got, (r, told), (big, tmp, sums) = rest[:6], rest[6:8], rest[8:]
    rows, tiles = own.shape[0], own.shape[1]
    assemble(big, own, got)
    conv_x(big, tmp)
    mean = centre(e)

    def ring(c, mine):
        s = pl.ds(c * 4, 4)
        back_v = -(v[s] * conv_yz(tmp, c * 4, 4, w_ref))
        combined = jnp.sum(back_v, axis=2, keepdims=True)
        inv = inv_a[s]
        r[s] = (wb[...] * combined - back_v) * inv
        if mine:
            part = combined[:, 2 : tiles + 2]
            sums[0] += jnp.sum(part * (-jnp.log(inv[:, 2 : tiles + 2]) - mean), axis=(0, 1))
            sums[1, 0:1] += jnp.sum(part, axis=(0, 1))

    sums[...] = jnp.zeros_like(sums)
    ring(0, False)
    ring((rows + 4) // 4, False)

    def middle(c, carry):
        ring(c, True)
        return carry

    lax.fori_loop(1, (rows + 4) // 4, middle, 0)
    early = before[...]
    told[...] = in_lanes(*[early[:, i : i + 1] for i in range(4)], over_lanes(sums[0]), over_lanes(sums[1, 0:1]), mean)


def fourth_kernel(w_ref, r, bu, e, gp, tmp2):
    conv_x(r, tmp2)

    def inner(c, carry):
        s = pl.ds(c * 4, 4)
        gp[s] = bu[s] + e[s] * conv_yz(tmp2, c * 4, 4, w_ref)
        return carry

    lax.fori_loop(0, gp.shape[0] // 4, inner, 0)


def last_kernel(cells, wb, heard, gp, dens, q, out, bary, theta_out, turn, sem):
    rows, tiles = gp.shape[0], gp.shape[1]
    weights = wb[:, 0:1]
    everyone = heard[...]
    total = jnp.sum(everyone, axis=0)
    mass, late = total[:, 0:1], total[:, 2:3]
    shift_k = jnp.log(F32(cells)) - jnp.log(mass)
    shift = jnp.sum(weights * shift_k, axis=0, keepdims=True)
    scale = jnp.exp(shift)
    last = weights * (scale * late)
    grad_sums = last + (last - weights * jnp.sum(last, axis=0, keepdims=True))
    coef = jnp.broadcast_to(grad_sums / mass, (K, L))
    scale_all = jnp.broadcast_to(scale, (K, L))
    copies = []
    for t in range(tiles):

        def rows_of(c, carry):
            for i in range(8):
                x = c * 8 + i
                turn[t, pl.ds(x, K, stride=rows), :] = gp[x, t] * scale_all - dens[x, t] * coef
            return carry

        lax.fori_loop(0, rows // 8, rows_of, 0)
        copies.append(pltpu.make_async_copy(turn.at[t], out.at[:, pl.ds(t * L, L)], sem.at[t]))
        copies[-1].start()
        bary[:, t * L : (t + 1) * L] = q[t] * scale
    second = everyone[:, :, 1:2] + (everyone[:, :, 3:4] + (2.0 * shift_k - shift)) * everyone[:, :, 2:3]
    first = everyone[:, :, 4:5] + (everyone[:, :, 6:7] + shift_k) * everyone[:, :, 5:6]
    weight_grad = scale * jnp.sum(first + second, axis=0)
    grad = weights * (weight_grad - jnp.sum(weights * weight_grad, axis=0, keepdims=True))
    theta_out[...] = jnp.broadcast_to(grad, (K, L))
    for c in copies:
        c.wait()


def call(kernel, outs, scratch, semaphores, args, kept=True, far_in=0, far_out=0):
    vmem, far = pl.BlockSpec(memory_space=pltpu.VMEM), pl.BlockSpec(memory_space=pl.ANY)
    near = len(args) - far_in
    args = [pltpu.with_memory_space_constraint(a, pltpu.VMEM) if kept and a.size > L * L * 4 else a for a in args[:near]] + args[near:]
    return pl.pallas_call(
        kernel,
        out_shape=[pltpu.VMEM(s, F32) if kept else jax.ShapeDtypeStruct(s, F32) for s in outs],
        in_specs=[vmem] * near + [far] * far_in,
        out_specs=[far] * far_out + [vmem] * (len(outs) - far_out),
        scratch_shapes=[pltpu.VMEM(s, F32) for s in scratch] + [pltpu.SemaphoreType.DMA((n,)) for n in semaphores],
        compiler_params=pltpu.CompilerParams(vmem_limit_bytes=VMEM),
    )(*args)


def partners(axis, parity):
    count = lax.axis_size(axis)
    found = {}
    for i in range(count):
        j = i + 1 if i % 2 == parity else i - 1
        if 0 <= j < count:
            found[i] = j
    return found


def swap(value, axis, parity):
    return lax.ppermute(value, axis, list(partners(axis, parity).items()))


def exchange(xa, xb, ya, yb, tiles):
    rxa, rxb = swap(xa, "gx", 0), swap(xb, "gx", 1)
    rya, ryb = swap(ya, "gy", 0), swap(yb, "gy", 1)
    py = lax.rem(lax.axis_index("gy"), 2)

    def corner(side):
        first = side * (tiles - HT)
        return jnp.concatenate([lax.dynamic_slice_in_dim(r, first, HT, axis=1) for r in (rxa, rxb)], axis=0)

    rca, rcb = swap(corner(1 - py), "gy", 0), swap(corner(py), "gy", 1)
    return rxa, rxb, rya, ryb, rca, rcb


def over_all(told):
    devices = lax.axis_size("gx") * lax.axis_size("gy")
    return lax.all_to_all(jnp.broadcast_to(told[None], (devices, K, L)), ("gx", "gy"), 0, 0, tiled=True)


def shards(log_dens, theta, cotangent):
    _, rows, merged = log_dens.shape
    tiles = merged // L
    cells = lax.axis_size("gx") * lax.axis_size("gy") * rows * merged
    wb = jnp.broadcast_to(jax.nn.softmax(theta)[:, None], (K, L))
    w = jnp.asarray(depth_weights())

    field, ringed, full = (rows, tiles, K, L), (rows + 8, tiles + 4, K, L), (rows + 16, tiles + 8, K, L)
    tmp, tmp2 = (rows + 8, tiles + 8, K, L), (rows, tiles + 4, K, L)
    acc, turn = (2, K, L), (tiles, K * rows, L)

    def edges(more, more_y):
        return [(HALO + more, tiles, K, L)] * 2 + [(rows + more_y, HT, K, L)] * 2

    logs = log_dens.reshape(K * rows, merged)
    dens, e, mass, *sent = call(start_kernel, [field, field, (K, L)] + edges(0, 0), [turn, (tiles, K, L)], [tiles], [logs], far_in=1)
    got = exchange(*sent, tiles)
    inv_a, v, u, inv_s, *sent = call(
        first_kernel, [ringed, ringed, field, field] + edges(1, rows // 8), [full, tmp], [], [w, wb, cotangent, dens, e, *got]
    )
    got = exchange(*sent, tiles)
    bu, z, q, told, *sent = call(
        second_kernel, [field, field, (tiles, rows, L), (K, L)] + edges(0, 0),
        [full, tmp, ringed, (tiles + 8, rows + 16, L), acc], [], [w, wb, mass, cotangent, inv_s, u, *got],
    )
    got = exchange(*sent, tiles)
    r, told = call(third_kernel, [ringed, (K, L)], [full, tmp, acc], [], [w, wb, told, inv_a, v, e, z, *got])
    heard = over_all(told)
    (gp,) = call(fourth_kernel, [field], [tmp2], [], [w, r, bu, e])
    grad, bary, grad_theta = call(
        functools.partial(last_kernel, cells), [(K * rows, merged), (rows, merged), (K, L)], [turn], [tiles],
        [wb, heard, gp, dens, q], False, 0, 1,
    )
    return bary, grad.reshape(K, rows, merged), grad_theta[:, 0]


def solution(mesh):
    placed = (P(None, "gx", "gy"), P(), P("gx", "gy"))
    return jax.shard_map(
        shards,
        mesh=mesh,
        in_specs=placed,
        out_specs=(P("gx", "gy"), P(None, "gx", "gy"), P()),
        check_vma=False,
    )
```

time: 209 us -> 178 us (0.85)
  blocking collectives: 35.7 us -> 0 us
  starting transfers between devices: 60.4 us -> 86.7 us
  Pallas kernels: 65.2 us -> 41.8 us
  other arithmetic: 13.6 us -> 3.27 us
  local copies, waits for them, and re-layouts: 5.59 us -> 14.4 us
  waiting for transfers between devices: 25.5 us -> 30.7 us
    all_to_all x1 -> x0, blocking collectives: 35.7 us -> none  [shards(): total = lax.all_to_all(local, ('gx', 'gy'), 0, 0, tiled=True).sum(axis=0)]
    all_to_all x0 -> x1, starting transfers between devices: none -> 26.3 us  [over_all(): lax.all_to_all(jnp.broadcast_to(told[None], (devices, K, L)), ('gx', 'gy'...]
    pallas_call x5 -> x6, Pallas kernels: 65.2 us -> 41.8 us  [call(): pl.pallas_call(kernel, out_shape=[pltpu.VMEM(s, F32) if kept else jax.Sha...]
    unnamed x42 -> x30, local copies, waits for them, and re-layouts: 1.45 us -> 12.7 us
    reduce_sum x5 -> x1, other arithmetic: 8.2 us -> 1.25 us  [shards(): wb = jnp.broadcast_to(jax.nn.softmax(theta)[:, None], (K, L))]
    all_to_all x0 -> x1, waiting for transfers between devices: none -> 5.08 us  [over_all(): lax.all_to_all(jnp.broadcast_to(told[None], (devices, K, L)), ('gx', 'gy'...]
    mul x1 -> x0, other arithmetic: 3.13 us -> none  [shards(): grad_theta = weights * (weight_grad - jnp.sum(weights * weight_grad))]
  transfers between devices with their start and end apart: 18 -> 19, of which waited for: 7 -> 8; matrix products, arithmetic and copies ran while one was open for 2% -> 2% of each run, Pallas kernels for 0% -> 2%
where the time goes in v2:
time: 178 us
  starting transfers between devices  86.7 us (49%)
  Pallas kernels  41.8 us (23%)
  waiting for transfers between devices  30.7 us (17%)
  local copies, waits for them, and re-layouts  14.4 us (8%)
  other arithmetic  3.27 us (2%)
    ppermute x18, starting transfers between devices, swap(): return lax.ppermute(value, axis, list(partners(axis, parity).items()))  60.4 us
    pallas_call x6, Pallas kernels, call(): pl.pallas_call(kernel, out_shape=[pltpu.VMEM(s, F32) if kept else jax.Sha...  41.8 us
    all_to_all x1, starting transfers between devices, over_all(): lax.all_to_all(jnp.broadcast_to(told[None], (devices, K, L)), ('gx', 'gy'...  26.3 us
    ppermute x18, waiting for transfers between devices, swap(): return lax.ppermute(value, axis, list(partners(axis, parity).items()))  25.7 us
    unnamed x30, local copies, waits for them, and re-layouts  12.7 us
    all_to_all x1, waiting for transfers between devices, over_all(): lax.all_to_all(jnp.broadcast_to(told[None], (devices, K, L)), ('gx', 'gy'...  5.08 us
  transfers between devices with their start and end apart: 19, of which 8 were waited for; matrix products, arithmetic and copies ran while one was open for 2% of the time, Pallas kernels for 2%

profile of v2, /device:TPU:1, one launch (start us, length us, event | category | flops | bytes accessed | tf_op | source)
XLA Modules:
  0.0 177.8 jit_solution(13869020134508842231)
XLA Ops:
  0.6 0.0 copy-start.14
  0.7 1.6 copy-done.10
  2.2 4.8 %shard_map.67 = (f32[32,16,8,128]{3,2,1,0:T(8,128)S(1)}, f32[32,16,8,128]{3,2,1,0:T(8,128)S(1)}, f32[8,128]{1,0:T(8,128)S(1)}, f32[8,16,8,128]{3,2,1,0:T(8,128)}...) custom-call(f32[256,2048]{1,0:T(8,128)S(1)} %bitcast.2), custom_call_target="tpu_custom_call" | custom-call | tf_op jit(solution)/shard_map/pallas_call | solution.py:370
  7.0 0.0 copy-start
  7.1 1.3 copy-done
  8.4 2.1 %collective-permute-start = (f32[8,16,8,128]{3,2,1,0:T(8,128)}, f32[8,16,8,128]{3,2,1,0:T(8,128)S(1)}, u32[]{:S(2)}, u32[]{:S(2)}) collective-permute-start(f32[8,16,8,128]{3,2,1,0:T(8,128)} %get-tuple-element.34), channel_id=1, source_target_pairs={{0,16},{16,0},{32,48},{48,32},{64,80},{80,64},{96,112},{112,96},{1... | collective-permute-start | bytes 1572872 | tf_op jit(solution)/shard_map/ppermute | solution.py:391
  10.5 0.7 collective-permute-start.1
  11.2 1.0 collective-permute-start.2
  12.2 4.6 %collective-permute-start.3 = (f32[32,4,8,128]{3,2,1,0:T(8,128)}, f32[32,4,8,128]{3,2,1,0:T(8,128)}, u32[]{:S(2)}, u32[]{:S(2)}) collective-permute-start(f32[32,4,8,128]{3,2,1,0:T(8,128)} %get-tuple-element.37), channel_id=1, source_target_pairs={{1,2},{2,1},{3,4},{4,3},{5,6},{6,5},{7,8},{8,7},{9,10},{10,9},{11,... | collective-permute-start | bytes 1572872 | tf_op jit(solution)/shard_map/ppermute | solution.py:391
  16.8 0.6 reduce_max.9
  17.4 4.5 %collective-permute-done.rest_0_ = f32[8,16,8,128]{3,2,1,0:T(8,128)S(1)} collective-permute-done((f32[8,16,8,128]{3,2,1,0:T(8,128)}, f32[8,16,8,128]{3,2,1,0:T(8,128)S(1)}, u32[]{:S(2)}, u32[]{:S(2)}) %collective-permute-start) | collective-permute-done | bytes 524320 | tf_op jit(solution)/shard_map/ppermute | solution.py:391
  22.0 0.0 collective-permute-done.1.rest_1_
  22.0 1.7 collective-permute-start.4
  23.8 4.7 %collective-permute-start.5 = (f32[16,4,8,128]{3,2,1,0:T(8,128)S(1)}, f32[16,4,8,128]{3,2,1,0:T(8,128)S(1)}, u32[]{:S(2)}, u32[]{:S(2)}) collective-permute-start(f32[16,4,8,128]{3,2,1,0:T(8,128)S(1)} %pad_maximum_fusion.3), channel_id=1, source_target_pairs={{1,2},{2,1},{3,4},{4,3},{5,6},{6,5},{7,8},{8,7},{9,10},{10,9},{11,... | collective-permute-start | bytes 786440 | tf_op jit(solution)/shard_map/ppermute | solution.py:391
  28.5 1.3 fusion
  29.8 1.3 broadcast_divide_fusion
  31.1 0.0 collective-permute-done.2.rest_2_
  31.1 0.0 collective-permute-done.3.rest_3_
  31.1 0.0 collective-permute-done.4.rest_4_
  31.1 3.9 %collective-permute-done.5.rest_5_ = f32[16,4,8,128]{3,2,1,0:T(8,128)S(1)} collective-permute-done((f32[16,4,8,128]{3,2,1,0:T(8,128)S(1)}, f32[16,4,8,128]{3,2,1,0:T(8,128)S(1)}, u32[]{:S(2)}, u32[]{:S(2)}) %collective-permute-start.5) | collective-permute-done | bytes 262176 | tf_op jit(solution)/shard_map/ppermute | solution.py:391
  34.9 0.1 broadcast_in_dim.4.wb
  35.0 0.0 copy-done.11
  35.0 11.9 %shard_map.68 = (f32[40,20,8,128]{3,2,1,0:T(8,128)S(1)}, f32[40,20,8,128]{3,2,1,0:T(8,128)S(1)}, f32[32,16,8,128]{3,2,1,0:T(8,128)S(1)}, f32[32,16,8,128]{3,2,1,...) custom-call(bf16[256,256]{1,0:T(8,128)(2,1)S(1)} %copy-done.7, ...), custom_call_target="tpu_custom_call" | custom-call | tf_op jit(solution)/shard_map/pallas_call | solution.py:370
  46.9 4.4 %collective-permute-start.6 = (f32[9,16,8,128]{3,2,1,0:T(8,128)S(1)}, f32[9,16,8,128]{3,2,1,0:T(8,128)S(1)}, u32[]{:S(2)}, u32[]{:S(2)}) collective-permute-start(f32[9,16,8,128]{3,2,1,0:T(8,128)S(1)} %get-tuple-element.40), channel_id=1, source_target_pairs={{0,16},{16,0},{32,48},{48,32},{64,80},{80,64},{96,112},{112,96},{1... | collective-permute-start | bytes 1769480 | tf_op jit(solution)/shard_map/ppermute | solution.py:391
  51.3 0.7 collective-permute-start.7
  52.0 0.1 collective-permute-start.8
  52.0 6.3 %collective-permute-start.9 = (f32[36,4,8,128]{3,2,1,0:T(8,128)S(1)}, f32[36,4,8,128]{3,2,1,0:T(8,128)S(1)}, u32[]{:S(2)}, u32[]{:S(2)}) collective-permute-start(f32[36,4,8,128]{3,2,1,0:T(8,128)S(1)} %get-tuple-element.43), channel_id=1, source_target_pairs={{1,2},{2,1},{3,4},{4,3},{5,6},{6,5},{7,8},{8,7},{9,10},{10,9},{11,... | collective-permute-start | bytes 1769480 | tf_op jit(solution)/shard_map/ppermute | solution.py:391
  58.4 0.1 collective-permute-done.6.rest_0_
  58.6 0.0 collective-permute-done.7.rest_1_
  58.6 0.1 collective-permute-start.10
  58.8 9.7 %collective-permute-start.11 = (f32[18,4,8,128]{3,2,1,0:T(8,128)S(1)}, f32[18,4,8,128]{3,2,1,0:T(8,128)S(1)}, u32[]{:S(2)}, u32[]{:S(2)}) collective-permute-start(f32[18,4,8,128]{3,2,1,0:T(8,128)S(1)} %pad_maximum_fusion.1), channel_id=1, source_target_pairs={{1,2},{2,1},{3,4},{4,3},{5,6},{6,5},{7,8},{8,7},{9,10},{10,9},{11,... | collective-permute-start | bytes 884744 | tf_op jit(solution)/shard_map/ppermute | solution.py:391
  68.4 0.0 collective-permute-done.8.rest_2_
  68.5 3.3 %collective-permute-done.9.rest_3_ = f32[36,4,8,128]{3,2,1,0:T(8,128)S(1)} collective-permute-done((f32[36,4,8,128]{3,2,1,0:T(8,128)S(1)}, f32[36,4,8,128]{3,2,1,0:T(8,128)S(1)}, u32[]{:S(2)}, u32[]{:S(2)}) %collective-permute-start.9) | collective-permute-done | bytes 589856 | tf_op jit(solution)/shard_map/ppermute | solution.py:391
  71.7 0.0 collective-permute-done.10.rest_4_
  71.7 6.0 %collective-permute-done.11.rest_5_ = f32[18,4,8,128]{3,2,1,0:T(8,128)S(1)} collective-permute-done((f32[18,4,8,128]{3,2,1,0:T(8,128)S(1)}, f32[18,4,8,128]{3,2,1,0:T(8,128)S(1)}, u32[]{:S(2)}, u32[]{:S(2)}) %collective-permute-start.11) | collective-permute-done | bytes 294944 | tf_op jit(solution)/shard_map/ppermute | solution.py:391
  77.7 11.1 %shard_map.69 = (f32[32,16,8,128]{3,2,1,0:T(8,128)S(1)}, f32[32,16,8,128]{3,2,1,0:T(8,128)S(1)}, f32[16,32,128]{2,1,0:T(8,128)S(1)}, f32[8,128]{1,0:T(8,128)S(1)...) custom-call(bf16[256,256]{1,0:T(8,128)(2,1)S(1)} %copy-done.7, ...), custom_call_target="tpu_custom_call" | custom-call | tf_op jit(solution)/shard_map/pallas_call | solution.py:370
  88.8 0.0 copy-start.12
  88.8 8.5 %collective-permute-start.12 = (f32[8,16,8,128]{3,2,1,0:T(8,128)S(1)}, f32[8,16,8,128]{3,2,1,0:T(8,128)S(1)}, u32[]{:S(2)}, u32[]{:S(2)}) collective-permute-start(f32[8,16,8,128]{3,2,1,0:T(8,128)S(1)} %get-tuple-element.48), channel_id=1, source_target_pairs={{0,16},{16,0},{32,48},{48,32},{64,80},{80,64},{96,112},{112,96},{1... | collective-permute-start | bytes 1572872 | tf_op jit(solution)/shard_map/ppermute | solution.py:391
  97.3 0.7 collective-permute-start.13
  98.0 0.1 collective-permute-start.14
  98.1 6.7 %collective-permute-start.15 = (f32[32,4,8,128]{3,2,1,0:T(8,128)S(1)}, f32[32,4,8,128]{3,2,1,0:T(8,128)S(1)}, u32[]{:S(2)}, u32[]{:S(2)}) collective-permute-start(f32[32,4,8,128]{3,2,1,0:T(8,128)S(1)} %get-tuple-element.51), channel_id=1, source_target_pairs={{1,2},{2,1},{3,4},{4,3},{5,6},{6,5},{7,8},{8,7},{9,10},{10,9},{11,... | collective-permute-start | bytes 1572872 | tf_op jit(solution)/shard_map/ppermute | solution.py:391
  104.8 0.0 collective-permute-done.12.rest_0_
  104.8 0.0 collective-permute-done.13.rest_1_
  104.9 0.1 collective-permute-start.16
  105.0 8.3 %collective-permute-start.17 = (f32[16,4,8,128]{3,2,1,0:T(8,128)S(1)}, f32[16,4,8,128]{3,2,1,0:T(8,128)S(1)}, u32[]{:S(2)}, u32[]{:S(2)}) collective-permute-start(f32[16,4,8,128]{3,2,1,0:T(8,128)S(1)} %pad_maximum_fusion.5), channel_id=1, source_target_pairs={{1,2},{2,1},{3,4},{4,3},{5,6},{6,5},{7,8},{8,7},{9,10},{10,9},{11,... | collective-permute-start | bytes 786440 | tf_op jit(solution)/shard_map/ppermute | solution.py:391
  113.3 0.0 collective-permute-done.14.rest_2_
  113.3 2.5 %collective-permute-done.15.rest_3_ = f32[32,4,8,128]{3,2,1,0:T(8,128)S(1)} collective-permute-done((f32[32,4,8,128]{3,2,1,0:T(8,128)S(1)}, f32[32,4,8,128]{3,2,1,0:T(8,128)S(1)}, u32[]{:S(2)}, u32[]{:S(2)}) %collective-permute-start.15) | collective-permute-done | bytes 524320 | tf_op jit(solution)/shard_map/ppermute | solution.py:391
  115.8 0.0 collective-permute-done.16.rest_4_
  115.8 5.4 %collective-permute-done.17.rest_5_ = f32[16,4,8,128]{3,2,1,0:T(8,128)S(1)} collective-permute-done((f32[16,4,8,128]{3,2,1,0:T(8,128)S(1)}, f32[16,4,8,128]{3,2,1,0:T(8,128)S(1)}, u32[]{:S(2)}, u32[]{:S(2)}) %collective-permute-start.17) | collective-permute-done | bytes 262176 | tf_op jit(solution)/shard_map/ppermute | solution.py:391
  121.2 6.4 %shard_map.70 = (f32[40,20,8,128]{3,2,1,0:T(8,128)S(1)}, f32[8,128]{1,0:T(8,128)S(1)}) custom-call(bf16[256,256]{1,0:T(8,128)(2,1)S(1)} %copy-done.7, f32[8,128]{1,0:T(8,128)S(1)} %broadcast_in_dim.4.wb, f32[8,128]{1,0:T(8,128)S(1)} %get-tuple-element.44.before, f32[40,20,8,128]{3,2,1,0:T(8,128)S(1)} %get-tuple-element.45.inv_a, ...), custom_call_target="tpu_custom_call" | custom-call | tf_op jit(solution)/shard_map/pallas_call | solution.py:370
  127.6 0.0 copy-done.12
  127.6 0.0 copy-start.5
  127.7 1.7 copy-done.5
  129.4 0.8 broadcast_in_dim.5
  130.2 26.3 %all-to-all-start = ((f32[128,8,128]{2,1,0:T(8,128)}), f32[128,8,128]{2,1,0:T(8,128)S(1)}, u32[]{:S(2)}, u32[]{:S(2)}) async-start(f32[128,8,128]{2,1,0:T(8,128)} %broadcast_in_dim.5), calls=%async_computation | async-start | bytes 1048576 | tf_op jit(solution)/shard_map/all_to_all | solution.py:409
  156.5 1.9 %copy-done.6 = f32[40,20,8,128]{3,2,1,0:T(8,128)S(1)} copy-done((f32[40,20,8,128]{3,2,1,0:T(8,128)S(1)}, f32[40,20,8,128]{3,2,1,0:T(8,128)}, u32[]{:S(2)}) %copy-start.6) | copy-done | bytes 3276824
  158.4 1.6 copy-done.9
  160.0 3.9 %shard_map.71.gp = f32[32,16,8,128]{3,2,1,0:T(8,128)S(1)} custom-call(bf16[256,256]{1,0:T(8,128)(2,1)S(1)} %copy-done.7, f32[40,20,8,128]{3,2,1,0:T(8,128)S(1)} %copy-done.6, f32[32,16,8,128]{3,2,1,0:T(8,128)S(1)} %copy-done.9, f32[32,16,8,128]{3,2,1,0:T(8,128)S(1)} %get-tuple-element.33.own.e), custom_call_target="tpu_custom_call" | custom-call | tf_op jit(solution)/shard_map/pallas_call | solution.py:370
  163.9 1.3 copy-done.3
  165.3 5.1 %all-to-all-done.heard = f32[128,8,128]{2,1,0:T(8,128)S(1)} async-done(((f32[128,8,128]{2,1,0:T(8,128)}), f32[128,8,128]{2,1,0:T(8,128)S(1)}, u32[]{:S(2)}, u32[]{:S(2)}) %all-to-all-start) | async-done | bytes 524320 | tf_op jit(solution)/shard_map/all_to_all | solution.py:409
  170.3 1.6 copy-done.2
  171.9 1.6 copy-done.4
  173.5 3.7 %shard_map.72 = (f32[256,2048]{1,0:T(8,128)}, f32[32,2048]{1,0:T(8,128)}, f32[8,128]{1,0:T(8,128)S(1)}) custom-call(f32[8,128]{1,0:T(8,128)S(1)} %broadcast_in_dim.4.wb, f32[128,8,128]{2,1,0:T(8,128)S(1)} %all-to-all-done.heard, f32[32,16,8,128]{3,2,1,0:T(8,128)S(1)} %copy-done.4, f32[32,16,8,128]{3,2,1,0:T(8,128)S(1)} %copy-done.2, ...), custom_call_target="tpu_custom_call" | custom-call | tf_op jit(solution)/shard_map/pallas_call | solution.py:370
  177.2 0.6 slice_reduce_fusion
  (28 shorter events, 0.3 us)
Async XLA Ops:
  0.6 16.2 %copy-start.14 = (f32[8]{0:T(128)S(1)}, f32[8]{0:T(128)}, u32[]{:S(2)}) copy-start(f32[8]{0:T(128)} %param.5) | copy-start | bytes 100
  0.6 1.6 copy-start.10
  2.2 32.8 %copy-start.7 = (bf16[256,256]{1,0:T(8,128)(2,1)S(1)}, bf16[256,256]{1,0:T(8,128)(2,1)}, u32[]{:S(2)}) copy-start(bf16[256,256]{1,0:T(8,128)(2,1)} %constant.21.clone.w_ref) | copy-start | bytes 393220
  2.2 32.8 %copy-start.11 = (f32[32,2048]{1,0:T(8,128)S(1)}, f32[32,2048]{1,0:T(8,128)}, u32[]{:S(2)}) copy-start(f32[32,2048]{1,0:T(8,128)} %cot.3) | copy-start | bytes 786436
  7.0 1.3 copy-start
  8.4 13.6 %collective-permute-start = (f32[8,16,8,128]{3,2,1,0:T(8,128)}, f32[8,16,8,128]{3,2,1,0:T(8,128)S(1)}, u32[]{:S(2)}, u32[]{:S(2)}) collective-permute-start(f32[8,16,8,128]{3,2,1,0:T(8,128)} %get-tuple-element.34), channel_id=1, source_target_pairs={{0,16},{16,0},{32,48},{48,32},{64,80},{80,64},{96,112},{112,96},{1... | collective-permute-start | bytes 1572872 | tf_op jit(solution)/shard_map/ppermute | solution.py:391
  10.5 11.5 %collective-permute-start.1 = (f32[8,16,8,128]{3,2,1,0:T(8,128)}, f32[8,16,8,128]{3,2,1,0:T(8,128)S(1)}, u32[]{:S(2)}, u32[]{:S(2)}) collective-permute-start(f32[8,16,8,128]{3,2,1,0:T(8,128)} %get-tuple-element.35), channel_id=1, source_target_pairs={{16,32},{32,16},{48,64},{64,48},{80,96},{96,80},{17,33},{33,17},{4... | collective-permute-start | bytes 1572872 | tf_op jit(solution)/shard_map/ppermute | solution.py:391
  11.2 19.9 %collective-permute-start.2 = (f32[32,4,8,128]{3,2,1,0:T(8,128)}, f32[32,4,8,128]{3,2,1,0:T(8,128)}, u32[]{:S(2)}, u32[]{:S(2)}) collective-permute-start(f32[32,4,8,128]{3,2,1,0:T(8,128)} %get-tuple-element.36), channel_id=1, source_target_pairs={{0,1},{1,0},{2,3},{3,2},{4,5},{5,4},{6,7},{7,6},{8,9},{9,8},{10,11... | collective-permute-start | bytes 1572872 | tf_op jit(solution)/shard_map/ppermute | solution.py:391
  12.2 18.9 %collective-permute-start.3 = (f32[32,4,8,128]{3,2,1,0:T(8,128)}, f32[32,4,8,128]{3,2,1,0:T(8,128)}, u32[]{:S(2)}, u32[]{:S(2)}) collective-permute-start(f32[32,4,8,128]{3,2,1,0:T(8,128)} %get-tuple-element.37), channel_id=1, source_target_pairs={{1,2},{2,1},{3,4},{4,3},{5,6},{6,5},{7,8},{8,7},{9,10},{10,9},{11,... | collective-permute-start | bytes 1572872 | tf_op jit(solution)/shard_map/ppermute | solution.py:391
  17.4 17.6 %copy-start.1 = (f32[32,16,8,128]{3,2,1,0:T(8,128)S(1)}, f32[32,16,8,128]{3,2,1,0:T(8,128)}, u32[]{:S(2)}) copy-start(f32[32,16,8,128]{3,2,1,0:T(8,128)} %copy-done) | copy-start | bytes 6291460
  22.0 9.1 %collective-permute-start.4 = (f32[16,4,8,128]{3,2,1,0:T(8,128)S(1)}, f32[16,4,8,128]{3,2,1,0:T(8,128)S(1)}, u32[]{:S(2)}, u32[]{:S(2)}) collective-permute-start(f32[16,4,8,128]{3,2,1,0:T(8,128)S(1)} %pad_maximum_fusion.2), channel_id=1, source_target_pairs={{0,1},{1,0},{2,3},{3,2},{4,5},{5,4},{6,7},{7,6},{8,9},{9,8},{10,11... | collective-permute-start | bytes 786440 | tf_op jit(solution)/shard_map/ppermute | solution.py:391
  23.8 11.2 %collective-permute-start.5 = (f32[16,4,8,128]{3,2,1,0:T(8,128)S(1)}, f32[16,4,8,128]{3,2,1,0:T(8,128)S(1)}, u32[]{:S(2)}, u32[]{:S(2)}) collective-permute-start(f32[16,4,8,128]{3,2,1,0:T(8,128)S(1)} %pad_maximum_fusion.3), channel_id=1, source_target_pairs={{1,2},{2,1},{3,4},{4,3},{5,6},{6,5},{7,8},{8,7},{9,10},{10,9},{11,... | collective-permute-start | bytes 786440 | tf_op jit(solution)/shard_map/ppermute | solution.py:391
  46.9 11.7 %collective-permute-start.6 = (f32[9,16,8,128]{3,2,1,0:T(8,128)S(1)}, f32[9,16,8,128]{3,2,1,0:T(8,128)S(1)}, u32[]{:S(2)}, u32[]{:S(2)}) collective-permute-start(f32[9,16,8,128]{3,2,1,0:T(8,128)S(1)} %get-tuple-element.40), channel_id=1, source_target_pairs={{0,16},{16,0},{32,48},{48,32},{64,80},{80,64},{96,112},{112,96},{1... | collective-permute-start | bytes 1769480 | tf_op jit(solution)/shard_map/ppermute | solution.py:391
  51.3 7.3 %collective-permute-start.7 = (f32[9,16,8,128]{3,2,1,0:T(8,128)S(1)}, f32[9,16,8,128]{3,2,1,0:T(8,128)S(1)}, u32[]{:S(2)}, u32[]{:S(2)}) collective-permute-start(f32[9,16,8,128]{3,2,1,0:T(8,128)S(1)} %get-tuple-element.41), channel_id=1, source_target_pairs={{16,32},{32,16},{48,64},{64,48},{80,96},{96,80},{17,33},{33,17},{4... | collective-permute-start | bytes 1769480 | tf_op jit(solution)/shard_map/ppermute | solution.py:391
  52.0 16.5 %collective-permute-start.8 = (f32[36,4,8,128]{3,2,1,0:T(8,128)S(1)}, f32[36,4,8,128]{3,2,1,0:T(8,128)S(1)}, u32[]{:S(2)}, u32[]{:S(2)}) collective-permute-start(f32[36,4,8,128]{3,2,1,0:T(8,128)S(1)} %get-tuple-element.42), channel_id=1, source_target_pairs={{0,1},{1,0},{2,3},{3,2},{4,5},{5,4},{6,7},{7,6},{8,9},{9,8},{10,11... | collective-permute-start | bytes 1769480 | tf_op jit(solution)/shard_map/ppermute | solution.py:391
  52.0 19.7 %collective-permute-start.9 = (f32[36,4,8,128]{3,2,1,0:T(8,128)S(1)}, f32[36,4,8,128]{3,2,1,0:T(8,128)S(1)}, u32[]{:S(2)}, u32[]{:S(2)}) collective-permute-start(f32[36,4,8,128]{3,2,1,0:T(8,128)S(1)} %get-tuple-element.43), channel_id=1, source_target_pairs={{1,2},{2,1},{3,4},{4,3},{5,6},{6,5},{7,8},{8,7},{9,10},{10,9},{11,... | collective-permute-start | bytes 1769480 | tf_op jit(solution)/shard_map/ppermute | solution.py:391
  58.6 13.1 %collective-permute-start.10 = (f32[18,4,8,128]{3,2,1,0:T(8,128)S(1)}, f32[18,4,8,128]{3,2,1,0:T(8,128)S(1)}, u32[]{:S(2)}, u32[]{:S(2)}) collective-permute-start(f32[18,4,8,128]{3,2,1,0:T(8,128)S(1)} %pad_maximum_fusion), channel_id=1, source_target_pairs={{0,1},{1,0},{2,3},{3,2},{4,5},{5,4},{6,7},{7,6},{8,9},{9,8},{10,11... | collective-permute-start | bytes 884744 | tf_op jit(solution)/shard_map/ppermute | solution.py:391
  58.8 18.9 %collective-permute-start.11 = (f32[18,4,8,128]{3,2,1,0:T(8,128)S(1)}, f32[18,4,8,128]{3,2,1,0:T(8,128)S(1)}, u32[]{:S(2)}, u32[]{:S(2)}) collective-permute-start(f32[18,4,8,128]{3,2,1,0:T(8,128)S(1)} %pad_maximum_fusion.1), channel_id=1, source_target_pairs={{1,2},{2,1},{3,4},{4,3},{5,6},{6,5},{7,8},{8,7},{9,10},{10,9},{11,... | collective-permute-start | bytes 884744 | tf_op jit(solution)/shard_map/ppermute | solution.py:391
  88.8 32.4 %copy-start.8 = (f32[32,16,8,128]{3,2,1,0:T(8,128)}, f32[32,16,8,128]{3,2,1,0:T(8,128)S(1)}, u32[]{:S(2)}) copy-start(f32[32,16,8,128]{3,2,1,0:T(8,128)S(1)} %get-tuple-element.54.bu) | copy-start | bytes 6291460
  88.8 38.8 %copy-start.12 = (f32[16,32,128]{2,1,0:T(8,128)}, f32[16,32,128]{2,1,0:T(8,128)S(1)}, u32[]{:S(2)}) copy-start(f32[16,32,128]{2,1,0:T(8,128)S(1)} %get-tuple-element.55.q) | copy-start | bytes 786436
  88.8 16.0 %collective-permute-start.12 = (f32[8,16,8,128]{3,2,1,0:T(8,128)S(1)}, f32[8,16,8,128]{3,2,1,0:T(8,128)S(1)}, u32[]{:S(2)}, u32[]{:S(2)}) collective-permute-start(f32[8,16,8,128]{3,2,1,0:T(8,128)S(1)} %get-tuple-element.48), channel_id=1, source_target_pairs={{0,16},{16,0},{32,48},{48,32},{64,80},{80,64},{96,112},{112,96},{1... | collective-permute-start | bytes 1572872 | tf_op jit(solution)/shard_map/ppermute | solution.py:391
  97.3 7.5 %collective-permute-start.13 = (f32[8,16,8,128]{3,2,1,0:T(8,128)S(1)}, f32[8,16,8,128]{3,2,1,0:T(8,128)S(1)}, u32[]{:S(2)}, u32[]{:S(2)}) collective-permute-start(f32[8,16,8,128]{3,2,1,0:T(8,128)S(1)} %get-tuple-element.49), channel_id=1, source_target_pairs={{16,32},{32,16},{48,64},{64,48},{80,96},{96,80},{17,33},{33,17},{4... | collective-permute-start | bytes 1572872 | tf_op jit(solution)/shard_map/ppermute | solution.py:391
  98.0 15.3 %collective-permute-start.14 = (f32[32,4,8,128]{3,2,1,0:T(8,128)S(1)}, f32[32,4,8,128]{3,2,1,0:T(8,128)S(1)}, u32[]{:S(2)}, u32[]{:S(2)}) collective-permute-start(f32[32,4,8,128]{3,2,1,0:T(8,128)S(1)} %get-tuple-element.50), channel_id=1, source_target_pairs={{0,1},{1,0},{2,3},{3,2},{4,5},{5,4},{6,7},{7,6},{8,9},{9,8},{10,11... | collective-permute-start | bytes 1572872 | tf_op jit(solution)/shard_map/ppermute | solution.py:391
  98.1 17.7 %collective-permute-start.15 = (f32[32,4,8,128]{3,2,1,0:T(8,128)S(1)}, f32[32,4,8,128]{3,2,1,0:T(8,128)S(1)}, u32[]{:S(2)}, u32[]{:S(2)}) collective-permute-start(f32[32,4,8,128]{3,2,1,0:T(8,128)S(1)} %get-tuple-element.51), channel_id=1, source_target_pairs={{1,2},{2,1},{3,4},{4,3},{5,6},{6,5},{7,8},{8,7},{9,10},{10,9},{11,... | collective-permute-start | bytes 1572872 | tf_op jit(solution)/shard_map/ppermute | solution.py:391
  104.9 10.9 %collective-permute-start.16 = (f32[16,4,8,128]{3,2,1,0:T(8,128)S(1)}, f32[16,4,8,128]{3,2,1,0:T(8,128)S(1)}, u32[]{:S(2)}, u32[]{:S(2)}) collective-permute-start(f32[16,4,8,128]{3,2,1,0:T(8,128)S(1)} %pad_maximum_fusion.4), channel_id=1, source_target_pairs={{0,1},{1,0},{2,3},{3,2},{4,5},{5,4},{6,7},{7,6},{8,9},{9,8},{10,11... | collective-permute-start | bytes 786440 | tf_op jit(solution)/shard_map/ppermute | solution.py:391
  105.0 16.2 %collective-permute-start.17 = (f32[16,4,8,128]{3,2,1,0:T(8,128)S(1)}, f32[16,4,8,128]{3,2,1,0:T(8,128)S(1)}, u32[]{:S(2)}, u32[]{:S(2)}) collective-permute-start(f32[16,4,8,128]{3,2,1,0:T(8,128)S(1)} %pad_maximum_fusion.5), channel_id=1, source_target_pairs={{1,2},{2,1},{3,4},{4,3},{5,6},{6,5},{7,8},{8,7},{9,10},{10,9},{11,... | collective-permute-start | bytes 786440 | tf_op jit(solution)/shard_map/ppermute | solution.py:391
  127.6 1.7 copy-start.5
  130.2 40.1 %all-to-all-start = ((f32[128,8,128]{2,1,0:T(8,128)}), f32[128,8,128]{2,1,0:T(8,128)S(1)}, u32[]{:S(2)}, u32[]{:S(2)}) async-start(f32[128,8,128]{2,1,0:T(8,128)} %broadcast_in_dim.5), calls=%async_computation | async-start | bytes 1048576 | tf_op jit(solution)/shard_map/all_to_all | solution.py:409
  156.5 1.9 %copy-start.6 = (f32[40,20,8,128]{3,2,1,0:T(8,128)S(1)}, f32[40,20,8,128]{3,2,1,0:T(8,128)}, u32[]{:S(2)}) copy-start(f32[40,20,8,128]{3,2,1,0:T(8,128)} %copy-done.5) | copy-start | bytes 9830404
  158.4 1.6 copy-start.9
  160.0 10.3 %copy-start.13 = (f32[16,32,128]{2,1,0:T(8,128)S(1)}, f32[16,32,128]{2,1,0:T(8,128)}, u32[]{:S(2)}) copy-start(f32[16,32,128]{2,1,0:T(8,128)} %copy-done.12) | copy-start | bytes 786436
  163.9 1.4 copy-start.3
  170.3 1.6 copy-start.2
  171.9 1.6 copy-start.4

commit v3 on v2

v3 whole, which is shorter than its diff:
```python
import functools
import math

import jax
import jax.numpy as jnp
import numpy as np
from jax import lax
from jax.experimental import pallas as pl
from jax.experimental.pallas import tpu as pltpu
from jax.sharding import PartitionSpec as P

NZ = 64
K = 8
L = 128
HALO = 8
HT = HALO * NZ // L
VMEM = 24 * 1024 * 1024
F32 = jnp.float32
BF16 = jnp.bfloat16


def tap_list():
    raw_taps = [math.exp(-(offset * offset) / 8.0) for offset in range(-4, 5)]
    tap_total = 0.0
    for value in raw_taps:
        tap_total = tap_total + value
    return [value / tap_total for value in raw_taps]


G4, G3, G2, G1, G0 = tap_list()[:5]


def depth_weights():
    taps = tap_list()
    band = np.zeros((L, L), np.float32)
    for i in range(L):
        for j in range(L):
            if i // NZ == j // NZ and abs(i - j) <= 4:
                band[i, j] = taps[i - j + 4]
    high = band.astype(BF16)
    low = (band - high.astype(np.float32)).astype(BF16)
    half = np.concatenate([high, low], axis=1)
    return np.concatenate([half, half], axis=0)


def nine(at):
    return (G0 * at(4) + G1 * (at(3) + at(5))) + (G2 * (at(2) + at(6)) + G3 * (at(1) + at(7))) + G4 * (at(0) + at(8))


def conv_xz(src, dst, w_ref, shift, ranges):
    rows = dst.shape[0]

    def pair(i, first):
        t = first + 2 * i
        two = pl.ds(t, 2)
        for x in range(0, rows, 8):
            block = src[x : x + 16, pl.ds(t - shift, 2)]
            dst[x : x + 8, two] = nine(lambda j: block[j : j + 8])
        value = dst[:, two].reshape(rows * 2 * K, L)
        high = value.astype(BF16)
        low = (value - high.astype(F32)).astype(BF16)
        both = jnp.dot(jnp.concatenate([high, low], axis=1), w_ref[...], preferred_element_type=F32)
        dst[:, two] = (both[:, :L] + both[:, L:]).reshape(rows, 2, K, L)
        return first

    for first, end in ranges:
        lax.fori_loop(0, (end - first) // 2, pair, first)


def conv_y(src, first, rows, tile, n):
    value = src[pl.ds(first, rows), tile : tile + n + 4]
    flat = (rows * (n + 3) * K, L)
    lane = lax.broadcasted_iota(jnp.int32, flat, 1)
    mixed = jnp.where(lane < NZ, value[:, 1:].reshape(flat), value[:, :-1].reshape(flat))
    odd = pltpu.roll(mixed, NZ, axis=1).reshape(rows, n + 3, K, L)
    return (G0 * value[:, 2 : n + 2] + G1 * (odd[:, 1 : n + 1] + odd[:, 2 : n + 2])) + (
        G2 * (value[:, 1 : n + 1] + value[:, 3 : n + 3]) + G3 * (odd[:, 0:n] + odd[:, 3 : n + 3])
    ) + G4 * (value[:, 0:n] + value[:, 4 : n + 4])


def parities():
    return lax.rem(lax.axis_index("gx"), 2), lax.rem(lax.axis_index("gy"), 2)


def sides(rows, tiles):
    px, py = parities()
    return ((1 - px) * (rows + HALO), px * (rows + HALO)), ((1 - py) * (tiles + HT), py * (tiles + HT))


def join_rows(big, own, xa, xb):
    rows = own.shape[0]
    (row_a, row_b), _ = sides(rows, own.shape[1])
    big[HALO : HALO + rows] = own[...]
    big[pl.ds(row_a, HALO)] = xa[0:HALO]
    big[pl.ds(row_b, HALO)] = xb[0:HALO]


def join_ends(ends, rows, slabs, ya, yb, ca, cb):
    (row_a, row_b), _ = sides(rows, 0)
    _, py = parities()
    for col, y, c in (((1 - py) * HT, ya, ca), (py * HT, yb, cb)):
        lanes = pl.ds(col, HT)
        ends[pl.ds(HALO, rows), lanes] = y[0:rows]
        ends[pl.ds(row_a, HALO), lanes] = c[0:HALO]
        ends[pl.ds(row_b, HALO), lanes] = c[slabs : slabs + HALO]


def give_edges(own, outs):
    xa, xb, ya, yb = outs
    rows, tiles = own.shape[0], own.shape[1]
    px, py = parities()
    xa[0:HALO] = own[pl.ds((1 - px) * (rows - HALO), HALO)]
    xb[0:HALO] = own[pl.ds(px * (rows - HALO), HALO)]
    ya[0:rows] = own[:, pl.ds((1 - py) * (tiles - HT), HT)]
    yb[0:rows] = own[:, pl.ds(py * (tiles - HT), HT)]


def clear_outside(fields, ranges, ends):
    rows, tiles = fields[0].shape[0], fields[0].shape[1]
    gx, gy = lax.axis_index("gx"), lax.axis_index("gy")

    def zero(first, count, ts):
        def write():
            for f in fields:
                for start, end in ts:
                    f[first : first + count, start:end] = jnp.zeros((count, end - start, K, L), F32)

        return write

    pl.when(gx == 0)(zero(0, 4, ranges))
    pl.when(gx == lax.axis_size("gx") - 1)(zero(rows - 4, 4, ranges))
    if ends:
        pl.when(gy == 0)(zero(0, rows, [(0, 2)]))
        pl.when(gy == lax.axis_size("gy") - 1)(zero(0, rows, [(tiles - 2, tiles)]))


def parts(tiles, inner):
    if inner:
        return [(HT, tiles + HT)], [(HT, tiles)], [(HT, tiles)], [(HT, tiles - HT)]
    return (
        [(0, HT), (tiles + HT, tiles + 2 * HT)],
        [(0, HT), (tiles, tiles + HT)],
        [(0, HT), (tiles, tiles + HT)],
        [(0, HT), (tiles - HT, tiles)],
    )


def first_conv(inner, src, tmp, w_ref, tiles):
    whole = parts(tiles, inner)[0]
    if inner:
        conv_xz(src, tmp, w_ref, HT, whole)
    else:
        conv_xz(src, tmp, w_ref, 0, whole[:1])
        conv_xz(src, tmp, w_ref, tiles, whole[1:])


def inside(at, count):
    total = jnp.zeros(at.shape, F32)
    for offset, tap in zip(range(-4, 5), tap_list()):
        total = total + jnp.where((at + offset >= 0) & (at + offset < count), F32(tap), F32(0.0))
    return total


def in_lanes(*columns):
    lane = lax.broadcasted_iota(jnp.int32, (K, L), 1)
    out = jnp.zeros((K, L), F32)
    for i, c in enumerate(columns):
        out = jnp.where(lane == i, c, out)
    return out


def over_lanes(value):
    return jnp.sum(value, axis=1, keepdims=True)


def centre(field):
    return jnp.log(over_lanes(field[field.shape[0] // 2, field.shape[1] // 2]) * (1.0 / L))


def start_kernel(log_ref, dens, e, mass, *rest):
    edges, (turn, around, sem) = rest[:4], rest[4:]
    rows, tiles = dens.shape[0], dens.shape[1]
    loads = [pltpu.make_async_copy(log_ref.at[:, pl.ds(t * L, L)], turn.at[t], sem.at[t]) for t in range(tiles)]
    for c in loads:
        c.start()
    lane = lax.broadcasted_iota(jnp.int32, (K, L), 1)
    depth = inside(lane % NZ, NZ)
    first = lax.axis_index("gy") * (tiles * L // NZ)
    for t in range(tiles):
        along = inside(first + t * (L // NZ) + lane // NZ, lax.axis_size("gy") * (tiles * L // NZ))
        around[t] = 1.0 / (along * depth)
    for c in loads:
        c.wait()

    def row(x, acc):
        across = 1.0 / inside(jnp.full((K, L), lax.axis_index("gx") * rows + x), lax.axis_size("gx") * rows)
        for t in range(tiles):
            d = jnp.exp(turn[t, pl.ds(x, K, stride=rows), :])
            dens[x, t] = d
            e[x, t] = d * (around[t] * across)
            acc = acc + d
        return acc

    mass[...] = lax.fori_loop(0, rows, row, jnp.zeros((K, L), F32))
    give_edges(e, edges)


def first_fields(inner, wb, w_ref, dens, src, tmp, v, inv_a, tmp2, u, inv_s):
    rows, tiles = dens.shape[0], dens.shape[1]
    _, outs, again, last = parts(tiles, inner)
    first_conv(inner, src, tmp, w_ref, tiles)

    def ring(c, carry):
        s = pl.ds(c * 4, 4)
        for start, end in outs:
            spread = jnp.log(conv_y(tmp, c * 4, 4, start, end - start))
            log_q = jnp.sum(wb[...] * spread, axis=2, keepdims=True)
            v[s, start:end] = jnp.exp(log_q - spread)
            inv_a[s, start:end] = jnp.exp(-spread)
        return carry

    lax.fori_loop(0, (rows + 8) // 4, ring, 0)
    clear_outside((v, inv_a), outs, not inner)
    conv_xz(v, tmp2, w_ref, 0, again)

    def second(c, carry):
        s = pl.ds(c * 4, 4)
        for start, end in last:
            inv = 1.0 / conv_y(tmp2, c * 4, 4, start, end - start)
            inv_s[s, start:end] = inv
            u[s, start:end] = dens[s, start:end] * inv
        return carry

    lax.fori_loop(0, rows // 4, second, 0)


def first_inner(w_ref, wb, dens, own, xa, xb, tmp, v, inv_a, tmp2, u, inv_s, big):
    join_rows(big, own, xa, xb)
    first_fields(True, wb, w_ref, dens, big, tmp, v, inv_a, tmp2, u, inv_s)


def first_outer(w_ref, wb, cot, dens, e, ya, yb, ca, cb, *rest):
    fields, dens_out, mean = rest[6:12], rest[12], rest[13]
    edges, (ends, sem) = rest[14:18], rest[18:]
    rows, tiles = dens.shape[0], dens.shape[1]
    kept = pltpu.make_async_copy(dens, dens_out, sem.at[0])
    kept.start()
    mean[...] = jnp.broadcast_to(centre(e), (K, L))
    join_ends(ends, rows, HALO, ya, yb, ca, cb)
    first_fields(False, wb, w_ref, dens, ends, *fields)
    give_edges(fields[4], edges)
    xa, xb, ya, yb = edges
    px, py = parities()
    row_a = pl.ds(pl.multiple_of((1 - px) * (rows - 8), 8), 8)
    row_b = pl.ds(pl.multiple_of(px * (rows - 8), 8), 8)
    for t in range(tiles):
        xa[HALO, t] = cot[row_a, t * L : (t + 1) * L]
        xb[HALO, t] = cot[row_b, t * L : (t + 1) * L]
    for out, side in ((ya, 1 - py), (yb, py)):
        for t in range(HT):
            lanes = pl.ds(pl.multiple_of((side * (tiles - HT) + t) * L, L), L)
            for b in range(rows // 8):
                out[rows + b, t] = cot[b * 8 : b * 8 + 8, lanes]
    kept.wait()


def second_fields(inner, wb, w_ref, mean, cots, own, inv_s, src, tmp, r, tmp2, bu, z, q, sums):
    rows, tiles = own.shape[0], own.shape[1]
    _, outs, again, last = parts(tiles, inner)
    first_conv(inner, src, tmp, w_ref, tiles)

    def ring(c, mine):
        acc_k = jnp.zeros((K, L), F32)
        acc_s = jnp.zeros((1, L), F32)
        for start, end in outs:
            spread = jnp.log(conv_y(tmp, c * 4, 4, start, end - start))
            log_q = jnp.sum(wb[...] * spread, axis=2, keepdims=True)
            ratio = wb[...] * jnp.exp(log_q - spread)
            for i in range(4):
                for t in range(start, end):
                    cell = cots[t + 2, pl.ds(c * 4 + i + 4, 1), :]
                    r[c * 4 + i, t] = ratio[i, t - start] * cell
                    if mine and 2 <= t < tiles + 2:
                        row_q = jnp.exp(log_q[i, t - start])
                        q[t - 2, pl.ds(c * 4 + i - 4, 1), :] = row_q[0:1]
                        combined = cell * row_q[0:1]
                        acc_s = acc_s + combined
                        acc_k = acc_k + combined * (spread[i, t - start] - mean)
        if mine:
            sums[0] += acc_k
            sums[1, 0:1] += acc_s

    ring(0, False)
    ring((rows + 4) // 4, False)

    def middle(c, carry):
        ring(c, True)
        return carry

    lax.fori_loop(1, (rows + 4) // 4, middle, 0)
    clear_outside((r,), outs, not inner)
    conv_xz(r, tmp2, w_ref, 0, again)

    def second(c, carry):
        s = pl.ds(c * 4, 4)
        for start, end in last:
            back = own[s, start:end] * conv_y(tmp2, c * 4, 4, start, end - start)
            bu[s, start:end] = back
            z[s, start:end] = back * inv_s[s, start:end]
        return carry

    lax.fori_loop(0, rows // 4, second, 0)


def second_inner(w_ref, wb, cot, inv_s, own, xa, xb, tmp, r, tmp2, bu, z, q, sums, big, cots):
    rows, tiles = own.shape[0], own.shape[1]
    join_rows(big, own, xa, xb)
    (row_a, row_b), _ = sides(rows, tiles)
    for t in range(tiles):
        cots[HT + t, HALO : HALO + rows] = cot[:, t * L : (t + 1) * L]
        cots[HT + t, pl.ds(pl.multiple_of(row_a, 8), 8)] = xa[HALO, t]
        cots[HT + t, pl.ds(pl.multiple_of(row_b, 8), 8)] = xb[HALO, t]
    sums[...] = jnp.zeros_like(sums)
    second_fields(True, wb, w_ref, centre(own), cots, own, inv_s, big, tmp, r, tmp2, bu, z, q, sums)


def second_outer(w_ref, wb, mass, cot, inv_s, own, xa, xb, ya, yb, ca, cb, *rest):
    tmp, r, tmp2, bu, z, q, sums = rest[7:14]
    told, edges, (ends, cots) = rest[14], rest[15:19], rest[19:]
    rows, tiles = own.shape[0], own.shape[1]
    slabs = xa.shape[0]
    join_ends(ends, rows, slabs, ya, yb, ca, cb)
    (row_a, row_b), (col_a, col_b) = sides(rows, tiles)
    row_a, row_b = pl.ds(pl.multiple_of(row_a, 8), 8), pl.ds(pl.multiple_of(row_b, 8), 8)
    for t in (0, 1, tiles - 2, tiles - 1):
        cots[HT + t, HALO : HALO + rows] = cot[:, t * L : (t + 1) * L]
        cots[HT + t, row_a] = xa[HALO, t]
        cots[HT + t, row_b] = xb[HALO, t]
    for col, y, c in ((col_a, ya, ca), (col_b, yb, cb)):
        for t in range(HT):
            for b in range(rows // 8):
                cots[col + t, HALO + b * 8 : HALO + b * 8 + 8] = y[rows + b, t]
            cots[col + t, row_a] = c[HALO, t]
            cots[col + t, row_b] = c[slabs + HALO, t]
    mean = centre(own)
    second_fields(False, wb, w_ref, mean, cots, own, inv_s, ends, tmp, r, tmp2, bu, z, q, sums)
    told[...] = in_lanes(over_lanes(mass[...]), over_lanes(sums[0]), over_lanes(sums[1, 0:1]), mean)
    give_edges(z, edges)


def third_fields(inner, wb, w_ref, mean, inv_a, v, e, bu, src, tmp, r, tmp2, gp, sums):
    rows, tiles = e.shape[0], e.shape[1]
    _, outs, again, last = parts(tiles, inner)
    first_conv(inner, src, tmp, w_ref, tiles)

    def ring(c, mine):
        s = pl.ds(c * 4, 4)
        for start, end in outs:
            back_v = -(v[s, start:end] * conv_y(tmp, c * 4, 4, start, end - start))
            combined = jnp.sum(back_v, axis=2, keepdims=True)
            inv = inv_a[s, start:end]
            r[s, start:end] = (wb[...] * combined - back_v) * inv
            if mine:
                low, high = max(start, 2) - start, min(end, tiles + 2) - start
                part = combined[:, low:high]
                sums[0] += jnp.sum(part * (-jnp.log(inv[:, low:high]) - mean), axis=(0, 1))
                sums[1, 0:1] += jnp.sum(part, axis=(0, 1))

    ring(0, False)
    ring((rows + 4) // 4, False)

    def middle(c, carry):
        ring(c, True)
        return carry

    lax.fori_loop(1, (rows + 4) // 4, middle, 0)
    conv_xz(r, tmp2, w_ref, 0, again)

    def second(c, carry):
        s = pl.ds(c * 4, 4)
        for start, end in last:
            gp[s, start:end] = bu[s, start:end] + e[s, start:end] * conv_y(tmp2, c * 4, 4, start, end - start)
        return carry

    lax.fori_loop(0, rows // 4, second, 0)


def third_inner(w_ref, wb, mean, inv_a, v, e, bu, own, xa, xb, tmp, r, tmp2, gp, sums, big):
    join_rows(big, own, xa, xb)
    sums[...] = jnp.zeros_like(sums)
    third_fields(True, wb, w_ref, mean[...], inv_a, v, e, bu, big, tmp, r, tmp2, gp, sums)


def third_outer(w_ref, wb, mean, before, inv_a, v, e, bu, q, ya, yb, ca, cb, *rest):
    tmp, r, tmp2, gp, sums = rest[5:10]
    gp_out, q_out, told, ends, sem = rest[10:]
    rows, tiles = e.shape[0], e.shape[1]
    middle = pl.ds(HT, tiles - 2 * HT)
    copies = [pltpu.make_async_copy(q, q_out, sem.at[0]), pltpu.make_async_copy(gp.at[:, middle], gp_out.at[:, middle], sem.at[1])]
    for c in copies:
        c.start()
    join_ends(ends, rows, HALO, ya, yb, ca, cb)
    third_fields(False, wb, w_ref, mean[...], inv_a, v, e, bu, ends, tmp, r, tmp2, gp, sums)
    for i, first in enumerate((0, tiles - HT)):
        lanes = pl.ds(first, HT)
        copies.append(pltpu.make_async_copy(gp.at[:, lanes], gp_out.at[:, lanes], sem.at[i + 2]))
        copies[-1].start()
    early = before[...]
    told[...] = in_lanes(
        *[early[:, i : i + 1] for i in range(4)], over_lanes(sums[0]), over_lanes(sums[1, 0:1]), mean[:, 0:1]
    )
    for c in copies:
        c.wait()


def last_kernel(cells, wb, heard, q, gp_far, dens_far, out, bary, theta_out, turn, gp, dens, sem):
    rows, tiles = gp.shape[0], gp.shape[1]
    loads = []
    for i, first in enumerate(range(0, tiles, 4)):
        lanes = pl.ds(first, 4)
        for j, (src, dst) in enumerate(((gp_far, gp), (dens_far, dens))):
            loads.append(pltpu.make_async_copy(src.at[:, lanes], dst.at[:, lanes], sem.at[tiles + 2 * i + j]))
            loads[-1].start()
    weights = wb[:, 0:1]
    everyone = heard[...]
    total = jnp.sum(everyone, axis=0)
    mass, late = total[:, 0:1], total[:, 2:3]
    shift_k = jnp.log(F32(cells)) - jnp.log(mass)
    shift = jnp.sum(weights * shift_k, axis=0, keepdims=True)
    scale = jnp.exp(shift)
    last = weights * (scale * late)
    grad_sums = last + (last - weights * jnp.sum(last, axis=0, keepdims=True))
    coef = jnp.broadcast_to(grad_sums / mass, (K, L))
    scale_all = jnp.broadcast_to(scale, (K, L))
    copies = []
    for t in range(tiles):

        def rows_of(c, carry):
            for i in range(8):
                x = c * 8 + i
                turn[t, pl.ds(x, K, stride=rows), :] = gp[x, t] * scale_all - dens[x, t] * coef
            return carry

        if t % 4 == 0:
            loads[t // 2].wait()
            loads[t // 2 + 1].wait()
        lax.fori_loop(0, rows // 8, rows_of, 0)
        copies.append(pltpu.make_async_copy(turn.at[t], out.at[:, pl.ds(t * L, L)], sem.at[t]))
        copies[-1].start()
        bary[:, t * L : (t + 1) * L] = q[t] * scale
    second = everyone[:, :, 1:2] + (everyone[:, :, 3:4] + (2.0 * shift_k - shift)) * everyone[:, :, 2:3]
    first = everyone[:, :, 4:5] + (everyone[:, :, 6:7] + shift_k) * everyone[:, :, 5:6]
    weight_grad = scale * jnp.sum(first + second, axis=0)
    grad = weights * (weight_grad - jnp.sum(weights * weight_grad, axis=0, keepdims=True))
    theta_out[...] = jnp.broadcast_to(grad, (K, L))
    for c in copies:
        c.wait()


def call(kernel, outs, scratch, semaphores, args, near_out=(), far_in=0, same=None):
    vmem, far = pl.BlockSpec(memory_space=pltpu.VMEM), pl.BlockSpec(memory_space=pl.ANY)
    near = len(args) - far_in
    args = [pltpu.with_memory_space_constraint(a, pltpu.VMEM if i < near else pltpu.HBM) for i, a in enumerate(args)]
    return pl.pallas_call(
        kernel,
        out_shape=outs,
        in_specs=[vmem] * near + [far] * far_in,
        out_specs=[far if i in near_out else vmem for i in range(len(outs))],
        scratch_shapes=[pltpu.VMEM(s, F32) for s in scratch] + [pltpu.SemaphoreType.DMA((n,)) for n in semaphores],
        input_output_aliases=same or {},
        compiler_params=pltpu.CompilerParams(vmem_limit_bytes=VMEM),
    )(*args)


def partners(axis, parity):
    count = lax.axis_size(axis)
    found = {}
    for i in range(count):
        j = i + 1 if i % 2 == parity else i - 1
        if 0 <= j < count:
            found[i] = j
    return found


def swap(value, axis, parity):
    return lax.ppermute(value, axis, list(partners(axis, parity).items()))


def exchange(xa, xb, ya, yb, tiles):
    rxa, rxb = swap(xa, "gx", 0), swap(xb, "gx", 1)
    rya, ryb = swap(ya, "gy", 0), swap(yb, "gy", 1)
    py = lax.rem(lax.axis_index("gy"), 2)

    def corner(side):
        first = side * (tiles - HT)
        return jnp.concatenate([lax.dynamic_slice_in_dim(r, first, HT, axis=1) for r in (rxa, rxb)], axis=0)

    rca, rcb = swap(corner(1 - py), "gy", 0), swap(corner(py), "gy", 1)
    return rxa, rxb, rya, ryb, rca, rcb


def over_all(told):
    devices = lax.axis_size("gx") * lax.axis_size("gy")
    return lax.all_to_all(jnp.broadcast_to(told[None], (devices, K, L)), ("gx", "gy"), 0, 0, tiled=True)


def shards(log_dens, theta, cotangent):
    _, rows, merged = log_dens.shape
    tiles = merged // L
    cells = lax.axis_size("gx") * lax.axis_size("gy") * rows * merged
    wb = jnp.broadcast_to(jax.nn.softmax(theta)[:, None], (K, L))
    w = jnp.asarray(depth_weights())

    field, ringed, big = (rows, tiles, K, L), (rows + 8, tiles + 4, K, L), (rows + 16, tiles, K, L)
    tmp, tmp2, ends = (rows + 8, tiles + 8, K, L), (rows, tiles + 4, K, L), (rows + 16, 2 * HT, K, L)
    acc, turn, small, cots, q_shape = (2, K, L), (tiles, K * rows, L), (K, L), (tiles + 8, rows + 16, L), (tiles, rows, L)

    def near(*shapes):
        return [pltpu.VMEM(s, F32) for s in shapes]

    def edges(more, more_y):
        return near(*[(HALO + more, tiles, K, L)] * 2, *[(rows + more_y, HT, K, L)] * 2)

    logs = log_dens.reshape(K * rows, merged)
    dens, e, mass, *sent = call(start_kernel, near(field, field, small) + edges(0, 0), [turn, (tiles, K, L)], [tiles], [logs], far_in=1)
    xa, xb, *others = exchange(*sent, tiles)
    held = [tmp, ringed, ringed, tmp2, field, field]
    held_now = call(first_inner, near(*held), [big], [], [w, wb, dens, e, xa, xb])
    _, v, inv_a, _, u, inv_s, dens_far, mean, *sent = call(
        first_outer, near(*held) + [pltpu.HBM(field, F32)] + near(small) + edges(1, rows // 8), [ends], [1],
        [w, wb, cotangent, dens, e, *others, *held_now], (6,), same={9 + i: i for i in range(6)},
    )
    xa, xb, *others = exchange(*sent, tiles)
    held = [tmp, ringed, tmp2, field, field, q_shape, acc]
    held_now = call(second_inner, near(*held), [big, cots], [], [w, wb, cotangent, inv_s, u, xa, xb])
    _, _, _, bu, z, q, _, told, *sent = call(
        second_outer, near(*held, small) + edges(0, 0), [ends, cots], [],
        [w, wb, mass, cotangent, inv_s, u, xa, xb, *others, *held_now], same={12 + i: i for i in range(7)},
    )
    xa, xb, *others = exchange(*sent, tiles)
    held = [tmp, ringed, tmp2, field, acc]
    held_now = call(third_inner, near(*held), [big], [], [w, wb, mean, inv_a, v, e, bu, z, xa, xb])
    *_, gp_far, q_far, told = call(
        third_outer, near(*held) + [pltpu.HBM(field, F32), pltpu.HBM(q_shape, F32)] + near(small), [ends], [4],
        [w, wb, mean, told, inv_a, v, e, bu, q, *others, *held_now], (5, 6), same={13 + i: i for i in range(5)},
    )
    plain = [jax.ShapeDtypeStruct(s, F32) for s in ((K * rows, merged), (rows, merged), small)]
    grad, bary, grad_theta = call(
        functools.partial(last_kernel, cells), plain, [turn, field, field], [tiles + tiles // 2],
        [wb, over_all(told), q_far, gp_far, dens_far], (0,), 2,
    )
    return bary, grad.reshape(K, rows, merged), grad_theta[:, 0]


def solution(mesh):
    placed = (P(None, "gx", "gy"), P(), P("gx", "gy"))
    return jax.shard_map(
        shards,
        mesh=mesh,
        in_specs=placed,
        out_specs=(P("gx", "gy"), P(None, "gx", "gy"), P()),
        check_vma=False,
    )
```

time: 178 us -> 171 us (0.961)
  blocking collectives: 0 us -> 36.1 us
  starting transfers between devices: 86.7 us -> 53 us
  waiting for transfers between devices: 30.7 us -> 9.53 us
  Pallas kernels: 41.8 us -> 54.9 us
  local copies, waits for them, and re-layouts: 14.4 us -> 12.1 us
    all_to_all x0 -> x1, blocking collectives: none -> 36.1 us  [over_all(): lax.all_to_all(jnp.broadcast_to(told[None], (devices, K, L)), ('gx', 'gy'...]
    all_to_all x1 -> x0, starting transfers between devices: 26.3 us -> none  [over_all(): lax.all_to_all(jnp.broadcast_to(told[None], (devices, K, L)), ('gx', 'gy'...]
    ppermute x18, waiting for transfers between devices: 25.7 us -> 9.53 us  [swap(): return lax.ppermute(value, axis, list(partners(axis, parity).items()))]
    pallas_call x6 -> x8, Pallas kernels: 41.8 us -> 54.9 us  [call(): pl.pallas_call(kernel, out_shape=outs, in_specs=[vmem] * near + [far] * f...]
    ppermute x18, starting transfers between devices: 60.4 us -> 53 us  [swap(): return lax.ppermute(value, axis, list(partners(axis, parity).items()))]
    all_to_all x1 -> x0, waiting for transfers between devices: 5.08 us -> none  [over_all(): lax.all_to_all(jnp.broadcast_to(told[None], (devices, K, L)), ('gx', 'gy'...]
    unnamed x30 -> x24, local copies, waits for them, and re-layouts: 12.7 us -> 11.2 us
  transfers between devices with their start and end apart: 19 -> 18, of which waited for: 8 -> 3; matrix products, arithmetic and copies ran while one was open for 2% -> 2% of each run, Pallas kernels for 2% -> 14%
where the time goes in v3:
time: 171 us
  Pallas kernels  54.9 us (32%)
  starting transfers between devices  53 us (31%)
  blocking collectives  36.1 us (21%)
  local copies, waits for them, and re-layouts  12.1 us (7%)
  waiting for transfers between devices  9.53 us (6%)
  other arithmetic  3.93 us (2%)
    pallas_call x8, Pallas kernels, call(): pl.pallas_call(kernel, out_shape=outs, in_specs=[vmem] * near + [far] * f...  54.9 us
    ppermute x18, starting transfers between devices, swap(): return lax.ppermute(value, axis, list(partners(axis, parity).items()))  53 us
    all_to_all x1, blocking collectives, over_all(): lax.all_to_all(jnp.broadcast_to(told[None], (devices, K, L)), ('gx', 'gy'...  36.1 us
    unnamed x24, local copies, waits for them, and re-layouts  11.2 us
    ppermute x18, waiting for transfers between devices, swap(): return lax.ppermute(value, axis, list(partners(axis, parity).items()))  9.53 us
  transfers between devices with their start and end apart: 18, of which 3 were waited for; matrix products, arithmetic and copies ran while one was open for 2% of the time, Pallas kernels for 14%

profile of v3, /device:TPU:1, one launch (start us, length us, event | category | flops | bytes accessed | tf_op | source)
XLA Modules:
  0.0 170.7 jit_solution(1786803596703942488)
XLA Ops:
  0.6 0.0 copy-start.4
  0.6 0.0 copy-start.11
  0.7 6.0 %shard_map.67 = (f32[32,16,8,128]{3,2,1,0:T(8,128)S(1)}, f32[32,16,8,128]{3,2,1,0:T(8,128)S(1)}, f32[8,128]{1,0:T(8,128)S(1)}, f32[8,16,8,128]{3,2,1,0:T(8,128)}...) custom-call(f32[256,2048]{1,0:T(8,128)} %bitcast.2), custom_call_target="tpu_custom_call" | custom-call | tf_op jit(solution)/shard_map/pallas_call | solution.py:464
  6.7 0.0 copy-start
  6.7 1.3 copy-done
  8.0 2.1 %collective-permute-start.2 = (f32[8,16,8,128]{3,2,1,0:T(8,128)}, f32[8,16,8,128]{3,2,1,0:T(8,128)S(1)}, u32[]{:S(2)}, u32[]{:S(2)}) collective-permute-start(f32[8,16,8,128]{3,2,1,0:T(8,128)} %get-tuple-element.56), channel_id=1, source_target_pairs={{0,16},{16,0},{32,48},{48,32},{64,80},{80,64},{96,112},{112,96},{1... | collective-permute-start | bytes 1572872 | tf_op jit(solution)/shard_map/ppermute | solution.py:486
  10.1 0.7 collective-permute-start.3
  10.8 1.0 collective-permute-start
  11.8 4.6 %collective-permute-start.1 = (f32[32,4,8,128]{3,2,1,0:T(8,128)}, f32[32,4,8,128]{3,2,1,0:T(8,128)}, u32[]{:S(2)}, u32[]{:S(2)}) collective-permute-start(f32[32,4,8,128]{3,2,1,0:T(8,128)} %get-tuple-element.55), channel_id=1, source_target_pairs={{1,2},{2,1},{3,4},{4,3},{5,6},{6,5},{7,8},{8,7},{9,10},{10,9},{11,... | collective-permute-start | bytes 1572872 | tf_op jit(solution)/shard_map/ppermute | solution.py:486
  16.4 1.3 reduce_max.9
  17.7 3.9 %collective-permute-done.2.xa = f32[8,16,8,128]{3,2,1,0:T(8,128)S(1)} collective-permute-done((f32[8,16,8,128]{3,2,1,0:T(8,128)}, f32[8,16,8,128]{3,2,1,0:T(8,128)S(1)}, u32[]{:S(2)}, u32[]{:S(2)}) %collective-permute-start.2) | collective-permute-done | bytes 524320 | tf_op jit(solution)/shard_map/ppermute | solution.py:486
  21.6 0.0 collective-permute-done.3.xb
  21.6 1.7 %collective-permute-start.4 = (f32[16,4,8,128]{3,2,1,0:T(8,128)S(1)}, f32[16,4,8,128]{3,2,1,0:T(8,128)S(1)}, u32[]{:S(2)}, u32[]{:S(2)}) collective-permute-start(f32[16,4,8,128]{3,2,1,0:T(8,128)S(1)} %pad_maximum_fusion.2), channel_id=1, source_target_pairs={{0,1},{1,0},{2,3},{3,2},{4,5},{5,4},{6,7},{7,6},{8,9},{9,8},{10,11... | collective-permute-start | bytes 786440 | tf_op jit(solution)/shard_map/ppermute | solution.py:486
  23.4 4.7 %collective-permute-start.5 = (f32[16,4,8,128]{3,2,1,0:T(8,128)S(1)}, f32[16,4,8,128]{3,2,1,0:T(8,128)S(1)}, u32[]{:S(2)}, u32[]{:S(2)}) collective-permute-start(f32[16,4,8,128]{3,2,1,0:T(8,128)S(1)} %pad_maximum_fusion.3), channel_id=1, source_target_pairs={{1,2},{2,1},{3,4},{4,3},{5,6},{6,5},{7,8},{8,7},{9,10},{10,9},{11,... | collective-permute-start | bytes 786440 | tf_op jit(solution)/shard_map/ppermute | solution.py:486
  28.1 0.0 copy-done.11
  28.1 1.3 fusion
  29.4 1.3 broadcast_divide_fusion
  30.7 0.1 broadcast_in_dim.4.wb
  30.8 0.0 copy-done.1
  30.8 8.2 %shard_map.68 = (f32[40,24,8,128]{3,2,1,0:T(8,128)S(1)}, f32[40,20,8,128]{3,2,1,0:T(8,128)S(1)}, f32[40,20,8,128]{3,2,1,0:T(8,128)S(1)}, f32[32,20,8,128]{3,2,1,...) custom-call(bf16[256,256]{1,0:T(8,128)(2,1)S(1)} %copy-done.4, ...), custom_call_target="tpu_custom_call" | custom-call | tf_op jit(solution)/shard_map/pallas_call | solution.py:464
  39.0 0.0 collective-permute-done.ya
  39.0 0.0 collective-permute-done.1.yb
  39.0 0.0 collective-permute-done.4.ca
  39.0 0.0 collective-permute-done.5.cb
  39.0 7.1 %shard_map.69 = (f32[40,24,8,128]{3,2,1,0:T(8,128)S(1)}, f32[40,20,8,128]{3,2,1,0:T(8,128)S(1)}, f32[40,20,8,128]{3,2,1,0:T(8,128)S(1)}, f32[32,20,8,128]{3,2,1,...) custom-call(bf16[256,256]{1,0:T(8,128)(2,1)S(1)} %copy-done.4, ...), custom_call_target="tpu_custom_call", output_to_operand_aliasing={{0}: (9, {}), {1}: (10, {}), {2}: (11, {}), {3}: (12, {}), ... | custom-call | tf_op jit(solution)/shard_map/pallas_call | solution.py:464
  46.1 4.0 %collective-permute-start.6 = (f32[9,16,8,128]{3,2,1,0:T(8,128)S(1)}, f32[9,16,8,128]{3,2,1,0:T(8,128)S(1)}, u32[]{:S(2)}, u32[]{:S(2)}) collective-permute-start(f32[9,16,8,128]{3,2,1,0:T(8,128)S(1)} %get-tuple-element.68), channel_id=1, source_target_pairs={{0,16},{16,0},{32,48},{48,32},{64,80},{80,64},{96,112},{112,96},{1... | collective-permute-start | bytes 1769480 | tf_op jit(solution)/shard_map/ppermute | solution.py:486
  50.1 0.7 collective-permute-start.7
  50.8 0.1 collective-permute-start.8
  50.9 3.9 %collective-permute-start.9 = (f32[36,4,8,128]{3,2,1,0:T(8,128)S(1)}, f32[36,4,8,128]{3,2,1,0:T(8,128)S(1)}, u32[]{:S(2)}, u32[]{:S(2)}) collective-permute-start(f32[36,4,8,128]{3,2,1,0:T(8,128)S(1)} %get-tuple-element.71), channel_id=1, source_target_pairs={{1,2},{2,1},{3,4},{4,3},{5,6},{6,5},{7,8},{8,7},{9,10},{10,9},{11,... | collective-permute-start | bytes 1769480 | tf_op jit(solution)/shard_map/ppermute | solution.py:486
  54.8 5.3 %collective-permute-done.6.xa = f32[9,16,8,128]{3,2,1,0:T(8,128)S(1)} collective-permute-done((f32[9,16,8,128]{3,2,1,0:T(8,128)S(1)}, f32[9,16,8,128]{3,2,1,0:T(8,128)S(1)}, u32[]{:S(2)}, u32[]{:S(2)}) %collective-permute-start.6) | collective-permute-done | bytes 589856 | tf_op jit(solution)/shard_map/ppermute | solution.py:486
  60.1 0.0 collective-permute-done.7.xb
  60.2 0.1 collective-permute-start.10
  60.3 7.1 %collective-permute-start.11 = (f32[18,4,8,128]{3,2,1,0:T(8,128)S(1)}, f32[18,4,8,128]{3,2,1,0:T(8,128)S(1)}, u32[]{:S(2)}, u32[]{:S(2)}) collective-permute-start(f32[18,4,8,128]{3,2,1,0:T(8,128)S(1)} %pad_maximum_fusion.1), channel_id=1, source_target_pairs={{1,2},{2,1},{3,4},{4,3},{5,6},{6,5},{7,8},{8,7},{9,10},{10,9},{11,... | collective-permute-start | bytes 884744 | tf_op jit(solution)/shard_map/ppermute | solution.py:486
  67.4 8.5 %shard_map.70 = (f32[40,24,8,128]{3,2,1,0:T(8,128)S(1)}, f32[40,20,8,128]{3,2,1,0:T(8,128)S(1)}, f32[32,20,8,128]{3,2,1,0:T(8,128)S(1)}, f32[32,16,8,128]{3,2,1,...) custom-call(bf16[256,256]{1,0:T(8,128)(2,1)S(1)} %copy-done.4, ...), custom_call_target="tpu_custom_call" | custom-call | tf_op jit(solution)/shard_map/pallas_call | solution.py:464
  76.0 1.9 %copy-done.5 = f32[40,24,8,128]{3,2,1,0:T(8,128)} copy-done((f32[40,24,8,128]{3,2,1,0:T(8,128)}, f32[40,24,8,128]{3,2,1,0:T(8,128)S(1)}, u32[]{:S(2)}) %copy-start.5) | copy-done | bytes 3932184
  77.8 1.7 copy-done.7
  79.5 0.0 collective-permute-done.8.ya
  79.5 0.0 collective-permute-done.9.yb
  79.5 0.0 collective-permute-done.10.ca
  79.5 0.0 collective-permute-done.11.cb
  79.6 2.1 %copy-done.6 = f32[40,24,8,128]{3,2,1,0:T(8,128)S(1)} copy-done((f32[40,24,8,128]{3,2,1,0:T(8,128)S(1)}, f32[40,24,8,128]{3,2,1,0:T(8,128)}, u32[]{:S(2)}) %copy-start.6) | copy-done | bytes 3932184
  81.7 1.9 %copy-done.8 = f32[40,20,8,128]{3,2,1,0:T(8,128)S(1)} copy-done((f32[40,20,8,128]{3,2,1,0:T(8,128)S(1)}, f32[40,20,8,128]{3,2,1,0:T(8,128)}, u32[]{:S(2)}) %copy-start.8) | copy-done | bytes 3276824
  83.6 5.8 %shard_map.71 = (f32[40,24,8,128]{3,2,1,0:T(8,128)S(1)}, f32[40,20,8,128]{3,2,1,0:T(8,128)S(1)}, f32[32,20,8,128]{3,2,1,0:T(8,128)S(1)}, f32[32,16,8,128]{3,2,1,...) custom-call(bf16[256,256]{1,0:T(8,128)(2,1)S(1)} %copy-done.4, ...), custom_call_target="tpu_custom_call", output_to_operand_aliasing={{0}: (12, {}), {1}: (13, {}), {2}: (14, {}), {3}: (15, {}),... | custom-call | tf_op jit(solution)/shard_map/pallas_call | solution.py:464
  89.4 0.0 copy-start.2
  89.4 1.3 copy-done.2
  90.8 7.3 %collective-permute-start.14 = (f32[8,16,8,128]{3,2,1,0:T(8,128)S(1)}, f32[8,16,8,128]{3,2,1,0:T(8,128)S(1)}, u32[]{:S(2)}, u32[]{:S(2)}) collective-permute-start(f32[8,16,8,128]{3,2,1,0:T(8,128)S(1)} %get-tuple-element.86), channel_id=1, source_target_pairs={{0,16},{16,0},{32,48},{48,32},{64,80},{80,64},{96,112},{112,96},{1... | collective-permute-start | bytes 1572872 | tf_op jit(solution)/shard_map/ppermute | solution.py:486
  98.1 0.7 collective-permute-start.15
  98.7 0.1 collective-permute-start.12
  98.8 5.6 %collective-permute-start.13 = (f32[32,4,8,128]{3,2,1,0:T(8,128)S(1)}, f32[32,4,8,128]{3,2,1,0:T(8,128)S(1)}, u32[]{:S(2)}, u32[]{:S(2)}) collective-permute-start(f32[32,4,8,128]{3,2,1,0:T(8,128)S(1)} %get-tuple-element.85), channel_id=1, source_target_pairs={{1,2},{2,1},{3,4},{4,3},{5,6},{6,5},{7,8},{8,7},{9,10},{10,9},{11,... | collective-permute-start | bytes 1572872 | tf_op jit(solution)/shard_map/ppermute | solution.py:486
  104.5 0.3 collective-permute-done.14.xa
  104.8 0.0 collective-permute-done.15.xb
  104.9 0.1 collective-permute-start.16
  105.0 8.5 %collective-permute-start.17 = (f32[16,4,8,128]{3,2,1,0:T(8,128)S(1)}, f32[16,4,8,128]{3,2,1,0:T(8,128)S(1)}, u32[]{:S(2)}, u32[]{:S(2)}) collective-permute-start(f32[16,4,8,128]{3,2,1,0:T(8,128)S(1)} %pad_maximum_fusion.5), channel_id=1, source_target_pairs={{1,2},{2,1},{3,4},{4,3},{5,6},{6,5},{7,8},{8,7},{9,10},{10,9},{11,... | collective-permute-start | bytes 786440 | tf_op jit(solution)/shard_map/ppermute | solution.py:486
  113.5 0.0 copy-done.3
  113.5 8.0 %shard_map.72 = (f32[40,24,8,128]{3,2,1,0:T(8,128)S(1)}, f32[40,20,8,128]{3,2,1,0:T(8,128)S(1)}, f32[32,20,8,128]{3,2,1,0:T(8,128)S(1)}, f32[32,16,8,128]{3,2,1,0:T(8,128)S(1)}, f32[2,8,128]{2,1,0:T(8,128)S(1)}) custom-call(bf16[256,256]{1,0:T(8,128)(2,1)S(1)} %copy-done.4, f32[8,128]{1,0:T(8,128)S(1)} %broadcast_in_dim.4.wb, ...), custom_call_target="tpu_custom_call" | custom-call | tf_op jit(solution)/shard_map/pallas_call | solution.py:464
  121.5 0.0 collective-permute-done.12.ya
  121.5 0.0 collective-permute-done.13.yb
  121.6 0.0 collective-permute-done.16.ca
  121.6 0.0 collective-permute-done.17.cb
  121.6 6.5 %shard_map.73 = (f32[40,24,8,128]{3,2,1,0:T(8,128)S(1)}, f32[40,20,8,128]{3,2,1,0:T(8,128)S(1)}, f32[32,20,8,128]{3,2,1,0:T(8,128)S(1)}, f32[32,16,8,128]{3,2,1,...) custom-call(bf16[256,256]{1,0:T(8,128)(2,1)S(1)} %copy-done.4, ...), custom_call_target="tpu_custom_call", output_to_operand_aliasing={{0}: (13, {}), {1}: (14, {}), {2}: (15, {}), {3}: (16, {}),... | custom-call | tf_op jit(solution)/shard_map/pallas_call | solution.py:464
  128.1 36.1 %all_to_all.5.heard = f32[128,8,128]{2,1,0:T(8,128)S(1)} all-to-all(f32[128,8,128]{2,1,0:T(8,128)S(1)} %broadcast_in_dim.5), channel_id=1, replica_groups=mesh['gx'=8,'gy'=16] {'gx','gy'}, dimensions={0} | all-to-all | bytes 1048576 | tf_op jit(solution)/shard_map/all_to_all | solution.py:504
  164.3 0.9 copy-done.10
  165.2 4.8 %shard_map.74 = (f32[256,2048]{1,0:T(8,128)}, f32[32,2048]{1,0:T(8,128)}, f32[8,128]{1,0:T(8,128)S(1)}) custom-call(f32[8,128]{1,0:T(8,128)S(1)} %broadcast_in_dim.4.wb, f32[128,8,128]{2,1,0:T(8,128)S(1)} %all_to_all.5.heard, f32[16,32,128]{2,1,0:T(8,128)S(1)} %copy-done.10, f32[32,16,8,128]{3,2,1,0:T(8,128)} %get-tuple-element.96.gp_far, ...), custom_call_target="tpu_custom_call" | custom-call | tf_op jit(solution)/shard_map/pallas_call | solution.py:464
  170.0 0.6 slice_reduce_fusion
  (23 shorter events, 0.3 us)
Async XLA Ops:
  0.6 30.1 %copy-start.4 = (bf16[256,256]{1,0:T(8,128)(2,1)S(1)}, bf16[256,256]{1,0:T(8,128)(2,1)}, u32[]{:S(2)}) copy-start(bf16[256,256]{1,0:T(8,128)(2,1)} %constant.21.clone.w_ref) | copy-start | bytes 393220
  0.6 27.5 %copy-start.11 = (f32[8]{0:T(128)S(1)}, f32[8]{0:T(128)}, u32[]{:S(2)}) copy-start(f32[8]{0:T(128)} %param.5) | copy-start | bytes 100
  6.7 1.3 copy-start
  8.0 13.6 %collective-permute-start.2 = (f32[8,16,8,128]{3,2,1,0:T(8,128)}, f32[8,16,8,128]{3,2,1,0:T(8,128)S(1)}, u32[]{:S(2)}, u32[]{:S(2)}) collective-permute-start(f32[8,16,8,128]{3,2,1,0:T(8,128)} %get-tuple-element.56), channel_id=1, source_target_pairs={{0,16},{16,0},{32,48},{48,32},{64,80},{80,64},{96,112},{112,96},{1... | collective-permute-start | bytes 1572872 | tf_op jit(solution)/shard_map/ppermute | solution.py:486
  10.1 11.5 %collective-permute-start.3 = (f32[8,16,8,128]{3,2,1,0:T(8,128)}, f32[8,16,8,128]{3,2,1,0:T(8,128)S(1)}, u32[]{:S(2)}, u32[]{:S(2)}) collective-permute-start(f32[8,16,8,128]{3,2,1,0:T(8,128)} %get-tuple-element.57), channel_id=1, source_target_pairs={{16,32},{32,16},{48,64},{64,48},{80,96},{96,80},{17,33},{33,17},{4... | collective-permute-start | bytes 1572872 | tf_op jit(solution)/shard_map/ppermute | solution.py:486
  10.8 28.2 %collective-permute-start = (f32[32,4,8,128]{3,2,1,0:T(8,128)}, f32[32,4,8,128]{3,2,1,0:T(8,128)}, u32[]{:S(2)}, u32[]{:S(2)}) collective-permute-start(f32[32,4,8,128]{3,2,1,0:T(8,128)} %get-tuple-element.54), channel_id=1, source_target_pairs={{0,1},{1,0},{2,3},{3,2},{4,5},{5,4},{6,7},{7,6},{8,9},{9,8},{10,11... | collective-permute-start | bytes 1572872 | tf_op jit(solution)/shard_map/ppermute | solution.py:486
  11.8 27.1 %collective-permute-start.1 = (f32[32,4,8,128]{3,2,1,0:T(8,128)}, f32[32,4,8,128]{3,2,1,0:T(8,128)}, u32[]{:S(2)}, u32[]{:S(2)}) collective-permute-start(f32[32,4,8,128]{3,2,1,0:T(8,128)} %get-tuple-element.55), channel_id=1, source_target_pairs={{1,2},{2,1},{3,4},{4,3},{5,6},{6,5},{7,8},{8,7},{9,10},{10,9},{11,... | collective-permute-start | bytes 1572872 | tf_op jit(solution)/shard_map/ppermute | solution.py:486
  17.7 13.1 %copy-start.1 = (f32[32,16,8,128]{3,2,1,0:T(8,128)S(1)}, f32[32,16,8,128]{3,2,1,0:T(8,128)}, u32[]{:S(2)}) copy-start(f32[32,16,8,128]{3,2,1,0:T(8,128)} %copy-done) | copy-start | bytes 6291460
  21.6 17.3 %collective-permute-start.4 = (f32[16,4,8,128]{3,2,1,0:T(8,128)S(1)}, f32[16,4,8,128]{3,2,1,0:T(8,128)S(1)}, u32[]{:S(2)}, u32[]{:S(2)}) collective-permute-start(f32[16,4,8,128]{3,2,1,0:T(8,128)S(1)} %pad_maximum_fusion.2), channel_id=1, source_target_pairs={{0,1},{1,0},{2,3},{3,2},{4,5},{5,4},{6,7},{7,6},{8,9},{9,8},{10,11... | collective-permute-start | bytes 786440 | tf_op jit(solution)/shard_map/ppermute | solution.py:486
  23.4 15.6 %collective-permute-start.5 = (f32[16,4,8,128]{3,2,1,0:T(8,128)S(1)}, f32[16,4,8,128]{3,2,1,0:T(8,128)S(1)}, u32[]{:S(2)}, u32[]{:S(2)}) collective-permute-start(f32[16,4,8,128]{3,2,1,0:T(8,128)S(1)} %pad_maximum_fusion.3), channel_id=1, source_target_pairs={{1,2},{2,1},{3,4},{4,3},{5,6},{6,5},{7,8},{8,7},{9,10},{10,9},{11,... | collective-permute-start | bytes 786440 | tf_op jit(solution)/shard_map/ppermute | solution.py:486
  30.8 8.2 %copy-start.9 = (f32[32,2048]{1,0:T(8,128)S(1)}, f32[32,2048]{1,0:T(8,128)}, u32[]{:S(2)}) copy-start(f32[32,2048]{1,0:T(8,128)} %cot.5) | copy-start | bytes 786436
  46.1 14.0 %collective-permute-start.6 = (f32[9,16,8,128]{3,2,1,0:T(8,128)S(1)}, f32[9,16,8,128]{3,2,1,0:T(8,128)S(1)}, u32[]{:S(2)}, u32[]{:S(2)}) collective-permute-start(f32[9,16,8,128]{3,2,1,0:T(8,128)S(1)} %get-tuple-element.68), channel_id=1, source_target_pairs={{0,16},{16,0},{32,48},{48,32},{64,80},{80,64},{96,112},{112,96},{1... | collective-permute-start | bytes 1769480 | tf_op jit(solution)/shard_map/ppermute | solution.py:486
  50.1 10.0 %collective-permute-start.7 = (f32[9,16,8,128]{3,2,1,0:T(8,128)S(1)}, f32[9,16,8,128]{3,2,1,0:T(8,128)S(1)}, u32[]{:S(2)}, u32[]{:S(2)}) collective-permute-start(f32[9,16,8,128]{3,2,1,0:T(8,128)S(1)} %get-tuple-element.69), channel_id=1, source_target_pairs={{16,32},{32,16},{48,64},{64,48},{80,96},{96,80},{17,33},{33,17},{4... | collective-permute-start | bytes 1769480 | tf_op jit(solution)/shard_map/ppermute | solution.py:486
  50.8 28.7 %collective-permute-start.8 = (f32[36,4,8,128]{3,2,1,0:T(8,128)S(1)}, f32[36,4,8,128]{3,2,1,0:T(8,128)S(1)}, u32[]{:S(2)}, u32[]{:S(2)}) collective-permute-start(f32[36,4,8,128]{3,2,1,0:T(8,128)S(1)} %get-tuple-element.70), channel_id=1, source_target_pairs={{0,1},{1,0},{2,3},{3,2},{4,5},{5,4},{6,7},{7,6},{8,9},{9,8},{10,11... | collective-permute-start | bytes 1769480 | tf_op jit(solution)/shard_map/ppermute | solution.py:486
  50.9 28.6 %collective-permute-start.9 = (f32[36,4,8,128]{3,2,1,0:T(8,128)S(1)}, f32[36,4,8,128]{3,2,1,0:T(8,128)S(1)}, u32[]{:S(2)}, u32[]{:S(2)}) collective-permute-start(f32[36,4,8,128]{3,2,1,0:T(8,128)S(1)} %get-tuple-element.71), channel_id=1, source_target_pairs={{1,2},{2,1},{3,4},{4,3},{5,6},{6,5},{7,8},{8,7},{9,10},{10,9},{11,... | collective-permute-start | bytes 1769480 | tf_op jit(solution)/shard_map/ppermute | solution.py:486
  60.2 19.4 %collective-permute-start.10 = (f32[18,4,8,128]{3,2,1,0:T(8,128)S(1)}, f32[18,4,8,128]{3,2,1,0:T(8,128)S(1)}, u32[]{:S(2)}, u32[]{:S(2)}) collective-permute-start(f32[18,4,8,128]{3,2,1,0:T(8,128)S(1)} %pad_maximum_fusion), channel_id=1, source_target_pairs={{0,1},{1,0},{2,3},{3,2},{4,5},{5,4},{6,7},{7,6},{8,9},{9,8},{10,11... | collective-permute-start | bytes 884744 | tf_op jit(solution)/shard_map/ppermute | solution.py:486
  60.3 19.2 %collective-permute-start.11 = (f32[18,4,8,128]{3,2,1,0:T(8,128)S(1)}, f32[18,4,8,128]{3,2,1,0:T(8,128)S(1)}, u32[]{:S(2)}, u32[]{:S(2)}) collective-permute-start(f32[18,4,8,128]{3,2,1,0:T(8,128)S(1)} %pad_maximum_fusion.1), channel_id=1, source_target_pairs={{1,2},{2,1},{3,4},{4,3},{5,6},{6,5},{7,8},{8,7},{9,10},{10,9},{11,... | collective-permute-start | bytes 884744 | tf_op jit(solution)/shard_map/ppermute | solution.py:486
  75.9 1.9 %copy-start.5 = (f32[40,24,8,128]{3,2,1,0:T(8,128)}, f32[40,24,8,128]{3,2,1,0:T(8,128)S(1)}, u32[]{:S(2)}) copy-start(f32[40,24,8,128]{3,2,1,0:T(8,128)S(1)} %get-tuple-element.72.rest_0_) | copy-start | bytes 11796484
  77.8 1.7 copy-start.7
  79.5 2.1 %copy-start.6 = (f32[40,24,8,128]{3,2,1,0:T(8,128)S(1)}, f32[40,24,8,128]{3,2,1,0:T(8,128)}, u32[]{:S(2)}) copy-start(f32[40,24,8,128]{3,2,1,0:T(8,128)} %copy-done.5) | copy-start | bytes 11796484
  81.7 1.9 %copy-start.8 = (f32[40,20,8,128]{3,2,1,0:T(8,128)S(1)}, f32[40,20,8,128]{3,2,1,0:T(8,128)}, u32[]{:S(2)}) copy-start(f32[40,20,8,128]{3,2,1,0:T(8,128)} %copy-done.7) | copy-start | bytes 9830404
  89.4 1.3 copy-start.2
  90.8 22.8 %copy-start.3 = (f32[32,16,8,128]{3,2,1,0:T(8,128)S(1)}, f32[32,16,8,128]{3,2,1,0:T(8,128)}, u32[]{:S(2)}) copy-start(f32[32,16,8,128]{3,2,1,0:T(8,128)} %copy-done.2) | copy-start | bytes 6291460
  90.8 14.0 %collective-permute-start.14 = (f32[8,16,8,128]{3,2,1,0:T(8,128)S(1)}, f32[8,16,8,128]{3,2,1,0:T(8,128)S(1)}, u32[]{:S(2)}, u32[]{:S(2)}) collective-permute-start(f32[8,16,8,128]{3,2,1,0:T(8,128)S(1)} %get-tuple-element.86), channel_id=1, source_target_pairs={{0,16},{16,0},{32,48},{48,32},{64,80},{80,64},{96,112},{112,96},{1... | collective-permute-start | bytes 1572872 | tf_op jit(solution)/shard_map/ppermute | solution.py:486
  98.1 6.8 %collective-permute-start.15 = (f32[8,16,8,128]{3,2,1,0:T(8,128)S(1)}, f32[8,16,8,128]{3,2,1,0:T(8,128)S(1)}, u32[]{:S(2)}, u32[]{:S(2)}) collective-permute-start(f32[8,16,8,128]{3,2,1,0:T(8,128)S(1)} %get-tuple-element.87), channel_id=1, source_target_pairs={{16,32},{32,16},{48,64},{64,48},{80,96},{96,80},{17,33},{33,17},{4... | collective-permute-start | bytes 1572872 | tf_op jit(solution)/shard_map/ppermute | solution.py:486
  98.7 22.8 %collective-permute-start.12 = (f32[32,4,8,128]{3,2,1,0:T(8,128)S(1)}, f32[32,4,8,128]{3,2,1,0:T(8,128)S(1)}, u32[]{:S(2)}, u32[]{:S(2)}) collective-permute-start(f32[32,4,8,128]{3,2,1,0:T(8,128)S(1)} %get-tuple-element.84), channel_id=1, source_target_pairs={{0,1},{1,0},{2,3},{3,2},{4,5},{5,4},{6,7},{7,6},{8,9},{9,8},{10,11... | collective-permute-start | bytes 1572872 | tf_op jit(solution)/shard_map/ppermute | solution.py:486
  98.8 22.7 %collective-permute-start.13 = (f32[32,4,8,128]{3,2,1,0:T(8,128)S(1)}, f32[32,4,8,128]{3,2,1,0:T(8,128)S(1)}, u32[]{:S(2)}, u32[]{:S(2)}) collective-permute-start(f32[32,4,8,128]{3,2,1,0:T(8,128)S(1)} %get-tuple-element.85), channel_id=1, source_target_pairs={{1,2},{2,1},{3,4},{4,3},{5,6},{6,5},{7,8},{8,7},{9,10},{10,9},{11,... | collective-permute-start | bytes 1572872 | tf_op jit(solution)/shard_map/ppermute | solution.py:486
  104.9 16.7 %collective-permute-start.16 = (f32[16,4,8,128]{3,2,1,0:T(8,128)S(1)}, f32[16,4,8,128]{3,2,1,0:T(8,128)S(1)}, u32[]{:S(2)}, u32[]{:S(2)}) collective-permute-start(f32[16,4,8,128]{3,2,1,0:T(8,128)S(1)} %pad_maximum_fusion.4), channel_id=1, source_target_pairs={{0,1},{1,0},{2,3},{3,2},{4,5},{5,4},{6,7},{7,6},{8,9},{9,8},{10,11... | collective-permute-start | bytes 786440 | tf_op jit(solution)/shard_map/ppermute | solution.py:486
  105.0 16.6 %collective-permute-start.17 = (f32[16,4,8,128]{3,2,1,0:T(8,128)S(1)}, f32[16,4,8,128]{3,2,1,0:T(8,128)S(1)}, u32[]{:S(2)}, u32[]{:S(2)}) collective-permute-start(f32[16,4,8,128]{3,2,1,0:T(8,128)S(1)} %pad_maximum_fusion.5), channel_id=1, source_target_pairs={{1,2},{2,1},{3,4},{4,3},{5,6},{6,5},{7,8},{8,7},{9,10},{10,9},{11,... | collective-permute-start | bytes 786440 | tf_op jit(solution)/shard_map/ppermute | solution.py:486
  164.3 1.0 copy-start.10

commit v4 on v3

--- a/solution.py
+++ b/solution.py
@@ -14,7 +14,7 @@
 L = 128
 HALO = 8
 HT = HALO * NZ // L
-VMEM = 24 * 1024 * 1024
+VMEM = 14 * 1024 * 1024
 F32 = jnp.float32
 BF16 = jnp.bfloat16
 
@@ -101,8 +101,8 @@
     for col, y, c in (((1 - py) * HT, ya, ca), (py * HT, yb, cb)):
         lanes = pl.ds(col, HT)
         ends[pl.ds(HALO, rows), lanes] = y[0:rows]
-        ends[pl.ds(row_a, HALO), lanes] = c[0:HALO]
-        ends[pl.ds(row_b, HALO), lanes] = c[slabs : slabs + HALO]
+        ends[pl.ds(row_b, HALO), lanes] = c[0:HALO]
+        ends[pl.ds(row_a, HALO), lanes] = c[slabs : slabs + HALO]
 
 
 def give_edges(own, outs):
@@ -177,31 +177,43 @@
     return jnp.log(over_lanes(field[field.shape[0] // 2, field.shape[1] // 2]) * (1.0 / L))
 
 
-def start_kernel(log_ref, dens, e, mass, *rest):
-    edges, (turn, around, sem) = rest[:4], rest[4:]
+def start_kernel(theta, log_ref, dens, e, mass, wb, *rest):
+    edges, (turn, across, sem) = rest[:4], rest[4:]
     rows, tiles = dens.shape[0], dens.shape[1]
     loads = [pltpu.make_async_copy(log_ref.at[:, pl.ds(t * L, L)], turn.at[t], sem.at[t]) for t in range(tiles)]
     for c in loads:
         c.start()
+    density = lax.broadcasted_iota(jnp.int32, (K, L), 0)
     lane = lax.broadcasted_iota(jnp.int32, (K, L), 1)
+    logits = jnp.zeros((K, L), F32)
+    for k in range(K):
+        logits = jnp.where(density == k, theta[k], logits)
+    powers = jnp.exp(logits - jnp.max(logits, axis=0, keepdims=True))
+    wb[...] = powers / jnp.sum(powers, axis=0, keepdims=True)
     depth = inside(lane % NZ, NZ)
     first = lax.axis_index("gy") * (tiles * L // NZ)
+
+    def factor(x, carry):
+        across[x] = 1.0 / inside(jnp.full((K, L), lax.axis_index("gx") * rows + x), lax.axis_size("gx") * rows)
+        return carry
+
+    lax.fori_loop(0, rows, factor, 0)
+    mass[...] = jnp.zeros((K, L), F32)
     for t in range(tiles):
         along = inside(first + t * (L // NZ) + lane // NZ, lax.axis_size("gy") * (tiles * L // NZ))
-        around[t] = 1.0 / (along * depth)
-    for c in loads:
-        c.wait()
-
-    def row(x, acc):
-        across = 1.0 / inside(jnp.full((K, L), lax.axis_index("gx") * rows + x), lax.axis_size("gx") * rows)
-        for t in range(tiles):
-            d = jnp.exp(turn[t, pl.ds(x, K, stride=rows), :])
-            dens[x, t] = d
-            e[x, t] = d * (around[t] * across)
-            acc = acc + d
-        return acc
-
-    mass[...] = lax.fori_loop(0, rows, row, jnp.zeros((K, L), F32))
+        around = 1.0 / (along * depth)
+        loads[t].wait()
+
+        def some(c, acc):
+            for i in range(8):
+                x = c * 8 + i
+                d = jnp.exp(turn[t, pl.ds(x, K, stride=rows), :])
+                dens[x, t] = d
+                e[x, t] = d * (around * across[x])
+                acc = acc + d
+            return acc
+
+        mass[...] += lax.fori_loop(0, rows // 8, some, jnp.zeros((K, L), F32))
     give_edges(e, edges)
 
 
@@ -234,12 +246,12 @@
     lax.fori_loop(0, rows // 4, second, 0)
 
 
-def first_inner(w_ref, wb, dens, own, xa, xb, tmp, v, inv_a, tmp2, u, inv_s, big):
+def first_inner(w_ref, wb, dens, own, xb, xa, tmp, v, inv_a, tmp2, u, inv_s, big):
     join_rows(big, own, xa, xb)
     first_fields(True, wb, w_ref, dens, big, tmp, v, inv_a, tmp2, u, inv_s)
 
 
-def first_outer(w_ref, wb, cot, dens, e, ya, yb, ca, cb, *rest):
+def first_outer(w_ref, wb, cot, dens, e, yb, ya, cb, ca, *rest):
     fields, dens_out, mean = rest[6:12], rest[12], rest[13]
     edges, (ends, sem) = rest[14:18], rest[18:]
     rows, tiles = dens.shape[0], dens.shape[1]
@@ -312,7 +324,7 @@
     lax.fori_loop(0, rows // 4, second, 0)
 
 
-def second_inner(w_ref, wb, cot, inv_s, own, xa, xb, tmp, r, tmp2, bu, z, q, sums, big, cots):
+def second_inner(w_ref, wb, cot, inv_s, own, xb, xa, tmp, r, tmp2, bu, z, q, sums, big, cots):
     rows, tiles = own.shape[0], own.shape[1]
     join_rows(big, own, xa, xb)
     (row_a, row_b), _ = sides(rows, tiles)
@@ -324,7 +336,7 @@
     second_fields(True, wb, w_ref, centre(own), cots, own, inv_s, big, tmp, r, tmp2, bu, z, q, sums)
 
 
-def second_outer(w_ref, wb, mass, cot, inv_s, own, xa, xb, ya, yb, ca, cb, *rest):
+def second_outer(w_ref, wb, mass, cot, inv_s, own, xb, xa, yb, ya, cb, ca, *rest):
     tmp, r, tmp2, bu, z, q, sums = rest[7:14]
     told, edges, (ends, cots) = rest[14], rest[15:19], rest[19:]
     rows, tiles = own.shape[0], own.shape[1]
@@ -340,8 +352,8 @@
         for t in range(HT):
             for b in range(rows // 8):
                 cots[col + t, HALO + b * 8 : HALO + b * 8 + 8] = y[rows + b, t]
-            cots[col + t, row_a] = c[HALO, t]
-            cots[col + t, row_b] = c[slabs + HALO, t]
+            cots[col + t, row_b] = c[HALO, t]
+            cots[col + t, row_a] = c[slabs + HALO, t]
     mean = centre(own)
     second_fields(False, wb, w_ref, mean, cots, own, inv_s, ends, tmp, r, tmp2, bu, z, q, sums)
     told[...] = in_lanes(over_lanes(mass[...]), over_lanes(sums[0]), over_lanes(sums[1, 0:1]), mean)
@@ -385,13 +397,13 @@
     lax.fori_loop(0, rows // 4, second, 0)
 
 
-def third_inner(w_ref, wb, mean, inv_a, v, e, bu, own, xa, xb, tmp, r, tmp2, gp, sums, big):
+def third_inner(w_ref, wb, mean, inv_a, v, e, bu, own, xb, xa, tmp, r, tmp2, gp, sums, big):
     join_rows(big, own, xa, xb)
     sums[...] = jnp.zeros_like(sums)
     third_fields(True, wb, w_ref, mean[...], inv_a, v, e, bu, big, tmp, r, tmp2, gp, sums)
 
 
-def third_outer(w_ref, wb, mean, before, inv_a, v, e, bu, q, ya, yb, ca, cb, *rest):
+def third_outer(w_ref, wb, mean, before, inv_a, v, e, bu, q, yb, ya, cb, ca, *rest):
     tmp, r, tmp2, gp, sums = rest[5:10]
     gp_out, q_out, told, ends, sem = rest[10:]
     rows, tiles = e.shape[0], e.shape[1]
@@ -457,19 +469,19 @@
         c.wait()
 
 
-def call(kernel, outs, scratch, semaphores, args, near_out=(), far_in=0, same=None):
+def call(kernel, outs, scratch, semaphores, args, near_out=(), far_in=0, same=None, numbers=()):
     vmem, far = pl.BlockSpec(memory_space=pltpu.VMEM), pl.BlockSpec(memory_space=pl.ANY)
     near = len(args) - far_in
     args = [pltpu.with_memory_space_constraint(a, pltpu.VMEM if i < near else pltpu.HBM) for i, a in enumerate(args)]
     return pl.pallas_call(
         kernel,
         out_shape=outs,
-        in_specs=[vmem] * near + [far] * far_in,
+        in_specs=[pl.BlockSpec(memory_space=pltpu.SMEM)] * len(numbers) + [vmem] * near + [far] * far_in,
         out_specs=[far if i in near_out else vmem for i in range(len(outs))],
         scratch_shapes=[pltpu.VMEM(s, F32) for s in scratch] + [pltpu.SemaphoreType.DMA((n,)) for n in semaphores],
         input_output_aliases=same or {},
         compiler_params=pltpu.CompilerParams(vmem_limit_bytes=VMEM),
-    )(*args)
+    )(*numbers, *args)
 
 
 def partners(axis, parity):
@@ -487,16 +499,17 @@
 
 
 def exchange(xa, xb, ya, yb, tiles):
-    rxa, rxb = swap(xa, "gx", 0), swap(xb, "gx", 1)
-    rya, ryb = swap(ya, "gy", 0), swap(yb, "gy", 1)
+    rxb, ryb = swap(xb, "gx", 1), swap(yb, "gy", 1)
+    rxa, rya = swap(xa, "gx", 0), swap(ya, "gy", 0)
     py = lax.rem(lax.axis_index("gy"), 2)
 
     def corner(side):
         first = side * (tiles - HT)
-        return jnp.concatenate([lax.dynamic_slice_in_dim(r, first, HT, axis=1) for r in (rxa, rxb)], axis=0)
-
-    rca, rcb = swap(corner(1 - py), "gy", 0), swap(corner(py), "gy", 1)
-    return rxa, rxb, rya, ryb, rca, rcb
+        return jnp.concatenate([lax.dynamic_slice_in_dim(r, first, HT, axis=1) for r in (rxb, rxa)], axis=0)
+
+    rcb = swap(corner(py), "gy", 1)
+    rca = swap(corner(1 - py), "gy", 0)
+    return rxa, rxb, ryb, rya, rcb, rca
 
 
 def over_all(told):
@@ -508,7 +521,6 @@
     _, rows, merged = log_dens.shape
     tiles = merged // L
     cells = lax.axis_size("gx") * lax.axis_size("gy") * rows * merged
-    wb = jnp.broadcast_to(jax.nn.softmax(theta)[:, None], (K, L))
     w = jnp.asarray(depth_weights())
 
     field, ringed, big = (rows, tiles, K, L), (rows + 8, tiles + 4, K, L), (rows + 16, tiles, K, L)
@@ -522,24 +534,26 @@
         return near(*[(HALO + more, tiles, K, L)] * 2, *[(rows + more_y, HT, K, L)] * 2)
 
     logs = log_dens.reshape(K * rows, merged)
-    dens, e, mass, *sent = call(start_kernel, near(field, field, small) + edges(0, 0), [turn, (tiles, K, L)], [tiles], [logs], far_in=1)
+    dens, e, mass, wb, *sent = call(
+        start_kernel, near(field, field, small, small) + edges(0, 0), [turn, (rows, K, L)], [tiles], [logs], far_in=1, numbers=(theta,)
+    )
     xa, xb, *others = exchange(*sent, tiles)
     held = [tmp, ringed, ringed, tmp2, field, field]
-    held_now = call(first_inner, near(*held), [big], [], [w, wb, dens, e, xa, xb])
+    held_now = call(first_inner, near(*held), [big], [], [w, wb, dens, e, xb, xa])
     _, v, inv_a, _, u, inv_s, dens_far, mean, *sent = call(
         first_outer, near(*held) + [pltpu.HBM(field, F32)] + near(small) + edges(1, rows // 8), [ends], [1],
         [w, wb, cotangent, dens, e, *others, *held_now], (6,), same={9 + i: i for i in range(6)},
     )
     xa, xb, *others = exchange(*sent, tiles)
     held = [tmp, ringed, tmp2, field, field, q_shape, acc]
-    held_now = call(second_inner, near(*held), [big, cots], [], [w, wb, cotangent, inv_s, u, xa, xb])
+    held_now = call(second_inner, near(*held), [big, cots], [], [w, wb, cotangent, inv_s, u, xb, xa])
     _, _, _, bu, z, q, _, told, *sent = call(
         second_outer, near(*held, small) + edges(0, 0), [ends, cots], [],
-        [w, wb, mass, cotangent, inv_s, u, xa, xb, *others, *held_now], same={12 + i: i for i in range(7)},
+        [w, wb, mass, cotangent, inv_s, u, xb, xa, *others, *held_now], same={12 + i: i for i in range(7)},
     )
     xa, xb, *others = exchange(*sent, tiles)
     held = [tmp, ringed, tmp2, field, acc]
-    held_now = call(third_inner, near(*held), [big], [], [w, wb, mean, inv_a, v, e, bu, z, xa, xb])
+    held_now = call(third_inner, near(*held), [big], [], [w, wb, mean, inv_a, v, e, bu, z, xb, xa])
     *_, gp_far, q_far, told = call(
         third_outer, near(*held) + [pltpu.HBM(field, F32), pltpu.HBM(q_shape, F32)] + near(small), [ends], [4],
         [w, wb, mean, told, inv_a, v, e, bu, q, *others, *held_now], (5, 6), same={13 + i: i for i in range(5)},

time: 171 us -> 164 us (0.959)
  waiting for transfers between devices: 9.53 us -> 18 us
  local copies, waits for them, and re-layouts: 12.1 us -> 3.77 us
  other arithmetic: 3.93 us -> 0.12 us
  blocking collectives: 36.1 us -> 32.6 us
    ppermute x18, waiting for transfers between devices: 9.53 us -> 18 us  [swap(): return lax.ppermute(value, axis, list(partners(axis, parity).items()))]
    unnamed x24 -> x12, local copies, waits for them, and re-layouts: 11.2 us -> 2.97 us
    all_to_all x1, blocking collectives: 36.1 us -> 32.6 us  [over_all(): lax.all_to_all(jnp.broadcast_to(told[None], (devices, K, L)), ('gx', 'gy'...]
  transfers between devices with their start and end apart: 18 -> 18, of which waited for: 3 -> 3; matrix products, arithmetic and copies ran while one was open for 2% -> 0% of each run, Pallas kernels for 14% -> 15%
where the time goes in v4:
time: 164 us; the launch traced here: 163 us
  Pallas kernels  54.3 us (33%)
  starting transfers between devices  53.2 us (32%)
  blocking collectives  32.6 us (20%)
  waiting for transfers between devices  18 us (11%)
  local copies, waits for them, and re-layouts  3.77 us (2%)
    pallas_call x8, Pallas kernels, call(): pl.pallas_call(kernel, out_shape=outs, in_specs=[pl.BlockSpec(memory_spac...  54.3 us
    ppermute x18, starting transfers between devices, swap(): return lax.ppermute(value, axis, list(partners(axis, parity).items()))  53.2 us
    all_to_all x1, blocking collectives, over_all(): lax.all_to_all(jnp.broadcast_to(told[None], (devices, K, L)), ('gx', 'gy'...  32.6 us
    ppermute x18, waiting for transfers between devices, swap(): return lax.ppermute(value, axis, list(partners(axis, parity).items()))  18 us
  transfers between devices with their start and end apart: 18, of which 3 were waited for; matrix products, arithmetic and copies ran while one was open for 0% of the time, Pallas kernels for 15%

profile of v4, /device:TPU:1, one launch (start us, length us, event | category | flops | bytes accessed | tf_op | source)
XLA Modules:
  0.0 163.2 jit_solution(18098681140627466896)
XLA Ops:
  0.6 0.0 copy-start.2
  0.6 0.0 copy-start.5
  0.7 0.7 copy-done.5
  1.3 5.4 %shard_map.67 = (f32[32,16,8,128]{3,2,1,0:T(8,128)S(1)}, f32[32,16,8,128]{3,2,1,0:T(8,128)S(1)}, f32[8,128]{1,0:T(8,128)S(1)}, f32[8,128]{1,0:T(8,128)S(1)}, f32...) custom-call(f32[8]{0:T(128)S(1)} %copy-done.5, ...), custom_call_target="tpu_custom_call" | custom-call | tf_op jit(solution)/shard_map/pallas_call | solution.py:476
  6.8 0.0 copy-start
  6.8 1.3 copy-done
  8.1 0.7 collective-permute-start.2
  8.8 4.7 %collective-permute-start.3 = (f32[8,16,8,128]{3,2,1,0:T(8,128)}, f32[8,16,8,128]{3,2,1,0:T(8,128)S(1)}, u32[]{:S(2)}, u32[]{:S(2)}) collective-permute-start(f32[8,16,8,128]{3,2,1,0:T(8,128)} %get-tuple-element.59), channel_id=1, source_target_pairs={{0,16},{16,0},{32,48},{48,32},{64,80},{80,64},{96,112},{112,96},{1... | collective-permute-start | bytes 1572872 | tf_op jit(solution)/shard_map/ppermute | solution.py:498
  13.5 5.8 %collective-permute-start = (f32[32,4,8,128]{3,2,1,0:T(8,128)}, f32[32,4,8,128]{3,2,1,0:T(8,128)}, u32[]{:S(2)}, u32[]{:S(2)}) collective-permute-start(f32[32,4,8,128]{3,2,1,0:T(8,128)} %get-tuple-element.56), channel_id=1, source_target_pairs={{1,2},{2,1},{3,4},{4,3},{5,6},{6,5},{7,8},{8,7},{9,10},{10,9},{11,... | collective-permute-start | bytes 1572872 | tf_op jit(solution)/shard_map/ppermute | solution.py:498
  19.3 0.1 collective-permute-start.1
  19.4 0.0 copy-start.1
  19.4 0.0 collective-permute-done.2.xb
  19.4 5.6 %collective-permute-done.3.xa = f32[8,16,8,128]{3,2,1,0:T(8,128)S(1)} collective-permute-done((f32[8,16,8,128]{3,2,1,0:T(8,128)}, f32[8,16,8,128]{3,2,1,0:T(8,128)S(1)}, u32[]{:S(2)}, u32[]{:S(2)}) %collective-permute-start.3) | collective-permute-done | bytes 524320 | tf_op jit(solution)/shard_map/ppermute | solution.py:498
  25.1 6.1 %collective-permute-start.4 = (f32[16,4,8,128]{3,2,1,0:T(8,128)S(1)}, f32[16,4,8,128]{3,2,1,0:T(8,128)S(1)}, u32[]{:S(2)}, u32[]{:S(2)}) collective-permute-start(f32[16,4,8,128]{3,2,1,0:T(8,128)S(1)} %pad_maximum_fusion.2), channel_id=1, source_target_pairs={{1,2},{2,1},{3,4},{4,3},{5,6},{6,5},{7,8},{8,7},{9,10},{10,9},{11,... | collective-permute-start | bytes 786440 | tf_op jit(solution)/shard_map/ppermute | solution.py:498
  31.2 0.1 collective-permute-start.5
  31.3 0.0 copy-done.2
  31.3 0.0 copy-done.1
  31.3 0.0 copy-start.3
  31.3 8.2 %shard_map.68 = (f32[40,24,8,128]{3,2,1,0:T(8,128)S(1)}, f32[40,20,8,128]{3,2,1,0:T(8,128)S(1)}, f32[40,20,8,128]{3,2,1,0:T(8,128)S(1)}, f32[32,20,8,128]{3,2,1,...) custom-call(bf16[256,256]{1,0:T(8,128)(2,1)S(1)} %copy-done.2, ...), custom_call_target="tpu_custom_call" | custom-call | tf_op jit(solution)/shard_map/pallas_call | solution.py:476
  39.5 0.0 collective-permute-done.yb
  39.5 0.0 collective-permute-done.1.ya
  39.5 0.0 collective-permute-done.4.cb
  39.6 0.0 collective-permute-done.5.ca
  39.6 0.0 copy-done.3
  39.6 7.1 %shard_map.69 = (f32[40,24,8,128]{3,2,1,0:T(8,128)S(1)}, f32[40,20,8,128]{3,2,1,0:T(8,128)S(1)}, f32[40,20,8,128]{3,2,1,0:T(8,128)S(1)}, f32[32,20,8,128]{3,2,1,...) custom-call(bf16[256,256]{1,0:T(8,128)(2,1)S(1)} %copy-done.2, ...), custom_call_target="tpu_custom_call", output_to_operand_aliasing={{0}: (9, {}), {1}: (10, {}), {2}: (11, {}), {3}: (12, {}), ... | custom-call | tf_op jit(solution)/shard_map/pallas_call | solution.py:476
  46.7 0.7 collective-permute-start.6
  47.4 2.9 %collective-permute-start.7 = (f32[9,16,8,128]{3,2,1,0:T(8,128)S(1)}, f32[9,16,8,128]{3,2,1,0:T(8,128)S(1)}, u32[]{:S(2)}, u32[]{:S(2)}) collective-permute-start(f32[9,16,8,128]{3,2,1,0:T(8,128)S(1)} %get-tuple-element.71), channel_id=1, source_target_pairs={{0,16},{16,0},{32,48},{48,32},{64,80},{80,64},{96,112},{112,96},{1... | collective-permute-start | bytes 1769480 | tf_op jit(solution)/shard_map/ppermute | solution.py:498
  50.2 4.6 %collective-permute-start.8 = (f32[36,4,8,128]{3,2,1,0:T(8,128)S(1)}, f32[36,4,8,128]{3,2,1,0:T(8,128)S(1)}, u32[]{:S(2)}, u32[]{:S(2)}) collective-permute-start(f32[36,4,8,128]{3,2,1,0:T(8,128)S(1)} %get-tuple-element.72), channel_id=1, source_target_pairs={{1,2},{2,1},{3,4},{4,3},{5,6},{6,5},{7,8},{8,7},{9,10},{10,9},{11,... | collective-permute-start | bytes 1769480 | tf_op jit(solution)/shard_map/ppermute | solution.py:498
  54.9 0.1 collective-permute-start.9
  55.0 0.0 collective-permute-done.6.xb
  55.0 8.1 %collective-permute-done.7.xa = f32[9,16,8,128]{3,2,1,0:T(8,128)S(1)} collective-permute-done((f32[9,16,8,128]{3,2,1,0:T(8,128)S(1)}, f32[9,16,8,128]{3,2,1,0:T(8,128)S(1)}, u32[]{:S(2)}, u32[]{:S(2)}) %collective-permute-start.7) | collective-permute-done | bytes 589856 | tf_op jit(solution)/shard_map/ppermute | solution.py:498
  63.2 5.0 %collective-permute-start.10 = (f32[18,4,8,128]{3,2,1,0:T(8,128)S(1)}, f32[18,4,8,128]{3,2,1,0:T(8,128)S(1)}, u32[]{:S(2)}, u32[]{:S(2)}) collective-permute-start(f32[18,4,8,128]{3,2,1,0:T(8,128)S(1)} %pad_maximum_fusion), channel_id=1, source_target_pairs={{1,2},{2,1},{3,4},{4,3},{5,6},{6,5},{7,8},{8,7},{9,10},{10,9},{11,... | collective-permute-start | bytes 884744 | tf_op jit(solution)/shard_map/ppermute | solution.py:498
  68.2 0.1 collective-permute-start.11
  68.3 8.5 %shard_map.70 = (f32[40,24,8,128]{3,2,1,0:T(8,128)S(1)}, f32[40,20,8,128]{3,2,1,0:T(8,128)S(1)}, f32[32,20,8,128]{3,2,1,0:T(8,128)S(1)}, f32[32,16,8,128]{3,2,1,...) custom-call(bf16[256,256]{1,0:T(8,128)(2,1)S(1)} %copy-done.2, ...), custom_call_target="tpu_custom_call" | custom-call | tf_op jit(solution)/shard_map/pallas_call | solution.py:476
  76.8 0.0 collective-permute-done.8.yb
  76.8 0.0 collective-permute-done.9.ya
  76.9 0.0 collective-permute-done.10.cb
  76.9 0.0 collective-permute-done.11.ca
  76.9 5.9 %shard_map.71 = (f32[40,24,8,128]{3,2,1,0:T(8,128)S(1)}, f32[40,20,8,128]{3,2,1,0:T(8,128)S(1)}, f32[32,20,8,128]{3,2,1,0:T(8,128)S(1)}, f32[32,16,8,128]{3,2,1,...) custom-call(bf16[256,256]{1,0:T(8,128)(2,1)S(1)} %copy-done.2, ...), custom_call_target="tpu_custom_call", output_to_operand_aliasing={{0}: (12, {}), {1}: (13, {}), {2}: (14, {}), {3}: (15, {}),... | custom-call | tf_op jit(solution)/shard_map/pallas_call | solution.py:476
  82.8 0.7 collective-permute-start.14
  83.5 6.8 %collective-permute-start.15 = (f32[8,16,8,128]{3,2,1,0:T(8,128)S(1)}, f32[8,16,8,128]{3,2,1,0:T(8,128)S(1)}, u32[]{:S(2)}, u32[]{:S(2)}) collective-permute-start(f32[8,16,8,128]{3,2,1,0:T(8,128)S(1)} %get-tuple-element.89), channel_id=1, source_target_pairs={{0,16},{16,0},{32,48},{48,32},{64,80},{80,64},{96,112},{112,96},{1... | collective-permute-start | bytes 1572872 | tf_op jit(solution)/shard_map/ppermute | solution.py:498
  90.3 7.1 %collective-permute-start.12 = (f32[32,4,8,128]{3,2,1,0:T(8,128)S(1)}, f32[32,4,8,128]{3,2,1,0:T(8,128)S(1)}, u32[]{:S(2)}, u32[]{:S(2)}) collective-permute-start(f32[32,4,8,128]{3,2,1,0:T(8,128)S(1)} %get-tuple-element.86), channel_id=1, source_target_pairs={{1,2},{2,1},{3,4},{4,3},{5,6},{6,5},{7,8},{8,7},{9,10},{10,9},{11,... | collective-permute-start | bytes 1572872 | tf_op jit(solution)/shard_map/ppermute | solution.py:498
  97.4 0.1 collective-permute-start.13
  97.5 0.0 collective-permute-done.14.xb
  97.5 4.2 %collective-permute-done.15.xa = f32[8,16,8,128]{3,2,1,0:T(8,128)S(1)} collective-permute-done((f32[8,16,8,128]{3,2,1,0:T(8,128)S(1)}, f32[8,16,8,128]{3,2,1,0:T(8,128)S(1)}, u32[]{:S(2)}, u32[]{:S(2)}) %collective-permute-start.15) | collective-permute-done | bytes 524320 | tf_op jit(solution)/shard_map/ppermute | solution.py:498
  101.8 7.5 %collective-permute-start.16 = (f32[16,4,8,128]{3,2,1,0:T(8,128)S(1)}, f32[16,4,8,128]{3,2,1,0:T(8,128)S(1)}, u32[]{:S(2)}, u32[]{:S(2)}) collective-permute-start(f32[16,4,8,128]{3,2,1,0:T(8,128)S(1)} %pad_maximum_fusion.4), channel_id=1, source_target_pairs={{1,2},{2,1},{3,4},{4,3},{5,6},{6,5},{7,8},{8,7},{9,10},{10,9},{11,... | collective-permute-start | bytes 786440 | tf_op jit(solution)/shard_map/ppermute | solution.py:498
  109.3 0.3 collective-permute-start.17
  109.6 8.0 %shard_map.72 = (f32[40,24,8,128]{3,2,1,0:T(8,128)S(1)}, f32[40,20,8,128]{3,2,1,0:T(8,128)S(1)}, f32[32,20,8,128]{3,2,1,0:T(8,128)S(1)}, f32[32,16,8,128]{3,2,1,0:T(8,128)S(1)}, f32[2,8,128]{2,1,0:T(8,128)S(1)}) custom-call(bf16[256,256]{1,0:T(8,128)(2,1)S(1)} %copy-done.2, f32[8,128]{1,0:T(8,128)S(1)} %get-tuple-element.53.wb, ...), custom_call_target="tpu_custom_call" | custom-call | tf_op jit(solution)/shard_map/pallas_call | solution.py:476
  117.6 0.0 collective-permute-done.12.yb
  117.6 0.0 collective-permute-done.13.ya
  117.6 0.0 collective-permute-done.16.cb
  117.6 0.0 collective-permute-done.17.ca
  117.6 6.5 %shard_map.73 = (f32[40,24,8,128]{3,2,1,0:T(8,128)S(1)}, f32[40,20,8,128]{3,2,1,0:T(8,128)S(1)}, f32[32,20,8,128]{3,2,1,0:T(8,128)S(1)}, f32[32,16,8,128]{3,2,1,...) custom-call(bf16[256,256]{1,0:T(8,128)(2,1)S(1)} %copy-done.2, ...), custom_call_target="tpu_custom_call", output_to_operand_aliasing={{0}: (13, {}), {1}: (14, {}), {2}: (15, {}), {3}: (16, {}),... | custom-call | tf_op jit(solution)/shard_map/pallas_call | solution.py:476
  124.1 32.6 %all_to_all.5.heard = f32[128,8,128]{2,1,0:T(8,128)S(1)} all-to-all(f32[128,8,128]{2,1,0:T(8,128)S(1)} %broadcast_in_dim.2), channel_id=1, replica_groups=mesh['gx'=8,'gy'=16] {'gx','gy'}, dimensions={0} | all-to-all | bytes 1048576 | tf_op jit(solution)/shard_map/all_to_all | solution.py:517
  156.8 0.0 copy-start.4
  156.8 0.9 copy-done.4
  157.7 4.8 %shard_map.74 = (f32[256,2048]{1,0:T(8,128)}, f32[32,2048]{1,0:T(8,128)}, f32[8,128]{1,0:T(8,128)S(1)}) custom-call(f32[8,128]{1,0:T(8,128)S(1)} %get-tuple-element.53.wb, f32[128,8,128]{2,1,0:T(8,128)S(1)} %all_to_all.5.heard, f32[16,32,128]{2,1,0:T(8,128)S(1)} %copy-done.4, f32[32,16,8,128]{3,2,1,0:T(8,128)} %get-tuple-element.98.gp_far, ...), custom_call_target="tpu_custom_call" | custom-call | tf_op jit(solution)/shard_map/pallas_call | solution.py:476
  162.5 0.6 slice_reduce_fusion
  (13 shorter events, 0.3 us)
Async XLA Ops:
  0.6 30.7 %copy-start.2 = (bf16[256,256]{1,0:T(8,128)(2,1)S(1)}, bf16[256,256]{1,0:T(8,128)(2,1)}, u32[]{:S(2)}) copy-start(bf16[256,256]{1,0:T(8,128)(2,1)} %constant.17.clone.w_ref) | copy-start | bytes 393220
  0.6 0.7 copy-start.5
  6.8 1.3 copy-start
  8.1 11.3 %collective-permute-start.2 = (f32[8,16,8,128]{3,2,1,0:T(8,128)}, f32[8,16,8,128]{3,2,1,0:T(8,128)S(1)}, u32[]{:S(2)}, u32[]{:S(2)}) collective-permute-start(f32[8,16,8,128]{3,2,1,0:T(8,128)} %get-tuple-element.58), channel_id=1, source_target_pairs={{16,32},{32,16},{48,64},{64,48},{80,96},{96,80},{17,33},{33,17},{4... | collective-permute-start | bytes 1572872 | tf_op jit(solution)/shard_map/ppermute | solution.py:498
  8.8 16.3 %collective-permute-start.3 = (f32[8,16,8,128]{3,2,1,0:T(8,128)}, f32[8,16,8,128]{3,2,1,0:T(8,128)S(1)}, u32[]{:S(2)}, u32[]{:S(2)}) collective-permute-start(f32[8,16,8,128]{3,2,1,0:T(8,128)} %get-tuple-element.59), channel_id=1, source_target_pairs={{0,16},{16,0},{32,48},{48,32},{64,80},{80,64},{96,112},{112,96},{1... | collective-permute-start | bytes 1572872 | tf_op jit(solution)/shard_map/ppermute | solution.py:498
  13.5 26.0 %collective-permute-start = (f32[32,4,8,128]{3,2,1,0:T(8,128)}, f32[32,4,8,128]{3,2,1,0:T(8,128)}, u32[]{:S(2)}, u32[]{:S(2)}) collective-permute-start(f32[32,4,8,128]{3,2,1,0:T(8,128)} %get-tuple-element.56), channel_id=1, source_target_pairs={{1,2},{2,1},{3,4},{4,3},{5,6},{6,5},{7,8},{8,7},{9,10},{10,9},{11,... | collective-permute-start | bytes 1572872 | tf_op jit(solution)/shard_map/ppermute | solution.py:498
  19.3 20.3 %collective-permute-start.1 = (f32[32,4,8,128]{3,2,1,0:T(8,128)}, f32[32,4,8,128]{3,2,1,0:T(8,128)}, u32[]{:S(2)}, u32[]{:S(2)}) collective-permute-start(f32[32,4,8,128]{3,2,1,0:T(8,128)} %get-tuple-element.57), channel_id=1, source_target_pairs={{0,1},{1,0},{2,3},{3,2},{4,5},{5,4},{6,7},{7,6},{8,9},{9,8},{10,11... | collective-permute-start | bytes 1572872 | tf_op jit(solution)/shard_map/ppermute | solution.py:498
  19.4 11.9 %copy-start.1 = (f32[32,16,8,128]{3,2,1,0:T(8,128)S(1)}, f32[32,16,8,128]{3,2,1,0:T(8,128)}, u32[]{:S(2)}) copy-start(f32[32,16,8,128]{3,2,1,0:T(8,128)} %copy-done) | copy-start | bytes 6291460
  25.1 14.5 %collective-permute-start.4 = (f32[16,4,8,128]{3,2,1,0:T(8,128)S(1)}, f32[16,4,8,128]{3,2,1,0:T(8,128)S(1)}, u32[]{:S(2)}, u32[]{:S(2)}) collective-permute-start(f32[16,4,8,128]{3,2,1,0:T(8,128)S(1)} %pad_maximum_fusion.2), channel_id=1, source_target_pairs={{1,2},{2,1},{3,4},{4,3},{5,6},{6,5},{7,8},{8,7},{9,10},{10,9},{11,... | collective-permute-start | bytes 786440 | tf_op jit(solution)/shard_map/ppermute | solution.py:498
  31.2 8.4 %collective-permute-start.5 = (f32[16,4,8,128]{3,2,1,0:T(8,128)S(1)}, f32[16,4,8,128]{3,2,1,0:T(8,128)S(1)}, u32[]{:S(2)}, u32[]{:S(2)}) collective-permute-start(f32[16,4,8,128]{3,2,1,0:T(8,128)S(1)} %pad_maximum_fusion.3), channel_id=1, source_target_pairs={{0,1},{1,0},{2,3},{3,2},{4,5},{5,4},{6,7},{7,6},{8,9},{9,8},{10,11... | collective-permute-start | bytes 786440 | tf_op jit(solution)/shard_map/ppermute | solution.py:498
  31.3 8.3 %copy-start.3 = (f32[32,2048]{1,0:T(8,128)S(1)}, f32[32,2048]{1,0:T(8,128)}, u32[]{:S(2)}) copy-start(f32[32,2048]{1,0:T(8,128)} %cot.5) | copy-start | bytes 786436
  46.7 8.3 %collective-permute-start.6 = (f32[9,16,8,128]{3,2,1,0:T(8,128)S(1)}, f32[9,16,8,128]{3,2,1,0:T(8,128)S(1)}, u32[]{:S(2)}, u32[]{:S(2)}) collective-permute-start(f32[9,16,8,128]{3,2,1,0:T(8,128)S(1)} %get-tuple-element.70), channel_id=1, source_target_pairs={{16,32},{32,16},{48,64},{64,48},{80,96},{96,80},{17,33},{33,17},{4... | collective-permute-start | bytes 1769480 | tf_op jit(solution)/shard_map/ppermute | solution.py:498
  47.4 15.8 %collective-permute-start.7 = (f32[9,16,8,128]{3,2,1,0:T(8,128)S(1)}, f32[9,16,8,128]{3,2,1,0:T(8,128)S(1)}, u32[]{:S(2)}, u32[]{:S(2)}) collective-permute-start(f32[9,16,8,128]{3,2,1,0:T(8,128)S(1)} %get-tuple-element.71), channel_id=1, source_target_pairs={{0,16},{16,0},{32,48},{48,32},{64,80},{80,64},{96,112},{112,96},{1... | collective-permute-start | bytes 1769480 | tf_op jit(solution)/shard_map/ppermute | solution.py:498
  50.2 26.6 %collective-permute-start.8 = (f32[36,4,8,128]{3,2,1,0:T(8,128)S(1)}, f32[36,4,8,128]{3,2,1,0:T(8,128)S(1)}, u32[]{:S(2)}, u32[]{:S(2)}) collective-permute-start(f32[36,4,8,128]{3,2,1,0:T(8,128)S(1)} %get-tuple-element.72), channel_id=1, source_target_pairs={{1,2},{2,1},{3,4},{4,3},{5,6},{6,5},{7,8},{8,7},{9,10},{10,9},{11,... | collective-permute-start | bytes 1769480 | tf_op jit(solution)/shard_map/ppermute | solution.py:498
  54.9 22.0 %collective-permute-start.9 = (f32[36,4,8,128]{3,2,1,0:T(8,128)S(1)}, f32[36,4,8,128]{3,2,1,0:T(8,128)S(1)}, u32[]{:S(2)}, u32[]{:S(2)}) collective-permute-start(f32[36,4,8,128]{3,2,1,0:T(8,128)S(1)} %get-tuple-element.73), channel_id=1, source_target_pairs={{0,1},{1,0},{2,3},{3,2},{4,5},{5,4},{6,7},{7,6},{8,9},{9,8},{10,11... | collective-permute-start | bytes 1769480 | tf_op jit(solution)/shard_map/ppermute | solution.py:498
  63.2 13.6 %collective-permute-start.10 = (f32[18,4,8,128]{3,2,1,0:T(8,128)S(1)}, f32[18,4,8,128]{3,2,1,0:T(8,128)S(1)}, u32[]{:S(2)}, u32[]{:S(2)}) collective-permute-start(f32[18,4,8,128]{3,2,1,0:T(8,128)S(1)} %pad_maximum_fusion), channel_id=1, source_target_pairs={{1,2},{2,1},{3,4},{4,3},{5,6},{6,5},{7,8},{8,7},{9,10},{10,9},{11,... | collective-permute-start | bytes 884744 | tf_op jit(solution)/shard_map/ppermute | solution.py:498
  68.2 8.6 %collective-permute-start.11 = (f32[18,4,8,128]{3,2,1,0:T(8,128)S(1)}, f32[18,4,8,128]{3,2,1,0:T(8,128)S(1)}, u32[]{:S(2)}, u32[]{:S(2)}) collective-permute-start(f32[18,4,8,128]{3,2,1,0:T(8,128)S(1)} %pad_maximum_fusion.1), channel_id=1, source_target_pairs={{0,1},{1,0},{2,3},{3,2},{4,5},{5,4},{6,7},{7,6},{8,9},{9,8},{10,11... | collective-permute-start | bytes 884744 | tf_op jit(solution)/shard_map/ppermute | solution.py:498
  82.8 14.7 %collective-permute-start.14 = (f32[8,16,8,128]{3,2,1,0:T(8,128)S(1)}, f32[8,16,8,128]{3,2,1,0:T(8,128)S(1)}, u32[]{:S(2)}, u32[]{:S(2)}) collective-permute-start(f32[8,16,8,128]{3,2,1,0:T(8,128)S(1)} %get-tuple-element.88), channel_id=1, source_target_pairs={{16,32},{32,16},{48,64},{64,48},{80,96},{96,80},{17,33},{33,17},{4... | collective-permute-start | bytes 1572872 | tf_op jit(solution)/shard_map/ppermute | solution.py:498
  83.5 18.3 %collective-permute-start.15 = (f32[8,16,8,128]{3,2,1,0:T(8,128)S(1)}, f32[8,16,8,128]{3,2,1,0:T(8,128)S(1)}, u32[]{:S(2)}, u32[]{:S(2)}) collective-permute-start(f32[8,16,8,128]{3,2,1,0:T(8,128)S(1)} %get-tuple-element.89), channel_id=1, source_target_pairs={{0,16},{16,0},{32,48},{48,32},{64,80},{80,64},{96,112},{112,96},{1... | collective-permute-start | bytes 1572872 | tf_op jit(solution)/shard_map/ppermute | solution.py:498
  90.3 27.3 %collective-permute-start.12 = (f32[32,4,8,128]{3,2,1,0:T(8,128)S(1)}, f32[32,4,8,128]{3,2,1,0:T(8,128)S(1)}, u32[]{:S(2)}, u32[]{:S(2)}) collective-permute-start(f32[32,4,8,128]{3,2,1,0:T(8,128)S(1)} %get-tuple-element.86), channel_id=1, source_target_pairs={{1,2},{2,1},{3,4},{4,3},{5,6},{6,5},{7,8},{8,7},{9,10},{10,9},{11,... | collective-permute-start | bytes 1572872 | tf_op jit(solution)/shard_map/ppermute | solution.py:498
  97.4 20.2 %collective-permute-start.13 = (f32[32,4,8,128]{3,2,1,0:T(8,128)S(1)}, f32[32,4,8,128]{3,2,1,0:T(8,128)S(1)}, u32[]{:S(2)}, u32[]{:S(2)}) collective-permute-start(f32[32,4,8,128]{3,2,1,0:T(8,128)S(1)} %get-tuple-element.87), channel_id=1, source_target_pairs={{0,1},{1,0},{2,3},{3,2},{4,5},{5,4},{6,7},{7,6},{8,9},{9,8},{10,11... | collective-permute-start | bytes 1572872 | tf_op jit(solution)/shard_map/ppermute | solution.py:498
  101.8 15.8 %collective-permute-start.16 = (f32[16,4,8,128]{3,2,1,0:T(8,128)S(1)}, f32[16,4,8,128]{3,2,1,0:T(8,128)S(1)}, u32[]{:S(2)}, u32[]{:S(2)}) collective-permute-start(f32[16,4,8,128]{3,2,1,0:T(8,128)S(1)} %pad_maximum_fusion.4), channel_id=1, source_target_pairs={{1,2},{2,1},{3,4},{4,3},{5,6},{6,5},{7,8},{8,7},{9,10},{10,9},{11,... | collective-permute-start | bytes 786440 | tf_op jit(solution)/shard_map/ppermute | solution.py:498
  109.3 8.3 %collective-permute-start.17 = (f32[16,4,8,128]{3,2,1,0:T(8,128)S(1)}, f32[16,4,8,128]{3,2,1,0:T(8,128)S(1)}, u32[]{:S(2)}, u32[]{:S(2)}) collective-permute-start(f32[16,4,8,128]{3,2,1,0:T(8,128)S(1)} %pad_maximum_fusion.5), channel_id=1, source_target_pairs={{0,1},{1,0},{2,3},{3,2},{4,5},{5,4},{6,7},{7,6},{8,9},{9,8},{10,11... | collective-permute-start | bytes 786440 | tf_op jit(solution)/shard_map/ppermute | solution.py:498
  156.8 1.0 copy-start.4

commit v5 on v4

--- a/solution.py
+++ b/solution.py
@@ -47,24 +47,33 @@
     return (G0 * at(4) + G1 * (at(3) + at(5))) + (G2 * (at(2) + at(6)) + G3 * (at(1) + at(7))) + G4 * (at(0) + at(8))
 
 
-def conv_xz(src, dst, w_ref, shift, ranges):
+def conv_xz(src, dst, w_ref, pieces):
     rows = dst.shape[0]
 
-    def pair(i, first):
-        t = first + 2 * i
-        two = pl.ds(t, 2)
-        for x in range(0, rows, 8):
-            block = src[x : x + 16, pl.ds(t - shift, 2)]
-            dst[x : x + 8, two] = nine(lambda j: block[j : j + 8])
-        value = dst[:, two].reshape(rows * 2 * K, L)
-        high = value.astype(BF16)
-        low = (value - high.astype(F32)).astype(BF16)
-        both = jnp.dot(jnp.concatenate([high, low], axis=1), w_ref[...], preferred_element_type=F32)
-        dst[:, two] = (both[:, :L] + both[:, L:]).reshape(rows, 2, K, L)
-        return first
-
-    for first, end in ranges:
-        lax.fori_loop(0, (end - first) // 2, pair, first)
+    def some(now):
+        for t, u in now:
+            along = []
+            for i in range(4):
+                for x in range(0, rows, 8):
+                    block = src[x : x + 16, u + i]
+                    along.append(nine(lambda j: block[j : j + 8]).reshape(8 * K, L))
+            value = jnp.concatenate(along, axis=0)
+            high = value.astype(BF16)
+            low = (value - high.astype(F32)).astype(BF16)
+            both = jnp.dot(jnp.concatenate([high, low], axis=1), w_ref[...], preferred_element_type=F32)
+            out = both[:, :L] + both[:, L:]
+            for i in range(4):
+                dst[:, t + i] = out[i * rows * K : (i + 1) * rows * K].reshape(rows, K, L)
+
+    if len(pieces) < 4:
+        some(pieces)
+    else:
+
+        def two(i, carry):
+            some([(t + 8 * i, u + 8 * i) for t, u in pieces[:2]])
+            return carry
+
+        lax.fori_loop(0, len(pieces) // 2, two, 0)
 
 
 def conv_y(src, first, rows, tile, n):
@@ -136,22 +145,11 @@
 
 def parts(tiles, inner):
     if inner:
-        return [(HT, tiles + HT)], [(HT, tiles)], [(HT, tiles)], [(HT, tiles - HT)]
-    return (
-        [(0, HT), (tiles + HT, tiles + 2 * HT)],
-        [(0, HT), (tiles, tiles + HT)],
-        [(0, HT), (tiles, tiles + HT)],
-        [(0, HT), (tiles - HT, tiles)],
-    )
-
-
-def first_conv(inner, src, tmp, w_ref, tiles):
-    whole = parts(tiles, inner)[0]
-    if inner:
-        conv_xz(src, tmp, w_ref, HT, whole)
-    else:
-        conv_xz(src, tmp, w_ref, 0, whole[:1])
-        conv_xz(src, tmp, w_ref, tiles, whole[1:])
+        starts, outs, last = range(HT, tiles + HT, 4), [(HT, tiles)], [(HT, tiles - HT)]
+        again = range(HT, tiles, 4)
+        return [(t, t - HT) for t in starts], outs, [(t, t) for t in again], last
+    outs, last = [(0, HT), (tiles, tiles + HT)], [(0, HT), (tiles - HT, tiles)]
+    return [(0, 0), (tiles + HT, HT)], outs, [(0, 0), (tiles, tiles)], last
 
 
 def inside(at, count):
@@ -177,8 +175,8 @@
     return jnp.log(over_lanes(field[field.shape[0] // 2, field.shape[1] // 2]) * (1.0 / L))
 
 
-def start_kernel(theta, log_ref, dens, e, mass, wb, *rest):
-    edges, (turn, across, sem) = rest[:4], rest[4:]
+def start_kernel(theta, log_ref, dens_out, e, mass, wb, *rest):
+    edges, (turn, across, dens, sem) = rest[:4], rest[4:]
     rows, tiles = dens.shape[0], dens.shape[1]
     loads = [pltpu.make_async_copy(log_ref.at[:, pl.ds(t * L, L)], turn.at[t], sem.at[t]) for t in range(tiles)]
     for c in loads:
@@ -214,36 +212,38 @@
             return acc
 
         mass[...] += lax.fori_loop(0, rows // 8, some, jnp.zeros((K, L), F32))
+        pltpu.make_async_copy(dens.at[:, t], dens_out.at[:, t], sem.at[tiles]).start()
     give_edges(e, edges)
+    pltpu.make_async_copy(dens, dens_out, sem.at[tiles]).wait()
 
 
 def first_fields(inner, wb, w_ref, dens, src, tmp, v, inv_a, tmp2, u, inv_s):
     rows, tiles = dens.shape[0], dens.shape[1]
-    _, outs, again, last = parts(tiles, inner)
-    first_conv(inner, src, tmp, w_ref, tiles)
+    first, outs, again, last = parts(tiles, inner)
+    conv_xz(src, tmp, w_ref, first)
 
     def ring(c, carry):
-        s = pl.ds(c * 4, 4)
+        s = pl.ds(c * 8, 8)
         for start, end in outs:
-            spread = jnp.log(conv_y(tmp, c * 4, 4, start, end - start))
+            spread = jnp.log(conv_y(tmp, c * 8, 8, start, end - start))
             log_q = jnp.sum(wb[...] * spread, axis=2, keepdims=True)
             v[s, start:end] = jnp.exp(log_q - spread)
             inv_a[s, start:end] = jnp.exp(-spread)
         return carry
 
-    lax.fori_loop(0, (rows + 8) // 4, ring, 0)
+    lax.fori_loop(0, (rows + 8) // 8, ring, 0)
     clear_outside((v, inv_a), outs, not inner)
-    conv_xz(v, tmp2, w_ref, 0, again)
+    conv_xz(v, tmp2, w_ref, again)
 
     def second(c, carry):
-        s = pl.ds(c * 4, 4)
+        s = pl.ds(c * 8, 8)
         for start, end in last:
-            inv = 1.0 / conv_y(tmp2, c * 4, 4, start, end - start)
+            inv = 1.0 / conv_y(tmp2, c * 8, 8, start, end - start)
             inv_s[s, start:end] = inv
             u[s, start:end] = dens[s, start:end] * inv
         return carry
 
-    lax.fori_loop(0, rows // 4, second, 0)
+    lax.fori_loop(0, rows // 8, second, 0)
 
 
 def first_inner(w_ref, wb, dens, own, xb, xa, tmp, v, inv_a, tmp2, u, inv_s, big):
@@ -252,11 +252,8 @@
 
 
 def first_outer(w_ref, wb, cot, dens, e, yb, ya, cb, ca, *rest):
-    fields, dens_out, mean = rest[6:12], rest[12], rest[13]
-    edges, (ends, sem) = rest[14:18], rest[18:]
+    fields, mean, edges, ends = rest[6:12], rest[12], rest[13:17], rest[17]
     rows, tiles = dens.shape[0], dens.shape[1]
-    kept = pltpu.make_async_copy(dens, dens_out, sem.at[0])
-    kept.start()
     mean[...] = jnp.broadcast_to(centre(e), (K, L))
     join_ends(ends, rows, HALO, ya, yb, ca, cb)
     first_fields(False, wb, w_ref, dens, ends, *fields)
@@ -273,28 +270,27 @@
             lanes = pl.ds(pl.multiple_of((side * (tiles - HT) + t) * L, L), L)
             for b in range(rows // 8):
                 out[rows + b, t] = cot[b * 8 : b * 8 + 8, lanes]
-    kept.wait()
 
 
 def second_fields(inner, wb, w_ref, mean, cots, own, inv_s, src, tmp, r, tmp2, bu, z, q, sums):
     rows, tiles = own.shape[0], own.shape[1]
-    _, outs, again, last = parts(tiles, inner)
-    first_conv(inner, src, tmp, w_ref, tiles)
-
-    def ring(c, mine):
+    first, outs, again, last = parts(tiles, inner)
+    conv_xz(src, tmp, w_ref, first)
+
+    def ring(x, count, mine):
         acc_k = jnp.zeros((K, L), F32)
         acc_s = jnp.zeros((1, L), F32)
         for start, end in outs:
-            spread = jnp.log(conv_y(tmp, c * 4, 4, start, end - start))
+            spread = jnp.log(conv_y(tmp, x, count, start, end - start))
             log_q = jnp.sum(wb[...] * spread, axis=2, keepdims=True)
             ratio = wb[...] * jnp.exp(log_q - spread)
-            for i in range(4):
+            for i in range(count):
                 for t in range(start, end):
-                    cell = cots[t + 2, pl.ds(c * 4 + i + 4, 1), :]
-                    r[c * 4 + i, t] = ratio[i, t - start] * cell
+                    cell = cots[t + 2, pl.ds(x + i + 4, 1), :]
+                    r[x + i, t] = ratio[i, t - start] * cell
                     if mine and 2 <= t < tiles + 2:
                         row_q = jnp.exp(log_q[i, t - start])
-                        q[t - 2, pl.ds(c * 4 + i - 4, 1), :] = row_q[0:1]
+                        q[t - 2, pl.ds(x + i - 4, 1), :] = row_q[0:1]
                         combined = cell * row_q[0:1]
                         acc_s = acc_s + combined
                         acc_k = acc_k + combined * (spread[i, t - start] - mean)
@@ -302,26 +298,26 @@
             sums[0] += acc_k
             sums[1, 0:1] += acc_s
 
-    ring(0, False)
-    ring((rows + 4) // 4, False)
+    ring(0, 4, False)
+    ring(rows + 4, 4, False)
 
     def middle(c, carry):
-        ring(c, True)
-        return carry
-
-    lax.fori_loop(1, (rows + 4) // 4, middle, 0)
+        ring(c * 8 + 4, 8, True)
+        return carry
+
+    lax.fori_loop(0, rows // 8, middle, 0)
     clear_outside((r,), outs, not inner)
-    conv_xz(r, tmp2, w_ref, 0, again)
+    conv_xz(r, tmp2, w_ref, again)
 
     def second(c, carry):
-        s = pl.ds(c * 4, 4)
+        s = pl.ds(c * 8, 8)
         for start, end in last:
-            back = own[s, start:end] * conv_y(tmp2, c * 4, 4, start, end - start)
+            back = own[s, start:end] * conv_y(tmp2, c * 8, 8, start, end - start)
             bu[s, start:end] = back
             z[s, start:end] = back * inv_s[s, start:end]
         return carry
 
-    lax.fori_loop(0, rows // 4, second, 0)
+    lax.fori_loop(0, rows // 8, second, 0)
 
 
 def second_inner(w_ref, wb, cot, inv_s, own, xb, xa, tmp, r, tmp2, bu, z, q, sums, big, cots):
@@ -362,13 +358,13 @@
 
 def third_fields(inner, wb, w_ref, mean, inv_a, v, e, bu, src, tmp, r, tmp2, gp, sums):
     rows, tiles = e.shape[0], e.shape[1]
-    _, outs, again, last = parts(tiles, inner)
-    first_conv(inner, src, tmp, w_ref, tiles)
-
-    def ring(c, mine):
-        s = pl.ds(c * 4, 4)
+    first, outs, again, last = parts(tiles, inner)
+    conv_xz(src, tmp, w_ref, first)
+
+    def ring(x, count, mine):
+        s = pl.ds(x, count)
         for start, end in outs:
-            back_v = -(v[s, start:end] * conv_y(tmp, c * 4, 4, start, end - start))
+            back_v = -(v[s, start:end] * conv_y(tmp, x, count, start, end - start))
             combined = jnp.sum(back_v, axis=2, keepdims=True)
             inv = inv_a[s, start:end]
             r[s, start:end] = (wb[...] * combined - back_v) * inv
@@ -378,23 +374,23 @@
                 sums[0] += jnp.sum(part * (-jnp.log(inv[:, low:high]) - mean), axis=(0, 1))
                 sums[1, 0:1] += jnp.sum(part, axis=(0, 1))
 
-    ring(0, False)
-    ring((rows + 4) // 4, False)
+    ring(0, 4, False)
+    ring(rows + 4, 4, False)
 
     def middle(c, carry):
-        ring(c, True)
-        return carry
-
-    lax.fori_loop(1, (rows + 4) // 4, middle, 0)
-    conv_xz(r, tmp2, w_ref, 0, again)
+        ring(c * 8 + 4, 8, True)
+        return carry
+
+    lax.fori_loop(0, rows // 8, middle, 0)
+    conv_xz(r, tmp2, w_ref, again)
 
     def second(c, carry):
-        s = pl.ds(c * 4, 4)
+        s = pl.ds(c * 8, 8)
         for start, end in last:
-            gp[s, start:end] = bu[s, start:end] + e[s, start:end] * conv_y(tmp2, c * 4, 4, start, end - start)
-        return carry
-
-    lax.fori_loop(0, rows // 4, second, 0)
+            gp[s, start:end] = bu[s, start:end] + e[s, start:end] * conv_y(tmp2, c * 8, 8, start, end - start)
+        return carry
+
+    lax.fori_loop(0, rows // 8, second, 0)
 
 
 def third_inner(w_ref, wb, mean, inv_a, v, e, bu, own, xb, xa, tmp, r, tmp2, gp, sums, big):
@@ -425,7 +421,7 @@
         c.wait()
 
 
-def last_kernel(cells, wb, heard, q, gp_far, dens_far, out, bary, theta_out, turn, gp, dens, sem):
+def last_kernel(cells, wb, heard, q_far, gp_far, dens_far, out, bary, theta_out, turn, gp, dens, q, sem):
     rows, tiles = gp.shape[0], gp.shape[1]
     loads = []
     for i, first in enumerate(range(0, tiles, 4)):
@@ -433,6 +429,8 @@
         for j, (src, dst) in enumerate(((gp_far, gp), (dens_far, dens))):
             loads.append(pltpu.make_async_copy(src.at[:, lanes], dst.at[:, lanes], sem.at[tiles + 2 * i + j]))
             loads[-1].start()
+    loads.append(pltpu.make_async_copy(q_far, q, sem.at[tiles + tiles // 2]))
+    loads[-1].start()
     weights = wb[:, 0:1]
     everyone = heard[...]
     total = jnp.sum(everyone, axis=0)
@@ -456,6 +454,8 @@
         if t % 4 == 0:
             loads[t // 2].wait()
             loads[t // 2 + 1].wait()
+        if t == 0:
+            loads[-1].wait()
         lax.fori_loop(0, rows // 8, rows_of, 0)
         copies.append(pltpu.make_async_copy(turn.at[t], out.at[:, pl.ds(t * L, L)], sem.at[t]))
         copies[-1].start()
@@ -535,14 +535,15 @@
 
     logs = log_dens.reshape(K * rows, merged)
     dens, e, mass, wb, *sent = call(
-        start_kernel, near(field, field, small, small) + edges(0, 0), [turn, (rows, K, L)], [tiles], [logs], far_in=1, numbers=(theta,)
+        start_kernel, [pltpu.HBM(field, F32)] + near(field, small, small) + edges(0, 0), [turn, (rows, K, L), field], [tiles + 1],
+        [logs], (0,), 1, numbers=(theta,),
     )
     xa, xb, *others = exchange(*sent, tiles)
     held = [tmp, ringed, ringed, tmp2, field, field]
     held_now = call(first_inner, near(*held), [big], [], [w, wb, dens, e, xb, xa])
-    _, v, inv_a, _, u, inv_s, dens_far, mean, *sent = call(
-        first_outer, near(*held) + [pltpu.HBM(field, F32)] + near(small) + edges(1, rows // 8), [ends], [1],
-        [w, wb, cotangent, dens, e, *others, *held_now], (6,), same={9 + i: i for i in range(6)},
+    _, v, inv_a, _, u, inv_s, mean, *sent = call(
+        first_outer, near(*held, small) + edges(1, rows // 8), [ends], [],
+        [w, wb, cotangent, dens, e, *others, *held_now], same={9 + i: i for i in range(6)},
     )
     xa, xb, *others = exchange(*sent, tiles)
     held = [tmp, ringed, tmp2, field, field, q_shape, acc]
@@ -560,8 +561,8 @@
     )
     plain = [jax.ShapeDtypeStruct(s, F32) for s in ((K * rows, merged), (rows, merged), small)]
     grad, bary, grad_theta = call(
-        functools.partial(last_kernel, cells), plain, [turn, field, field], [tiles + tiles // 2],
-        [wb, over_all(told), q_far, gp_far, dens_far], (0,), 2,
+        functools.partial(last_kernel, cells), plain, [turn, field, field, q_shape], [tiles + tiles // 2 + 1],
+        [wb, over_all(told), q_far, gp_far, dens], (0,), 3,
     )
     return bary, grad.reshape(K, rows, merged), grad_theta[:, 0]
 

time: 164 us -> 159 us (0.970)
  Pallas kernels: 54.3 us -> 45.5 us
  blocking collectives: 32.6 us -> 36 us
  local copies, waits for them, and re-layouts: 3.77 us -> 1.5 us
  waiting for transfers between devices: 18 us -> 19.7 us
    pallas_call x8, Pallas kernels: 54.3 us -> 45.5 us  [call(): pl.pallas_call(kernel, out_shape=outs, in_specs=[pl.BlockSpec(memory_spac...]
    all_to_all x1, blocking collectives: 32.6 us -> 36 us  [over_all(): lax.all_to_all(jnp.broadcast_to(told[None], (devices, K, L)), ('gx', 'gy'...]
    unnamed x12 -> x8, local copies, waits for them, and re-layouts: 2.97 us -> 0.7 us
    ppermute x18, waiting for transfers between devices: 18 us -> 19.7 us  [swap(): return lax.ppermute(value, axis, list(partners(axis, parity).items()))]
  transfers between devices with their start and end apart: 18 -> 18, of which waited for: 3 -> 3; matrix products, arithmetic and copies ran while one was open for 0% -> 0% of each run, Pallas kernels for 15% -> 12%
where the time goes in v5:
time: 159 us; the launch traced here: 158 us
  starting transfers between devices  54.2 us (34%)
  Pallas kernels  45.5 us (29%)
  blocking collectives  36 us (23%)
  waiting for transfers between devices  19.7 us (12%)
    ppermute x18, starting transfers between devices, swap(): return lax.ppermute(value, axis, list(partners(axis, parity).items()))  54.2 us
    pallas_call x8, Pallas kernels, call(): pl.pallas_call(kernel, out_shape=outs, in_specs=[pl.BlockSpec(memory_spac...  45.5 us
    all_to_all x1, blocking collectives, over_all(): lax.all_to_all(jnp.broadcast_to(told[None], (devices, K, L)), ('gx', 'gy'...  36 us
    ppermute x18, waiting for transfers between devices, swap(): return lax.ppermute(value, axis, list(partners(axis, parity).items()))  19.7 us
  transfers between devices with their start and end apart: 18, of which 3 were waited for; matrix products, arithmetic and copies ran while one was open for 0% of the time, Pallas kernels for 12%

profile of v5, /device:TPU:1, one launch (start us, length us, event | category | flops | bytes accessed | tf_op | source)
XLA Modules:
  0.0 158.1 jit_solution(13944553353099755678)
XLA Ops:
  0.6 0.0 copy-start.1
  0.6 0.0 copy-start.3
  0.7 0.7 copy-done.3
  1.3 6.0 %shard_map.67 = (f32[32,16,8,128]{3,2,1,0:T(8,128)}, f32[32,16,8,128]{3,2,1,0:T(8,128)S(1)}, f32[8,128]{1,0:T(8,128)S(1)}, f32[8,128]{1,0:T(8,128)S(1)}, f32[8,1...) custom-call(f32[8]{0:T(128)S(1)} %copy-done.3, ...), custom_call_target="tpu_custom_call" | custom-call | tf_op jit(solution)/shard_map/pallas_call | solution.py:476
  7.3 0.7 collective-permute-start.2
  8.0 4.7 %collective-permute-start.3 = (f32[8,16,8,128]{3,2,1,0:T(8,128)}, f32[8,16,8,128]{3,2,1,0:T(8,128)S(1)}, u32[]{:S(2)}, u32[]{:S(2)}) collective-permute-start(f32[8,16,8,128]{3,2,1,0:T(8,128)} %get-tuple-element.58), channel_id=1, source_target_pairs={{0,16},{16,0},{32,48},{48,32},{64,80},{80,64},{96,112},{112,96},{1... | collective-permute-start | bytes 1572872 | tf_op jit(solution)/shard_map/ppermute | solution.py:498
  12.8 5.8 %collective-permute-start = (f32[32,4,8,128]{3,2,1,0:T(8,128)}, f32[32,4,8,128]{3,2,1,0:T(8,128)}, u32[]{:S(2)}, u32[]{:S(2)}) collective-permute-start(f32[32,4,8,128]{3,2,1,0:T(8,128)} %get-tuple-element.55), channel_id=1, source_target_pairs={{1,2},{2,1},{3,4},{4,3},{5,6},{6,5},{7,8},{8,7},{9,10},{10,9},{11,... | collective-permute-start | bytes 1572872 | tf_op jit(solution)/shard_map/ppermute | solution.py:498
  18.5 0.1 collective-permute-start.1
  18.6 0.0 copy-start
  18.6 0.0 collective-permute-done.2.xb
  18.7 5.6 %collective-permute-done.3.xa = f32[8,16,8,128]{3,2,1,0:T(8,128)S(1)} collective-permute-done((f32[8,16,8,128]{3,2,1,0:T(8,128)}, f32[8,16,8,128]{3,2,1,0:T(8,128)S(1)}, u32[]{:S(2)}, u32[]{:S(2)}) %collective-permute-start.3) | collective-permute-done | bytes 524320 | tf_op jit(solution)/shard_map/ppermute | solution.py:498
  24.4 6.1 %collective-permute-start.4 = (f32[16,4,8,128]{3,2,1,0:T(8,128)S(1)}, f32[16,4,8,128]{3,2,1,0:T(8,128)S(1)}, u32[]{:S(2)}, u32[]{:S(2)}) collective-permute-start(f32[16,4,8,128]{3,2,1,0:T(8,128)S(1)} %pad_maximum_fusion.2), channel_id=1, source_target_pairs={{1,2},{2,1},{3,4},{4,3},{5,6},{6,5},{7,8},{8,7},{9,10},{10,9},{11,... | collective-permute-start | bytes 786440 | tf_op jit(solution)/shard_map/ppermute | solution.py:498
  30.5 0.1 collective-permute-start.5
  30.6 0.0 copy-done.1
  30.6 0.0 copy-done
  30.6 0.0 copy-start.2
  30.6 6.0 %shard_map.68 = (f32[40,24,8,128]{3,2,1,0:T(8,128)S(1)}, f32[40,20,8,128]{3,2,1,0:T(8,128)S(1)}, f32[40,20,8,128]{3,2,1,0:T(8,128)S(1)}, f32[32,20,8,128]{3,2,1,...) custom-call(bf16[256,256]{1,0:T(8,128)(2,1)S(1)} %copy-done.1, ...), custom_call_target="tpu_custom_call" | custom-call | tf_op jit(solution)/shard_map/pallas_call | solution.py:476
  36.6 0.0 collective-permute-done.yb
  36.6 0.0 collective-permute-done.1.ya
  36.6 0.0 collective-permute-done.4.cb
  36.6 0.0 collective-permute-done.5.ca
  36.6 0.0 copy-done.2
  36.6 5.5 %shard_map.69 = (f32[40,24,8,128]{3,2,1,0:T(8,128)S(1)}, f32[40,20,8,128]{3,2,1,0:T(8,128)S(1)}, f32[40,20,8,128]{3,2,1,0:T(8,128)S(1)}, f32[32,20,8,128]{3,2,1,...) custom-call(bf16[256,256]{1,0:T(8,128)(2,1)S(1)} %copy-done.1, ...), custom_call_target="tpu_custom_call", output_to_operand_aliasing={{0}: (9, {}), {1}: (10, {}), {2}: (11, {}), {3}: (12, {}), ... | custom-call | tf_op jit(solution)/shard_map/pallas_call | solution.py:476
  42.1 0.7 collective-permute-start.6
  42.8 2.9 %collective-permute-start.7 = (f32[9,16,8,128]{3,2,1,0:T(8,128)S(1)}, f32[9,16,8,128]{3,2,1,0:T(8,128)S(1)}, u32[]{:S(2)}, u32[]{:S(2)}) collective-permute-start(f32[9,16,8,128]{3,2,1,0:T(8,128)S(1)} %get-tuple-element.70), channel_id=1, source_target_pairs={{0,16},{16,0},{32,48},{48,32},{64,80},{80,64},{96,112},{112,96},{1... | collective-permute-start | bytes 1769480 | tf_op jit(solution)/shard_map/ppermute | solution.py:498
  45.7 4.6 %collective-permute-start.8 = (f32[36,4,8,128]{3,2,1,0:T(8,128)S(1)}, f32[36,4,8,128]{3,2,1,0:T(8,128)S(1)}, u32[]{:S(2)}, u32[]{:S(2)}) collective-permute-start(f32[36,4,8,128]{3,2,1,0:T(8,128)S(1)} %get-tuple-element.71), channel_id=1, source_target_pairs={{1,2},{2,1},{3,4},{4,3},{5,6},{6,5},{7,8},{8,7},{9,10},{10,9},{11,... | collective-permute-start | bytes 1769480 | tf_op jit(solution)/shard_map/ppermute | solution.py:498
  50.4 0.1 collective-permute-start.9
  50.5 0.0 collective-permute-done.6.xb
  50.5 8.1 %collective-permute-done.7.xa = f32[9,16,8,128]{3,2,1,0:T(8,128)S(1)} collective-permute-done((f32[9,16,8,128]{3,2,1,0:T(8,128)S(1)}, f32[9,16,8,128]{3,2,1,0:T(8,128)S(1)}, u32[]{:S(2)}, u32[]{:S(2)}) %collective-permute-start.7) | collective-permute-done | bytes 589856 | tf_op jit(solution)/shard_map/ppermute | solution.py:498
  58.7 5.0 %collective-permute-start.10 = (f32[18,4,8,128]{3,2,1,0:T(8,128)S(1)}, f32[18,4,8,128]{3,2,1,0:T(8,128)S(1)}, u32[]{:S(2)}, u32[]{:S(2)}) collective-permute-start(f32[18,4,8,128]{3,2,1,0:T(8,128)S(1)} %pad_maximum_fusion), channel_id=1, source_target_pairs={{1,2},{2,1},{3,4},{4,3},{5,6},{6,5},{7,8},{8,7},{9,10},{10,9},{11,... | collective-permute-start | bytes 884744 | tf_op jit(solution)/shard_map/ppermute | solution.py:498
  63.7 0.1 collective-permute-start.11
  63.8 6.7 %shard_map.70 = (f32[40,24,8,128]{3,2,1,0:T(8,128)S(1)}, f32[40,20,8,128]{3,2,1,0:T(8,128)S(1)}, f32[32,20,8,128]{3,2,1,0:T(8,128)S(1)}, f32[32,16,8,128]{3,2,1,...) custom-call(bf16[256,256]{1,0:T(8,128)(2,1)S(1)} %copy-done.1, ...), custom_call_target="tpu_custom_call" | custom-call | tf_op jit(solution)/shard_map/pallas_call | solution.py:476
  70.5 0.0 collective-permute-done.8.yb
  70.5 0.0 collective-permute-done.9.ya
  70.5 0.0 collective-permute-done.10.cb
  70.5 0.0 collective-permute-done.11.ca
  70.5 4.4 %shard_map.71 = (f32[40,24,8,128]{3,2,1,0:T(8,128)S(1)}, f32[40,20,8,128]{3,2,1,0:T(8,128)S(1)}, f32[32,20,8,128]{3,2,1,0:T(8,128)S(1)}, f32[32,16,8,128]{3,2,1,...) custom-call(bf16[256,256]{1,0:T(8,128)(2,1)S(1)} %copy-done.1, ...), custom_call_target="tpu_custom_call", output_to_operand_aliasing={{0}: (12, {}), {1}: (13, {}), {2}: (14, {}), {3}: (15, {}),... | custom-call | tf_op jit(solution)/shard_map/pallas_call | solution.py:476
  75.0 0.7 collective-permute-start.14
  75.7 10.6 %collective-permute-start.15 = (f32[8,16,8,128]{3,2,1,0:T(8,128)S(1)}, f32[8,16,8,128]{3,2,1,0:T(8,128)S(1)}, u32[]{:S(2)}, u32[]{:S(2)}) collective-permute-start(f32[8,16,8,128]{3,2,1,0:T(8,128)S(1)} %get-tuple-element.88), channel_id=1, source_target_pairs={{0,16},{16,0},{32,48},{48,32},{64,80},{80,64},{96,112},{112,96},{1... | collective-permute-start | bytes 1572872 | tf_op jit(solution)/shard_map/ppermute | solution.py:498
  86.2 5.5 %collective-permute-start.12 = (f32[32,4,8,128]{3,2,1,0:T(8,128)S(1)}, f32[32,4,8,128]{3,2,1,0:T(8,128)S(1)}, u32[]{:S(2)}, u32[]{:S(2)}) collective-permute-start(f32[32,4,8,128]{3,2,1,0:T(8,128)S(1)} %get-tuple-element.85), channel_id=1, source_target_pairs={{1,2},{2,1},{3,4},{4,3},{5,6},{6,5},{7,8},{8,7},{9,10},{10,9},{11,... | collective-permute-start | bytes 1572872 | tf_op jit(solution)/shard_map/ppermute | solution.py:498
  91.8 0.1 collective-permute-start.13
  91.9 0.0 collective-permute-done.14.xb
  91.9 5.9 %collective-permute-done.15.xa = f32[8,16,8,128]{3,2,1,0:T(8,128)S(1)} collective-permute-done((f32[8,16,8,128]{3,2,1,0:T(8,128)S(1)}, f32[8,16,8,128]{3,2,1,0:T(8,128)S(1)}, u32[]{:S(2)}, u32[]{:S(2)}) %collective-permute-start.15) | collective-permute-done | bytes 524320 | tf_op jit(solution)/shard_map/ppermute | solution.py:498
  97.9 6.4 %collective-permute-start.16 = (f32[16,4,8,128]{3,2,1,0:T(8,128)S(1)}, f32[16,4,8,128]{3,2,1,0:T(8,128)S(1)}, u32[]{:S(2)}, u32[]{:S(2)}) collective-permute-start(f32[16,4,8,128]{3,2,1,0:T(8,128)S(1)} %pad_maximum_fusion.4), channel_id=1, source_target_pairs={{1,2},{2,1},{3,4},{4,3},{5,6},{6,5},{7,8},{8,7},{9,10},{10,9},{11,... | collective-permute-start | bytes 786440 | tf_op jit(solution)/shard_map/ppermute | solution.py:498
  104.3 0.1 collective-permute-start.17
  104.4 6.0 %shard_map.72 = (f32[40,24,8,128]{3,2,1,0:T(8,128)S(1)}, f32[40,20,8,128]{3,2,1,0:T(8,128)S(1)}, f32[32,20,8,128]{3,2,1,0:T(8,128)S(1)}, f32[32,16,8,128]{3,2,1,0:T(8,128)S(1)}, f32[2,8,128]{2,1,0:T(8,128)S(1)}) custom-call(bf16[256,256]{1,0:T(8,128)(2,1)S(1)} %copy-done.1, f32[8,128]{1,0:T(8,128)S(1)} %get-tuple-element.52.wb, ...), custom_call_target="tpu_custom_call" | custom-call | tf_op jit(solution)/shard_map/pallas_call | solution.py:476
  110.4 0.0 collective-permute-done.12.yb
  110.4 0.0 collective-permute-done.13.ya
  110.4 0.0 collective-permute-done.16.cb
  110.4 0.0 collective-permute-done.17.ca
  110.5 5.1 %shard_map.73 = (f32[40,24,8,128]{3,2,1,0:T(8,128)S(1)}, f32[40,20,8,128]{3,2,1,0:T(8,128)S(1)}, f32[32,20,8,128]{3,2,1,0:T(8,128)S(1)}, f32[32,16,8,128]{3,2,1,...) custom-call(bf16[256,256]{1,0:T(8,128)(2,1)S(1)} %copy-done.1, ...), custom_call_target="tpu_custom_call", output_to_operand_aliasing={{0}: (13, {}), {1}: (14, {}), {2}: (15, {}), {3}: (16, {}),... | custom-call | tf_op jit(solution)/shard_map/pallas_call | solution.py:476
  115.6 36.0 %all_to_all.5.heard = f32[128,8,128]{2,1,0:T(8,128)S(1)} all-to-all(f32[128,8,128]{2,1,0:T(8,128)S(1)} %broadcast_in_dim.2), channel_id=1, replica_groups=mesh['gx'=8,'gy'=16] {'gx','gy'}, dimensions={0} | all-to-all | bytes 1048576 | tf_op jit(solution)/shard_map/all_to_all | solution.py:517
  151.6 5.9 %shard_map.74 = (f32[256,2048]{1,0:T(8,128)}, f32[32,2048]{1,0:T(8,128)}, f32[8,128]{1,0:T(8,128)S(1)}) custom-call(f32[8,128]{1,0:T(8,128)S(1)} %get-tuple-element.52.wb, f32[128,8,128]{2,1,0:T(8,128)S(1)} %all_to_all.5.heard, f32[16,32,128]{2,1,0:T(8,128)} %get-tuple-element.96.q_far, f32[32,16,8,128]{3,2,1,0:T(8,128)} %get-tuple-element.97.gp_far, ...), custom_call_target="tpu_custom_call" | custom-call | tf_op jit(solution)/shard_map/pallas_call | solution.py:476
  157.5 0.6 slice_reduce_fusion
  (13 shorter events, 0.3 us)
Async XLA Ops:
  0.6 29.9 %copy-start.1 = (bf16[256,256]{1,0:T(8,128)(2,1)S(1)}, bf16[256,256]{1,0:T(8,128)(2,1)}, u32[]{:S(2)}) copy-start(bf16[256,256]{1,0:T(8,128)(2,1)} %constant.17.clone.w_ref) | copy-start | bytes 393220
  0.6 0.7 copy-start.3
  7.3 11.3 %collective-permute-start.2 = (f32[8,16,8,128]{3,2,1,0:T(8,128)}, f32[8,16,8,128]{3,2,1,0:T(8,128)S(1)}, u32[]{:S(2)}, u32[]{:S(2)}) collective-permute-start(f32[8,16,8,128]{3,2,1,0:T(8,128)} %get-tuple-element.57), channel_id=1, source_target_pairs={{16,32},{32,16},{48,64},{64,48},{80,96},{96,80},{17,33},{33,17},{4... | collective-permute-start | bytes 1572872 | tf_op jit(solution)/shard_map/ppermute | solution.py:498
  8.0 16.3 %collective-permute-start.3 = (f32[8,16,8,128]{3,2,1,0:T(8,128)}, f32[8,16,8,128]{3,2,1,0:T(8,128)S(1)}, u32[]{:S(2)}, u32[]{:S(2)}) collective-permute-start(f32[8,16,8,128]{3,2,1,0:T(8,128)} %get-tuple-element.58), channel_id=1, source_target_pairs={{0,16},{16,0},{32,48},{48,32},{64,80},{80,64},{96,112},{112,96},{1... | collective-permute-start | bytes 1572872 | tf_op jit(solution)/shard_map/ppermute | solution.py:498
  12.8 23.8 %collective-permute-start = (f32[32,4,8,128]{3,2,1,0:T(8,128)}, f32[32,4,8,128]{3,2,1,0:T(8,128)}, u32[]{:S(2)}, u32[]{:S(2)}) collective-permute-start(f32[32,4,8,128]{3,2,1,0:T(8,128)} %get-tuple-element.55), channel_id=1, source_target_pairs={{1,2},{2,1},{3,4},{4,3},{5,6},{6,5},{7,8},{8,7},{9,10},{10,9},{11,... | collective-permute-start | bytes 1572872 | tf_op jit(solution)/shard_map/ppermute | solution.py:498
  18.5 18.1 %collective-permute-start.1 = (f32[32,4,8,128]{3,2,1,0:T(8,128)}, f32[32,4,8,128]{3,2,1,0:T(8,128)}, u32[]{:S(2)}, u32[]{:S(2)}) collective-permute-start(f32[32,4,8,128]{3,2,1,0:T(8,128)} %get-tuple-element.56), channel_id=1, source_target_pairs={{0,1},{1,0},{2,3},{3,2},{4,5},{5,4},{6,7},{7,6},{8,9},{9,8},{10,11... | collective-permute-start | bytes 1572872 | tf_op jit(solution)/shard_map/ppermute | solution.py:498
  18.6 11.9 %copy-start = (f32[32,16,8,128]{3,2,1,0:T(8,128)S(1)}, f32[32,16,8,128]{3,2,1,0:T(8,128)}, u32[]{:S(2)}) copy-start(f32[32,16,8,128]{3,2,1,0:T(8,128)} %get-tuple-element.53.dens.dens_far) | copy-start | bytes 6291460
  24.4 12.3 %collective-permute-start.4 = (f32[16,4,8,128]{3,2,1,0:T(8,128)S(1)}, f32[16,4,8,128]{3,2,1,0:T(8,128)S(1)}, u32[]{:S(2)}, u32[]{:S(2)}) collective-permute-start(f32[16,4,8,128]{3,2,1,0:T(8,128)S(1)} %pad_maximum_fusion.2), channel_id=1, source_target_pairs={{1,2},{2,1},{3,4},{4,3},{5,6},{6,5},{7,8},{8,7},{9,10},{10,9},{11,... | collective-permute-start | bytes 786440 | tf_op jit(solution)/shard_map/ppermute | solution.py:498
  30.5 6.1 %collective-permute-start.5 = (f32[16,4,8,128]{3,2,1,0:T(8,128)S(1)}, f32[16,4,8,128]{3,2,1,0:T(8,128)S(1)}, u32[]{:S(2)}, u32[]{:S(2)}) collective-permute-start(f32[16,4,8,128]{3,2,1,0:T(8,128)S(1)} %pad_maximum_fusion.3), channel_id=1, source_target_pairs={{0,1},{1,0},{2,3},{3,2},{4,5},{5,4},{6,7},{7,6},{8,9},{9,8},{10,11... | collective-permute-start | bytes 786440 | tf_op jit(solution)/shard_map/ppermute | solution.py:498
  30.6 6.0 %copy-start.2 = (f32[32,2048]{1,0:T(8,128)S(1)}, f32[32,2048]{1,0:T(8,128)}, u32[]{:S(2)}) copy-start(f32[32,2048]{1,0:T(8,128)} %cot.5) | copy-start | bytes 786436
  42.1 8.3 %collective-permute-start.6 = (f32[9,16,8,128]{3,2,1,0:T(8,128)S(1)}, f32[9,16,8,128]{3,2,1,0:T(8,128)S(1)}, u32[]{:S(2)}, u32[]{:S(2)}) collective-permute-start(f32[9,16,8,128]{3,2,1,0:T(8,128)S(1)} %get-tuple-element.69), channel_id=1, source_target_pairs={{16,32},{32,16},{48,64},{64,48},{80,96},{96,80},{17,33},{33,17},{4... | collective-permute-start | bytes 1769480 | tf_op jit(solution)/shard_map/ppermute | solution.py:498
  42.8 15.8 %collective-permute-start.7 = (f32[9,16,8,128]{3,2,1,0:T(8,128)S(1)}, f32[9,16,8,128]{3,2,1,0:T(8,128)S(1)}, u32[]{:S(2)}, u32[]{:S(2)}) collective-permute-start(f32[9,16,8,128]{3,2,1,0:T(8,128)S(1)} %get-tuple-element.70), channel_id=1, source_target_pairs={{0,16},{16,0},{32,48},{48,32},{64,80},{80,64},{96,112},{112,96},{1... | collective-permute-start | bytes 1769480 | tf_op jit(solution)/shard_map/ppermute | solution.py:498
  45.7 24.7 %collective-permute-start.8 = (f32[36,4,8,128]{3,2,1,0:T(8,128)S(1)}, f32[36,4,8,128]{3,2,1,0:T(8,128)S(1)}, u32[]{:S(2)}, u32[]{:S(2)}) collective-permute-start(f32[36,4,8,128]{3,2,1,0:T(8,128)S(1)} %get-tuple-element.71), channel_id=1, source_target_pairs={{1,2},{2,1},{3,4},{4,3},{5,6},{6,5},{7,8},{8,7},{9,10},{10,9},{11,... | collective-permute-start | bytes 1769480 | tf_op jit(solution)/shard_map/ppermute | solution.py:498
  50.4 20.1 %collective-permute-start.9 = (f32[36,4,8,128]{3,2,1,0:T(8,128)S(1)}, f32[36,4,8,128]{3,2,1,0:T(8,128)S(1)}, u32[]{:S(2)}, u32[]{:S(2)}) collective-permute-start(f32[36,4,8,128]{3,2,1,0:T(8,128)S(1)} %get-tuple-element.72), channel_id=1, source_target_pairs={{0,1},{1,0},{2,3},{3,2},{4,5},{5,4},{6,7},{7,6},{8,9},{9,8},{10,11... | collective-permute-start | bytes 1769480 | tf_op jit(solution)/shard_map/ppermute | solution.py:498
  58.7 11.8 %collective-permute-start.10 = (f32[18,4,8,128]{3,2,1,0:T(8,128)S(1)}, f32[18,4,8,128]{3,2,1,0:T(8,128)S(1)}, u32[]{:S(2)}, u32[]{:S(2)}) collective-permute-start(f32[18,4,8,128]{3,2,1,0:T(8,128)S(1)} %pad_maximum_fusion), channel_id=1, source_target_pairs={{1,2},{2,1},{3,4},{4,3},{5,6},{6,5},{7,8},{8,7},{9,10},{10,9},{11,... | collective-permute-start | bytes 884744 | tf_op jit(solution)/shard_map/ppermute | solution.py:498
  63.7 6.8 %collective-permute-start.11 = (f32[18,4,8,128]{3,2,1,0:T(8,128)S(1)}, f32[18,4,8,128]{3,2,1,0:T(8,128)S(1)}, u32[]{:S(2)}, u32[]{:S(2)}) collective-permute-start(f32[18,4,8,128]{3,2,1,0:T(8,128)S(1)} %pad_maximum_fusion.1), channel_id=1, source_target_pairs={{0,1},{1,0},{2,3},{3,2},{4,5},{5,4},{6,7},{7,6},{8,9},{9,8},{10,11... | collective-permute-start | bytes 884744 | tf_op jit(solution)/shard_map/ppermute | solution.py:498
  75.0 16.9 %collective-permute-start.14 = (f32[8,16,8,128]{3,2,1,0:T(8,128)S(1)}, f32[8,16,8,128]{3,2,1,0:T(8,128)S(1)}, u32[]{:S(2)}, u32[]{:S(2)}) collective-permute-start(f32[8,16,8,128]{3,2,1,0:T(8,128)S(1)} %get-tuple-element.87), channel_id=1, source_target_pairs={{16,32},{32,16},{48,64},{64,48},{80,96},{96,80},{17,33},{33,17},{4... | collective-permute-start | bytes 1572872 | tf_op jit(solution)/shard_map/ppermute | solution.py:498
  75.7 22.2 %collective-permute-start.15 = (f32[8,16,8,128]{3,2,1,0:T(8,128)S(1)}, f32[8,16,8,128]{3,2,1,0:T(8,128)S(1)}, u32[]{:S(2)}, u32[]{:S(2)}) collective-permute-start(f32[8,16,8,128]{3,2,1,0:T(8,128)S(1)} %get-tuple-element.88), channel_id=1, source_target_pairs={{0,16},{16,0},{32,48},{48,32},{64,80},{80,64},{96,112},{112,96},{1... | collective-permute-start | bytes 1572872 | tf_op jit(solution)/shard_map/ppermute | solution.py:498
  86.2 24.2 %collective-permute-start.12 = (f32[32,4,8,128]{3,2,1,0:T(8,128)S(1)}, f32[32,4,8,128]{3,2,1,0:T(8,128)S(1)}, u32[]{:S(2)}, u32[]{:S(2)}) collective-permute-start(f32[32,4,8,128]{3,2,1,0:T(8,128)S(1)} %get-tuple-element.85), channel_id=1, source_target_pairs={{1,2},{2,1},{3,4},{4,3},{5,6},{6,5},{7,8},{8,7},{9,10},{10,9},{11,... | collective-permute-start | bytes 1572872 | tf_op jit(solution)/shard_map/ppermute | solution.py:498
  91.8 18.6 %collective-permute-start.13 = (f32[32,4,8,128]{3,2,1,0:T(8,128)S(1)}, f32[32,4,8,128]{3,2,1,0:T(8,128)S(1)}, u32[]{:S(2)}, u32[]{:S(2)}) collective-permute-start(f32[32,4,8,128]{3,2,1,0:T(8,128)S(1)} %get-tuple-element.86), channel_id=1, source_target_pairs={{0,1},{1,0},{2,3},{3,2},{4,5},{5,4},{6,7},{7,6},{8,9},{9,8},{10,11... | collective-permute-start | bytes 1572872 | tf_op jit(solution)/shard_map/ppermute | solution.py:498
  97.9 12.6 %collective-permute-start.16 = (f32[16,4,8,128]{3,2,1,0:T(8,128)S(1)}, f32[16,4,8,128]{3,2,1,0:T(8,128)S(1)}, u32[]{:S(2)}, u32[]{:S(2)}) collective-permute-start(f32[16,4,8,128]{3,2,1,0:T(8,128)S(1)} %pad_maximum_fusion.4), channel_id=1, source_target_pairs={{1,2},{2,1},{3,4},{4,3},{5,6},{6,5},{7,8},{8,7},{9,10},{10,9},{11,... | collective-permute-start | bytes 786440 | tf_op jit(solution)/shard_map/ppermute | solution.py:498
  104.3 6.1 %collective-permute-start.17 = (f32[16,4,8,128]{3,2,1,0:T(8,128)S(1)}, f32[16,4,8,128]{3,2,1,0:T(8,128)S(1)}, u32[]{:S(2)}, u32[]{:S(2)}) collective-permute-start(f32[16,4,8,128]{3,2,1,0:T(8,128)S(1)} %pad_maximum_fusion.5), channel_id=1, source_target_pairs={{0,1},{1,0},{2,3},{3,2},{4,5},{5,4},{6,7},{7,6},{8,9},{9,8},{10,11... | collective-permute-start | bytes 786440 | tf_op jit(solution)/shard_map/ppermute | solution.py:498

commit v6 on v5

--- a/solution.py
+++ b/solution.py
@@ -104,24 +104,31 @@
     big[pl.ds(row_b, HALO)] = xb[0:HALO]
 
 
-def join_ends(ends, rows, slabs, ya, yb, ca, cb):
+def join_ends(ends, rows, slabs, ya, yb, ca, da, db):
     (row_a, row_b), _ = sides(rows, 0)
     _, py = parities()
-    for col, y, c in (((1 - py) * HT, ya, ca), (py * HT, yb, cb)):
-        lanes = pl.ds(col, HT)
-        ends[pl.ds(HALO, rows), lanes] = y[0:rows]
-        ends[pl.ds(row_b, HALO), lanes] = c[0:HALO]
-        ends[pl.ds(row_a, HALO), lanes] = c[slabs : slabs + HALO]
+    row_a, row_b, middle = pl.ds(row_a, HALO), pl.ds(row_b, HALO), pl.ds(HALO, rows)
+    col_a, col_b = pl.ds((1 - py) * HT, HT), pl.ds(py * HT, HT)
+    ends[middle, col_a] = ya[0:rows]
+    ends[row_b, col_a] = ca[0:HALO]
+    ends[row_a, col_a] = ca[slabs : slabs + HALO]
+    ends[middle, col_b] = yb[0:rows]
+    ends[row_a, col_b] = da[0:HALO]
+    ends[row_b, col_b] = db[0:HALO]
 
 
 def give_edges(own, outs):
-    xa, xb, ya, yb = outs
+    xa, xb, ya, yb, da, db = outs
     rows, tiles = own.shape[0], own.shape[1]
     px, py = parities()
-    xa[0:HALO] = own[pl.ds((1 - px) * (rows - HALO), HALO)]
-    xb[0:HALO] = own[pl.ds(px * (rows - HALO), HALO)]
-    ya[0:rows] = own[:, pl.ds((1 - py) * (tiles - HT), HT)]
-    yb[0:rows] = own[:, pl.ds(py * (tiles - HT), HT)]
+    row_a, row_b = pl.ds((1 - px) * (rows - HALO), HALO), pl.ds(px * (rows - HALO), HALO)
+    col_a, col_b = pl.ds((1 - py) * (tiles - HT), HT), pl.ds(py * (tiles - HT), HT)
+    xa[0:HALO] = own[row_a]
+    xb[0:HALO] = own[row_b]
+    ya[0:rows] = own[:, col_a]
+    yb[0:rows] = own[:, col_b]
+    da[0:HALO] = own[row_a, col_b]
+    db[0:HALO] = own[row_b, col_b]
 
 
 def clear_outside(fields, ranges, ends):
@@ -176,7 +183,7 @@
 
 
 def start_kernel(theta, log_ref, dens_out, e, mass, wb, *rest):
-    edges, (turn, across, dens, sem) = rest[:4], rest[4:]
+    edges, (turn, across, dens, sem) = rest[:6], rest[6:]
     rows, tiles = dens.shape[0], dens.shape[1]
     loads = [pltpu.make_async_copy(log_ref.at[:, pl.ds(t * L, L)], turn.at[t], sem.at[t]) for t in range(tiles)]
     for c in loads:
@@ -191,11 +198,8 @@
     depth = inside(lane % NZ, NZ)
     first = lax.axis_index("gy") * (tiles * L // NZ)
 
-    def factor(x, carry):
-        across[x] = 1.0 / inside(jnp.full((K, L), lax.axis_index("gx") * rows + x), lax.axis_size("gx") * rows)
-        return carry
-
-    lax.fori_loop(0, rows, factor, 0)
+    at = lax.axis_index("gx") * rows + lax.broadcasted_iota(jnp.int32, (rows, K, L), 0)
+    across[...] = 1.0 / inside(at, lax.axis_size("gx") * rows)
     mass[...] = jnp.zeros((K, L), F32)
     for t in range(tiles):
         along = inside(first + t * (L // NZ) + lane // NZ, lax.axis_size("gy") * (tiles * L // NZ))
@@ -251,14 +255,14 @@
     first_fields(True, wb, w_ref, dens, big, tmp, v, inv_a, tmp2, u, inv_s)
 
 
-def first_outer(w_ref, wb, cot, dens, e, yb, ya, cb, ca, *rest):
-    fields, mean, edges, ends = rest[6:12], rest[12], rest[13:17], rest[17]
+def first_outer(w_ref, wb, cot, dens, e, yb, ya, ca, da, db, *rest):
+    fields, mean, edges, ends = rest[6:12], rest[12], rest[13:19], rest[19]
     rows, tiles = dens.shape[0], dens.shape[1]
     mean[...] = jnp.broadcast_to(centre(e), (K, L))
-    join_ends(ends, rows, HALO, ya, yb, ca, cb)
+    join_ends(ends, rows, HALO, ya, yb, ca, da, db)
     first_fields(False, wb, w_ref, dens, ends, *fields)
     give_edges(fields[4], edges)
-    xa, xb, ya, yb = edges
+    xa, xb, ya, yb, da, db = edges
     px, py = parities()
     row_a = pl.ds(pl.multiple_of((1 - px) * (rows - 8), 8), 8)
     row_b = pl.ds(pl.multiple_of(px * (rows - 8), 8), 8)
@@ -270,6 +274,10 @@
             lanes = pl.ds(pl.multiple_of((side * (tiles - HT) + t) * L, L), L)
             for b in range(rows // 8):
                 out[rows + b, t] = cot[b * 8 : b * 8 + 8, lanes]
+    for t in range(HT):
+        lanes = pl.ds(pl.multiple_of((py * (tiles - HT) + t) * L, L), L)
+        da[HALO, t] = cot[row_a, lanes]
+        db[HALO, t] = cot[row_b, lanes]
 
 
 def second_fields(inner, wb, w_ref, mean, cots, own, inv_s, src, tmp, r, tmp2, bu, z, q, sums):
@@ -332,24 +340,27 @@
     second_fields(True, wb, w_ref, centre(own), cots, own, inv_s, big, tmp, r, tmp2, bu, z, q, sums)
 
 
-def second_outer(w_ref, wb, mass, cot, inv_s, own, xb, xa, yb, ya, cb, ca, *rest):
+def second_outer(w_ref, wb, mass, cot, inv_s, own, xb, xa, yb, ya, ca, da, db, *rest):
     tmp, r, tmp2, bu, z, q, sums = rest[7:14]
-    told, edges, (ends, cots) = rest[14], rest[15:19], rest[19:]
+    told, edges, (ends, cots) = rest[14], rest[15:21], rest[21:]
     rows, tiles = own.shape[0], own.shape[1]
     slabs = xa.shape[0]
-    join_ends(ends, rows, slabs, ya, yb, ca, cb)
+    join_ends(ends, rows, slabs, ya, yb, ca, da, db)
     (row_a, row_b), (col_a, col_b) = sides(rows, tiles)
     row_a, row_b = pl.ds(pl.multiple_of(row_a, 8), 8), pl.ds(pl.multiple_of(row_b, 8), 8)
     for t in (0, 1, tiles - 2, tiles - 1):
         cots[HT + t, HALO : HALO + rows] = cot[:, t * L : (t + 1) * L]
         cots[HT + t, row_a] = xa[HALO, t]
         cots[HT + t, row_b] = xb[HALO, t]
-    for col, y, c in ((col_a, ya, ca), (col_b, yb, cb)):
-        for t in range(HT):
-            for b in range(rows // 8):
-                cots[col + t, HALO + b * 8 : HALO + b * 8 + 8] = y[rows + b, t]
-            cots[col + t, row_b] = c[HALO, t]
-            cots[col + t, row_a] = c[slabs + HALO, t]
+    for t in range(HT):
+        for b in range(rows // 8):
+            some_rows = pl.ds(HALO + b * 8, 8)
+            cots[col_a + t, some_rows] = ya[rows + b, t]
+            cots[col_b + t, some_rows] = yb[rows + b, t]
+        cots[col_a + t, row_b] = ca[HALO, t]
+        cots[col_a + t, row_a] = ca[slabs + HALO, t]
+        cots[col_b + t, row_a] = da[HALO, t]
+        cots[col_b + t, row_b] = db[HALO, t]
     mean = centre(own)
     second_fields(False, wb, w_ref, mean, cots, own, inv_s, ends, tmp, r, tmp2, bu, z, q, sums)
     told[...] = in_lanes(over_lanes(mass[...]), over_lanes(sums[0]), over_lanes(sums[1, 0:1]), mean)
@@ -399,7 +410,7 @@
     third_fields(True, wb, w_ref, mean[...], inv_a, v, e, bu, big, tmp, r, tmp2, gp, sums)
 
 
-def third_outer(w_ref, wb, mean, before, inv_a, v, e, bu, q, yb, ya, cb, ca, *rest):
+def third_outer(w_ref, wb, mean, before, inv_a, v, e, bu, q, yb, ya, ca, da, db, *rest):
     tmp, r, tmp2, gp, sums = rest[5:10]
     gp_out, q_out, told, ends, sem = rest[10:]
     rows, tiles = e.shape[0], e.shape[1]
@@ -407,7 +418,7 @@
     copies = [pltpu.make_async_copy(q, q_out, sem.at[0]), pltpu.make_async_copy(gp.at[:, middle], gp_out.at[:, middle], sem.at[1])]
     for c in copies:
         c.start()
-    join_ends(ends, rows, HALO, ya, yb, ca, cb)
+    join_ends(ends, rows, HALO, ya, yb, ca, da, db)
     third_fields(False, wb, w_ref, mean[...], inv_a, v, e, bu, ends, tmp, r, tmp2, gp, sums)
     for i, first in enumerate((0, tiles - HT)):
         lanes = pl.ds(first, HT)
@@ -460,9 +471,10 @@
         copies.append(pltpu.make_async_copy(turn.at[t], out.at[:, pl.ds(t * L, L)], sem.at[t]))
         copies[-1].start()
         bary[:, t * L : (t + 1) * L] = q[t] * scale
-    second = everyone[:, :, 1:2] + (everyone[:, :, 3:4] + (2.0 * shift_k - shift)) * everyone[:, :, 2:3]
-    first = everyone[:, :, 4:5] + (everyone[:, :, 6:7] + shift_k) * everyone[:, :, 5:6]
-    weight_grad = scale * jnp.sum(first + second, axis=0)
+    offsets = in_lanes(0.0, 0.0, 0.0, 2.0 * shift_k - shift, 0.0, 0.0, shift_k)
+    turned = pltpu.roll(everyone.reshape(-1, L), 1, axis=1).reshape(everyone.shape)
+    back = jnp.sum((everyone + offsets) * turned, axis=0)
+    weight_grad = scale * (total[:, 1:2] + back[:, 3:4] + total[:, 4:5] + back[:, 6:7])
     grad = weights * (weight_grad - jnp.sum(weights * weight_grad, axis=0, keepdims=True))
     theta_out[...] = jnp.broadcast_to(grad, (K, L))
     for c in copies:
@@ -498,18 +510,21 @@
     return lax.ppermute(value, axis, list(partners(axis, parity).items()))
 
 
-def exchange(xa, xb, ya, yb, tiles):
+def swap_diagonal(value, parity_x, parity_y):
+    along_x, along_y, width = partners("gx", parity_x), partners("gy", parity_y), lax.axis_size("gy")
+    pairs = [(i * width + j, k * width + m) for i, k in along_x.items() for j, m in along_y.items()]
+    return lax.ppermute(value, ("gx", "gy"), pairs)
+
+
+def exchange(xa, xb, ya, yb, da, db, tiles):
     rxb, ryb = swap(xb, "gx", 1), swap(yb, "gy", 1)
+    rdb, rda = swap_diagonal(db, 1, 1), swap_diagonal(da, 0, 1)
     rxa, rya = swap(xa, "gx", 0), swap(ya, "gy", 0)
-    py = lax.rem(lax.axis_index("gy"), 2)
-
-    def corner(side):
-        first = side * (tiles - HT)
-        return jnp.concatenate([lax.dynamic_slice_in_dim(r, first, HT, axis=1) for r in (rxb, rxa)], axis=0)
-
-    rcb = swap(corner(py), "gy", 1)
-    rca = swap(corner(1 - py), "gy", 0)
-    return rxa, rxb, ryb, rya, rcb, rca
+    rxb, rxa, rdb, rda = lax.optimization_barrier((rxb, rxa, rdb, rda))
+    first = (1 - lax.rem(lax.axis_index("gy"), 2)) * (tiles - HT)
+    corner = jnp.concatenate([lax.dynamic_slice_in_dim(r, first, HT, axis=1) for r in (rxb, rxa)], axis=0)
+    rca = swap(corner, "gy", 0)
+    return rxa, rxb, ryb, rya, rca, rda, rdb
 
 
 def over_all(told):
@@ -531,7 +546,7 @@
         return [pltpu.VMEM(s, F32) for s in shapes]
 
     def edges(more, more_y):
-        return near(*[(HALO + more, tiles, K, L)] * 2, *[(rows + more_y, HT, K, L)] * 2)
+        return near(*[(HALO + more, tiles, K, L)] * 2, *[(rows + more_y, HT, K, L)] * 2, *[(HALO + more, HT, K, L)] * 2)
 
     logs = log_dens.reshape(K * rows, merged)
     dens, e, mass, wb, *sent = call(
@@ -543,21 +558,21 @@
     held_now = call(first_inner, near(*held), [big], [], [w, wb, dens, e, xb, xa])
     _, v, inv_a, _, u, inv_s, mean, *sent = call(
         first_outer, near(*held, small) + edges(1, rows // 8), [ends], [],
-        [w, wb, cotangent, dens, e, *others, *held_now], same={9 + i: i for i in range(6)},
+        [w, wb, cotangent, dens, e, *others, *held_now], same={10 + i: i for i in range(6)},
     )
     xa, xb, *others = exchange(*sent, tiles)
     held = [tmp, ringed, tmp2, field, field, q_shape, acc]
     held_now = call(second_inner, near(*held), [big, cots], [], [w, wb, cotangent, inv_s, u, xb, xa])
     _, _, _, bu, z, q, _, told, *sent = call(
         second_outer, near(*held, small) + edges(0, 0), [ends, cots], [],
-        [w, wb, mass, cotangent, inv_s, u, xb, xa, *others, *held_now], same={12 + i: i for i in range(7)},
+        [w, wb, mass, cotangent, inv_s, u, xb, xa, *others, *held_now], same={13 + i: i for i in range(7)},
     )
     xa, xb, *others = exchange(*sent, tiles)
     held = [tmp, ringed, tmp2, field, acc]
     held_now = call(third_inner, near(*held), [big], [], [w, wb, mean, inv_a, v, e, bu, z, xb, xa])
     *_, gp_far, q_far, told = call(
         third_outer, near(*held) + [pltpu.HBM(field, F32), pltpu.HBM(q_shape, F32)] + near(small), [ends], [4],
-        [w, wb, mean, told, inv_a, v, e, bu, q, *others, *held_now], (5, 6), same={13 + i: i for i in range(5)},
+        [w, wb, mean, told, inv_a, v, e, bu, q, *others, *held_now], (5, 6), same={14 + i: i for i in range(5)},
     )
     plain = [jax.ShapeDtypeStruct(s, F32) for s in ((K * rows, merged), (rows, merged), small)]
     grad, bary, grad_theta = call(

time: 159 us -> 158 us (level)
  waiting for transfers between devices: 19.7 us -> 14.9 us
  starting transfers between devices: 54.2 us -> 58.7 us
  blocking collectives: 36 us -> 34.2 us
    ppermute x0 -> x6, starting transfers between devices: none -> 30.4 us  [swap_diagonal(): return lax.ppermute(value, ('gx', 'gy'), pairs)]
    ppermute x18 -> x15, starting transfers between devices: 54.2 us -> 28.3 us  [swap(): return lax.ppermute(value, axis, list(partners(axis, parity).items()))]
    ppermute x18 -> x15, waiting for transfers between devices: 19.7 us -> 12.6 us  [swap(): return lax.ppermute(value, axis, list(partners(axis, parity).items()))]
    ppermute x0 -> x6, waiting for transfers between devices: none -> 2.29 us  [swap_diagonal(): return lax.ppermute(value, ('gx', 'gy'), pairs)]
    all_to_all x1, blocking collectives: 36 us -> 34.2 us  [over_all(): lax.all_to_all(jnp.broadcast_to(told[None], (devices, K, L)), ('gx', 'gy'...]
  transfers between devices with their start and end apart: 18 -> 21, of which waited for: 3 -> 5; matrix products, arithmetic and copies ran while one was open for 0% -> 0% of each run, Pallas kernels for 12% -> 12%
where the time goes in v6:
time: 158 us; the launch traced here: 157 us
  starting transfers between devices  58.7 us (37%)
  Pallas kernels  45.5 us (29%)
  blocking collectives  34.2 us (22%)
  waiting for transfers between devices  14.9 us (9%)
  local copies, waits for them, and re-layouts  3.03 us (2%)
    pallas_call x8, Pallas kernels, call(): pl.pallas_call(kernel, out_shape=outs, in_specs=[pl.BlockSpec(memory_spac...  45.5 us
    all_to_all x1, blocking collectives, over_all(): lax.all_to_all(jnp.broadcast_to(told[None], (devices, K, L)), ('gx', 'gy'...  34.2 us
    ppermute x6, starting transfers between devices, swap_diagonal(): return lax.ppermute(value, ('gx', 'gy'), pairs)  30.4 us
    ppermute x15, starting transfers between devices, swap(): return lax.ppermute(value, axis, list(partners(axis, parity).items()))  28.3 us
    ppermute x15, waiting for transfers between devices, swap(): return lax.ppermute(value, axis, list(partners(axis, parity).items()))  12.6 us
  transfers between devices with their start and end apart: 21, of which 5 were waited for; matrix products, arithmetic and copies ran while one was open for 0% of the time, Pallas kernels for 12%

profile of v6, /device:TPU:1, one launch (start us, length us, event | category | flops | bytes accessed | tf_op | source)
XLA Modules:
  0.0 157.4 jit_solution(13770322025584988517)
XLA Ops:
  0.6 0.0 copy-start.1
  0.6 0.0 copy-start.3
  0.7 0.7 copy-done.3
  1.3 6.0 %shard_map.67 = (f32[32,16,8,128]{3,2,1,0:T(8,128)}, f32[32,16,8,128]{3,2,1,0:T(8,128)S(1)}, f32[8,128]{1,0:T(8,128)S(1)}, f32[8,128]{1,0:T(8,128)S(1)}, f32[8,1...) custom-call(f32[8]{0:T(128)S(1)} %copy-done.3, ...), custom_call_target="tpu_custom_call" | custom-call | tf_op jit(solution)/shard_map/pallas_call | solution.py:488
  7.4 0.7 collective-permute-start.2
  8.1 4.7 %collective-permute-start.3 = (f32[8,16,8,128]{3,2,1,0:T(8,128)}, f32[8,16,8,128]{3,2,1,0:T(8,128)S(1)}, u32[]{:S(2)}, u32[]{:S(2)}) collective-permute-start(f32[8,16,8,128]{3,2,1,0:T(8,128)} %get-tuple-element.76), channel_id=1, source_target_pairs={{0,16},{16,0},{32,48},{48,32},{64,80},{80,64},{96,112},{112,96},{1... | collective-permute-start | bytes 1572872 | tf_op jit(solution)/shard_map/ppermute | solution.py:510
  12.8 0.7 collective-permute-start.4
  13.4 7.7 %collective-permute-start.5 = (f32[8,4,8,128]{3,2,1,0:T(8,128)}, f32[8,4,8,128]{3,2,1,0:T(8,128)S(1)}, u32[]{:S(2)}, u32[]{:S(2)}) collective-permute-start(f32[8,4,8,128]{3,2,1,0:T(8,128)} %get-tuple-element.78), channel_id=1, source_target_pairs={{1,18},{2,17},{3,20},{4,19},{5,22},{6,21},{7,24},{8,23},{9,26},{10... | collective-permute-start | bytes 393224 | tf_op jit(solution)/shard_map/ppermute | solution.py:516
  21.2 5.5 %collective-permute-start = (f32[32,4,8,128]{3,2,1,0:T(8,128)}, f32[32,4,8,128]{3,2,1,0:T(8,128)}, u32[]{:S(2)}, u32[]{:S(2)}) collective-permute-start(f32[32,4,8,128]{3,2,1,0:T(8,128)} %get-tuple-element.73), channel_id=1, source_target_pairs={{1,2},{2,1},{3,4},{4,3},{5,6},{6,5},{7,8},{8,7},{9,10},{10,9},{11,... | collective-permute-start | bytes 1572872 | tf_op jit(solution)/shard_map/ppermute | solution.py:510
  26.6 0.0 collective-permute-done.4.db
  26.7 0.1 collective-permute-start.1
  26.8 0.0 collective-permute-done.5.da
  26.8 0.0 collective-permute-done.2.xb
  26.8 0.4 collective-permute-done.3.xa
  27.2 1.6 %collective-permute-start.6 = (f32[16,4,8,128]{3,2,1,0:T(8,128)S(1)}, f32[16,4,8,128]{3,2,1,0:T(8,128)S(1)}, u32[]{:S(2)}, u32[]{:S(2)}) collective-permute-start(f32[16,4,8,128]{3,2,1,0:T(8,128)S(1)} %pad_maximum_fusion.1), channel_id=1, source_target_pairs={{0,1},{1,0},{2,3},{3,2},{4,5},{5,4},{6,7},{7,6},{8,9},{9,8},{10,11... | collective-permute-start | bytes 786440 | tf_op jit(solution)/shard_map/ppermute | solution.py:510
  28.8 0.0 copy-done.1
  28.8 0.0 copy-start
  28.8 1.6 %copy-done = f32[32,16,8,128]{3,2,1,0:T(8,128)S(1)} copy-done((f32[32,16,8,128]{3,2,1,0:T(8,128)S(1)}, f32[32,16,8,128]{3,2,1,0:T(8,128)}, u32[]{:S(2)}) %copy-start) | copy-done | bytes 2097176
  30.4 0.0 copy-start.2
  30.4 6.0 %shard_map.68 = (f32[40,24,8,128]{3,2,1,0:T(8,128)S(1)}, f32[40,20,8,128]{3,2,1,0:T(8,128)S(1)}, f32[40,20,8,128]{3,2,1,0:T(8,128)S(1)}, f32[32,20,8,128]{3,2,1,...) custom-call(bf16[256,256]{1,0:T(8,128)(2,1)S(1)} %copy-done.1, ...), custom_call_target="tpu_custom_call" | custom-call | tf_op jit(solution)/shard_map/pallas_call | solution.py:488
  36.4 1.2 collective-permute-done.yb
  37.6 0.0 collective-permute-done.1.ya
  37.6 0.0 collective-permute-done.6.ca
  37.6 0.0 copy-done.2
  37.6 5.5 %shard_map.69 = (f32[40,24,8,128]{3,2,1,0:T(8,128)S(1)}, f32[40,20,8,128]{3,2,1,0:T(8,128)S(1)}, f32[40,20,8,128]{3,2,1,0:T(8,128)S(1)}, f32[32,20,8,128]{3,2,1,...) custom-call(bf16[256,256]{1,0:T(8,128)(2,1)S(1)} %copy-done.1, ...), custom_call_target="tpu_custom_call", output_to_operand_aliasing={{0}: (10, {}), {1}: (11, {}), {2}: (12, {}), {3}: (13, {}),... | custom-call | tf_op jit(solution)/shard_map/pallas_call | solution.py:488
  43.2 0.7 collective-permute-start.7
  43.9 5.8 %collective-permute-start.8 = (f32[9,16,8,128]{3,2,1,0:T(8,128)S(1)}, f32[9,16,8,128]{3,2,1,0:T(8,128)S(1)}, u32[]{:S(2)}, u32[]{:S(2)}) collective-permute-start(f32[9,16,8,128]{3,2,1,0:T(8,128)S(1)} %get-tuple-element.94), channel_id=1, source_target_pairs={{0,16},{16,0},{32,48},{48,32},{64,80},{80,64},{96,112},{112,96},{1... | collective-permute-start | bytes 1769480 | tf_op jit(solution)/shard_map/ppermute | solution.py:510
  49.7 0.7 collective-permute-start.9
  50.4 10.9 %collective-permute-start.10 = (f32[9,4,8,128]{3,2,1,0:T(8,128)S(1)}, f32[9,4,8,128]{3,2,1,0:T(8,128)S(1)}, u32[]{:S(2)}, u32[]{:S(2)}) collective-permute-start(f32[9,4,8,128]{3,2,1,0:T(8,128)S(1)} %get-tuple-element.96), channel_id=1, source_target_pairs={{1,18},{2,17},{3,20},{4,19},{5,22},{6,21},{7,24},{8,23},{9,26},{10... | collective-permute-start | bytes 442376 | tf_op jit(solution)/shard_map/ppermute | solution.py:516
  61.3 2.9 %collective-permute-start.11 = (f32[36,4,8,128]{3,2,1,0:T(8,128)S(1)}, f32[36,4,8,128]{3,2,1,0:T(8,128)S(1)}, u32[]{:S(2)}, u32[]{:S(2)}) collective-permute-start(f32[36,4,8,128]{3,2,1,0:T(8,128)S(1)} %get-tuple-element.99), channel_id=1, source_target_pairs={{1,2},{2,1},{3,4},{4,3},{5,6},{6,5},{7,8},{8,7},{9,10},{10,9},{11,... | collective-permute-start | bytes 1769480 | tf_op jit(solution)/shard_map/ppermute | solution.py:510
  64.3 0.0 collective-permute-done.9.db
  64.3 0.1 collective-permute-start.12
  64.4 2.3 %collective-permute-done.10.da = f32[9,4,8,128]{3,2,1,0:T(8,128)S(1)} collective-permute-done((f32[9,4,8,128]{3,2,1,0:T(8,128)S(1)}, f32[9,4,8,128]{3,2,1,0:T(8,128)S(1)}, u32[]{:S(2)}, u32[]{:S(2)}) %collective-permute-start.10) | collective-permute-done | bytes 147488 | tf_op jit(solution)/shard_map/ppermute | solution.py:516
  66.6 0.0 collective-permute-done.7.xb
  66.6 0.0 collective-permute-done.8.xa
  66.7 0.1 collective-permute-start.13
  66.8 6.7 %shard_map.70 = (f32[40,24,8,128]{3,2,1,0:T(8,128)S(1)}, f32[40,20,8,128]{3,2,1,0:T(8,128)S(1)}, f32[32,20,8,128]{3,2,1,0:T(8,128)S(1)}, f32[32,16,8,128]{3,2,1,...) custom-call(bf16[256,256]{1,0:T(8,128)(2,1)S(1)} %copy-done.1, ...), custom_call_target="tpu_custom_call" | custom-call | tf_op jit(solution)/shard_map/pallas_call | solution.py:488
  73.5 6.8 %collective-permute-done.11.yb = f32[36,4,8,128]{3,2,1,0:T(8,128)S(1)} collective-permute-done((f32[36,4,8,128]{3,2,1,0:T(8,128)S(1)}, f32[36,4,8,128]{3,2,1,0:T(8,128)S(1)}, u32[]{:S(2)}, u32[]{:S(2)}) %collective-permute-start.11) | collective-permute-done | bytes 589856 | tf_op jit(solution)/shard_map/ppermute | solution.py:510
  80.3 0.0 collective-permute-done.12.ya
  80.3 0.0 collective-permute-done.13.ca
  80.3 4.4 %shard_map.71 = (f32[40,24,8,128]{3,2,1,0:T(8,128)S(1)}, f32[40,20,8,128]{3,2,1,0:T(8,128)S(1)}, f32[32,20,8,128]{3,2,1,0:T(8,128)S(1)}, f32[32,16,8,128]{3,2,1,...) custom-call(bf16[256,256]{1,0:T(8,128)(2,1)S(1)} %copy-done.1, ...), custom_call_target="tpu_custom_call", output_to_operand_aliasing={{0}: (13, {}), {1}: (14, {}), {2}: (15, {}), {3}: (16, {}),... | custom-call | tf_op jit(solution)/shard_map/pallas_call | solution.py:488
  84.7 0.7 collective-permute-start.16
  85.4 0.7 collective-permute-start.17
  86.1 0.7 collective-permute-start.18
  86.8 9.8 %collective-permute-start.19 = (f32[8,4,8,128]{3,2,1,0:T(8,128)S(1)}, f32[8,4,8,128]{3,2,1,0:T(8,128)S(1)}, u32[]{:S(2)}, u32[]{:S(2)}) collective-permute-start(f32[8,4,8,128]{3,2,1,0:T(8,128)S(1)} %get-tuple-element.120), channel_id=1, source_target_pairs={{1,18},{2,17},{3,20},{4,19},{5,22},{6,21},{7,24},{8,23},{9,26},{10... | collective-permute-start | bytes 393224 | tf_op jit(solution)/shard_map/ppermute | solution.py:516
  96.6 4.0 %collective-permute-start.14 = (f32[32,4,8,128]{3,2,1,0:T(8,128)S(1)}, f32[32,4,8,128]{3,2,1,0:T(8,128)S(1)}, u32[]{:S(2)}, u32[]{:S(2)}) collective-permute-start(f32[32,4,8,128]{3,2,1,0:T(8,128)S(1)} %get-tuple-element.115), channel_id=1, source_target_pairs={{1,2},{2,1},{3,4},{4,3},{5,6},{6,5},{7,8},{8,7},{9,10},{10,9},{11,... | collective-permute-start | bytes 1572872 | tf_op jit(solution)/shard_map/ppermute | solution.py:510
  100.6 0.0 collective-permute-done.18.db
  100.6 0.1 collective-permute-start.15
  100.7 0.0 collective-permute-done.19.da
  100.7 0.0 collective-permute-done.16.xb
  100.8 0.0 collective-permute-done.17.xa
  100.8 0.6 collective-permute-start.20
  101.4 6.0 %shard_map.72 = (f32[40,24,8,128]{3,2,1,0:T(8,128)S(1)}, f32[40,20,8,128]{3,2,1,0:T(8,128)S(1)}, f32[32,20,8,128]{3,2,1,0:T(8,128)S(1)}, f32[32,16,8,128]{3,2,1,0:T(8,128)S(1)}, f32[2,8,128]{2,1,0:T(8,128)S(1)}) custom-call(bf16[256,256]{1,0:T(8,128)(2,1)S(1)} %copy-done.1, f32[8,128]{1,0:T(8,128)S(1)} %get-tuple-element.70.wb, ...), custom_call_target="tpu_custom_call" | custom-call | tf_op jit(solution)/shard_map/pallas_call | solution.py:488
  107.4 4.3 %collective-permute-done.14.yb = f32[32,4,8,128]{3,2,1,0:T(8,128)S(1)} collective-permute-done((f32[32,4,8,128]{3,2,1,0:T(8,128)S(1)}, f32[32,4,8,128]{3,2,1,0:T(8,128)S(1)}, u32[]{:S(2)}, u32[]{:S(2)}) %collective-permute-start.14) | collective-permute-done | bytes 524320 | tf_op jit(solution)/shard_map/ppermute | solution.py:510
  111.7 0.0 collective-permute-done.15.ya
  111.7 0.0 collective-permute-done.20.ca
  111.7 5.1 %shard_map.73 = (f32[40,24,8,128]{3,2,1,0:T(8,128)S(1)}, f32[40,20,8,128]{3,2,1,0:T(8,128)S(1)}, f32[32,20,8,128]{3,2,1,0:T(8,128)S(1)}, f32[32,16,8,128]{3,2,1,...) custom-call(bf16[256,256]{1,0:T(8,128)(2,1)S(1)} %copy-done.1, ...), custom_call_target="tpu_custom_call", output_to_operand_aliasing={{0}: (14, {}), {1}: (15, {}), {2}: (16, {}), {3}: (17, {}),... | custom-call | tf_op jit(solution)/shard_map/pallas_call | solution.py:488
  116.9 34.2 %all_to_all.5.heard = f32[128,8,128]{2,1,0:T(8,128)S(1)} all-to-all(f32[128,8,128]{2,1,0:T(8,128)S(1)} %broadcast_in_dim.2), channel_id=1, replica_groups=mesh['gx'=8,'gy'=16] {'gx','gy'}, dimensions={0} | all-to-all | bytes 1048576 | tf_op jit(solution)/shard_map/all_to_all | solution.py:532
  151.1 5.7 %shard_map.74 = (f32[256,2048]{1,0:T(8,128)}, f32[32,2048]{1,0:T(8,128)}, f32[8,128]{1,0:T(8,128)S(1)}) custom-call(f32[8,128]{1,0:T(8,128)S(1)} %get-tuple-element.70.wb, f32[128,8,128]{2,1,0:T(8,128)S(1)} %all_to_all.5.heard, f32[16,32,128]{2,1,0:T(8,128)} %get-tuple-element.132.q_far, f32[32,16,8,128]{3,2,1,0:T(8,128)} %get-tuple-element.133.gp_far, ...), custom_call_target="tpu_custom_call" | custom-call | tf_op jit(solution)/shard_map/pallas_call | solution.py:488
  156.8 0.6 slice_reduce_fusion
  (9 shorter events, 0.2 us)
Async XLA Ops:
  0.6 28.2 %copy-start.1 = (bf16[256,256]{1,0:T(8,128)(2,1)S(1)}, bf16[256,256]{1,0:T(8,128)(2,1)}, u32[]{:S(2)}) copy-start(bf16[256,256]{1,0:T(8,128)(2,1)} %constant.17.clone.w_ref) | copy-start | bytes 393220
  0.6 0.7 copy-start.3
  7.4 19.4 %collective-permute-start.2 = (f32[8,16,8,128]{3,2,1,0:T(8,128)}, f32[8,16,8,128]{3,2,1,0:T(8,128)S(1)}, u32[]{:S(2)}, u32[]{:S(2)}) collective-permute-start(f32[8,16,8,128]{3,2,1,0:T(8,128)} %get-tuple-element.75), channel_id=1, source_target_pairs={{16,32},{32,16},{48,64},{64,48},{80,96},{96,80},{17,33},{33,17},{4... | collective-permute-start | bytes 1572872 | tf_op jit(solution)/shard_map/ppermute | solution.py:510
  8.1 19.1 %collective-permute-start.3 = (f32[8,16,8,128]{3,2,1,0:T(8,128)}, f32[8,16,8,128]{3,2,1,0:T(8,128)S(1)}, u32[]{:S(2)}, u32[]{:S(2)}) collective-permute-start(f32[8,16,8,128]{3,2,1,0:T(8,128)} %get-tuple-element.76), channel_id=1, source_target_pairs={{0,16},{16,0},{32,48},{48,32},{64,80},{80,64},{96,112},{112,96},{1... | collective-permute-start | bytes 1572872 | tf_op jit(solution)/shard_map/ppermute | solution.py:510
  12.8 13.9 %collective-permute-start.4 = (f32[8,4,8,128]{3,2,1,0:T(8,128)S(1)}, f32[8,4,8,128]{3,2,1,0:T(8,128)S(1)}, u32[]{:S(2)}, u32[]{:S(2)}) collective-permute-start(f32[8,4,8,128]{3,2,1,0:T(8,128)S(1)} %get-tuple-element.77), channel_id=1, source_target_pairs={{17,34},{18,33},{19,36},{20,35},{21,38},{22,37},{23,40},{24,39},{2... | collective-permute-start | bytes 393224 | tf_op jit(solution)/shard_map/ppermute | solution.py:516
  13.4 13.3 %collective-permute-start.5 = (f32[8,4,8,128]{3,2,1,0:T(8,128)}, f32[8,4,8,128]{3,2,1,0:T(8,128)S(1)}, u32[]{:S(2)}, u32[]{:S(2)}) collective-permute-start(f32[8,4,8,128]{3,2,1,0:T(8,128)} %get-tuple-element.78), channel_id=1, source_target_pairs={{1,18},{2,17},{3,20},{4,19},{5,22},{6,21},{7,24},{8,23},{9,26},{10... | collective-permute-start | bytes 393224 | tf_op jit(solution)/shard_map/ppermute | solution.py:516
  21.2 16.5 %collective-permute-start = (f32[32,4,8,128]{3,2,1,0:T(8,128)}, f32[32,4,8,128]{3,2,1,0:T(8,128)}, u32[]{:S(2)}, u32[]{:S(2)}) collective-permute-start(f32[32,4,8,128]{3,2,1,0:T(8,128)} %get-tuple-element.73), channel_id=1, source_target_pairs={{1,2},{2,1},{3,4},{4,3},{5,6},{6,5},{7,8},{8,7},{9,10},{10,9},{11,... | collective-permute-start | bytes 1572872 | tf_op jit(solution)/shard_map/ppermute | solution.py:510
  26.7 11.0 %collective-permute-start.1 = (f32[32,4,8,128]{3,2,1,0:T(8,128)}, f32[32,4,8,128]{3,2,1,0:T(8,128)}, u32[]{:S(2)}, u32[]{:S(2)}) collective-permute-start(f32[32,4,8,128]{3,2,1,0:T(8,128)} %get-tuple-element.74), channel_id=1, source_target_pairs={{0,1},{1,0},{2,3},{3,2},{4,5},{5,4},{6,7},{7,6},{8,9},{9,8},{10,11... | collective-permute-start | bytes 1572872 | tf_op jit(solution)/shard_map/ppermute | solution.py:510
  27.2 10.4 %collective-permute-start.6 = (f32[16,4,8,128]{3,2,1,0:T(8,128)S(1)}, f32[16,4,8,128]{3,2,1,0:T(8,128)S(1)}, u32[]{:S(2)}, u32[]{:S(2)}) collective-permute-start(f32[16,4,8,128]{3,2,1,0:T(8,128)S(1)} %pad_maximum_fusion.1), channel_id=1, source_target_pairs={{0,1},{1,0},{2,3},{3,2},{4,5},{5,4},{6,7},{7,6},{8,9},{9,8},{10,11... | collective-permute-start | bytes 786440 | tf_op jit(solution)/shard_map/ppermute | solution.py:510
  28.8 1.6 %copy-start = (f32[32,16,8,128]{3,2,1,0:T(8,128)S(1)}, f32[32,16,8,128]{3,2,1,0:T(8,128)}, u32[]{:S(2)}) copy-start(f32[32,16,8,128]{3,2,1,0:T(8,128)} %get-tuple-element.71.dens.dens_far) | copy-start | bytes 6291460
  30.4 7.2 %copy-start.2 = (f32[32,2048]{1,0:T(8,128)S(1)}, f32[32,2048]{1,0:T(8,128)}, u32[]{:S(2)}) copy-start(f32[32,2048]{1,0:T(8,128)} %cot.5) | copy-start | bytes 786436
  43.2 23.5 %collective-permute-start.7 = (f32[9,16,8,128]{3,2,1,0:T(8,128)S(1)}, f32[9,16,8,128]{3,2,1,0:T(8,128)S(1)}, u32[]{:S(2)}, u32[]{:S(2)}) collective-permute-start(f32[9,16,8,128]{3,2,1,0:T(8,128)S(1)} %get-tuple-element.93), channel_id=1, source_target_pairs={{16,32},{32,16},{48,64},{64,48},{80,96},{96,80},{17,33},{33,17},{4... | collective-permute-start | bytes 1769480 | tf_op jit(solution)/shard_map/ppermute | solution.py:510
  43.9 22.8 %collective-permute-start.8 = (f32[9,16,8,128]{3,2,1,0:T(8,128)S(1)}, f32[9,16,8,128]{3,2,1,0:T(8,128)S(1)}, u32[]{:S(2)}, u32[]{:S(2)}) collective-permute-start(f32[9,16,8,128]{3,2,1,0:T(8,128)S(1)} %get-tuple-element.94), channel_id=1, source_target_pairs={{0,16},{16,0},{32,48},{48,32},{64,80},{80,64},{96,112},{112,96},{1... | collective-permute-start | bytes 1769480 | tf_op jit(solution)/shard_map/ppermute | solution.py:510
  49.7 14.5 %collective-permute-start.9 = (f32[9,4,8,128]{3,2,1,0:T(8,128)S(1)}, f32[9,4,8,128]{3,2,1,0:T(8,128)S(1)}, u32[]{:S(2)}, u32[]{:S(2)}) collective-permute-start(f32[9,4,8,128]{3,2,1,0:T(8,128)S(1)} %get-tuple-element.95), channel_id=1, source_target_pairs={{17,34},{18,33},{19,36},{20,35},{21,38},{22,37},{23,40},{24,39},{2... | collective-permute-start | bytes 442376 | tf_op jit(solution)/shard_map/ppermute | solution.py:516
  50.4 16.2 %collective-permute-start.10 = (f32[9,4,8,128]{3,2,1,0:T(8,128)S(1)}, f32[9,4,8,128]{3,2,1,0:T(8,128)S(1)}, u32[]{:S(2)}, u32[]{:S(2)}) collective-permute-start(f32[9,4,8,128]{3,2,1,0:T(8,128)S(1)} %get-tuple-element.96), channel_id=1, source_target_pairs={{1,18},{2,17},{3,20},{4,19},{5,22},{6,21},{7,24},{8,23},{9,26},{10... | collective-permute-start | bytes 442376 | tf_op jit(solution)/shard_map/ppermute | solution.py:516
  61.3 18.9 %collective-permute-start.11 = (f32[36,4,8,128]{3,2,1,0:T(8,128)S(1)}, f32[36,4,8,128]{3,2,1,0:T(8,128)S(1)}, u32[]{:S(2)}, u32[]{:S(2)}) collective-permute-start(f32[36,4,8,128]{3,2,1,0:T(8,128)S(1)} %get-tuple-element.99), channel_id=1, source_target_pairs={{1,2},{2,1},{3,4},{4,3},{5,6},{6,5},{7,8},{8,7},{9,10},{10,9},{11,... | collective-permute-start | bytes 1769480 | tf_op jit(solution)/shard_map/ppermute | solution.py:510
  64.3 16.0 %collective-permute-start.12 = (f32[36,4,8,128]{3,2,1,0:T(8,128)S(1)}, f32[36,4,8,128]{3,2,1,0:T(8,128)S(1)}, u32[]{:S(2)}, u32[]{:S(2)}) collective-permute-start(f32[36,4,8,128]{3,2,1,0:T(8,128)S(1)} %get-tuple-element.100), channel_id=1, source_target_pairs={{0,1},{1,0},{2,3},{3,2},{4,5},{5,4},{6,7},{7,6},{8,9},{9,8},{10,11... | collective-permute-start | bytes 1769480 | tf_op jit(solution)/shard_map/ppermute | solution.py:510
  66.7 13.6 %collective-permute-start.13 = (f32[18,4,8,128]{3,2,1,0:T(8,128)S(1)}, f32[18,4,8,128]{3,2,1,0:T(8,128)S(1)}, u32[]{:S(2)}, u32[]{:S(2)}) collective-permute-start(f32[18,4,8,128]{3,2,1,0:T(8,128)S(1)} %pad_maximum_fusion), channel_id=1, source_target_pairs={{0,1},{1,0},{2,3},{3,2},{4,5},{5,4},{6,7},{7,6},{8,9},{9,8},{10,11... | collective-permute-start | bytes 884744 | tf_op jit(solution)/shard_map/ppermute | solution.py:510
  84.7 16.1 %collective-permute-start.16 = (f32[8,16,8,128]{3,2,1,0:T(8,128)S(1)}, f32[8,16,8,128]{3,2,1,0:T(8,128)S(1)}, u32[]{:S(2)}, u32[]{:S(2)}) collective-permute-start(f32[8,16,8,128]{3,2,1,0:T(8,128)S(1)} %get-tuple-element.117), channel_id=1, source_target_pairs={{16,32},{32,16},{48,64},{64,48},{80,96},{96,80},{17,33},{33,17},{4... | collective-permute-start | bytes 1572872 | tf_op jit(solution)/shard_map/ppermute | solution.py:510
  85.4 15.4 %collective-permute-start.17 = (f32[8,16,8,128]{3,2,1,0:T(8,128)S(1)}, f32[8,16,8,128]{3,2,1,0:T(8,128)S(1)}, u32[]{:S(2)}, u32[]{:S(2)}) collective-permute-start(f32[8,16,8,128]{3,2,1,0:T(8,128)S(1)} %get-tuple-element.118), channel_id=1, source_target_pairs={{0,16},{16,0},{32,48},{48,32},{64,80},{80,64},{96,112},{112,96},{1... | collective-permute-start | bytes 1572872 | tf_op jit(solution)/shard_map/ppermute | solution.py:510
  86.1 14.5 %collective-permute-start.18 = (f32[8,4,8,128]{3,2,1,0:T(8,128)S(1)}, f32[8,4,8,128]{3,2,1,0:T(8,128)S(1)}, u32[]{:S(2)}, u32[]{:S(2)}) collective-permute-start(f32[8,4,8,128]{3,2,1,0:T(8,128)S(1)} %get-tuple-element.119), channel_id=1, source_target_pairs={{17,34},{18,33},{19,36},{20,35},{21,38},{22,37},{23,40},{24,39},{2... | collective-permute-start | bytes 393224 | tf_op jit(solution)/shard_map/ppermute | solution.py:516
  86.8 13.9 %collective-permute-start.19 = (f32[8,4,8,128]{3,2,1,0:T(8,128)S(1)}, f32[8,4,8,128]{3,2,1,0:T(8,128)S(1)}, u32[]{:S(2)}, u32[]{:S(2)}) collective-permute-start(f32[8,4,8,128]{3,2,1,0:T(8,128)S(1)} %get-tuple-element.120), channel_id=1, source_target_pairs={{1,18},{2,17},{3,20},{4,19},{5,22},{6,21},{7,24},{8,23},{9,26},{10... | collective-permute-start | bytes 393224 | tf_op jit(solution)/shard_map/ppermute | solution.py:516
  96.6 15.1 %collective-permute-start.14 = (f32[32,4,8,128]{3,2,1,0:T(8,128)S(1)}, f32[32,4,8,128]{3,2,1,0:T(8,128)S(1)}, u32[]{:S(2)}, u32[]{:S(2)}) collective-permute-start(f32[32,4,8,128]{3,2,1,0:T(8,128)S(1)} %get-tuple-element.115), channel_id=1, source_target_pairs={{1,2},{2,1},{3,4},{4,3},{5,6},{6,5},{7,8},{8,7},{9,10},{10,9},{11,... | collective-permute-start | bytes 1572872 | tf_op jit(solution)/shard_map/ppermute | solution.py:510
  100.6 11.0 %collective-permute-start.15 = (f32[32,4,8,128]{3,2,1,0:T(8,128)S(1)}, f32[32,4,8,128]{3,2,1,0:T(8,128)S(1)}, u32[]{:S(2)}, u32[]{:S(2)}) collective-permute-start(f32[32,4,8,128]{3,2,1,0:T(8,128)S(1)} %get-tuple-element.116), channel_id=1, source_target_pairs={{0,1},{1,0},{2,3},{3,2},{4,5},{5,4},{6,7},{7,6},{8,9},{9,8},{10,11... | collective-permute-start | bytes 1572872 | tf_op jit(solution)/shard_map/ppermute | solution.py:510
  100.8 10.8 %collective-permute-start.20 = (f32[16,4,8,128]{3,2,1,0:T(8,128)S(1)}, f32[16,4,8,128]{3,2,1,0:T(8,128)S(1)}, u32[]{:S(2)}, u32[]{:S(2)}) collective-permute-start(f32[16,4,8,128]{3,2,1,0:T(8,128)S(1)} %pad_maximum_fusion.2), channel_id=1, source_target_pairs={{0,1},{1,0},{2,3},{3,2},{4,5},{5,4},{6,7},{7,6},{8,9},{9,8},{10,11... | collective-permute-start | bytes 786440 | tf_op jit(solution)/shard_map/ppermute | solution.py:510

commit v7 on v6

--- a/solution.py
+++ b/solution.py
@@ -520,7 +520,6 @@
     rxb, ryb = swap(xb, "gx", 1), swap(yb, "gy", 1)
     rdb, rda = swap_diagonal(db, 1, 1), swap_diagonal(da, 0, 1)
     rxa, rya = swap(xa, "gx", 0), swap(ya, "gy", 0)
-    rxb, rxa, rdb, rda = lax.optimization_barrier((rxb, rxa, rdb, rda))
     first = (1 - lax.rem(lax.axis_index("gy"), 2)) * (tiles - HT)
     corner = jnp.concatenate([lax.dynamic_slice_in_dim(r, first, HT, axis=1) for r in (rxb, rxa)], axis=0)
     rca = swap(corner, "gy", 0)

time: 158 us -> 158 us (level)
  starting transfers between devices: 58.7 us -> 66.5 us
  blocking collectives: 34.2 us -> 30 us
  waiting for transfers between devices: 14.9 us -> 11.7 us
    ppermute x15, starting transfers between devices: 28.3 us -> 35.6 us  [swap(): return lax.ppermute(value, axis, list(partners(axis, parity).items()))]
    all_to_all x1, blocking collectives: 34.2 us -> 30 us  [over_all(): lax.all_to_all(jnp.broadcast_to(told[None], (devices, K, L)), ('gx', 'gy'...]
    ppermute x6, waiting for transfers between devices: 2.29 us -> 0.02 us  [swap_diagonal(): return lax.ppermute(value, ('gx', 'gy'), pairs)]
  transfers between devices with their start and end apart: 21 -> 21, of which waited for: 5 -> 3; matrix products, arithmetic and copies ran while one was open for 0% -> 0% of each run, Pallas kernels for 12% -> 12%
where the time goes in v7:
time: 158 us
  starting transfers between devices  66.5 us (42%)
  Pallas kernels  45.5 us (29%)
  blocking collectives  30 us (19%)
  waiting for transfers between devices  11.7 us (7%)
  local copies, waits for them, and re-layouts  3.02 us (2%)
    pallas_call x8, Pallas kernels, call(): pl.pallas_call(kernel, out_shape=outs, in_specs=[pl.BlockSpec(memory_spac...  45.5 us
    ppermute x15, starting transfers between devices, swap(): return lax.ppermute(value, axis, list(partners(axis, parity).items()))  35.6 us
    ppermute x6, starting transfers between devices, swap_diagonal(): return lax.ppermute(value, ('gx', 'gy'), pairs)  30.9 us
    all_to_all x1, blocking collectives, over_all(): lax.all_to_all(jnp.broadcast_to(told[None], (devices, K, L)), ('gx', 'gy'...  30 us
    ppermute x15, waiting for transfers between devices, swap(): return lax.ppermute(value, axis, list(partners(axis, parity).items()))  11.7 us
  transfers between devices with their start and end apart: 21, of which 3 were waited for; matrix products, arithmetic and copies ran while one was open for 0% of the time, Pallas kernels for 12%

profile of v7, /device:TPU:1, one launch (start us, length us, event | category | flops | bytes accessed | tf_op | source)
XLA Modules:
  0.0 157.8 jit_solution(6013312441534759330)
XLA Ops:
  0.6 0.0 copy-start.1
  0.6 0.0 copy-start.3
  0.7 0.7 copy-done.3
  1.3 6.0 %shard_map.67 = (f32[32,16,8,128]{3,2,1,0:T(8,128)}, f32[32,16,8,128]{3,2,1,0:T(8,128)S(1)}, f32[8,128]{1,0:T(8,128)S(1)}, f32[8,128]{1,0:T(8,128)S(1)}, f32[8,1...) custom-call(f32[8]{0:T(128)S(1)} %copy-done.3, ...), custom_call_target="tpu_custom_call" | custom-call | tf_op jit(solution)/shard_map/pallas_call | solution.py:488
  7.4 0.7 collective-permute-start.2
  8.1 4.7 %collective-permute-start.3 = (f32[8,16,8,128]{3,2,1,0:T(8,128)}, f32[8,16,8,128]{3,2,1,0:T(8,128)S(1)}, u32[]{:S(2)}, u32[]{:S(2)}) collective-permute-start(f32[8,16,8,128]{3,2,1,0:T(8,128)} %get-tuple-element.64), channel_id=1, source_target_pairs={{0,16},{16,0},{32,48},{48,32},{64,80},{80,64},{96,112},{112,96},{1... | collective-permute-start | bytes 1572872 | tf_op jit(solution)/shard_map/ppermute | solution.py:510
  12.8 5.8 %collective-permute-start = (f32[32,4,8,128]{3,2,1,0:T(8,128)}, f32[32,4,8,128]{3,2,1,0:T(8,128)}, u32[]{:S(2)}, u32[]{:S(2)}) collective-permute-start(f32[32,4,8,128]{3,2,1,0:T(8,128)} %get-tuple-element.61), channel_id=1, source_target_pairs={{1,2},{2,1},{3,4},{4,3},{5,6},{6,5},{7,8},{8,7},{9,10},{10,9},{11,... | collective-permute-start | bytes 1572872 | tf_op jit(solution)/shard_map/ppermute | solution.py:510
  18.5 0.1 collective-permute-start.1
  18.6 0.0 collective-permute-done.2.xb
  18.7 5.6 %collective-permute-done.3.xa = f32[8,16,8,128]{3,2,1,0:T(8,128)S(1)} collective-permute-done((f32[8,16,8,128]{3,2,1,0:T(8,128)}, f32[8,16,8,128]{3,2,1,0:T(8,128)S(1)}, u32[]{:S(2)}, u32[]{:S(2)}) %collective-permute-start.3) | collective-permute-done | bytes 524320 | tf_op jit(solution)/shard_map/ppermute | solution.py:510
  24.4 1.6 %collective-permute-start.4 = (f32[16,4,8,128]{3,2,1,0:T(8,128)S(1)}, f32[16,4,8,128]{3,2,1,0:T(8,128)S(1)}, u32[]{:S(2)}, u32[]{:S(2)}) collective-permute-start(f32[16,4,8,128]{3,2,1,0:T(8,128)S(1)} %pad_maximum_fusion.1), channel_id=1, source_target_pairs={{0,1},{1,0},{2,3},{3,2},{4,5},{5,4},{6,7},{7,6},{8,9},{9,8},{10,11... | collective-permute-start | bytes 786440 | tf_op jit(solution)/shard_map/ppermute | solution.py:510
  26.0 5.7 %collective-permute-start.5 = (f32[8,4,8,128]{3,2,1,0:T(8,128)S(1)}, f32[8,4,8,128]{3,2,1,0:T(8,128)S(1)}, u32[]{:S(2)}, u32[]{:S(2)}) collective-permute-start(f32[8,4,8,128]{3,2,1,0:T(8,128)S(1)} %get-tuple-element.65), channel_id=1, source_target_pairs={{1,18},{2,17},{3,20},{4,19},{5,22},{6,21},{7,24},{8,23},{9,26},{10... | collective-permute-start | bytes 393224 | tf_op jit(solution)/shard_map/ppermute | solution.py:516
  31.7 0.7 collective-permute-start.6
  32.4 0.0 copy-done.1
  32.4 0.0 copy-start
  32.4 1.6 %copy-done = f32[32,16,8,128]{3,2,1,0:T(8,128)S(1)} copy-done((f32[32,16,8,128]{3,2,1,0:T(8,128)S(1)}, f32[32,16,8,128]{3,2,1,0:T(8,128)}, u32[]{:S(2)}) %copy-start) | copy-done | bytes 2097176
  34.0 0.0 copy-start.2
  34.0 6.0 %shard_map.68 = (f32[40,24,8,128]{3,2,1,0:T(8,128)S(1)}, f32[40,20,8,128]{3,2,1,0:T(8,128)S(1)}, f32[40,20,8,128]{3,2,1,0:T(8,128)S(1)}, f32[32,20,8,128]{3,2,1,...) custom-call(bf16[256,256]{1,0:T(8,128)(2,1)S(1)} %copy-done.1, ...), custom_call_target="tpu_custom_call" | custom-call | tf_op jit(solution)/shard_map/pallas_call | solution.py:488
  40.0 0.0 collective-permute-done.5.da
  40.0 0.0 collective-permute-done.6.db
  40.0 0.0 collective-permute-done.yb
  40.0 0.0 collective-permute-done.1.ya
  40.0 0.0 collective-permute-done.4.ca
  40.1 0.0 copy-done.2
  40.1 5.5 %shard_map.69 = (f32[40,24,8,128]{3,2,1,0:T(8,128)S(1)}, f32[40,20,8,128]{3,2,1,0:T(8,128)S(1)}, f32[40,20,8,128]{3,2,1,0:T(8,128)S(1)}, f32[32,20,8,128]{3,2,1,...) custom-call(bf16[256,256]{1,0:T(8,128)(2,1)S(1)} %copy-done.1, ...), custom_call_target="tpu_custom_call", output_to_operand_aliasing={{0}: (10, {}), {1}: (11, {}), {2}: (12, {}), {3}: (13, {}),... | custom-call | tf_op jit(solution)/shard_map/pallas_call | solution.py:488
  45.6 0.7 collective-permute-start.7
  46.3 7.0 %collective-permute-start.8 = (f32[9,16,8,128]{3,2,1,0:T(8,128)S(1)}, f32[9,16,8,128]{3,2,1,0:T(8,128)S(1)}, u32[]{:S(2)}, u32[]{:S(2)}) collective-permute-start(f32[9,16,8,128]{3,2,1,0:T(8,128)S(1)} %get-tuple-element.78), channel_id=1, source_target_pairs={{0,16},{16,0},{32,48},{48,32},{64,80},{80,64},{96,112},{112,96},{1... | collective-permute-start | bytes 1769480 | tf_op jit(solution)/shard_map/ppermute | solution.py:510
  53.3 4.8 %collective-permute-start.9 = (f32[36,4,8,128]{3,2,1,0:T(8,128)S(1)}, f32[36,4,8,128]{3,2,1,0:T(8,128)S(1)}, u32[]{:S(2)}, u32[]{:S(2)}) collective-permute-start(f32[36,4,8,128]{3,2,1,0:T(8,128)S(1)} %get-tuple-element.79), channel_id=1, source_target_pairs={{1,2},{2,1},{3,4},{4,3},{5,6},{6,5},{7,8},{8,7},{9,10},{10,9},{11,... | collective-permute-start | bytes 1769480 | tf_op jit(solution)/shard_map/ppermute | solution.py:510
  58.2 0.1 collective-permute-start.10
  58.3 0.0 collective-permute-done.7.xb
  58.3 2.3 %collective-permute-done.8.xa = f32[9,16,8,128]{3,2,1,0:T(8,128)S(1)} collective-permute-done((f32[9,16,8,128]{3,2,1,0:T(8,128)S(1)}, f32[9,16,8,128]{3,2,1,0:T(8,128)S(1)}, u32[]{:S(2)}, u32[]{:S(2)}) %collective-permute-start.8) | collective-permute-done | bytes 589856 | tf_op jit(solution)/shard_map/ppermute | solution.py:510
  60.7 0.1 collective-permute-start.11
  60.8 13.0 %collective-permute-start.12 = (f32[9,4,8,128]{3,2,1,0:T(8,128)S(1)}, f32[9,4,8,128]{3,2,1,0:T(8,128)S(1)}, u32[]{:S(2)}, u32[]{:S(2)}) collective-permute-start(f32[9,4,8,128]{3,2,1,0:T(8,128)S(1)} %get-tuple-element.81), channel_id=1, source_target_pairs={{1,18},{2,17},{3,20},{4,19},{5,22},{6,21},{7,24},{8,23},{9,26},{10... | collective-permute-start | bytes 442376 | tf_op jit(solution)/shard_map/ppermute | solution.py:516
  73.8 0.7 collective-permute-start.13
  74.4 6.7 %shard_map.70 = (f32[40,24,8,128]{3,2,1,0:T(8,128)S(1)}, f32[40,20,8,128]{3,2,1,0:T(8,128)S(1)}, f32[32,20,8,128]{3,2,1,0:T(8,128)S(1)}, f32[32,16,8,128]{3,2,1,...) custom-call(bf16[256,256]{1,0:T(8,128)(2,1)S(1)} %copy-done.1, ...), custom_call_target="tpu_custom_call" | custom-call | tf_op jit(solution)/shard_map/pallas_call | solution.py:488
  81.1 0.0 collective-permute-done.12.da
  81.1 0.0 collective-permute-done.13.db
  81.1 0.0 collective-permute-done.9.yb
  81.2 0.0 collective-permute-done.10.ya
  81.2 0.0 collective-permute-done.11.ca
  81.2 4.4 %shard_map.71 = (f32[40,24,8,128]{3,2,1,0:T(8,128)S(1)}, f32[40,20,8,128]{3,2,1,0:T(8,128)S(1)}, f32[32,20,8,128]{3,2,1,0:T(8,128)S(1)}, f32[32,16,8,128]{3,2,1,...) custom-call(bf16[256,256]{1,0:T(8,128)(2,1)S(1)} %copy-done.1, ...), custom_call_target="tpu_custom_call", output_to_operand_aliasing={{0}: (13, {}), {1}: (14, {}), {2}: (15, {}), {3}: (16, {}),... | custom-call | tf_op jit(solution)/shard_map/pallas_call | solution.py:488
  85.6 0.7 collective-permute-start.16
  86.3 6.4 %collective-permute-start.17 = (f32[8,16,8,128]{3,2,1,0:T(8,128)S(1)}, f32[8,16,8,128]{3,2,1,0:T(8,128)S(1)}, u32[]{:S(2)}, u32[]{:S(2)}) collective-permute-start(f32[8,16,8,128]{3,2,1,0:T(8,128)S(1)} %get-tuple-element.98), channel_id=1, source_target_pairs={{0,16},{16,0},{32,48},{48,32},{64,80},{80,64},{96,112},{112,96},{1... | collective-permute-start | bytes 1572872 | tf_op jit(solution)/shard_map/ppermute | solution.py:510
  92.7 2.7 %collective-permute-start.14 = (f32[32,4,8,128]{3,2,1,0:T(8,128)S(1)}, f32[32,4,8,128]{3,2,1,0:T(8,128)S(1)}, u32[]{:S(2)}, u32[]{:S(2)}) collective-permute-start(f32[32,4,8,128]{3,2,1,0:T(8,128)S(1)} %get-tuple-element.95), channel_id=1, source_target_pairs={{1,2},{2,1},{3,4},{4,3},{5,6},{6,5},{7,8},{8,7},{9,10},{10,9},{11,... | collective-permute-start | bytes 1572872 | tf_op jit(solution)/shard_map/ppermute | solution.py:510
  95.5 0.1 collective-permute-start.15
  95.5 0.0 collective-permute-done.16.xb
  95.6 3.7 %collective-permute-done.17.xa = f32[8,16,8,128]{3,2,1,0:T(8,128)S(1)} collective-permute-done((f32[8,16,8,128]{3,2,1,0:T(8,128)S(1)}, f32[8,16,8,128]{3,2,1,0:T(8,128)S(1)}, u32[]{:S(2)}, u32[]{:S(2)}) %collective-permute-start.17) | collective-permute-done | bytes 524320 | tf_op jit(solution)/shard_map/ppermute | solution.py:510
  99.3 0.1 collective-permute-start.18
  99.4 10.2 %collective-permute-start.19 = (f32[8,4,8,128]{3,2,1,0:T(8,128)S(1)}, f32[8,4,8,128]{3,2,1,0:T(8,128)S(1)}, u32[]{:S(2)}, u32[]{:S(2)}) collective-permute-start(f32[8,4,8,128]{3,2,1,0:T(8,128)S(1)} %get-tuple-element.99), channel_id=1, source_target_pairs={{1,18},{2,17},{3,20},{4,19},{5,22},{6,21},{7,24},{8,23},{9,26},{10... | collective-permute-start | bytes 393224 | tf_op jit(solution)/shard_map/ppermute | solution.py:516
  109.6 0.7 collective-permute-start.20
  110.3 6.0 %shard_map.72 = (f32[40,24,8,128]{3,2,1,0:T(8,128)S(1)}, f32[40,20,8,128]{3,2,1,0:T(8,128)S(1)}, f32[32,20,8,128]{3,2,1,0:T(8,128)S(1)}, f32[32,16,8,128]{3,2,1,0:T(8,128)S(1)}, f32[2,8,128]{2,1,0:T(8,128)S(1)}) custom-call(bf16[256,256]{1,0:T(8,128)(2,1)S(1)} %copy-done.1, f32[8,128]{1,0:T(8,128)S(1)} %get-tuple-element.58.wb, ...), custom_call_target="tpu_custom_call" | custom-call | tf_op jit(solution)/shard_map/pallas_call | solution.py:488
  116.3 0.0 collective-permute-done.19.da
  116.3 0.0 collective-permute-done.20.db
  116.3 0.0 collective-permute-done.14.yb
  116.4 0.0 collective-permute-done.15.ya
  116.4 0.0 collective-permute-done.18.ca
  116.4 5.1 %shard_map.73 = (f32[40,24,8,128]{3,2,1,0:T(8,128)S(1)}, f32[40,20,8,128]{3,2,1,0:T(8,128)S(1)}, f32[32,20,8,128]{3,2,1,0:T(8,128)S(1)}, f32[32,16,8,128]{3,2,1,...) custom-call(bf16[256,256]{1,0:T(8,128)(2,1)S(1)} %copy-done.1, ...), custom_call_target="tpu_custom_call", output_to_operand_aliasing={{0}: (14, {}), {1}: (15, {}), {2}: (16, {}), {3}: (17, {}),... | custom-call | tf_op jit(solution)/shard_map/pallas_call | solution.py:488
  121.5 30.0 %all_to_all.5.heard = f32[128,8,128]{2,1,0:T(8,128)S(1)} all-to-all(f32[128,8,128]{2,1,0:T(8,128)S(1)} %broadcast_in_dim.2), channel_id=1, replica_groups=mesh['gx'=8,'gy'=16] {'gx','gy'}, dimensions={0} | all-to-all | bytes 1048576 | tf_op jit(solution)/shard_map/all_to_all | solution.py:531
  151.5 5.7 %shard_map.74 = (f32[256,2048]{1,0:T(8,128)}, f32[32,2048]{1,0:T(8,128)}, f32[8,128]{1,0:T(8,128)S(1)}) custom-call(f32[8,128]{1,0:T(8,128)S(1)} %get-tuple-element.58.wb, f32[128,8,128]{2,1,0:T(8,128)S(1)} %all_to_all.5.heard, f32[16,32,128]{2,1,0:T(8,128)} %get-tuple-element.108.q_far, f32[32,16,8,128]{3,2,1,0:T(8,128)} %get-tuple-element.109.gp_far, ...), custom_call_target="tpu_custom_call" | custom-call | tf_op jit(solution)/shard_map/pallas_call | solution.py:488
  157.2 0.6 slice_reduce_fusion
  (10 shorter events, 0.2 us)
Async XLA Ops:
  0.6 31.8 %copy-start.1 = (bf16[256,256]{1,0:T(8,128)(2,1)S(1)}, bf16[256,256]{1,0:T(8,128)(2,1)}, u32[]{:S(2)}) copy-start(bf16[256,256]{1,0:T(8,128)(2,1)} %constant.17.clone.w_ref) | copy-start | bytes 393220
  0.6 0.7 copy-start.3
  7.4 11.3 %collective-permute-start.2 = (f32[8,16,8,128]{3,2,1,0:T(8,128)}, f32[8,16,8,128]{3,2,1,0:T(8,128)S(1)}, u32[]{:S(2)}, u32[]{:S(2)}) collective-permute-start(f32[8,16,8,128]{3,2,1,0:T(8,128)} %get-tuple-element.63), channel_id=1, source_target_pairs={{16,32},{32,16},{48,64},{64,48},{80,96},{96,80},{17,33},{33,17},{4... | collective-permute-start | bytes 1572872 | tf_op jit(solution)/shard_map/ppermute | solution.py:510
  8.1 16.3 %collective-permute-start.3 = (f32[8,16,8,128]{3,2,1,0:T(8,128)}, f32[8,16,8,128]{3,2,1,0:T(8,128)S(1)}, u32[]{:S(2)}, u32[]{:S(2)}) collective-permute-start(f32[8,16,8,128]{3,2,1,0:T(8,128)} %get-tuple-element.64), channel_id=1, source_target_pairs={{0,16},{16,0},{32,48},{48,32},{64,80},{80,64},{96,112},{112,96},{1... | collective-permute-start | bytes 1572872 | tf_op jit(solution)/shard_map/ppermute | solution.py:510
  12.8 27.3 %collective-permute-start = (f32[32,4,8,128]{3,2,1,0:T(8,128)}, f32[32,4,8,128]{3,2,1,0:T(8,128)}, u32[]{:S(2)}, u32[]{:S(2)}) collective-permute-start(f32[32,4,8,128]{3,2,1,0:T(8,128)} %get-tuple-element.61), channel_id=1, source_target_pairs={{1,2},{2,1},{3,4},{4,3},{5,6},{6,5},{7,8},{8,7},{9,10},{10,9},{11,... | collective-permute-start | bytes 1572872 | tf_op jit(solution)/shard_map/ppermute | solution.py:510
  18.5 21.5 %collective-permute-start.1 = (f32[32,4,8,128]{3,2,1,0:T(8,128)}, f32[32,4,8,128]{3,2,1,0:T(8,128)}, u32[]{:S(2)}, u32[]{:S(2)}) collective-permute-start(f32[32,4,8,128]{3,2,1,0:T(8,128)} %get-tuple-element.62), channel_id=1, source_target_pairs={{0,1},{1,0},{2,3},{3,2},{4,5},{5,4},{6,7},{7,6},{8,9},{9,8},{10,11... | collective-permute-start | bytes 1572872 | tf_op jit(solution)/shard_map/ppermute | solution.py:510
  24.4 15.7 %collective-permute-start.4 = (f32[16,4,8,128]{3,2,1,0:T(8,128)S(1)}, f32[16,4,8,128]{3,2,1,0:T(8,128)S(1)}, u32[]{:S(2)}, u32[]{:S(2)}) collective-permute-start(f32[16,4,8,128]{3,2,1,0:T(8,128)S(1)} %pad_maximum_fusion.1), channel_id=1, source_target_pairs={{0,1},{1,0},{2,3},{3,2},{4,5},{5,4},{6,7},{7,6},{8,9},{9,8},{10,11... | collective-permute-start | bytes 786440 | tf_op jit(solution)/shard_map/ppermute | solution.py:510
  26.0 14.0 %collective-permute-start.5 = (f32[8,4,8,128]{3,2,1,0:T(8,128)S(1)}, f32[8,4,8,128]{3,2,1,0:T(8,128)S(1)}, u32[]{:S(2)}, u32[]{:S(2)}) collective-permute-start(f32[8,4,8,128]{3,2,1,0:T(8,128)S(1)} %get-tuple-element.65), channel_id=1, source_target_pairs={{1,18},{2,17},{3,20},{4,19},{5,22},{6,21},{7,24},{8,23},{9,26},{10... | collective-permute-start | bytes 393224 | tf_op jit(solution)/shard_map/ppermute | solution.py:516
  31.7 8.3 %collective-permute-start.6 = (f32[8,4,8,128]{3,2,1,0:T(8,128)S(1)}, f32[8,4,8,128]{3,2,1,0:T(8,128)S(1)}, u32[]{:S(2)}, u32[]{:S(2)}) collective-permute-start(f32[8,4,8,128]{3,2,1,0:T(8,128)S(1)} %get-tuple-element.66), channel_id=1, source_target_pairs={{17,34},{18,33},{19,36},{20,35},{21,38},{22,37},{23,40},{24,39},{2... | collective-permute-start | bytes 393224 | tf_op jit(solution)/shard_map/ppermute | solution.py:516
  32.4 1.6 %copy-start = (f32[32,16,8,128]{3,2,1,0:T(8,128)S(1)}, f32[32,16,8,128]{3,2,1,0:T(8,128)}, u32[]{:S(2)}) copy-start(f32[32,16,8,128]{3,2,1,0:T(8,128)} %get-tuple-element.59.dens.dens_far) | copy-start | bytes 6291460
  34.0 6.1 %copy-start.2 = (f32[32,2048]{1,0:T(8,128)S(1)}, f32[32,2048]{1,0:T(8,128)}, u32[]{:S(2)}) copy-start(f32[32,2048]{1,0:T(8,128)} %cot.5) | copy-start | bytes 786436
  45.6 12.6 %collective-permute-start.7 = (f32[9,16,8,128]{3,2,1,0:T(8,128)S(1)}, f32[9,16,8,128]{3,2,1,0:T(8,128)S(1)}, u32[]{:S(2)}, u32[]{:S(2)}) collective-permute-start(f32[9,16,8,128]{3,2,1,0:T(8,128)S(1)} %get-tuple-element.77), channel_id=1, source_target_pairs={{16,32},{32,16},{48,64},{64,48},{80,96},{96,80},{17,33},{33,17},{4... | collective-permute-start | bytes 1769480 | tf_op jit(solution)/shard_map/ppermute | solution.py:510
  46.3 14.3 %collective-permute-start.8 = (f32[9,16,8,128]{3,2,1,0:T(8,128)S(1)}, f32[9,16,8,128]{3,2,1,0:T(8,128)S(1)}, u32[]{:S(2)}, u32[]{:S(2)}) collective-permute-start(f32[9,16,8,128]{3,2,1,0:T(8,128)S(1)} %get-tuple-element.78), channel_id=1, source_target_pairs={{0,16},{16,0},{32,48},{48,32},{64,80},{80,64},{96,112},{112,96},{1... | collective-permute-start | bytes 1769480 | tf_op jit(solution)/shard_map/ppermute | solution.py:510
  53.3 27.8 %collective-permute-start.9 = (f32[36,4,8,128]{3,2,1,0:T(8,128)S(1)}, f32[36,4,8,128]{3,2,1,0:T(8,128)S(1)}, u32[]{:S(2)}, u32[]{:S(2)}) collective-permute-start(f32[36,4,8,128]{3,2,1,0:T(8,128)S(1)} %get-tuple-element.79), channel_id=1, source_target_pairs={{1,2},{2,1},{3,4},{4,3},{5,6},{6,5},{7,8},{8,7},{9,10},{10,9},{11,... | collective-permute-start | bytes 1769480 | tf_op jit(solution)/shard_map/ppermute | solution.py:510
  58.2 23.0 %collective-permute-start.10 = (f32[36,4,8,128]{3,2,1,0:T(8,128)S(1)}, f32[36,4,8,128]{3,2,1,0:T(8,128)S(1)}, u32[]{:S(2)}, u32[]{:S(2)}) collective-permute-start(f32[36,4,8,128]{3,2,1,0:T(8,128)S(1)} %get-tuple-element.80), channel_id=1, source_target_pairs={{0,1},{1,0},{2,3},{3,2},{4,5},{5,4},{6,7},{7,6},{8,9},{9,8},{10,11... | collective-permute-start | bytes 1769480 | tf_op jit(solution)/shard_map/ppermute | solution.py:510
  60.7 20.5 %collective-permute-start.11 = (f32[18,4,8,128]{3,2,1,0:T(8,128)S(1)}, f32[18,4,8,128]{3,2,1,0:T(8,128)S(1)}, u32[]{:S(2)}, u32[]{:S(2)}) collective-permute-start(f32[18,4,8,128]{3,2,1,0:T(8,128)S(1)} %pad_maximum_fusion), channel_id=1, source_target_pairs={{0,1},{1,0},{2,3},{3,2},{4,5},{5,4},{6,7},{7,6},{8,9},{9,8},{10,11... | collective-permute-start | bytes 884744 | tf_op jit(solution)/shard_map/ppermute | solution.py:510
  60.8 20.4 %collective-permute-start.12 = (f32[9,4,8,128]{3,2,1,0:T(8,128)S(1)}, f32[9,4,8,128]{3,2,1,0:T(8,128)S(1)}, u32[]{:S(2)}, u32[]{:S(2)}) collective-permute-start(f32[9,4,8,128]{3,2,1,0:T(8,128)S(1)} %get-tuple-element.81), channel_id=1, source_target_pairs={{1,18},{2,17},{3,20},{4,19},{5,22},{6,21},{7,24},{8,23},{9,26},{10... | collective-permute-start | bytes 442376 | tf_op jit(solution)/shard_map/ppermute | solution.py:516
  73.8 7.4 %collective-permute-start.13 = (f32[9,4,8,128]{3,2,1,0:T(8,128)S(1)}, f32[9,4,8,128]{3,2,1,0:T(8,128)S(1)}, u32[]{:S(2)}, u32[]{:S(2)}) collective-permute-start(f32[9,4,8,128]{3,2,1,0:T(8,128)S(1)} %get-tuple-element.82), channel_id=1, source_target_pairs={{17,34},{18,33},{19,36},{20,35},{21,38},{22,37},{23,40},{24,39},{2... | collective-permute-start | bytes 442376 | tf_op jit(solution)/shard_map/ppermute | solution.py:516
  85.6 9.9 %collective-permute-start.16 = (f32[8,16,8,128]{3,2,1,0:T(8,128)S(1)}, f32[8,16,8,128]{3,2,1,0:T(8,128)S(1)}, u32[]{:S(2)}, u32[]{:S(2)}) collective-permute-start(f32[8,16,8,128]{3,2,1,0:T(8,128)S(1)} %get-tuple-element.97), channel_id=1, source_target_pairs={{16,32},{32,16},{48,64},{64,48},{80,96},{96,80},{17,33},{33,17},{4... | collective-permute-start | bytes 1572872 | tf_op jit(solution)/shard_map/ppermute | solution.py:510
  86.3 13.0 %collective-permute-start.17 = (f32[8,16,8,128]{3,2,1,0:T(8,128)S(1)}, f32[8,16,8,128]{3,2,1,0:T(8,128)S(1)}, u32[]{:S(2)}, u32[]{:S(2)}) collective-permute-start(f32[8,16,8,128]{3,2,1,0:T(8,128)S(1)} %get-tuple-element.98), channel_id=1, source_target_pairs={{0,16},{16,0},{32,48},{48,32},{64,80},{80,64},{96,112},{112,96},{1... | collective-permute-start | bytes 1572872 | tf_op jit(solution)/shard_map/ppermute | solution.py:510
  92.7 23.6 %collective-permute-start.14 = (f32[32,4,8,128]{3,2,1,0:T(8,128)S(1)}, f32[32,4,8,128]{3,2,1,0:T(8,128)S(1)}, u32[]{:S(2)}, u32[]{:S(2)}) collective-permute-start(f32[32,4,8,128]{3,2,1,0:T(8,128)S(1)} %get-tuple-element.95), channel_id=1, source_target_pairs={{1,2},{2,1},{3,4},{4,3},{5,6},{6,5},{7,8},{8,7},{9,10},{10,9},{11,... | collective-permute-start | bytes 1572872 | tf_op jit(solution)/shard_map/ppermute | solution.py:510
  95.5 20.9 %collective-permute-start.15 = (f32[32,4,8,128]{3,2,1,0:T(8,128)S(1)}, f32[32,4,8,128]{3,2,1,0:T(8,128)S(1)}, u32[]{:S(2)}, u32[]{:S(2)}) collective-permute-start(f32[32,4,8,128]{3,2,1,0:T(8,128)S(1)} %get-tuple-element.96), channel_id=1, source_target_pairs={{0,1},{1,0},{2,3},{3,2},{4,5},{5,4},{6,7},{7,6},{8,9},{9,8},{10,11... | collective-permute-start | bytes 1572872 | tf_op jit(solution)/shard_map/ppermute | solution.py:510
  99.3 17.0 %collective-permute-start.18 = (f32[16,4,8,128]{3,2,1,0:T(8,128)S(1)}, f32[16,4,8,128]{3,2,1,0:T(8,128)S(1)}, u32[]{:S(2)}, u32[]{:S(2)}) collective-permute-start(f32[16,4,8,128]{3,2,1,0:T(8,128)S(1)} %pad_maximum_fusion.2), channel_id=1, source_target_pairs={{0,1},{1,0},{2,3},{3,2},{4,5},{5,4},{6,7},{7,6},{8,9},{9,8},{10,11... | collective-permute-start | bytes 786440 | tf_op jit(solution)/shard_map/ppermute | solution.py:510
  99.4 16.9 %collective-permute-start.19 = (f32[8,4,8,128]{3,2,1,0:T(8,128)S(1)}, f32[8,4,8,128]{3,2,1,0:T(8,128)S(1)}, u32[]{:S(2)}, u32[]{:S(2)}) collective-permute-start(f32[8,4,8,128]{3,2,1,0:T(8,128)S(1)} %get-tuple-element.99), channel_id=1, source_target_pairs={{1,18},{2,17},{3,20},{4,19},{5,22},{6,21},{7,24},{8,23},{9,26},{10... | collective-permute-start | bytes 393224 | tf_op jit(solution)/shard_map/ppermute | solution.py:516
  109.6 6.7 %collective-permute-start.20 = (f32[8,4,8,128]{3,2,1,0:T(8,128)S(1)}, f32[8,4,8,128]{3,2,1,0:T(8,128)S(1)}, u32[]{:S(2)}, u32[]{:S(2)}) collective-permute-start(f32[8,4,8,128]{3,2,1,0:T(8,128)S(1)} %get-tuple-element.100), channel_id=1, source_target_pairs={{17,34},{18,33},{19,36},{20,35},{21,38},{22,37},{23,40},{24,39},{2... | collective-permute-start | bytes 393224 | tf_op jit(solution)/shard_map/ppermute | solution.py:516

commit v8 on v6

--- a/solution.py
+++ b/solution.py
@@ -221,7 +221,7 @@
     pltpu.make_async_copy(dens, dens_out, sem.at[tiles]).wait()
 
 
-def first_fields(inner, wb, w_ref, dens, src, tmp, v, inv_a, tmp2, u, inv_s):
+def first_fields(inner, wb, w_ref, dens, src, tmp, v, inv_a, tmp2, u, inv_s, load):
     rows, tiles = dens.shape[0], dens.shape[1]
     first, outs, again, last = parts(tiles, inner)
     conv_xz(src, tmp, w_ref, first)
@@ -238,6 +238,7 @@
     lax.fori_loop(0, (rows + 8) // 8, ring, 0)
     clear_outside((v, inv_a), outs, not inner)
     conv_xz(v, tmp2, w_ref, again)
+    load.wait()
 
     def second(c, carry):
         s = pl.ds(c * 8, 8)
@@ -250,17 +251,21 @@
     lax.fori_loop(0, rows // 8, second, 0)
 
 
-def first_inner(w_ref, wb, dens, own, xb, xa, tmp, v, inv_a, tmp2, u, inv_s, big):
+def first_inner(w_ref, wb, own, xb, xa, dens_far, tmp, v, inv_a, tmp2, u, inv_s, big, dens, sem):
+    load = pltpu.make_async_copy(dens_far, dens, sem.at[0])
+    load.start()
     join_rows(big, own, xa, xb)
-    first_fields(True, wb, w_ref, dens, big, tmp, v, inv_a, tmp2, u, inv_s)
-
-
-def first_outer(w_ref, wb, cot, dens, e, yb, ya, ca, da, db, *rest):
-    fields, mean, edges, ends = rest[6:12], rest[12], rest[13:19], rest[19]
+    first_fields(True, wb, w_ref, dens, big, tmp, v, inv_a, tmp2, u, inv_s, load)
+
+
+def first_outer(w_ref, wb, cot, e, yb, ya, ca, da, db, *rest):
+    dens_far, fields, mean, edges, (ends, dens, sem) = rest[6], rest[7:13], rest[13], rest[14:20], rest[20:]
     rows, tiles = dens.shape[0], dens.shape[1]
+    load = pltpu.make_async_copy(dens_far, dens, sem.at[0])
+    load.start()
     mean[...] = jnp.broadcast_to(centre(e), (K, L))
     join_ends(ends, rows, HALO, ya, yb, ca, da, db)
-    first_fields(False, wb, w_ref, dens, ends, *fields)
+    first_fields(False, wb, w_ref, dens, ends, *fields, load)
     give_edges(fields[4], edges)
     xa, xb, ya, yb, da, db = edges
     px, py = parities()
@@ -555,10 +560,10 @@
     )
     xa, xb, *others = exchange(*sent, tiles)
     held = [tmp, ringed, ringed, tmp2, field, field]
-    held_now = call(first_inner, near(*held), [big], [], [w, wb, dens, e, xb, xa])
+    held_now = call(first_inner, near(*held), [big, field], [1], [w, wb, e, xb, xa, dens], far_in=1)
     _, v, inv_a, _, u, inv_s, mean, *sent = call(
-        first_outer, near(*held, small) + edges(1, rows // 8), [ends], [],
-        [w, wb, cotangent, dens, e, *others, *held_now], same={10 + i: i for i in range(6)},
+        first_outer, near(*held, small) + edges(1, rows // 8), [ends, field], [1],
+        [w, wb, cotangent, e, *others, *held_now, dens], far_in=1, same={9 + i: i for i in range(6)},
     )
     xa, xb, *others = exchange(*sent, tiles)
     held = [tmp, ringed, tmp2, field, field, q_shape, acc]

time: 158 us -> 158 us (level)
  waiting for transfers between devices: 14.9 us -> 16.6 us
  local copies, waits for them, and re-layouts: 3.03 us -> 1.44 us
    ppermute x15, starting transfers between devices: 28.3 us -> 26.6 us  [swap(): return lax.ppermute(value, axis, list(partners(axis, parity).items()))]
    ppermute x15, waiting for transfers between devices: 12.6 us -> 14.3 us  [swap(): return lax.ppermute(value, axis, list(partners(axis, parity).items()))]
    ppermute x6, starting transfers between devices: 30.4 us -> 32.1 us  [swap_diagonal(): return lax.ppermute(value, ('gx', 'gy'), pairs)]
    unnamed x8 -> x6, local copies, waits for them, and re-layouts: 2.29 us -> 0.69 us
where the time goes in v8:
time: 158 us; the launch traced here: 157 us
  starting transfers between devices  58.7 us (37%)
  Pallas kernels  45.4 us (29%)
  blocking collectives  34.2 us (22%)
  waiting for transfers between devices  16.6 us (11%)
    pallas_call x8, Pallas kernels, call(): pl.pallas_call(kernel, out_shape=outs, in_specs=[pl.BlockSpec(memory_spac...  45.4 us
    all_to_all x1, blocking collectives, over_all(): lax.all_to_all(jnp.broadcast_to(told[None], (devices, K, L)), ('gx', 'gy'...  34.2 us
    ppermute x6, starting transfers between devices, swap_diagonal(): return lax.ppermute(value, ('gx', 'gy'), pairs)  32.1 us
    ppermute x15, starting transfers between devices, swap(): return lax.ppermute(value, axis, list(partners(axis, parity).items()))  26.6 us
    ppermute x15, waiting for transfers between devices, swap(): return lax.ppermute(value, axis, list(partners(axis, parity).items()))  14.3 us
  transfers between devices with their start and end apart: 21, of which 5 were waited for; matrix products, arithmetic and copies ran while one was open for 0% of the time, Pallas kernels for 12%

profile of v8, /device:TPU:1, one launch (start us, length us, event | category | flops | bytes accessed | tf_op | source)
XLA Modules:
  0.0 157.3 jit_solution(15366324171572727801)
XLA Ops:
  0.6 0.0 copy-start
  0.6 0.0 copy-start.2
  0.7 0.7 copy-done.2
  1.3 6.0 %shard_map.67 = (f32[32,16,8,128]{3,2,1,0:T(8,128)}, f32[32,16,8,128]{3,2,1,0:T(8,128)S(1)}, f32[8,128]{1,0:T(8,128)S(1)}, f32[8,128]{1,0:T(8,128)S(1)}, f32[8,1...) custom-call(f32[8]{0:T(128)S(1)} %copy-done.2, ...), custom_call_target="tpu_custom_call" | custom-call | tf_op jit(solution)/shard_map/pallas_call | solution.py:493
  7.4 0.7 collective-permute-start.2
  8.1 4.7 %collective-permute-start.3 = (f32[8,16,8,128]{3,2,1,0:T(8,128)}, f32[8,16,8,128]{3,2,1,0:T(8,128)S(1)}, u32[]{:S(2)}, u32[]{:S(2)}) collective-permute-start(f32[8,16,8,128]{3,2,1,0:T(8,128)} %get-tuple-element.75), channel_id=1, source_target_pairs={{0,16},{16,0},{32,48},{48,32},{64,80},{80,64},{96,112},{112,96},{1... | collective-permute-start | bytes 1572872 | tf_op jit(solution)/shard_map/ppermute | solution.py:515
  12.8 0.7 collective-permute-start.4
  13.4 7.7 %collective-permute-start.5 = (f32[8,4,8,128]{3,2,1,0:T(8,128)}, f32[8,4,8,128]{3,2,1,0:T(8,128)S(1)}, u32[]{:S(2)}, u32[]{:S(2)}) collective-permute-start(f32[8,4,8,128]{3,2,1,0:T(8,128)} %get-tuple-element.77), channel_id=1, source_target_pairs={{1,18},{2,17},{3,20},{4,19},{5,22},{6,21},{7,24},{8,23},{9,26},{10... | collective-permute-start | bytes 393224 | tf_op jit(solution)/shard_map/ppermute | solution.py:521
  21.2 5.5 %collective-permute-start = (f32[32,4,8,128]{3,2,1,0:T(8,128)}, f32[32,4,8,128]{3,2,1,0:T(8,128)}, u32[]{:S(2)}, u32[]{:S(2)}) collective-permute-start(f32[32,4,8,128]{3,2,1,0:T(8,128)} %get-tuple-element.72), channel_id=1, source_target_pairs={{1,2},{2,1},{3,4},{4,3},{5,6},{6,5},{7,8},{8,7},{9,10},{10,9},{11,... | collective-permute-start | bytes 1572872 | tf_op jit(solution)/shard_map/ppermute | solution.py:515
  26.6 0.0 collective-permute-done.4.db
  26.7 0.1 collective-permute-start.1
  26.8 0.0 collective-permute-done.5.da
  26.8 0.0 collective-permute-done.2.xb
  26.8 0.4 collective-permute-done.3.xa
  27.2 1.6 %collective-permute-start.6 = (f32[16,4,8,128]{3,2,1,0:T(8,128)S(1)}, f32[16,4,8,128]{3,2,1,0:T(8,128)S(1)}, u32[]{:S(2)}, u32[]{:S(2)}) collective-permute-start(f32[16,4,8,128]{3,2,1,0:T(8,128)S(1)} %pad_maximum_fusion.1), channel_id=1, source_target_pairs={{0,1},{1,0},{2,3},{3,2},{4,5},{5,4},{6,7},{7,6},{8,9},{9,8},{10,11... | collective-permute-start | bytes 786440 | tf_op jit(solution)/shard_map/ppermute | solution.py:515
  28.8 0.0 copy-done
  28.8 0.0 copy-start.1
  28.8 6.0 %shard_map.68 = (f32[40,24,8,128]{3,2,1,0:T(8,128)S(1)}, f32[40,20,8,128]{3,2,1,0:T(8,128)S(1)}, f32[40,20,8,128]{3,2,1,0:T(8,128)S(1)}, f32[32,20,8,128]{3,2,1,...) custom-call(bf16[256,256]{1,0:T(8,128)(2,1)S(1)} %copy-done, ...), custom_call_target="tpu_custom_call" | custom-call | tf_op jit(solution)/shard_map/pallas_call | solution.py:493
  34.8 2.8 %collective-permute-done.yb = f32[32,4,8,128]{3,2,1,0:T(8,128)} collective-permute-done((f32[32,4,8,128]{3,2,1,0:T(8,128)}, f32[32,4,8,128]{3,2,1,0:T(8,128)}, u32[]{:S(2)}, u32[]{:S(2)}) %collective-permute-start) | collective-permute-done | bytes 524320 | tf_op jit(solution)/shard_map/ppermute | solution.py:515
  37.6 0.0 collective-permute-done.1.ya
  37.6 0.0 collective-permute-done.6.ca
  37.6 0.0 copy-done.1
  37.6 5.5 %shard_map.69 = (f32[40,24,8,128]{3,2,1,0:T(8,128)S(1)}, f32[40,20,8,128]{3,2,1,0:T(8,128)S(1)}, f32[40,20,8,128]{3,2,1,0:T(8,128)S(1)}, f32[32,20,8,128]{3,2,1,...) custom-call(bf16[256,256]{1,0:T(8,128)(2,1)S(1)} %copy-done, ...), custom_call_target="tpu_custom_call", output_to_operand_aliasing={{0}: (9, {}), {1}: (10, {}), {2}: (11, {}), {3}: (12, {}), ... | custom-call | tf_op jit(solution)/shard_map/pallas_call | solution.py:493
  43.2 0.7 collective-permute-start.7
  43.9 4.3 %collective-permute-start.8 = (f32[9,16,8,128]{3,2,1,0:T(8,128)S(1)}, f32[9,16,8,128]{3,2,1,0:T(8,128)S(1)}, u32[]{:S(2)}, u32[]{:S(2)}) collective-permute-start(f32[9,16,8,128]{3,2,1,0:T(8,128)S(1)} %get-tuple-element.94), channel_id=1, source_target_pairs={{0,16},{16,0},{32,48},{48,32},{64,80},{80,64},{96,112},{112,96},{1... | collective-permute-start | bytes 1769480 | tf_op jit(solution)/shard_map/ppermute | solution.py:515
  48.1 0.7 collective-permute-start.9
  48.8 12.5 %collective-permute-start.10 = (f32[9,4,8,128]{3,2,1,0:T(8,128)S(1)}, f32[9,4,8,128]{3,2,1,0:T(8,128)S(1)}, u32[]{:S(2)}, u32[]{:S(2)}) collective-permute-start(f32[9,4,8,128]{3,2,1,0:T(8,128)S(1)} %get-tuple-element.96), channel_id=1, source_target_pairs={{1,18},{2,17},{3,20},{4,19},{5,22},{6,21},{7,24},{8,23},{9,26},{10... | collective-permute-start | bytes 442376 | tf_op jit(solution)/shard_map/ppermute | solution.py:521
  61.3 2.9 %collective-permute-start.11 = (f32[36,4,8,128]{3,2,1,0:T(8,128)S(1)}, f32[36,4,8,128]{3,2,1,0:T(8,128)S(1)}, u32[]{:S(2)}, u32[]{:S(2)}) collective-permute-start(f32[36,4,8,128]{3,2,1,0:T(8,128)S(1)} %get-tuple-element.99), channel_id=1, source_target_pairs={{1,2},{2,1},{3,4},{4,3},{5,6},{6,5},{7,8},{8,7},{9,10},{10,9},{11,... | collective-permute-start | bytes 1769480 | tf_op jit(solution)/shard_map/ppermute | solution.py:515
  64.3 0.0 collective-permute-done.9.db
  64.3 0.1 collective-permute-start.12
  64.4 2.3 %collective-permute-done.10.da = f32[9,4,8,128]{3,2,1,0:T(8,128)S(1)} collective-permute-done((f32[9,4,8,128]{3,2,1,0:T(8,128)S(1)}, f32[9,4,8,128]{3,2,1,0:T(8,128)S(1)}, u32[]{:S(2)}, u32[]{:S(2)}) %collective-permute-start.10) | collective-permute-done | bytes 147488 | tf_op jit(solution)/shard_map/ppermute | solution.py:521
  66.6 0.0 collective-permute-done.7.xb
  66.6 0.0 collective-permute-done.8.xa
  66.7 0.1 collective-permute-start.13
  66.8 6.7 %shard_map.70 = (f32[40,24,8,128]{3,2,1,0:T(8,128)S(1)}, f32[40,20,8,128]{3,2,1,0:T(8,128)S(1)}, f32[32,20,8,128]{3,2,1,0:T(8,128)S(1)}, f32[32,16,8,128]{3,2,1,...) custom-call(bf16[256,256]{1,0:T(8,128)(2,1)S(1)} %copy-done, ...), custom_call_target="tpu_custom_call" | custom-call | tf_op jit(solution)/shard_map/pallas_call | solution.py:493
  73.5 6.8 %collective-permute-done.11.yb = f32[36,4,8,128]{3,2,1,0:T(8,128)S(1)} collective-permute-done((f32[36,4,8,128]{3,2,1,0:T(8,128)S(1)}, f32[36,4,8,128]{3,2,1,0:T(8,128)S(1)}, u32[]{:S(2)}, u32[]{:S(2)}) %collective-permute-start.11) | collective-permute-done | bytes 589856 | tf_op jit(solution)/shard_map/ppermute | solution.py:515
  80.3 0.0 collective-permute-done.12.ya
  80.3 0.0 collective-permute-done.13.ca
  80.3 4.4 %shard_map.71 = (f32[40,24,8,128]{3,2,1,0:T(8,128)S(1)}, f32[40,20,8,128]{3,2,1,0:T(8,128)S(1)}, f32[32,20,8,128]{3,2,1,0:T(8,128)S(1)}, f32[32,16,8,128]{3,2,1,...) custom-call(bf16[256,256]{1,0:T(8,128)(2,1)S(1)} %copy-done, ...), custom_call_target="tpu_custom_call", output_to_operand_aliasing={{0}: (13, {}), {1}: (14, {}), {2}: (15, {}), {3}: (16, {}),... | custom-call | tf_op jit(solution)/shard_map/pallas_call | solution.py:493
  84.7 0.7 collective-permute-start.16
  85.4 0.7 collective-permute-start.17
  86.1 0.7 collective-permute-start.18
  86.7 9.9 %collective-permute-start.19 = (f32[8,4,8,128]{3,2,1,0:T(8,128)S(1)}, f32[8,4,8,128]{3,2,1,0:T(8,128)S(1)}, u32[]{:S(2)}, u32[]{:S(2)}) collective-permute-start(f32[8,4,8,128]{3,2,1,0:T(8,128)S(1)} %get-tuple-element.120), channel_id=1, source_target_pairs={{1,18},{2,17},{3,20},{4,19},{5,22},{6,21},{7,24},{8,23},{9,26},{10... | collective-permute-start | bytes 393224 | tf_op jit(solution)/shard_map/ppermute | solution.py:521
  96.6 4.0 %collective-permute-start.14 = (f32[32,4,8,128]{3,2,1,0:T(8,128)S(1)}, f32[32,4,8,128]{3,2,1,0:T(8,128)S(1)}, u32[]{:S(2)}, u32[]{:S(2)}) collective-permute-start(f32[32,4,8,128]{3,2,1,0:T(8,128)S(1)} %get-tuple-element.115), channel_id=1, source_target_pairs={{1,2},{2,1},{3,4},{4,3},{5,6},{6,5},{7,8},{8,7},{9,10},{10,9},{11,... | collective-permute-start | bytes 1572872 | tf_op jit(solution)/shard_map/ppermute | solution.py:515
  100.6 0.0 collective-permute-done.18.db
  100.6 0.1 collective-permute-start.15
  100.7 0.0 collective-permute-done.19.da
  100.7 0.0 collective-permute-done.16.xb
  100.8 0.0 collective-permute-done.17.xa
  100.8 0.6 collective-permute-start.20
  101.4 6.0 %shard_map.72 = (f32[40,24,8,128]{3,2,1,0:T(8,128)S(1)}, f32[40,20,8,128]{3,2,1,0:T(8,128)S(1)}, f32[32,20,8,128]{3,2,1,0:T(8,128)S(1)}, f32[32,16,8,128]{3,2,1,0:T(8,128)S(1)}, f32[2,8,128]{2,1,0:T(8,128)S(1)}) custom-call(bf16[256,256]{1,0:T(8,128)(2,1)S(1)} %copy-done, f32[8,128]{1,0:T(8,128)S(1)} %get-tuple-element.70.wb, ...), custom_call_target="tpu_custom_call" | custom-call | tf_op jit(solution)/shard_map/pallas_call | solution.py:493
  107.4 4.3 %collective-permute-done.14.yb = f32[32,4,8,128]{3,2,1,0:T(8,128)S(1)} collective-permute-done((f32[32,4,8,128]{3,2,1,0:T(8,128)S(1)}, f32[32,4,8,128]{3,2,1,0:T(8,128)S(1)}, u32[]{:S(2)}, u32[]{:S(2)}) %collective-permute-start.14) | collective-permute-done | bytes 524320 | tf_op jit(solution)/shard_map/ppermute | solution.py:515
  111.7 0.0 collective-permute-done.15.ya
  111.7 0.0 collective-permute-done.20.ca
  111.7 5.0 %shard_map.73 = (f32[40,24,8,128]{3,2,1,0:T(8,128)S(1)}, f32[40,20,8,128]{3,2,1,0:T(8,128)S(1)}, f32[32,20,8,128]{3,2,1,0:T(8,128)S(1)}, f32[32,16,8,128]{3,2,1,...) custom-call(bf16[256,256]{1,0:T(8,128)(2,1)S(1)} %copy-done, ...), custom_call_target="tpu_custom_call", output_to_operand_aliasing={{0}: (14, {}), {1}: (15, {}), {2}: (16, {}), {3}: (17, {}),... | custom-call | tf_op jit(solution)/shard_map/pallas_call | solution.py:493
  116.8 34.2 %all_to_all.5.heard = f32[128,8,128]{2,1,0:T(8,128)S(1)} all-to-all(f32[128,8,128]{2,1,0:T(8,128)S(1)} %broadcast_in_dim.2), channel_id=1, replica_groups=mesh['gx'=8,'gy'=16] {'gx','gy'}, dimensions={0} | all-to-all | bytes 1048576 | tf_op jit(solution)/shard_map/all_to_all | solution.py:537
  151.0 5.7 %shard_map.74 = (f32[256,2048]{1,0:T(8,128)}, f32[32,2048]{1,0:T(8,128)}, f32[8,128]{1,0:T(8,128)S(1)}) custom-call(f32[8,128]{1,0:T(8,128)S(1)} %get-tuple-element.70.wb, f32[128,8,128]{2,1,0:T(8,128)S(1)} %all_to_all.5.heard, f32[16,32,128]{2,1,0:T(8,128)} %get-tuple-element.132.q_far, f32[32,16,8,128]{3,2,1,0:T(8,128)} %get-tuple-element.133.gp_far, ...), custom_call_target="tpu_custom_call" | custom-call | tf_op jit(solution)/shard_map/pallas_call | solution.py:493
  156.7 0.6 slice_reduce_fusion
  (9 shorter events, 0.2 us)
Async XLA Ops:
  0.6 28.2 %copy-start = (bf16[256,256]{1,0:T(8,128)(2,1)S(1)}, bf16[256,256]{1,0:T(8,128)(2,1)}, u32[]{:S(2)}) copy-start(bf16[256,256]{1,0:T(8,128)(2,1)} %constant.17.clone.w_ref) | copy-start | bytes 393220
  0.6 0.7 copy-start.2
  7.4 19.4 %collective-permute-start.2 = (f32[8,16,8,128]{3,2,1,0:T(8,128)}, f32[8,16,8,128]{3,2,1,0:T(8,128)S(1)}, u32[]{:S(2)}, u32[]{:S(2)}) collective-permute-start(f32[8,16,8,128]{3,2,1,0:T(8,128)} %get-tuple-element.74), channel_id=1, source_target_pairs={{16,32},{32,16},{48,64},{64,48},{80,96},{96,80},{17,33},{33,17},{4... | collective-permute-start | bytes 1572872 | tf_op jit(solution)/shard_map/ppermute | solution.py:515
  8.1 19.1 %collective-permute-start.3 = (f32[8,16,8,128]{3,2,1,0:T(8,128)}, f32[8,16,8,128]{3,2,1,0:T(8,128)S(1)}, u32[]{:S(2)}, u32[]{:S(2)}) collective-permute-start(f32[8,16,8,128]{3,2,1,0:T(8,128)} %get-tuple-element.75), channel_id=1, source_target_pairs={{0,16},{16,0},{32,48},{48,32},{64,80},{80,64},{96,112},{112,96},{1... | collective-permute-start | bytes 1572872 | tf_op jit(solution)/shard_map/ppermute | solution.py:515
  12.8 13.9 %collective-permute-start.4 = (f32[8,4,8,128]{3,2,1,0:T(8,128)S(1)}, f32[8,4,8,128]{3,2,1,0:T(8,128)S(1)}, u32[]{:S(2)}, u32[]{:S(2)}) collective-permute-start(f32[8,4,8,128]{3,2,1,0:T(8,128)S(1)} %get-tuple-element.76), channel_id=1, source_target_pairs={{17,34},{18,33},{19,36},{20,35},{21,38},{22,37},{23,40},{24,39},{2... | collective-permute-start | bytes 393224 | tf_op jit(solution)/shard_map/ppermute | solution.py:521
  13.4 13.3 %collective-permute-start.5 = (f32[8,4,8,128]{3,2,1,0:T(8,128)}, f32[8,4,8,128]{3,2,1,0:T(8,128)S(1)}, u32[]{:S(2)}, u32[]{:S(2)}) collective-permute-start(f32[8,4,8,128]{3,2,1,0:T(8,128)} %get-tuple-element.77), channel_id=1, source_target_pairs={{1,18},{2,17},{3,20},{4,19},{5,22},{6,21},{7,24},{8,23},{9,26},{10... | collective-permute-start | bytes 393224 | tf_op jit(solution)/shard_map/ppermute | solution.py:521
  21.2 16.5 %collective-permute-start = (f32[32,4,8,128]{3,2,1,0:T(8,128)}, f32[32,4,8,128]{3,2,1,0:T(8,128)}, u32[]{:S(2)}, u32[]{:S(2)}) collective-permute-start(f32[32,4,8,128]{3,2,1,0:T(8,128)} %get-tuple-element.72), channel_id=1, source_target_pairs={{1,2},{2,1},{3,4},{4,3},{5,6},{6,5},{7,8},{8,7},{9,10},{10,9},{11,... | collective-permute-start | bytes 1572872 | tf_op jit(solution)/shard_map/ppermute | solution.py:515
  26.7 11.0 %collective-permute-start.1 = (f32[32,4,8,128]{3,2,1,0:T(8,128)}, f32[32,4,8,128]{3,2,1,0:T(8,128)}, u32[]{:S(2)}, u32[]{:S(2)}) collective-permute-start(f32[32,4,8,128]{3,2,1,0:T(8,128)} %get-tuple-element.73), channel_id=1, source_target_pairs={{0,1},{1,0},{2,3},{3,2},{4,5},{5,4},{6,7},{7,6},{8,9},{9,8},{10,11... | collective-permute-start | bytes 1572872 | tf_op jit(solution)/shard_map/ppermute | solution.py:515
  27.2 10.4 %collective-permute-start.6 = (f32[16,4,8,128]{3,2,1,0:T(8,128)S(1)}, f32[16,4,8,128]{3,2,1,0:T(8,128)S(1)}, u32[]{:S(2)}, u32[]{:S(2)}) collective-permute-start(f32[16,4,8,128]{3,2,1,0:T(8,128)S(1)} %pad_maximum_fusion.1), channel_id=1, source_target_pairs={{0,1},{1,0},{2,3},{3,2},{4,5},{5,4},{6,7},{7,6},{8,9},{9,8},{10,11... | collective-permute-start | bytes 786440 | tf_op jit(solution)/shard_map/ppermute | solution.py:515
  28.8 8.8 %copy-start.1 = (f32[32,2048]{1,0:T(8,128)S(1)}, f32[32,2048]{1,0:T(8,128)}, u32[]{:S(2)}) copy-start(f32[32,2048]{1,0:T(8,128)} %cot.5) | copy-start | bytes 786436
  43.2 23.5 %collective-permute-start.7 = (f32[9,16,8,128]{3,2,1,0:T(8,128)S(1)}, f32[9,16,8,128]{3,2,1,0:T(8,128)S(1)}, u32[]{:S(2)}, u32[]{:S(2)}) collective-permute-start(f32[9,16,8,128]{3,2,1,0:T(8,128)S(1)} %get-tuple-element.93), channel_id=1, source_target_pairs={{16,32},{32,16},{48,64},{64,48},{80,96},{96,80},{17,33},{33,17},{4... | collective-permute-start | bytes 1769480 | tf_op jit(solution)/shard_map/ppermute | solution.py:515
  43.9 22.8 %collective-permute-start.8 = (f32[9,16,8,128]{3,2,1,0:T(8,128)S(1)}, f32[9,16,8,128]{3,2,1,0:T(8,128)S(1)}, u32[]{:S(2)}, u32[]{:S(2)}) collective-permute-start(f32[9,16,8,128]{3,2,1,0:T(8,128)S(1)} %get-tuple-element.94), channel_id=1, source_target_pairs={{0,16},{16,0},{32,48},{48,32},{64,80},{80,64},{96,112},{112,96},{1... | collective-permute-start | bytes 1769480 | tf_op jit(solution)/shard_map/ppermute | solution.py:515
  48.1 16.1 %collective-permute-start.9 = (f32[9,4,8,128]{3,2,1,0:T(8,128)S(1)}, f32[9,4,8,128]{3,2,1,0:T(8,128)S(1)}, u32[]{:S(2)}, u32[]{:S(2)}) collective-permute-start(f32[9,4,8,128]{3,2,1,0:T(8,128)S(1)} %get-tuple-element.95), channel_id=1, source_target_pairs={{17,34},{18,33},{19,36},{20,35},{21,38},{22,37},{23,40},{24,39},{2... | collective-permute-start | bytes 442376 | tf_op jit(solution)/shard_map/ppermute | solution.py:521
  48.8 17.8 %collective-permute-start.10 = (f32[9,4,8,128]{3,2,1,0:T(8,128)S(1)}, f32[9,4,8,128]{3,2,1,0:T(8,128)S(1)}, u32[]{:S(2)}, u32[]{:S(2)}) collective-permute-start(f32[9,4,8,128]{3,2,1,0:T(8,128)S(1)} %get-tuple-element.96), channel_id=1, source_target_pairs={{1,18},{2,17},{3,20},{4,19},{5,22},{6,21},{7,24},{8,23},{9,26},{10... | collective-permute-start | bytes 442376 | tf_op jit(solution)/shard_map/ppermute | solution.py:521
  61.3 18.9 %collective-permute-start.11 = (f32[36,4,8,128]{3,2,1,0:T(8,128)S(1)}, f32[36,4,8,128]{3,2,1,0:T(8,128)S(1)}, u32[]{:S(2)}, u32[]{:S(2)}) collective-permute-start(f32[36,4,8,128]{3,2,1,0:T(8,128)S(1)} %get-tuple-element.99), channel_id=1, source_target_pairs={{1,2},{2,1},{3,4},{4,3},{5,6},{6,5},{7,8},{8,7},{9,10},{10,9},{11,... | collective-permute-start | bytes 1769480 | tf_op jit(solution)/shard_map/ppermute | solution.py:515
  64.3 16.0 %collective-permute-start.12 = (f32[36,4,8,128]{3,2,1,0:T(8,128)S(1)}, f32[36,4,8,128]{3,2,1,0:T(8,128)S(1)}, u32[]{:S(2)}, u32[]{:S(2)}) collective-permute-start(f32[36,4,8,128]{3,2,1,0:T(8,128)S(1)} %get-tuple-element.100), channel_id=1, source_target_pairs={{0,1},{1,0},{2,3},{3,2},{4,5},{5,4},{6,7},{7,6},{8,9},{9,8},{10,11... | collective-permute-start | bytes 1769480 | tf_op jit(solution)/shard_map/ppermute | solution.py:515
  66.7 13.6 %collective-permute-start.13 = (f32[18,4,8,128]{3,2,1,0:T(8,128)S(1)}, f32[18,4,8,128]{3,2,1,0:T(8,128)S(1)}, u32[]{:S(2)}, u32[]{:S(2)}) collective-permute-start(f32[18,4,8,128]{3,2,1,0:T(8,128)S(1)} %pad_maximum_fusion), channel_id=1, source_target_pairs={{0,1},{1,0},{2,3},{3,2},{4,5},{5,4},{6,7},{7,6},{8,9},{9,8},{10,11... | collective-permute-start | bytes 884744 | tf_op jit(solution)/shard_map/ppermute | solution.py:515
  84.7 16.0 %collective-permute-start.16 = (f32[8,16,8,128]{3,2,1,0:T(8,128)S(1)}, f32[8,16,8,128]{3,2,1,0:T(8,128)S(1)}, u32[]{:S(2)}, u32[]{:S(2)}) collective-permute-start(f32[8,16,8,128]{3,2,1,0:T(8,128)S(1)} %get-tuple-element.117), channel_id=1, source_target_pairs={{16,32},{32,16},{48,64},{64,48},{80,96},{96,80},{17,33},{33,17},{4... | collective-permute-start | bytes 1572872 | tf_op jit(solution)/shard_map/ppermute | solution.py:515
  85.4 15.3 %collective-permute-start.17 = (f32[8,16,8,128]{3,2,1,0:T(8,128)S(1)}, f32[8,16,8,128]{3,2,1,0:T(8,128)S(1)}, u32[]{:S(2)}, u32[]{:S(2)}) collective-permute-start(f32[8,16,8,128]{3,2,1,0:T(8,128)S(1)} %get-tuple-element.118), channel_id=1, source_target_pairs={{0,16},{16,0},{32,48},{48,32},{64,80},{80,64},{96,112},{112,96},{1... | collective-permute-start | bytes 1572872 | tf_op jit(solution)/shard_map/ppermute | solution.py:515
  86.1 14.6 %collective-permute-start.18 = (f32[8,4,8,128]{3,2,1,0:T(8,128)S(1)}, f32[8,4,8,128]{3,2,1,0:T(8,128)S(1)}, u32[]{:S(2)}, u32[]{:S(2)}) collective-permute-start(f32[8,4,8,128]{3,2,1,0:T(8,128)S(1)} %get-tuple-element.119), channel_id=1, source_target_pairs={{17,34},{18,33},{19,36},{20,35},{21,38},{22,37},{23,40},{24,39},{2... | collective-permute-start | bytes 393224 | tf_op jit(solution)/shard_map/ppermute | solution.py:521
  86.7 14.0 %collective-permute-start.19 = (f32[8,4,8,128]{3,2,1,0:T(8,128)S(1)}, f32[8,4,8,128]{3,2,1,0:T(8,128)S(1)}, u32[]{:S(2)}, u32[]{:S(2)}) collective-permute-start(f32[8,4,8,128]{3,2,1,0:T(8,128)S(1)} %get-tuple-element.120), channel_id=1, source_target_pairs={{1,18},{2,17},{3,20},{4,19},{5,22},{6,21},{7,24},{8,23},{9,26},{10... | collective-permute-start | bytes 393224 | tf_op jit(solution)/shard_map/ppermute | solution.py:521
  96.6 15.1 %collective-permute-start.14 = (f32[32,4,8,128]{3,2,1,0:T(8,128)S(1)}, f32[32,4,8,128]{3,2,1,0:T(8,128)S(1)}, u32[]{:S(2)}, u32[]{:S(2)}) collective-permute-start(f32[32,4,8,128]{3,2,1,0:T(8,128)S(1)} %get-tuple-element.115), channel_id=1, source_target_pairs={{1,2},{2,1},{3,4},{4,3},{5,6},{6,5},{7,8},{8,7},{9,10},{10,9},{11,... | collective-permute-start | bytes 1572872 | tf_op jit(solution)/shard_map/ppermute | solution.py:515
  100.6 11.1 %collective-permute-start.15 = (f32[32,4,8,128]{3,2,1,0:T(8,128)S(1)}, f32[32,4,8,128]{3,2,1,0:T(8,128)S(1)}, u32[]{:S(2)}, u32[]{:S(2)}) collective-permute-start(f32[32,4,8,128]{3,2,1,0:T(8,128)S(1)} %get-tuple-element.116), channel_id=1, source_target_pairs={{0,1},{1,0},{2,3},{3,2},{4,5},{5,4},{6,7},{7,6},{8,9},{9,8},{10,11... | collective-permute-start | bytes 1572872 | tf_op jit(solution)/shard_map/ppermute | solution.py:515
  100.8 10.9 %collective-permute-start.20 = (f32[16,4,8,128]{3,2,1,0:T(8,128)S(1)}, f32[16,4,8,128]{3,2,1,0:T(8,128)S(1)}, u32[]{:S(2)}, u32[]{:S(2)}) collective-permute-start(f32[16,4,8,128]{3,2,1,0:T(8,128)S(1)} %pad_maximum_fusion.2), channel_id=1, source_target_pairs={{0,1},{1,0},{2,3},{3,2},{4,5},{5,4},{6,7},{7,6},{8,9},{9,8},{10,11... | collective-permute-start | bytes 786440 | tf_op jit(solution)/shard_map/ppermute | solution.py:515

commit v9 on v8

--- a/solution.py
+++ b/solution.py
@@ -515,20 +515,24 @@
     return lax.ppermute(value, axis, list(partners(axis, parity).items()))
 
 
-def swap_diagonal(value, parity_x, parity_y):
-    along_x, along_y, width = partners("gx", parity_x), partners("gy", parity_y), lax.axis_size("gy")
-    pairs = [(i * width + j, k * width + m) for i, k in along_x.items() for j, m in along_y.items()]
-    return lax.ppermute(value, ("gx", "gy"), pairs)
-
-
 def exchange(xa, xb, ya, yb, da, db, tiles):
+    del da, db
     rxb, ryb = swap(xb, "gx", 1), swap(yb, "gy", 1)
-    rdb, rda = swap_diagonal(db, 1, 1), swap_diagonal(da, 0, 1)
     rxa, rya = swap(xa, "gx", 0), swap(ya, "gy", 0)
-    rxb, rxa, rdb, rda = lax.optimization_barrier((rxb, rxa, rdb, rda))
-    first = (1 - lax.rem(lax.axis_index("gy"), 2)) * (tiles - HT)
+    px, py = lax.rem(lax.axis_index("gx"), 2), lax.rem(lax.axis_index("gy"), 2)
+    first = (1 - py) * (tiles - HT)
     corner = jnp.concatenate([lax.dynamic_slice_in_dim(r, first, HT, axis=1) for r in (rxb, rxa)], axis=0)
     rca = swap(corner, "gy", 0)
+    slabs = xa.shape[0] - HALO
+    rows = ryb.shape[0] if slabs == 0 else ryb.shape[0] * 8 // 9
+
+    def facing(side):
+        taken = [lax.dynamic_slice_in_dim(ryb, side * (rows - HALO), HALO, axis=0)]
+        if slabs:
+            taken.append(lax.dynamic_slice_in_dim(ryb, rows + side * (rows // 8 - 1), 1, axis=0))
+        return jnp.concatenate(taken, axis=0)
+
+    rdb, rda = swap(facing(px), "gx", 1), swap(facing(1 - px), "gx", 0)
     return rxa, rxb, ryb, rya, rca, rda, rdb
 
 

time: 158 us -> 189 us (1.20)
  waiting for transfers between devices: 16.6 us -> 34.6 us
  local copies, waits for them, and re-layouts: 1.44 us -> 13.5 us
  Pallas kernels: 45.4 us -> 49.5 us
  starting transfers between devices: 58.7 us -> 54.7 us
    ppermute x6 -> x0, starting transfers between devices: 32.1 us -> none  [swap_diagonal(): return lax.ppermute(value, ('gx', 'gy'), pairs)]
    ppermute x15 -> x21, starting transfers between devices: 26.6 us -> 54.7 us  [swap(): return lax.ppermute(value, axis, list(partners(axis, parity).items()))]
    ppermute x15 -> x21, waiting for transfers between devices: 14.3 us -> 34.6 us  [swap(): return lax.ppermute(value, axis, list(partners(axis, parity).items()))]
    unnamed x6 -> x28, local copies, waits for them, and re-layouts: 0.69 us -> 10.1 us
    pallas_call x8, Pallas kernels: 45.4 us -> 49.5 us  [call(): pl.pallas_call(kernel, out_shape=outs, in_specs=[pl.BlockSpec(memory_spac...]
    ppermute x6 -> x0, waiting for transfers between devices: 2.29 us -> none  [swap_diagonal(): return lax.ppermute(value, ('gx', 'gy'), pairs)]
  transfers between devices with their start and end apart: 21 -> 21, of which waited for: 5 -> 6; matrix products, arithmetic and copies ran while one was open for 0% -> 2% of each run, Pallas kernels for 12% -> 10%
where the time goes in v9:
time: 189 us; the launch traced here: 188 us
  starting transfers between devices  54.7 us (29%)
  Pallas kernels  49.5 us (26%)
  waiting for transfers between devices  34.6 us (18%)
  blocking collectives  34.2 us (18%)
  local copies, waits for them, and re-layouts  13.5 us (7%)
    ppermute x21, starting transfers between devices, swap(): return lax.ppermute(value, axis, list(partners(axis, parity).items()))  54.7 us
    pallas_call x8, Pallas kernels, call(): pl.pallas_call(kernel, out_shape=outs, in_specs=[pl.BlockSpec(memory_spac...  49.5 us
    ppermute x21, waiting for transfers between devices, swap(): return lax.ppermute(value, axis, list(partners(axis, parity).items()))  34.6 us
    all_to_all x1, blocking collectives, over_all(): lax.all_to_all(jnp.broadcast_to(told[None], (devices, K, L)), ('gx', 'gy'...  34.2 us
    unnamed x28, local copies, waits for them, and re-layouts  10.1 us
  transfers between devices with their start and end apart: 21, of which 6 were waited for; matrix products, arithmetic and copies ran while one was open for 2% of the time, Pallas kernels for 10%

profile of v9, /device:TPU:1, one launch (start us, length us, event | category | flops | bytes accessed | tf_op | source)
XLA Modules:
  0.0 188.4 jit_solution(383703073471107825)
XLA Ops:
  0.6 0.0 copy-start.9
  0.7 0.7 copy-done.12
  1.3 6.1 %shard_map.67 = (f32[32,16,8,128]{3,2,1,0:T(8,128)}, f32[32,16,8,128]{3,2,1,0:T(8,128)S(1)}, f32[8,128]{1,0:T(8,128)S(1)}, f32[8,128]{1,0:T(8,128)S(1)}, f32[8,1...) custom-call(f32[8]{0:T(128)S(1)} %copy-done.12, ...), custom_call_target="tpu_custom_call" | custom-call | tf_op jit(solution)/shard_map/pallas_call | solution.py:493
  7.4 0.7 collective-permute-start.2
  8.1 4.7 %collective-permute-start.3 = (f32[8,16,8,128]{3,2,1,0:T(8,128)}, f32[8,16,8,128]{3,2,1,0:T(8,128)}, u32[]{:S(2)}, u32[]{:S(2)}) collective-permute-start(f32[8,16,8,128]{3,2,1,0:T(8,128)} %get-tuple-element.57), channel_id=1, source_target_pairs={{0,16},{16,0},{32,48},{48,32},{64,80},{80,64},{96,112},{112,96},{1... | collective-permute-start | bytes 1572872 | tf_op jit(solution)/shard_map/ppermute | solution.py:515
  12.8 5.8 %collective-permute-start = (f32[32,4,8,128]{3,2,1,0:T(8,128)}, f32[32,4,8,128]{3,2,1,0:T(8,128)S(1)}, u32[]{:S(2)}, u32[]{:S(2)}) collective-permute-start(f32[32,4,8,128]{3,2,1,0:T(8,128)} %get-tuple-element.54), channel_id=1, source_target_pairs={{1,2},{2,1},{3,4},{4,3},{5,6},{6,5},{7,8},{8,7},{9,10},{10,9},{11,... | collective-permute-start | bytes 1572872 | tf_op jit(solution)/shard_map/ppermute | solution.py:515
  18.6 0.1 collective-permute-start.1
  18.7 0.0 collective-permute-done.2.xb
  18.7 5.7 %collective-permute-done.3.xa = f32[8,16,8,128]{3,2,1,0:T(8,128)} collective-permute-done((f32[8,16,8,128]{3,2,1,0:T(8,128)}, f32[8,16,8,128]{3,2,1,0:T(8,128)}, u32[]{:S(2)}, u32[]{:S(2)}) %collective-permute-start.3) | collective-permute-done | bytes 524320 | tf_op jit(solution)/shard_map/ppermute | solution.py:515
  24.5 0.9 constant_dynamic-slice_fusion.12
  25.4 0.7 pad_maximum_fusion.1
  26.1 1.5 collective-permute-start.4
  27.7 2.3 %collective-permute-done.yb = f32[32,4,8,128]{3,2,1,0:T(8,128)S(1)} collective-permute-done((f32[32,4,8,128]{3,2,1,0:T(8,128)}, f32[32,4,8,128]{3,2,1,0:T(8,128)S(1)}, u32[]{:S(2)}, u32[]{:S(2)}) %collective-permute-start) | collective-permute-done | bytes 524320 | tf_op jit(solution)/shard_map/ppermute | solution.py:515
  30.0 0.7 collective-permute-start.6
  30.7 2.6 %collective-permute-start.5 = (f32[8,4,8,128]{3,2,1,0:T(8,128)S(1)}, f32[8,4,8,128]{3,2,1,0:T(8,128)S(1)}, u32[]{:S(2)}, u32[]{:S(2)}) collective-permute-start(f32[8,4,8,128]{3,2,1,0:T(8,128)S(1)} %get-tuple-element.108), channel_id=1, source_target_pairs={{0,16},{16,0},{32,48},{48,32},{64,80},{80,64},{96,112},{112,96},{1... | collective-permute-start | bytes 393224 | tf_op jit(solution)/shard_map/ppermute | solution.py:515
  33.3 7.1 %shard_map.68 = (f32[40,24,8,128]{3,2,1,0:T(8,128)S(1)}, f32[40,20,8,128]{3,2,1,0:T(8,128)S(1)}, f32[40,20,8,128]{3,2,1,0:T(8,128)S(1)}, f32[32,20,8,128]{3,2,1,...) custom-call(bf16[256,256]{1,0:T(8,128)(2,1)S(1)} %copy-done.9, ...), custom_call_target="tpu_custom_call" | custom-call | tf_op jit(solution)/shard_map/pallas_call | solution.py:493
  40.4 0.0 collective-permute-done.1.ya
  40.4 0.0 collective-permute-done.6.db
  40.4 0.0 collective-permute-done.5.da
  40.4 0.0 collective-permute-done.4.ca
  40.4 6.7 %shard_map.69 = (f32[40,24,8,128]{3,2,1,0:T(8,128)S(1)}, f32[40,20,8,128]{3,2,1,0:T(8,128)S(1)}, f32[40,20,8,128]{3,2,1,0:T(8,128)S(1)}, f32[32,20,8,128]{3,2,1,...) custom-call(bf16[256,256]{1,0:T(8,128)(2,1)S(1)} %copy-done.9, ...), custom_call_target="tpu_custom_call", output_to_operand_aliasing={{0}: (9, {}), {1}: (10, {}), {2}: (11, {}), {3}: (12, {}), ... | custom-call | tf_op jit(solution)/shard_map/pallas_call | solution.py:493
  47.1 1.7 copy-done
  48.8 1.7 copy-done.2
  50.5 1.3 copy-done.4
  51.8 1.3 copy-done.6
  53.1 0.8 copy-done.13
  53.9 0.7 collective-permute-start.7
  54.6 13.1 %collective-permute-start.8 = (f32[9,16,8,128]{3,2,1,0:T(8,128)}, f32[9,16,8,128]{3,2,1,0:T(8,128)S(1)}, u32[]{:S(2)}, u32[]{:S(2)}) collective-permute-start(f32[9,16,8,128]{3,2,1,0:T(8,128)} %get-tuple-element.70), channel_id=1, source_target_pairs={{0,16},{16,0},{32,48},{48,32},{64,80},{80,64},{96,112},{112,96},{1... | collective-permute-start | bytes 1769480 | tf_op jit(solution)/shard_map/ppermute | solution.py:515
  67.7 3.6 %collective-permute-start.9 = (f32[36,4,8,128]{3,2,1,0:T(8,128)}, f32[36,4,8,128]{3,2,1,0:T(8,128)}, u32[]{:S(2)}, u32[]{:S(2)}) collective-permute-start(f32[36,4,8,128]{3,2,1,0:T(8,128)} %get-tuple-element.71), channel_id=1, source_target_pairs={{1,2},{2,1},{3,4},{4,3},{5,6},{6,5},{7,8},{8,7},{9,10},{10,9},{11,... | collective-permute-start | bytes 1769480 | tf_op jit(solution)/shard_map/ppermute | solution.py:515
  71.3 0.1 collective-permute-start.10
  71.4 0.0 collective-permute-done.7.xb
  71.5 3.8 %collective-permute-done.8.xa = f32[9,16,8,128]{3,2,1,0:T(8,128)S(1)} collective-permute-done((f32[9,16,8,128]{3,2,1,0:T(8,128)}, f32[9,16,8,128]{3,2,1,0:T(8,128)S(1)}, u32[]{:S(2)}, u32[]{:S(2)}) %collective-permute-start.8) | collective-permute-done | bytes 589856 | tf_op jit(solution)/shard_map/ppermute | solution.py:515
  75.2 0.1 collective-permute-start.11
  75.3 10.9 %collective-permute-done.9.yb = f32[36,4,8,128]{3,2,1,0:T(8,128)} collective-permute-done((f32[36,4,8,128]{3,2,1,0:T(8,128)}, f32[36,4,8,128]{3,2,1,0:T(8,128)}, u32[]{:S(2)}, u32[]{:S(2)}) %collective-permute-start.9) | collective-permute-done | bytes 589856 | tf_op jit(solution)/shard_map/ppermute | solution.py:515
  86.2 0.7 constant_dynamic-slice_fusion.4
  86.9 1.0 constant_dynamic-slice_fusion.5
  87.9 0.4 collective-permute-start.12
  88.4 0.7 collective-permute-start.13
  89.1 0.0 copy-start.7
  89.1 1.6 copy-done.7
  90.7 0.9 copy-done.11
  91.6 6.6 %shard_map.70 = (f32[40,24,8,128]{3,2,1,0:T(8,128)S(1)}, f32[40,20,8,128]{3,2,1,0:T(8,128)S(1)}, f32[32,20,8,128]{3,2,1,0:T(8,128)S(1)}, f32[32,16,8,128]{3,2,1,...) custom-call(bf16[256,256]{1,0:T(8,128)(2,1)S(1)} %copy-done.9, ...), custom_call_target="tpu_custom_call" | custom-call | tf_op jit(solution)/shard_map/pallas_call | solution.py:493
  98.3 0.0 collective-permute-done.10.ya
  98.3 0.0 collective-permute-done.12.da
  98.3 0.0 collective-permute-done.13.db
  98.3 0.0 collective-permute-done.11.ca
  98.3 6.3 %shard_map.71 = (f32[40,24,8,128]{3,2,1,0:T(8,128)S(1)}, f32[40,20,8,128]{3,2,1,0:T(8,128)S(1)}, f32[32,20,8,128]{3,2,1,0:T(8,128)S(1)}, f32[32,16,8,128]{3,2,1,...) custom-call(bf16[256,256]{1,0:T(8,128)(2,1)S(1)} %copy-done.9, ...), custom_call_target="tpu_custom_call", output_to_operand_aliasing={{0}: (13, {}), {1}: (14, {}), {2}: (15, {}), {3}: (16, {}),... | custom-call | tf_op jit(solution)/shard_map/pallas_call | solution.py:493
  104.6 0.7 collective-permute-start.16
  105.3 11.1 %collective-permute-start.17 = (f32[8,16,8,128]{3,2,1,0:T(8,128)S(1)}, f32[8,16,8,128]{3,2,1,0:T(8,128)S(1)}, u32[]{:S(2)}, u32[]{:S(2)}) collective-permute-start(f32[8,16,8,128]{3,2,1,0:T(8,128)S(1)} %get-tuple-element.88), channel_id=1, source_target_pairs={{0,16},{16,0},{32,48},{48,32},{64,80},{80,64},{96,112},{112,96},{1... | collective-permute-start | bytes 1572872 | tf_op jit(solution)/shard_map/ppermute | solution.py:515
  116.4 2.6 %collective-permute-start.14 = (f32[32,4,8,128]{3,2,1,0:T(8,128)S(1)}, f32[32,4,8,128]{3,2,1,0:T(8,128)S(1)}, u32[]{:S(2)}, u32[]{:S(2)}) collective-permute-start(f32[32,4,8,128]{3,2,1,0:T(8,128)S(1)} %get-tuple-element.85), channel_id=1, source_target_pairs={{1,2},{2,1},{3,4},{4,3},{5,6},{6,5},{7,8},{8,7},{9,10},{10,9},{11,... | collective-permute-start | bytes 1572872 | tf_op jit(solution)/shard_map/ppermute | solution.py:515
  119.0 0.1 collective-permute-start.15
  119.1 0.0 collective-permute-done.16.xb
  119.1 3.9 %collective-permute-done.17.xa = f32[8,16,8,128]{3,2,1,0:T(8,128)S(1)} collective-permute-done((f32[8,16,8,128]{3,2,1,0:T(8,128)S(1)}, f32[8,16,8,128]{3,2,1,0:T(8,128)S(1)}, u32[]{:S(2)}, u32[]{:S(2)}) %collective-permute-start.17) | collective-permute-done | bytes 524320 | tf_op jit(solution)/shard_map/ppermute | solution.py:515
  123.0 0.1 collective-permute-start.18
  123.1 8.0 %collective-permute-done.14.yb = f32[32,4,8,128]{3,2,1,0:T(8,128)S(1)} collective-permute-done((f32[32,4,8,128]{3,2,1,0:T(8,128)S(1)}, f32[32,4,8,128]{3,2,1,0:T(8,128)S(1)}, u32[]{:S(2)}, u32[]{:S(2)}) %collective-permute-start.14) | collective-permute-done | bytes 524320 | tf_op jit(solution)/shard_map/ppermute | solution.py:515
  131.1 0.7 collective-permute-start.20
  131.8 4.9 %collective-permute-start.19 = (f32[8,4,8,128]{3,2,1,0:T(8,128)S(1)}, f32[8,4,8,128]{3,2,1,0:T(8,128)S(1)}, u32[]{:S(2)}, u32[]{:S(2)}) collective-permute-start(f32[8,4,8,128]{3,2,1,0:T(8,128)S(1)} %get-tuple-element.106), channel_id=1, source_target_pairs={{0,16},{16,0},{32,48},{48,32},{64,80},{80,64},{96,112},{112,96},{1... | collective-permute-start | bytes 393224 | tf_op jit(solution)/shard_map/ppermute | solution.py:515
  136.7 6.0 %shard_map.72 = (f32[40,24,8,128]{3,2,1,0:T(8,128)S(1)}, f32[40,20,8,128]{3,2,1,0:T(8,128)S(1)}, f32[32,20,8,128]{3,2,1,0:T(8,128)S(1)}, f32[32,16,8,128]{3,2,1,0:T(8,128)S(1)}, f32[2,8,128]{2,1,0:T(8,128)S(1)}) custom-call(bf16[256,256]{1,0:T(8,128)(2,1)S(1)} %copy-done.9, f32[8,128]{1,0:T(8,128)S(1)} %get-tuple-element.52.wb, ...), custom_call_target="tpu_custom_call" | custom-call | tf_op jit(solution)/shard_map/pallas_call | solution.py:493
  142.7 0.0 collective-permute-done.15.ya
  142.7 0.0 collective-permute-done.18.ca
  142.8 5.1 %shard_map.73 = (f32[40,24,8,128]{3,2,1,0:T(8,128)S(1)}, f32[40,20,8,128]{3,2,1,0:T(8,128)S(1)}, f32[32,20,8,128]{3,2,1,0:T(8,128)S(1)}, f32[32,16,8,128]{3,2,1,...) custom-call(bf16[256,256]{1,0:T(8,128)(2,1)S(1)} %copy-done.9, ...), custom_call_target="tpu_custom_call", output_to_operand_aliasing={{0}: (14, {}), {1}: (15, {}), {2}: (16, {}), {3}: (17, {}),... | custom-call | tf_op jit(solution)/shard_map/pallas_call | solution.py:493
  147.9 34.2 %all_to_all.5.heard = f32[128,8,128]{2,1,0:T(8,128)S(1)} all-to-all(f32[128,8,128]{2,1,0:T(8,128)S(1)} %broadcast_in_dim.2), channel_id=1, replica_groups=mesh['gx'=8,'gy'=16] {'gx','gy'}, dimensions={0} | all-to-all | bytes 1048576 | tf_op jit(solution)/shard_map/all_to_all | solution.py:541
  182.1 5.7 %shard_map.74 = (f32[256,2048]{1,0:T(8,128)}, f32[32,2048]{1,0:T(8,128)}, f32[8,128]{1,0:T(8,128)S(1)}) custom-call(f32[8,128]{1,0:T(8,128)S(1)} %get-tuple-element.52.wb, f32[128,8,128]{2,1,0:T(8,128)S(1)} %all_to_all.5.heard, f32[16,32,128]{2,1,0:T(8,128)} %get-tuple-element.96.q_far, f32[32,16,8,128]{3,2,1,0:T(8,128)} %get-tuple-element.97.gp_far, ...), custom_call_target="tpu_custom_call" | custom-call | tf_op jit(solution)/shard_map/pallas_call | solution.py:493
  187.8 0.6 slice_reduce_fusion
  (32 shorter events, 0.2 us)
Async XLA Ops:
  0.6 32.6 %copy-start.9 = (bf16[256,256]{1,0:T(8,128)(2,1)S(1)}, bf16[256,256]{1,0:T(8,128)(2,1)}, u32[]{:S(2)}) copy-start(bf16[256,256]{1,0:T(8,128)(2,1)} %constant.35.clone.w_ref) | copy-start | bytes 393220
  0.6 0.7 copy-start.12
  7.4 11.3 %collective-permute-start.2 = (f32[8,16,8,128]{3,2,1,0:T(8,128)}, f32[8,16,8,128]{3,2,1,0:T(8,128)S(1)}, u32[]{:S(2)}, u32[]{:S(2)}) collective-permute-start(f32[8,16,8,128]{3,2,1,0:T(8,128)} %get-tuple-element.56), channel_id=1, source_target_pairs={{16,32},{32,16},{48,64},{64,48},{80,96},{96,80},{17,33},{33,17},{4... | collective-permute-start | bytes 1572872 | tf_op jit(solution)/shard_map/ppermute | solution.py:515
  8.1 16.4 %collective-permute-start.3 = (f32[8,16,8,128]{3,2,1,0:T(8,128)}, f32[8,16,8,128]{3,2,1,0:T(8,128)}, u32[]{:S(2)}, u32[]{:S(2)}) collective-permute-start(f32[8,16,8,128]{3,2,1,0:T(8,128)} %get-tuple-element.57), channel_id=1, source_target_pairs={{0,16},{16,0},{32,48},{48,32},{64,80},{80,64},{96,112},{112,96},{1... | collective-permute-start | bytes 1572872 | tf_op jit(solution)/shard_map/ppermute | solution.py:515
  12.8 17.1 %collective-permute-start = (f32[32,4,8,128]{3,2,1,0:T(8,128)}, f32[32,4,8,128]{3,2,1,0:T(8,128)S(1)}, u32[]{:S(2)}, u32[]{:S(2)}) collective-permute-start(f32[32,4,8,128]{3,2,1,0:T(8,128)} %get-tuple-element.54), channel_id=1, source_target_pairs={{1,2},{2,1},{3,4},{4,3},{5,6},{6,5},{7,8},{8,7},{9,10},{10,9},{11,... | collective-permute-start | bytes 1572872 | tf_op jit(solution)/shard_map/ppermute | solution.py:515
  18.6 21.8 %collective-permute-start.1 = (f32[32,4,8,128]{3,2,1,0:T(8,128)}, f32[32,4,8,128]{3,2,1,0:T(8,128)}, u32[]{:S(2)}, u32[]{:S(2)}) collective-permute-start(f32[32,4,8,128]{3,2,1,0:T(8,128)} %get-tuple-element.55), channel_id=1, source_target_pairs={{0,1},{1,0},{2,3},{3,2},{4,5},{5,4},{6,7},{7,6},{8,9},{9,8},{10,11... | collective-permute-start | bytes 1572872 | tf_op jit(solution)/shard_map/ppermute | solution.py:515
  26.1 14.3 %collective-permute-start.4 = (f32[16,4,8,128]{3,2,1,0:T(8,128)}, f32[16,4,8,128]{3,2,1,0:T(8,128)S(1)}, u32[]{:S(2)}, u32[]{:S(2)}) collective-permute-start(f32[16,4,8,128]{3,2,1,0:T(8,128)} %pad_maximum_fusion.1), channel_id=1, source_target_pairs={{0,1},{1,0},{2,3},{3,2},{4,5},{5,4},{6,7},{7,6},{8,9},{9,8},{10,11... | collective-permute-start | bytes 786440 | tf_op jit(solution)/shard_map/ppermute | solution.py:515
  30.0 10.4 %collective-permute-start.6 = (f32[8,4,8,128]{3,2,1,0:T(8,128)S(1)}, f32[8,4,8,128]{3,2,1,0:T(8,128)S(1)}, u32[]{:S(2)}, u32[]{:S(2)}) collective-permute-start(f32[8,4,8,128]{3,2,1,0:T(8,128)S(1)} %get-tuple-element.107), channel_id=1, source_target_pairs={{16,32},{32,16},{48,64},{64,48},{80,96},{96,80},{17,33},{33,17},{4... | collective-permute-start | bytes 393224 | tf_op jit(solution)/shard_map/ppermute | solution.py:515
  30.7 9.7 %collective-permute-start.5 = (f32[8,4,8,128]{3,2,1,0:T(8,128)S(1)}, f32[8,4,8,128]{3,2,1,0:T(8,128)S(1)}, u32[]{:S(2)}, u32[]{:S(2)}) collective-permute-start(f32[8,4,8,128]{3,2,1,0:T(8,128)S(1)} %get-tuple-element.108), channel_id=1, source_target_pairs={{0,16},{16,0},{32,48},{48,32},{64,80},{80,64},{96,112},{112,96},{1... | collective-permute-start | bytes 393224 | tf_op jit(solution)/shard_map/ppermute | solution.py:515
  33.3 7.2 %copy-start.10 = (f32[32,2048]{1,0:T(8,128)S(1)}, f32[32,2048]{1,0:T(8,128)}, u32[]{:S(2)}) copy-start(f32[32,2048]{1,0:T(8,128)} %cot.5) | copy-start | bytes 786436
  47.1 1.7 copy-start
  48.8 1.7 copy-start.2
  50.5 1.3 copy-start.4
  51.8 1.3 copy-start.6
  53.1 0.8 copy-start.13
  53.9 17.5 %collective-permute-start.7 = (f32[9,16,8,128]{3,2,1,0:T(8,128)}, f32[9,16,8,128]{3,2,1,0:T(8,128)S(1)}, u32[]{:S(2)}, u32[]{:S(2)}) collective-permute-start(f32[9,16,8,128]{3,2,1,0:T(8,128)} %get-tuple-element.69), channel_id=1, source_target_pairs={{16,32},{32,16},{48,64},{64,48},{80,96},{96,80},{17,33},{33,17},{4... | collective-permute-start | bytes 1769480 | tf_op jit(solution)/shard_map/ppermute | solution.py:515
  54.6 20.6 %collective-permute-start.8 = (f32[9,16,8,128]{3,2,1,0:T(8,128)}, f32[9,16,8,128]{3,2,1,0:T(8,128)S(1)}, u32[]{:S(2)}, u32[]{:S(2)}) collective-permute-start(f32[9,16,8,128]{3,2,1,0:T(8,128)} %get-tuple-element.70), channel_id=1, source_target_pairs={{0,16},{16,0},{32,48},{48,32},{64,80},{80,64},{96,112},{112,96},{1... | collective-permute-start | bytes 1769480 | tf_op jit(solution)/shard_map/ppermute | solution.py:515
  67.7 18.5 %collective-permute-start.9 = (f32[36,4,8,128]{3,2,1,0:T(8,128)}, f32[36,4,8,128]{3,2,1,0:T(8,128)}, u32[]{:S(2)}, u32[]{:S(2)}) collective-permute-start(f32[36,4,8,128]{3,2,1,0:T(8,128)} %get-tuple-element.71), channel_id=1, source_target_pairs={{1,2},{2,1},{3,4},{4,3},{5,6},{6,5},{7,8},{8,7},{9,10},{10,9},{11,... | collective-permute-start | bytes 1769480 | tf_op jit(solution)/shard_map/ppermute | solution.py:515
  71.3 17.8 %copy-start.5 = (f32[32,16,8,128]{3,2,1,0:T(8,128)S(1)}, f32[32,16,8,128]{3,2,1,0:T(8,128)}, u32[]{:S(2)}) copy-start(f32[32,16,8,128]{3,2,1,0:T(8,128)} %copy-done.4) | copy-start | bytes 6291460
  71.3 26.9 %collective-permute-start.10 = (f32[36,4,8,128]{3,2,1,0:T(8,128)}, f32[36,4,8,128]{3,2,1,0:T(8,128)S(1)}, u32[]{:S(2)}, u32[]{:S(2)}) collective-permute-start(f32[36,4,8,128]{3,2,1,0:T(8,128)} %copy-done.13), channel_id=1, source_target_pairs={{0,1},{1,0},{2,3},{3,2},{4,5},{5,4},{6,7},{7,6},{8,9},{9,8},{10,11... | collective-permute-start | bytes 1769480 | tf_op jit(solution)/shard_map/ppermute | solution.py:515
  75.2 23.1 %collective-permute-start.11 = (f32[18,4,8,128]{3,2,1,0:T(8,128)S(1)}, f32[18,4,8,128]{3,2,1,0:T(8,128)S(1)}, u32[]{:S(2)}, u32[]{:S(2)}) collective-permute-start(f32[18,4,8,128]{3,2,1,0:T(8,128)S(1)} %pad_maximum_fusion), channel_id=1, source_target_pairs={{0,1},{1,0},{2,3},{3,2},{4,5},{5,4},{6,7},{7,6},{8,9},{9,8},{10,11... | collective-permute-start | bytes 884744 | tf_op jit(solution)/shard_map/ppermute | solution.py:515
  87.9 10.3 %collective-permute-start.12 = (f32[9,4,8,128]{3,2,1,0:T(8,128)S(1)}, f32[9,4,8,128]{3,2,1,0:T(8,128)S(1)}, u32[]{:S(2)}, u32[]{:S(2)}) collective-permute-start(f32[9,4,8,128]{3,2,1,0:T(8,128)S(1)} %pad_maximum_fusion.3), channel_id=1, source_target_pairs={{0,16},{16,0},{32,48},{48,32},{64,80},{80,64},{96,112},{112,96},{1... | collective-permute-start | bytes 442376 | tf_op jit(solution)/shard_map/ppermute | solution.py:515
  88.4 9.9 %collective-permute-start.13 = (f32[9,4,8,128]{3,2,1,0:T(8,128)S(1)}, f32[9,4,8,128]{3,2,1,0:T(8,128)S(1)}, u32[]{:S(2)}, u32[]{:S(2)}) collective-permute-start(f32[9,4,8,128]{3,2,1,0:T(8,128)S(1)} %pad_maximum_fusion.4), channel_id=1, source_target_pairs={{16,32},{32,16},{48,64},{64,48},{80,96},{96,80},{17,33},{33,17},{4... | collective-permute-start | bytes 442376 | tf_op jit(solution)/shard_map/ppermute | solution.py:515
  89.1 1.6 copy-start.7
  90.7 0.9 copy-start.11
  91.6 6.7 %copy-start.8 = (f32[32,16,8,128]{3,2,1,0:T(8,128)S(1)}, f32[32,16,8,128]{3,2,1,0:T(8,128)}, u32[]{:S(2)}) copy-start(f32[32,16,8,128]{3,2,1,0:T(8,128)} %copy-done.6) | copy-start | bytes 6291460
  98.3 38.4 %copy-start.1 = (f32[40,20,8,128]{3,2,1,0:T(8,128)S(1)}, f32[40,20,8,128]{3,2,1,0:T(8,128)}, u32[]{:S(2)}) copy-start(f32[40,20,8,128]{3,2,1,0:T(8,128)} %copy-done) | copy-start | bytes 9830404
  98.3 38.4 %copy-start.3 = (f32[40,20,8,128]{3,2,1,0:T(8,128)S(1)}, f32[40,20,8,128]{3,2,1,0:T(8,128)}, u32[]{:S(2)}) copy-start(f32[40,20,8,128]{3,2,1,0:T(8,128)} %copy-done.2) | copy-start | bytes 9830404
  104.6 14.4 %collective-permute-start.16 = (f32[8,16,8,128]{3,2,1,0:T(8,128)S(1)}, f32[8,16,8,128]{3,2,1,0:T(8,128)S(1)}, u32[]{:S(2)}, u32[]{:S(2)}) collective-permute-start(f32[8,16,8,128]{3,2,1,0:T(8,128)S(1)} %get-tuple-element.87), channel_id=1, source_target_pairs={{16,32},{32,16},{48,64},{64,48},{80,96},{96,80},{17,33},{33,17},{4... | collective-permute-start | bytes 1572872 | tf_op jit(solution)/shard_map/ppermute | solution.py:515
  105.3 17.6 %collective-permute-start.17 = (f32[8,16,8,128]{3,2,1,0:T(8,128)S(1)}, f32[8,16,8,128]{3,2,1,0:T(8,128)S(1)}, u32[]{:S(2)}, u32[]{:S(2)}) collective-permute-start(f32[8,16,8,128]{3,2,1,0:T(8,128)S(1)} %get-tuple-element.88), channel_id=1, source_target_pairs={{0,16},{16,0},{32,48},{48,32},{64,80},{80,64},{96,112},{112,96},{1... | collective-permute-start | bytes 1572872 | tf_op jit(solution)/shard_map/ppermute | solution.py:515
  116.4 14.7 %collective-permute-start.14 = (f32[32,4,8,128]{3,2,1,0:T(8,128)S(1)}, f32[32,4,8,128]{3,2,1,0:T(8,128)S(1)}, u32[]{:S(2)}, u32[]{:S(2)}) collective-permute-start(f32[32,4,8,128]{3,2,1,0:T(8,128)S(1)} %get-tuple-element.85), channel_id=1, source_target_pairs={{1,2},{2,1},{3,4},{4,3},{5,6},{6,5},{7,8},{8,7},{9,10},{10,9},{11,... | collective-permute-start | bytes 1572872 | tf_op jit(solution)/shard_map/ppermute | solution.py:515
  119.0 23.8 %collective-permute-start.15 = (f32[32,4,8,128]{3,2,1,0:T(8,128)S(1)}, f32[32,4,8,128]{3,2,1,0:T(8,128)S(1)}, u32[]{:S(2)}, u32[]{:S(2)}) collective-permute-start(f32[32,4,8,128]{3,2,1,0:T(8,128)S(1)} %get-tuple-element.86), channel_id=1, source_target_pairs={{0,1},{1,0},{2,3},{3,2},{4,5},{5,4},{6,7},{7,6},{8,9},{9,8},{10,11... | collective-permute-start | bytes 1572872 | tf_op jit(solution)/shard_map/ppermute | solution.py:515
  123.0 19.8 %collective-permute-start.18 = (f32[16,4,8,128]{3,2,1,0:T(8,128)S(1)}, f32[16,4,8,128]{3,2,1,0:T(8,128)S(1)}, u32[]{:S(2)}, u32[]{:S(2)}) collective-permute-start(f32[16,4,8,128]{3,2,1,0:T(8,128)S(1)} %pad_maximum_fusion.2), channel_id=1, source_target_pairs={{0,1},{1,0},{2,3},{3,2},{4,5},{5,4},{6,7},{7,6},{8,9},{9,8},{10,11... | collective-permute-start | bytes 786440 | tf_op jit(solution)/shard_map/ppermute | solution.py:515
  131.1 11.6 %collective-permute-start.20 = (f32[8,4,8,128]{3,2,1,0:T(8,128)S(1)}, f32[8,4,8,128]{3,2,1,0:T(8,128)S(1)}, u32[]{:S(2)}, u32[]{:S(2)}) collective-permute-start(f32[8,4,8,128]{3,2,1,0:T(8,128)S(1)} %get-tuple-element.105), channel_id=1, source_target_pairs={{16,32},{32,16},{48,64},{64,48},{80,96},{96,80},{17,33},{33,17},{4... | collective-permute-start | bytes 393224 | tf_op jit(solution)/shard_map/ppermute | solution.py:515
  131.8 10.9 %collective-permute-start.19 = (f32[8,4,8,128]{3,2,1,0:T(8,128)S(1)}, f32[8,4,8,128]{3,2,1,0:T(8,128)S(1)}, u32[]{:S(2)}, u32[]{:S(2)}) collective-permute-start(f32[8,4,8,128]{3,2,1,0:T(8,128)S(1)} %get-tuple-element.106), channel_id=1, source_target_pairs={{0,16},{16,0},{32,48},{48,32},{64,80},{80,64},{96,112},{112,96},{1... | collective-permute-start | bytes 393224 | tf_op jit(solution)/shard_map/ppermute | solution.py:515

commit v10 on v8

--- a/solution.py
+++ b/solution.py
@@ -481,7 +481,8 @@
     back = jnp.sum((everyone + offsets) * turned, axis=0)
     weight_grad = scale * (total[:, 1:2] + back[:, 3:4] + total[:, 4:5] + back[:, 6:7])
     grad = weights * (weight_grad - jnp.sum(weights * weight_grad, axis=0, keepdims=True))
-    theta_out[...] = jnp.broadcast_to(grad, (K, L))
+    for k in range(K):
+        theta_out[k] = grad[k, 0]
     for c in copies:
         c.wait()
 
@@ -494,7 +495,7 @@
         kernel,
         out_shape=outs,
         in_specs=[pl.BlockSpec(memory_space=pltpu.SMEM)] * len(numbers) + [vmem] * near + [far] * far_in,
-        out_specs=[far if i in near_out else vmem for i in range(len(outs))],
+        out_specs=[far if i in near_out else vmem if len(o.shape) > 1 else pl.BlockSpec(memory_space=pltpu.SMEM) for i, o in enumerate(outs)],
         scratch_shapes=[pltpu.VMEM(s, F32) for s in scratch] + [pltpu.SemaphoreType.DMA((n,)) for n in semaphores],
         input_output_aliases=same or {},
         compiler_params=pltpu.CompilerParams(vmem_limit_bytes=VMEM),
@@ -579,12 +580,12 @@
         third_outer, near(*held) + [pltpu.HBM(field, F32), pltpu.HBM(q_shape, F32)] + near(small), [ends], [4],
         [w, wb, mean, told, inv_a, v, e, bu, q, *others, *held_now], (5, 6), same={14 + i: i for i in range(5)},
     )
-    plain = [jax.ShapeDtypeStruct(s, F32) for s in ((K * rows, merged), (rows, merged), small)]
+    plain = [jax.ShapeDtypeStruct(s, F32) for s in ((K * rows, merged), (rows, merged), (K,))]
     grad, bary, grad_theta = call(
         functools.partial(last_kernel, cells), plain, [turn, field, field, q_shape], [tiles + tiles // 2 + 1],
         [wb, over_all(told), q_far, gp_far, dens], (0,), 3,
     )
-    return bary, grad.reshape(K, rows, merged), grad_theta[:, 0]
+    return bary, grad.reshape(K, rows, merged), grad_theta
 
 
 def solution(mesh):

time: 158 us -> 157 us (level)
  no operation moved by 1% of the time
where the time goes in v10:
time: 157 us
  starting transfers between devices  58.7 us (37%)
  Pallas kernels  45.4 us (29%)
  blocking collectives  34.2 us (22%)
  waiting for transfers between devices  16.6 us (11%)
    pallas_call x8, Pallas kernels, call(): pl.pallas_call(kernel, out_shape=outs, in_specs=[pl.BlockSpec(memory_spac...  45.4 us
    all_to_all x1, blocking collectives, over_all(): lax.all_to_all(jnp.broadcast_to(told[None], (devices, K, L)), ('gx', 'gy'...  34.2 us
    ppermute x6, starting transfers between devices, swap_diagonal(): return lax.ppermute(value, ('gx', 'gy'), pairs)  32.1 us
    ppermute x15, starting transfers between devices, swap(): return lax.ppermute(value, axis, list(partners(axis, parity).items()))  26.6 us
    ppermute x15, waiting for transfers between devices, swap(): return lax.ppermute(value, axis, list(partners(axis, parity).items()))  14.3 us
  transfers between devices with their start and end apart: 21, of which 5 were waited for; matrix products, arithmetic and copies ran while one was open for 0% of the time, Pallas kernels for 12%

profile of v10, /device:TPU:1, one launch (start us, length us, event | category | flops | bytes accessed | tf_op | source)
XLA Modules:
  0.0 156.9 jit_solution(10609264172417137868)
XLA Ops:
  0.6 0.0 copy-start
  0.6 0.0 copy-start.2
  0.7 0.7 copy-done.2
  1.3 6.0 %shard_map.67 = (f32[32,16,8,128]{3,2,1,0:T(8,128)}, f32[32,16,8,128]{3,2,1,0:T(8,128)S(1)}, f32[8,128]{1,0:T(8,128)S(1)}, f32[8,128]{1,0:T(8,128)S(1)}, f32[8,1...) custom-call(f32[8]{0:T(128)S(1)} %copy-done.2, ...), custom_call_target="tpu_custom_call" | custom-call | tf_op jit(solution)/shard_map/pallas_call | solution.py:494
  7.4 0.7 collective-permute-start.2
  8.1 4.7 %collective-permute-start.3 = (f32[8,16,8,128]{3,2,1,0:T(8,128)}, f32[8,16,8,128]{3,2,1,0:T(8,128)S(1)}, u32[]{:S(2)}, u32[]{:S(2)}) collective-permute-start(f32[8,16,8,128]{3,2,1,0:T(8,128)} %get-tuple-element.75), channel_id=1, source_target_pairs={{0,16},{16,0},{32,48},{48,32},{64,80},{80,64},{96,112},{112,96},{1... | collective-permute-start | bytes 1572872 | tf_op jit(solution)/shard_map/ppermute | solution.py:516
  12.8 0.7 collective-permute-start.4
  13.5 7.7 %collective-permute-start.5 = (f32[8,4,8,128]{3,2,1,0:T(8,128)}, f32[8,4,8,128]{3,2,1,0:T(8,128)S(1)}, u32[]{:S(2)}, u32[]{:S(2)}) collective-permute-start(f32[8,4,8,128]{3,2,1,0:T(8,128)} %get-tuple-element.77), channel_id=1, source_target_pairs={{1,18},{2,17},{3,20},{4,19},{5,22},{6,21},{7,24},{8,23},{9,26},{10... | collective-permute-start | bytes 393224 | tf_op jit(solution)/shard_map/ppermute | solution.py:522
  21.2 5.5 %collective-permute-start = (f32[32,4,8,128]{3,2,1,0:T(8,128)}, f32[32,4,8,128]{3,2,1,0:T(8,128)}, u32[]{:S(2)}, u32[]{:S(2)}) collective-permute-start(f32[32,4,8,128]{3,2,1,0:T(8,128)} %get-tuple-element.72), channel_id=1, source_target_pairs={{1,2},{2,1},{3,4},{4,3},{5,6},{6,5},{7,8},{8,7},{9,10},{10,9},{11,... | collective-permute-start | bytes 1572872 | tf_op jit(solution)/shard_map/ppermute | solution.py:516
  26.7 0.0 collective-permute-done.4.db
  26.7 0.1 collective-permute-start.1
  26.8 0.0 collective-permute-done.5.da
  26.8 0.0 collective-permute-done.2.xb
  26.8 0.4 collective-permute-done.3.xa
  27.2 1.6 %collective-permute-start.6 = (f32[16,4,8,128]{3,2,1,0:T(8,128)S(1)}, f32[16,4,8,128]{3,2,1,0:T(8,128)S(1)}, u32[]{:S(2)}, u32[]{:S(2)}) collective-permute-start(f32[16,4,8,128]{3,2,1,0:T(8,128)S(1)} %pad_maximum_fusion.1), channel_id=1, source_target_pairs={{0,1},{1,0},{2,3},{3,2},{4,5},{5,4},{6,7},{7,6},{8,9},{9,8},{10,11... | collective-permute-start | bytes 786440 | tf_op jit(solution)/shard_map/ppermute | solution.py:516
  28.8 0.0 copy-done
  28.8 0.0 copy-start.1
  28.8 6.0 %shard_map.68 = (f32[40,24,8,128]{3,2,1,0:T(8,128)S(1)}, f32[40,20,8,128]{3,2,1,0:T(8,128)S(1)}, f32[40,20,8,128]{3,2,1,0:T(8,128)S(1)}, f32[32,20,8,128]{3,2,1,...) custom-call(bf16[256,256]{1,0:T(8,128)(2,1)S(1)} %copy-done, ...), custom_call_target="tpu_custom_call" | custom-call | tf_op jit(solution)/shard_map/pallas_call | solution.py:494
  34.8 2.8 %collective-permute-done.yb = f32[32,4,8,128]{3,2,1,0:T(8,128)} collective-permute-done((f32[32,4,8,128]{3,2,1,0:T(8,128)}, f32[32,4,8,128]{3,2,1,0:T(8,128)}, u32[]{:S(2)}, u32[]{:S(2)}) %collective-permute-start) | collective-permute-done | bytes 524320 | tf_op jit(solution)/shard_map/ppermute | solution.py:516
  37.6 0.0 collective-permute-done.1.ya
  37.6 0.0 collective-permute-done.6.ca
  37.6 0.0 copy-done.1
  37.6 5.5 %shard_map.69 = (f32[40,24,8,128]{3,2,1,0:T(8,128)S(1)}, f32[40,20,8,128]{3,2,1,0:T(8,128)S(1)}, f32[40,20,8,128]{3,2,1,0:T(8,128)S(1)}, f32[32,20,8,128]{3,2,1,...) custom-call(bf16[256,256]{1,0:T(8,128)(2,1)S(1)} %copy-done, ...), custom_call_target="tpu_custom_call", output_to_operand_aliasing={{0}: (9, {}), {1}: (10, {}), {2}: (11, {}), {3}: (12, {}), ... | custom-call | tf_op jit(solution)/shard_map/pallas_call | solution.py:494
  43.2 0.7 collective-permute-start.7
  43.9 4.3 %collective-permute-start.8 = (f32[9,16,8,128]{3,2,1,0:T(8,128)S(1)}, f32[9,16,8,128]{3,2,1,0:T(8,128)S(1)}, u32[]{:S(2)}, u32[]{:S(2)}) collective-permute-start(f32[9,16,8,128]{3,2,1,0:T(8,128)S(1)} %get-tuple-element.94), channel_id=1, source_target_pairs={{0,16},{16,0},{32,48},{48,32},{64,80},{80,64},{96,112},{112,96},{1... | collective-permute-start | bytes 1769480 | tf_op jit(solution)/shard_map/ppermute | solution.py:516
  48.2 0.7 collective-permute-start.9
  48.8 12.5 %collective-permute-start.10 = (f32[9,4,8,128]{3,2,1,0:T(8,128)S(1)}, f32[9,4,8,128]{3,2,1,0:T(8,128)S(1)}, u32[]{:S(2)}, u32[]{:S(2)}) collective-permute-start(f32[9,4,8,128]{3,2,1,0:T(8,128)S(1)} %get-tuple-element.96), channel_id=1, source_target_pairs={{1,18},{2,17},{3,20},{4,19},{5,22},{6,21},{7,24},{8,23},{9,26},{10... | collective-permute-start | bytes 442376 | tf_op jit(solution)/shard_map/ppermute | solution.py:522
  61.3 2.9 %collective-permute-start.11 = (f32[36,4,8,128]{3,2,1,0:T(8,128)S(1)}, f32[36,4,8,128]{3,2,1,0:T(8,128)S(1)}, u32[]{:S(2)}, u32[]{:S(2)}) collective-permute-start(f32[36,4,8,128]{3,2,1,0:T(8,128)S(1)} %get-tuple-element.99), channel_id=1, source_target_pairs={{1,2},{2,1},{3,4},{4,3},{5,6},{6,5},{7,8},{8,7},{9,10},{10,9},{11,... | collective-permute-start | bytes 1769480 | tf_op jit(solution)/shard_map/ppermute | solution.py:516
  64.3 0.0 collective-permute-done.9.db
  64.3 0.1 collective-permute-start.12
  64.4 2.3 %collective-permute-done.10.da = f32[9,4,8,128]{3,2,1,0:T(8,128)S(1)} collective-permute-done((f32[9,4,8,128]{3,2,1,0:T(8,128)S(1)}, f32[9,4,8,128]{3,2,1,0:T(8,128)S(1)}, u32[]{:S(2)}, u32[]{:S(2)}) %collective-permute-start.10) | collective-permute-done | bytes 147488 | tf_op jit(solution)/shard_map/ppermute | solution.py:522
  66.6 0.0 collective-permute-done.7.xb
  66.6 0.0 collective-permute-done.8.xa
  66.7 0.1 collective-permute-start.13
  66.8 6.7 %shard_map.70 = (f32[40,24,8,128]{3,2,1,0:T(8,128)S(1)}, f32[40,20,8,128]{3,2,1,0:T(8,128)S(1)}, f32[32,20,8,128]{3,2,1,0:T(8,128)S(1)}, f32[32,16,8,128]{3,2,1,...) custom-call(bf16[256,256]{1,0:T(8,128)(2,1)S(1)} %copy-done, ...), custom_call_target="tpu_custom_call" | custom-call | tf_op jit(solution)/shard_map/pallas_call | solution.py:494
  73.5 6.8 %collective-permute-done.11.yb = f32[36,4,8,128]{3,2,1,0:T(8,128)S(1)} collective-permute-done((f32[36,4,8,128]{3,2,1,0:T(8,128)S(1)}, f32[36,4,8,128]{3,2,1,0:T(8,128)S(1)}, u32[]{:S(2)}, u32[]{:S(2)}) %collective-permute-start.11) | collective-permute-done | bytes 589856 | tf_op jit(solution)/shard_map/ppermute | solution.py:516
  80.3 0.0 collective-permute-done.12.ya
  80.3 0.0 collective-permute-done.13.ca
  80.3 4.4 %shard_map.71 = (f32[40,24,8,128]{3,2,1,0:T(8,128)S(1)}, f32[40,20,8,128]{3,2,1,0:T(8,128)S(1)}, f32[32,20,8,128]{3,2,1,0:T(8,128)S(1)}, f32[32,16,8,128]{3,2,1,...) custom-call(bf16[256,256]{1,0:T(8,128)(2,1)S(1)} %copy-done, ...), custom_call_target="tpu_custom_call", output_to_operand_aliasing={{0}: (13, {}), {1}: (14, {}), {2}: (15, {}), {3}: (16, {}),... | custom-call | tf_op jit(solution)/shard_map/pallas_call | solution.py:494
  84.7 0.7 collective-permute-start.16
  85.4 0.7 collective-permute-start.17
  86.1 0.7 collective-permute-start.18
  86.7 9.9 %collective-permute-start.19 = (f32[8,4,8,128]{3,2,1,0:T(8,128)S(1)}, f32[8,4,8,128]{3,2,1,0:T(8,128)S(1)}, u32[]{:S(2)}, u32[]{:S(2)}) collective-permute-start(f32[8,4,8,128]{3,2,1,0:T(8,128)S(1)} %get-tuple-element.120), channel_id=1, source_target_pairs={{1,18},{2,17},{3,20},{4,19},{5,22},{6,21},{7,24},{8,23},{9,26},{10... | collective-permute-start | bytes 393224 | tf_op jit(solution)/shard_map/ppermute | solution.py:522
  96.6 4.0 %collective-permute-start.14 = (f32[32,4,8,128]{3,2,1,0:T(8,128)S(1)}, f32[32,4,8,128]{3,2,1,0:T(8,128)S(1)}, u32[]{:S(2)}, u32[]{:S(2)}) collective-permute-start(f32[32,4,8,128]{3,2,1,0:T(8,128)S(1)} %get-tuple-element.115), channel_id=1, source_target_pairs={{1,2},{2,1},{3,4},{4,3},{5,6},{6,5},{7,8},{8,7},{9,10},{10,9},{11,... | collective-permute-start | bytes 1572872 | tf_op jit(solution)/shard_map/ppermute | solution.py:516
  100.6 0.0 collective-permute-done.18.db
  100.6 0.1 collective-permute-start.15
  100.7 0.0 collective-permute-done.19.da
  100.8 0.0 collective-permute-done.16.xb
  100.8 0.0 collective-permute-done.17.xa
  100.9 0.6 collective-permute-start.20
  101.4 6.0 %shard_map.72 = (f32[40,24,8,128]{3,2,1,0:T(8,128)S(1)}, f32[40,20,8,128]{3,2,1,0:T(8,128)S(1)}, f32[32,20,8,128]{3,2,1,0:T(8,128)S(1)}, f32[32,16,8,128]{3,2,1,0:T(8,128)S(1)}, f32[2,8,128]{2,1,0:T(8,128)S(1)}) custom-call(bf16[256,256]{1,0:T(8,128)(2,1)S(1)} %copy-done, f32[8,128]{1,0:T(8,128)S(1)} %get-tuple-element.70.wb, ...), custom_call_target="tpu_custom_call" | custom-call | tf_op jit(solution)/shard_map/pallas_call | solution.py:494
  107.4 4.3 %collective-permute-done.14.yb = f32[32,4,8,128]{3,2,1,0:T(8,128)S(1)} collective-permute-done((f32[32,4,8,128]{3,2,1,0:T(8,128)S(1)}, f32[32,4,8,128]{3,2,1,0:T(8,128)S(1)}, u32[]{:S(2)}, u32[]{:S(2)}) %collective-permute-start.14) | collective-permute-done | bytes 524320 | tf_op jit(solution)/shard_map/ppermute | solution.py:516
  111.7 0.0 collective-permute-done.15.ya
  111.7 0.0 collective-permute-done.20.ca
  111.7 5.0 %shard_map.73 = (f32[40,24,8,128]{3,2,1,0:T(8,128)S(1)}, f32[40,20,8,128]{3,2,1,0:T(8,128)S(1)}, f32[32,20,8,128]{3,2,1,0:T(8,128)S(1)}, f32[32,16,8,128]{3,2,1,...) custom-call(bf16[256,256]{1,0:T(8,128)(2,1)S(1)} %copy-done, ...), custom_call_target="tpu_custom_call", output_to_operand_aliasing={{0}: (14, {}), {1}: (15, {}), {2}: (16, {}), {3}: (17, {}),... | custom-call | tf_op jit(solution)/shard_map/pallas_call | solution.py:494
  116.8 34.2 %all_to_all.5.heard = f32[128,8,128]{2,1,0:T(8,128)S(1)} all-to-all(f32[128,8,128]{2,1,0:T(8,128)S(1)} %broadcast_in_dim.2), channel_id=1, replica_groups=mesh['gx'=8,'gy'=16] {'gx','gy'}, dimensions={0} | all-to-all | bytes 1048576 | tf_op jit(solution)/shard_map/all_to_all | solution.py:538
  151.0 5.7 %shard_map.74 = (f32[256,2048]{1,0:T(8,128)}, f32[32,2048]{1,0:T(8,128)}, f32[8]{0:T(128)}) custom-call(f32[8,128]{1,0:T(8,128)S(1)} %get-tuple-element.70.wb, f32[128,8,128]{2,1,0:T(8,128)S(1)} %all_to_all.5.heard, f32[16,32,128]{2,1,0:T(8,128)} %get-tuple-element.132.q_far, f32[32,16,8,128]{3,2,1,0:T(8,128)} %get-tuple-element.133.gp_far, ...), custom_call_target="tpu_custom_call" | custom-call | tf_op jit(solution)/shard_map/pallas_call | solution.py:494
  (9 shorter events, 0.2 us)
Async XLA Ops:
  0.6 28.2 %copy-start = (bf16[256,256]{1,0:T(8,128)(2,1)S(1)}, bf16[256,256]{1,0:T(8,128)(2,1)}, u32[]{:S(2)}) copy-start(bf16[256,256]{1,0:T(8,128)(2,1)} %constant.17.clone.w_ref) | copy-start | bytes 393220
  0.6 0.7 copy-start.2
  7.4 19.4 %collective-permute-start.2 = (f32[8,16,8,128]{3,2,1,0:T(8,128)}, f32[8,16,8,128]{3,2,1,0:T(8,128)S(1)}, u32[]{:S(2)}, u32[]{:S(2)}) collective-permute-start(f32[8,16,8,128]{3,2,1,0:T(8,128)} %get-tuple-element.74), channel_id=1, source_target_pairs={{16,32},{32,16},{48,64},{64,48},{80,96},{96,80},{17,33},{33,17},{4... | collective-permute-start | bytes 1572872 | tf_op jit(solution)/shard_map/ppermute | solution.py:516
  8.1 19.1 %collective-permute-start.3 = (f32[8,16,8,128]{3,2,1,0:T(8,128)}, f32[8,16,8,128]{3,2,1,0:T(8,128)S(1)}, u32[]{:S(2)}, u32[]{:S(2)}) collective-permute-start(f32[8,16,8,128]{3,2,1,0:T(8,128)} %get-tuple-element.75), channel_id=1, source_target_pairs={{0,16},{16,0},{32,48},{48,32},{64,80},{80,64},{96,112},{112,96},{1... | collective-permute-start | bytes 1572872 | tf_op jit(solution)/shard_map/ppermute | solution.py:516
  12.8 13.9 %collective-permute-start.4 = (f32[8,4,8,128]{3,2,1,0:T(8,128)S(1)}, f32[8,4,8,128]{3,2,1,0:T(8,128)S(1)}, u32[]{:S(2)}, u32[]{:S(2)}) collective-permute-start(f32[8,4,8,128]{3,2,1,0:T(8,128)S(1)} %get-tuple-element.76), channel_id=1, source_target_pairs={{17,34},{18,33},{19,36},{20,35},{21,38},{22,37},{23,40},{24,39},{2... | collective-permute-start | bytes 393224 | tf_op jit(solution)/shard_map/ppermute | solution.py:522
  13.5 13.3 %collective-permute-start.5 = (f32[8,4,8,128]{3,2,1,0:T(8,128)}, f32[8,4,8,128]{3,2,1,0:T(8,128)S(1)}, u32[]{:S(2)}, u32[]{:S(2)}) collective-permute-start(f32[8,4,8,128]{3,2,1,0:T(8,128)} %get-tuple-element.77), channel_id=1, source_target_pairs={{1,18},{2,17},{3,20},{4,19},{5,22},{6,21},{7,24},{8,23},{9,26},{10... | collective-permute-start | bytes 393224 | tf_op jit(solution)/shard_map/ppermute | solution.py:522
  21.2 16.5 %collective-permute-start = (f32[32,4,8,128]{3,2,1,0:T(8,128)}, f32[32,4,8,128]{3,2,1,0:T(8,128)}, u32[]{:S(2)}, u32[]{:S(2)}) collective-permute-start(f32[32,4,8,128]{3,2,1,0:T(8,128)} %get-tuple-element.72), channel_id=1, source_target_pairs={{1,2},{2,1},{3,4},{4,3},{5,6},{6,5},{7,8},{8,7},{9,10},{10,9},{11,... | collective-permute-start | bytes 1572872 | tf_op jit(solution)/shard_map/ppermute | solution.py:516
  26.7 11.0 %collective-permute-start.1 = (f32[32,4,8,128]{3,2,1,0:T(8,128)}, f32[32,4,8,128]{3,2,1,0:T(8,128)}, u32[]{:S(2)}, u32[]{:S(2)}) collective-permute-start(f32[32,4,8,128]{3,2,1,0:T(8,128)} %get-tuple-element.73), channel_id=1, source_target_pairs={{0,1},{1,0},{2,3},{3,2},{4,5},{5,4},{6,7},{7,6},{8,9},{9,8},{10,11... | collective-permute-start | bytes 1572872 | tf_op jit(solution)/shard_map/ppermute | solution.py:516
  27.2 10.4 %collective-permute-start.6 = (f32[16,4,8,128]{3,2,1,0:T(8,128)S(1)}, f32[16,4,8,128]{3,2,1,0:T(8,128)S(1)}, u32[]{:S(2)}, u32[]{:S(2)}) collective-permute-start(f32[16,4,8,128]{3,2,1,0:T(8,128)S(1)} %pad_maximum_fusion.1), channel_id=1, source_target_pairs={{0,1},{1,0},{2,3},{3,2},{4,5},{5,4},{6,7},{7,6},{8,9},{9,8},{10,11... | collective-permute-start | bytes 786440 | tf_op jit(solution)/shard_map/ppermute | solution.py:516
  28.8 8.8 %copy-start.1 = (f32[32,2048]{1,0:T(8,128)S(1)}, f32[32,2048]{1,0:T(8,128)}, u32[]{:S(2)}) copy-start(f32[32,2048]{1,0:T(8,128)} %cot.5) | copy-start | bytes 786436
  43.2 23.5 %collective-permute-start.7 = (f32[9,16,8,128]{3,2,1,0:T(8,128)S(1)}, f32[9,16,8,128]{3,2,1,0:T(8,128)S(1)}, u32[]{:S(2)}, u32[]{:S(2)}) collective-permute-start(f32[9,16,8,128]{3,2,1,0:T(8,128)S(1)} %get-tuple-element.93), channel_id=1, source_target_pairs={{16,32},{32,16},{48,64},{64,48},{80,96},{96,80},{17,33},{33,17},{4... | collective-permute-start | bytes 1769480 | tf_op jit(solution)/shard_map/ppermute | solution.py:516
  43.9 22.8 %collective-permute-start.8 = (f32[9,16,8,128]{3,2,1,0:T(8,128)S(1)}, f32[9,16,8,128]{3,2,1,0:T(8,128)S(1)}, u32[]{:S(2)}, u32[]{:S(2)}) collective-permute-start(f32[9,16,8,128]{3,2,1,0:T(8,128)S(1)} %get-tuple-element.94), channel_id=1, source_target_pairs={{0,16},{16,0},{32,48},{48,32},{64,80},{80,64},{96,112},{112,96},{1... | collective-permute-start | bytes 1769480 | tf_op jit(solution)/shard_map/ppermute | solution.py:516
  48.2 16.1 %collective-permute-start.9 = (f32[9,4,8,128]{3,2,1,0:T(8,128)S(1)}, f32[9,4,8,128]{3,2,1,0:T(8,128)S(1)}, u32[]{:S(2)}, u32[]{:S(2)}) collective-permute-start(f32[9,4,8,128]{3,2,1,0:T(8,128)S(1)} %get-tuple-element.95), channel_id=1, source_target_pairs={{17,34},{18,33},{19,36},{20,35},{21,38},{22,37},{23,40},{24,39},{2... | collective-permute-start | bytes 442376 | tf_op jit(solution)/shard_map/ppermute | solution.py:522
  48.8 17.8 %collective-permute-start.10 = (f32[9,4,8,128]{3,2,1,0:T(8,128)S(1)}, f32[9,4,8,128]{3,2,1,0:T(8,128)S(1)}, u32[]{:S(2)}, u32[]{:S(2)}) collective-permute-start(f32[9,4,8,128]{3,2,1,0:T(8,128)S(1)} %get-tuple-element.96), channel_id=1, source_target_pairs={{1,18},{2,17},{3,20},{4,19},{5,22},{6,21},{7,24},{8,23},{9,26},{10... | collective-permute-start | bytes 442376 | tf_op jit(solution)/shard_map/ppermute | solution.py:522
  61.3 18.9 %collective-permute-start.11 = (f32[36,4,8,128]{3,2,1,0:T(8,128)S(1)}, f32[36,4,8,128]{3,2,1,0:T(8,128)S(1)}, u32[]{:S(2)}, u32[]{:S(2)}) collective-permute-start(f32[36,4,8,128]{3,2,1,0:T(8,128)S(1)} %get-tuple-element.99), channel_id=1, source_target_pairs={{1,2},{2,1},{3,4},{4,3},{5,6},{6,5},{7,8},{8,7},{9,10},{10,9},{11,... | collective-permute-start | bytes 1769480 | tf_op jit(solution)/shard_map/ppermute | solution.py:516
  64.3 16.0 %collective-permute-start.12 = (f32[36,4,8,128]{3,2,1,0:T(8,128)S(1)}, f32[36,4,8,128]{3,2,1,0:T(8,128)S(1)}, u32[]{:S(2)}, u32[]{:S(2)}) collective-permute-start(f32[36,4,8,128]{3,2,1,0:T(8,128)S(1)} %get-tuple-element.100), channel_id=1, source_target_pairs={{0,1},{1,0},{2,3},{3,2},{4,5},{5,4},{6,7},{7,6},{8,9},{9,8},{10,11... | collective-permute-start | bytes 1769480 | tf_op jit(solution)/shard_map/ppermute | solution.py:516
  66.7 13.6 %collective-permute-start.13 = (f32[18,4,8,128]{3,2,1,0:T(8,128)S(1)}, f32[18,4,8,128]{3,2,1,0:T(8,128)S(1)}, u32[]{:S(2)}, u32[]{:S(2)}) collective-permute-start(f32[18,4,8,128]{3,2,1,0:T(8,128)S(1)} %pad_maximum_fusion), channel_id=1, source_target_pairs={{0,1},{1,0},{2,3},{3,2},{4,5},{5,4},{6,7},{7,6},{8,9},{9,8},{10,11... | collective-permute-start | bytes 884744 | tf_op jit(solution)/shard_map/ppermute | solution.py:516
  84.7 16.0 %collective-permute-start.16 = (f32[8,16,8,128]{3,2,1,0:T(8,128)S(1)}, f32[8,16,8,128]{3,2,1,0:T(8,128)S(1)}, u32[]{:S(2)}, u32[]{:S(2)}) collective-permute-start(f32[8,16,8,128]{3,2,1,0:T(8,128)S(1)} %get-tuple-element.117), channel_id=1, source_target_pairs={{16,32},{32,16},{48,64},{64,48},{80,96},{96,80},{17,33},{33,17},{4... | collective-permute-start | bytes 1572872 | tf_op jit(solution)/shard_map/ppermute | solution.py:516
  85.4 15.3 %collective-permute-start.17 = (f32[8,16,8,128]{3,2,1,0:T(8,128)S(1)}, f32[8,16,8,128]{3,2,1,0:T(8,128)S(1)}, u32[]{:S(2)}, u32[]{:S(2)}) collective-permute-start(f32[8,16,8,128]{3,2,1,0:T(8,128)S(1)} %get-tuple-element.118), channel_id=1, source_target_pairs={{0,16},{16,0},{32,48},{48,32},{64,80},{80,64},{96,112},{112,96},{1... | collective-permute-start | bytes 1572872 | tf_op jit(solution)/shard_map/ppermute | solution.py:516
  86.1 14.6 %collective-permute-start.18 = (f32[8,4,8,128]{3,2,1,0:T(8,128)S(1)}, f32[8,4,8,128]{3,2,1,0:T(8,128)S(1)}, u32[]{:S(2)}, u32[]{:S(2)}) collective-permute-start(f32[8,4,8,128]{3,2,1,0:T(8,128)S(1)} %get-tuple-element.119), channel_id=1, source_target_pairs={{17,34},{18,33},{19,36},{20,35},{21,38},{22,37},{23,40},{24,39},{2... | collective-permute-start | bytes 393224 | tf_op jit(solution)/shard_map/ppermute | solution.py:522
  86.7 14.0 %collective-permute-start.19 = (f32[8,4,8,128]{3,2,1,0:T(8,128)S(1)}, f32[8,4,8,128]{3,2,1,0:T(8,128)S(1)}, u32[]{:S(2)}, u32[]{:S(2)}) collective-permute-start(f32[8,4,8,128]{3,2,1,0:T(8,128)S(1)} %get-tuple-element.120), channel_id=1, source_target_pairs={{1,18},{2,17},{3,20},{4,19},{5,22},{6,21},{7,24},{8,23},{9,26},{10... | collective-permute-start | bytes 393224 | tf_op jit(solution)/shard_map/ppermute | solution.py:522
  96.6 15.1 %collective-permute-start.14 = (f32[32,4,8,128]{3,2,1,0:T(8,128)S(1)}, f32[32,4,8,128]{3,2,1,0:T(8,128)S(1)}, u32[]{:S(2)}, u32[]{:S(2)}) collective-permute-start(f32[32,4,8,128]{3,2,1,0:T(8,128)S(1)} %get-tuple-element.115), channel_id=1, source_target_pairs={{1,2},{2,1},{3,4},{4,3},{5,6},{6,5},{7,8},{8,7},{9,10},{10,9},{11,... | collective-permute-start | bytes 1572872 | tf_op jit(solution)/shard_map/ppermute | solution.py:516
  100.6 11.1 %collective-permute-start.15 = (f32[32,4,8,128]{3,2,1,0:T(8,128)S(1)}, f32[32,4,8,128]{3,2,1,0:T(8,128)S(1)}, u32[]{:S(2)}, u32[]{:S(2)}) collective-permute-start(f32[32,4,8,128]{3,2,1,0:T(8,128)S(1)} %get-tuple-element.116), channel_id=1, source_target_pairs={{0,1},{1,0},{2,3},{3,2},{4,5},{5,4},{6,7},{7,6},{8,9},{9,8},{10,11... | collective-permute-start | bytes 1572872 | tf_op jit(solution)/shard_map/ppermute | solution.py:516
  100.9 10.9 %collective-permute-start.20 = (f32[16,4,8,128]{3,2,1,0:T(8,128)S(1)}, f32[16,4,8,128]{3,2,1,0:T(8,128)S(1)}, u32[]{:S(2)}, u32[]{:S(2)}) collective-permute-start(f32[16,4,8,128]{3,2,1,0:T(8,128)S(1)} %pad_maximum_fusion.2), channel_id=1, source_target_pairs={{0,1},{1,0},{2,3},{3,2},{4,5},{5,4},{6,7},{7,6},{8,9},{9,8},{10,11... | collective-permute-start | bytes 786440 | tf_op jit(solution)/shard_map/ppermute | solution.py:516
